TPU v7x, 32 devices: a whole 2x2x4 slice. The times are simulated.
32 devices in a mesh: seq: 8 (over z, y), prompt: 4 (over x, core).
Axes of the slice: x: 2, y: 2, z: 4, core: 2. Of those that a mesh axis runs over, the one named last changes fastest.
Arguments:
- queries: bfloat16 [8192, 1024], P(('prompt', 'seq')), parts along dimension 0, may hold values from -6 to 6
- keys: bfloat16 [8192, 1024], P(('prompt', 'seq')), parts along dimension 0, may hold values from -6 to 6
- values: bfloat16 [8192, 1024], P(('prompt', 'seq')), parts along dimension 0, may hold values from -6 to 6
- cotangent: bfloat16 [8192, 1024], P(('prompt', 'seq')), parts along dimension 0, may hold values from -6 to 6
- restrict_one: bfloat16 [8, 256], replicated, may hold values from -0.375 to 0.375
- restrict_two: bfloat16 [4, 256], replicated, may hold values from -0.375 to 0.375
Outputs:
- attended: bfloat16 [8192, 1024], P(('prompt', 'seq')), parts along dimension 0
- grad_q: bfloat16 [8192, 1024], P(('prompt', 'seq')), parts along dimension 0
- grad_k: bfloat16 [8192, 1024], P(('prompt', 'seq')), parts along dimension 0
- grad_v: bfloat16 [8192, 1024], P(('prompt', 'seq')), parts along dimension 0
There are 4 independent parts, one for each index of `prompt`. A program takes and returns all parts, laid end to end along the dimension named above; an argument that names none is the same for every part. Nothing has to cross between parts.
All inputs are finite; a program needn't handle non-finite values.
Results may differ from a plain program's by a relative error of at most 0.02.
Values may be sent and summed in bfloat16 or wider, within the bound.
No kernel may reach another device: no remote copies, remote signals or barrier semaphores. Data moves between devices by JAX's collectives and lax.ppermute only.
A program may use at most 128 MiB of HBM per device.

v0:
```python
import math

import jax
import jax.numpy as jnp
from jax import lax
from jax.sharding import PartitionSpec as P

HEAD_DIM = 64


level_one_bias = math.log(32.0)
level_two_bias = math.log(64.0)
masked_bias = -1e30


def padded(value, sides, width):
    for axis, dim in sides:
        size, length = (lax.axis_size(axis), value.shape[dim])
        up = [(i, (i + 1) % size) for i in range(size - 1)]
        down = [(j, i) for i, j in up]
        last = lax.slice_in_dim(value, length - width, length, axis=dim)
        first = lax.slice_in_dim(value, 0, width, axis=dim)
        before = lax.ppermute(last, axis, up)
        after = lax.ppermute(first, axis, down)
        value = jnp.concatenate([before, value, after], axis=dim)
    return value


def from_behind(value, axis, by):
    size = lax.axis_size(axis)
    pairs = [(i, i + by) for i in range(size) if 0 <= i + by < size]
    return lax.ppermute(value, axis, pairs)


def key_terms(score_grad, weights, query_group, cotangent_group, lower, upper, scaling):
    grad_key = (
        jnp.einsum("hqk,qhd->khd", score_grad, query_group, preferred_element_type=jnp.float32)
        * scaling
    )
    grad_value = jnp.einsum(
        "hqk,qhd->khd", weights, cotangent_group, preferred_element_type=jnp.float32
    )
    key_count = upper - lower
    return (grad_key.reshape(key_count, -1), grad_value.reshape(key_count, -1))


def per_device(queries, keys, values, cotangent, restrict_one, restrict_two):
    row_count = queries.shape[0]
    width = queries.shape[1]
    head_count = width // HEAD_DIM
    group_size = 2
    scaling = 1.0 / math.sqrt(HEAD_DIM)
    one_rows = restrict_one.shape[0]
    two_rows = restrict_two.shape[0]
    device_count = lax.axis_size("seq")
    position = lax.axis_index("seq")
    paired = jnp.concatenate([keys, values], axis=1)
    coarse_one = jnp.dot(restrict_one, paired, preferred_element_type=jnp.float32).astype(
        jnp.bfloat16
    )
    coarse_two = jnp.dot(restrict_two, paired, preferred_element_type=jnp.float32).astype(
        jnp.bfloat16
    )
    near_keys = padded(paired, (("seq", 0),), row_count)
    received = []
    for offset in (3, 2, -2, -3):
        received.append(from_behind(coarse_one, "seq", offset))
    middle_keys = jnp.concatenate(received, axis=0)
    distant_keys = lax.all_gather(coarse_two, "seq", axis=0, tiled=True)
    key_rows = jnp.concatenate([near_keys, middle_keys, distant_keys], axis=0)
    key_count = key_rows.shape[0]
    near_place = position + jnp.repeat(jnp.array([-1, 0, 1], dtype=jnp.int32), row_count)
    middle_place = position + jnp.repeat(jnp.array([-3, -2, 2, 3], dtype=jnp.int32), one_rows)
    far_block = jnp.repeat(jnp.arange(device_count, dtype=jnp.int32), two_rows)
    key_bias = jnp.concatenate(
        [
            jnp.where((near_place >= 0) & (near_place < device_count), 0.0, masked_bias),
            jnp.where(
                (middle_place >= 0) & (middle_place < device_count), level_one_bias, masked_bias
            ),
            jnp.where(jnp.abs(far_block - position) >= 4, level_two_bias, masked_bias),
        ]
    ).astype(jnp.float32)
    query_heads = queries.reshape(row_count, head_count, HEAD_DIM)
    cotangent_heads = cotangent.reshape(row_count, head_count, HEAD_DIM)
    key_heads = key_rows[:, :width].reshape(key_count, head_count, HEAD_DIM)
    value_heads = key_rows[:, width:].reshape(key_count, head_count, HEAD_DIM)
    attended_parts = []
    grad_query_parts = []
    lse_parts = []
    delta_parts = []
    key_grad_parts = []
    value_grad_parts = []
    for group_index in range(head_count // group_size):
        lower = group_index * group_size
        upper = lower + group_size
        query_group = query_heads[:, lower:upper]
        cotangent_group = cotangent_heads[:, lower:upper]
        key_group = key_heads[:, lower:upper]
        value_group = value_heads[:, lower:upper]
        scores = (
            jnp.einsum("qhd,khd->hqk", query_group, key_group, preferred_element_type=jnp.float32)
            * scaling
            + key_bias
        )
        highest = jnp.max(scores, axis=2)
        raised = jnp.exp(scores - highest[:, :, None])
        row_total = jnp.sum(raised, axis=2)
        log_total = highest + jnp.log(row_total)
        probs = raised * (1.0 / row_total)[:, :, None]
        weights = probs.astype(jnp.bfloat16)
        attended_group = jnp.einsum(
            "hqk,khd->qhd", weights, value_group, preferred_element_type=jnp.float32
        ).astype(jnp.bfloat16)
        delta = jnp.einsum(
            "qhd,qhd->hq", cotangent_group, attended_group, preferred_element_type=jnp.float32
        )
        dots = jnp.einsum(
            "qhd,khd->hqk", cotangent_group, value_group, preferred_element_type=jnp.float32
        )
        score_grad = (probs * (dots - delta[:, :, None])).astype(jnp.bfloat16)
        grad_query = (
            jnp.einsum("hqk,khd->qhd", score_grad, key_group, preferred_element_type=jnp.float32)
            * scaling
        )
        attended_parts.append(attended_group.reshape(row_count, -1))
        grad_query_parts.append(grad_query.reshape(row_count, -1))
        lse_parts.append(log_total)
        delta_parts.append(delta)
        grad_key, grad_value = key_terms(
            score_grad, weights, query_group, cotangent_group, 0, key_count, scaling
        )
        key_grad_parts.append(grad_key)
        value_grad_parts.append(grad_value)
    attended = jnp.concatenate(attended_parts, axis=1)
    grad_q = jnp.concatenate(grad_query_parts, axis=1).astype(jnp.bfloat16)
    all_grads = jnp.concatenate(
        [jnp.concatenate(key_grad_parts, axis=1), jnp.concatenate(value_grad_parts, axis=1)], axis=1
    )
    own_grads = all_grads[row_count : 2 * row_count]
    for offset, piece in (
        (1, all_grads[2 * row_count : 3 * row_count]),
        (-1, all_grads[:row_count]),
    ):
        own_grads = own_grads + from_behind(piece.astype(jnp.bfloat16), "seq", offset).astype(
            piece.dtype
        )
    coarse_grads = all_grads[3 * row_count :]
    middle_sum = jnp.zeros((one_rows, 2 * width), jnp.float32)
    for slot, offset in enumerate((3, 2, -2, -3)):
        piece = coarse_grads[slot * one_rows : (slot + 1) * one_rows]
        middle_sum = middle_sum + from_behind(piece.astype(jnp.bfloat16), "seq", -offset).astype(
            piece.dtype
        )
    far_sum = lax.psum_scatter(
        coarse_grads[4 * one_rows :].astype(jnp.bfloat16), "seq", scatter_dimension=0, tiled=True
    ).astype(jnp.float32)
    total = own_grads + jnp.dot(
        restrict_one.astype(jnp.float32).T, middle_sum, precision=lax.Precision.HIGHEST
    )
    total = total + jnp.dot(
        restrict_two.astype(jnp.float32).T, far_sum, precision=lax.Precision.HIGHEST
    )
    return (
        attended,
        grad_q,
        total[:, :width].astype(jnp.bfloat16),
        total[:, width:].astype(jnp.bfloat16),
    )


def solution(mesh):
    in_specs = (
        P(("prompt", "seq"), None),
        P(("prompt", "seq"), None),
        P(("prompt", "seq"), None),
        P(("prompt", "seq"), None),
        P(),
        P(),
    )
    out_specs = (
        P(("prompt", "seq"), None),
        P(("prompt", "seq"), None),
        P(("prompt", "seq"), None),
        P(("prompt", "seq"), None),
    )
    return jax.shard_map(
        per_device, mesh=mesh, in_specs=in_specs, out_specs=out_specs, check_vma=False
    )
```

profile of v0, /device:TPU:0, one launch (start us, length us, event | category | flops | bytes accessed | tf_op | source)
XLA Modules:
  0.0 360.6 jit_solution(10816003518951378445)
XLA Ops:
  9.5 5.9 %collective-permute-start = (bf16[256,2048]{1,0:T(8,128)(2,1)S(1)}, bf16[256,2048]{1,0:T(8,128)(2,1)}, u32[]{:S(2)}, u32[]{:S(2)}) collective-permute-start(bf16[256,2048]{1,0:T(8,128)(2,1)S(1)} %constant_dynamic-update-slice_fusion), channel_id=1, source_target_pairs={{0,4},{4,8},{8,12},{12,16},{16,20},{20,24},{24,28},{1,5},{5,9},{9,... | collective-permute-start | bytes 3145736 | tf_op jit(solution)/shard_map/ppermute | solution.py:23
  16.9 4.6 %collective-permute-start.2 = (bf16[8,2048]{1,0:T(8,128)(2,1)S(1)}, bf16[8,2048]{1,0:T(8,128)(2,1)S(1)}, u32[]{:S(2)}, u32[]{:S(2)}) collective-permute-start(bf16[8,2048]{1,0:T(8,128)(2,1)S(1)} %fusion.8), channel_id=1, source_target_pairs={{0,12},{4,16},{8,20},{12,24},{16,28},{1,13},{5,17},{9,21},{13,25},... | collective-permute-start | bytes 98312 | tf_op jit(solution)/shard_map/ppermute | solution.py:32
  21.5 3.5 collective-permute-start.3
  26.6 59.5 %all-gather = bf16[8,4,2048]{2,1,0:T(4,128)(2,1)S(1)} all-gather(bf16[1,4,2048]{2,1,0:T(4,128)(2,1)S(1)} %fusion.9), channel_id=1, replica_groups=mesh['seq'=8,'prompt'=4] {'seq'}, dimensions={0}, use_global_device_ids=true | all-gather | bytes 147456 | tf_op jit(solution)/shard_map/all_gather | solution.py:69
  87.5 2.1 copy.128
  92.2 1.3 constant_dynamic-update-slice_fusion.9
  93.8 3.8 %collective-permute-done.5 = bf16[8,2048]{1,0:T(8,128)(2,1)S(1)} collective-permute-done((bf16[8,2048]{1,0:T(8,128)(2,1)S(1)}, bf16[8,2048]{1,0:T(8,128)(2,1)S(1)}, u32[]{:S(2)}, u32[]{:S(2)}) %collective-permute-start.5) | collective-permute-done | bytes 32800 | tf_op jit(solution)/shard_map/ppermute | solution.py:32
  97.7 1.7 fusion.212
  99.3 1.7 copy.118
  101.0 2.5 multiply_add_fusion.7
  103.5 1.7 multiply_add_fusion.6
  105.2 1.6 multiply_add_fusion.5
  106.8 1.7 multiply_add_fusion.4
  108.5 1.7 multiply_add_fusion.3
  110.2 1.6 multiply_add_fusion.2
  111.8 1.6 multiply_add_fusion.1
  113.9 3.8 %copy.117 = bf16[832,1024]{0,1:T(8,128)(2,1)} copy(bf16[832,1024]{1,0:T(8,128)(2,1)} %get-tuple-element.31) | data formatting | bytes 3407872 | tf_op jit(solution)/shard_map/slice | solution.py:87
  117.7 3.2 fusion.214
  120.9 1.6 fusion.215
  122.5 2.7 convolution_convert_fusion.9
  125.2 2.7 convolution_convert_fusion.8
  128.0 3.0 fusion.216
  131.0 2.7 convolution_convert_fusion.7
  133.8 3.1 fusion.217
  136.9 2.7 convolution_convert_fusion.6
  139.6 3.0 fusion.218
  142.7 2.7 convolution_convert_fusion.5
  145.4 3.1 fusion.219
  148.5 2.7 convolution_convert_fusion.4
  151.3 3.0 fusion.220
  154.3 2.8 convolution_convert_fusion.3
  157.1 1.6 fusion.221
  158.7 3.2 fusion.143
  162.0 2.2 fusion.29
  181.5 2.8 fusion.71
  184.3 2.8 fusion.80
  187.1 2.8 fusion.89
  189.9 2.8 fusion.98
  192.7 2.8 fusion.107
  195.5 2.8 fusion.116
  198.3 2.8 fusion.125
  201.2 2.2 fusion.134
  203.4 2.1 copy.137
  205.4 1.9 constant_dynamic-update-slice_fusion.41
  213.0 2.1 fusion.22
  217.2 2.0 copy.145
  219.2 2.0 copy.146
  222.2 2.0 copy.148
  224.2 2.0 copy.149
  227.1 2.0 copy.151
  230.3 1.9 constant_dynamic-update-slice_fusion.40
  232.2 1.9 constant_dynamic-update-slice_fusion.39
  234.1 1.9 constant_dynamic-update-slice_fusion.38
  246.3 3.4 convert.61
  249.9 1.4 fusion.211
  261.4 5.6 %collective-permute-start.6 = (bf16[256,2048]{1,0:T(8,128)(2,1)}, bf16[256,2048]{1,0:T(8,128)(2,1)}, u32[]{:S(2)}, u32[]{:S(2)}) collective-permute-start(bf16[256,2048]{1,0:T(8,128)(2,1)} %get-tuple-element.28), channel_id=1, source_target_pairs={{0,4},{4,8},{8,12},{12,16},{16,20},{20,24},{24,28},{1,5},{5,9},{9,... | collective-permute-start | bytes 3145736 | tf_op jit(solution)/shard_map/ppermute | solution.py:32
  267.1 1.5 collective-permute-start.11
  269.9 1.4 collective-permute-start.9
  271.3 1.5 constant_dynamic-update-slice_fusion.16
  272.8 1.5 constant_dynamic-update-slice_fusion.15
  274.3 1.5 constant_dynamic-update-slice_fusion.14
  284.3 63.1 %all-reduce.3.cloned.1.call-done = bf16[32,2048]{0,1:T(8,128)(2,1)} async-done(((bf16[32,2048]{0,1:T(8,128)(2,1)}), bf16[32,2048]{0,1:T(8,128)(2,1)}) %all-reduce.3.cloned.1.call-update) | async-done | bytes 131088
  347.4 1.6 convolution_bitcast_fusion
  349.1 3.6 %fusion.13 = bf16[256,2048]{1,0:T(8,128)(2,1)S(1)} fusion(f32[256,2048]{1,0:T(8,128)S(1)} %convolution_bitcast_fusion, f32[832,2048]{1,0:T(8,128)} %constant_dynamic-update-slice_fusion.26, bf16[256,2048]{1,0:T(8,128)(2,1)} %collective-permute-done.7, bf16[256,2048]{1,0:T(8,128)(2,1)} %collective-permute-done.6, bf16[8,256]{1,0:T(8,128)(2,1)S(1)} %copy-done, ...), kind=kOutput, calls=%fused_computation.18 | convolution fusion | flops 54116352 | bytes 7475200 | tf_op jit(solution)/shard_map/dot_general | solution.py:158
  (279 shorter events, 68.7 us)
Async XLA Ops:
  7.2 9.5 %copy-start = (bf16[8,256]{1,0:T(8,128)(2,1)S(1)}, bf16[8,256]{1,0:T(8,128)(2,1)}, u32[]{:S(2)}) copy-start(bf16[8,256]{1,0:T(8,128)(2,1)} %param.12) | copy-start | bytes 12292
  7.2 19.1 %copy-start.49 = (bf16[4,256]{1,0:T(4,128)(2,1)S(1)}, bf16[4,256]{1,0:T(4,128)(2,1)}, u32[]{:S(2)}) copy-start(bf16[4,256]{1,0:T(4,128)(2,1)} %param.13) | copy-start | bytes 6148
  7.2 340.2 %all-reduce.3.cloned.1.call-start = ((), (), s32[]{:S(2)}) async-start(), calls=%async_computation | async-start | bytes 1048576
  8.3 77.9 %copy-start.74 = (s32[4]{0:T(128)S(1)}, s32[4]{0:T(128)}, u32[]{:S(2)}) copy-start(s32[4]{0:T(128)} %constant.13.clone) | copy-start | bytes 52
  8.3 78.1 %copy-start.73 = (s32[3]{0:T(128)S(1)}, s32[3]{0:T(128)}, u32[]{:S(2)}) copy-start(s32[3]{0:T(128)} %constant.12.clone) | copy-start | bytes 40
  8.3 78.2 %copy-start.32 = (bf16[256,1024]{1,0:T(8,128)(2,1)S(1)}, bf16[256,1024]{1,0:T(8,128)(2,1)}, u32[]{:S(2)}) copy-start(bf16[256,1024]{1,0:T(8,128)(2,1)} %param.8) | copy-start | bytes 1572868
  9.5 81.4 %collective-permute-start = (bf16[256,2048]{1,0:T(8,128)(2,1)S(1)}, bf16[256,2048]{1,0:T(8,128)(2,1)}, u32[]{:S(2)}, u32[]{:S(2)}) collective-permute-start(bf16[256,2048]{1,0:T(8,128)(2,1)S(1)} %constant_dynamic-update-slice_fusion), channel_id=1, source_target_pairs={{0,4},{4,8},{8,12},{12,16},{16,20},{20,24},{24,28},{1,5},{5,9},{9,... | collective-permute-start | bytes 3145736 | tf_op jit(solution)/shard_map/ppermute | solution.py:23
  15.4 78.3 %collective-permute-start.1 = (bf16[256,2048]{1,0:T(8,128)(2,1)S(1)}, bf16[256,2048]{1,0:T(8,128)(2,1)S(1)}, u32[]{:S(2)}, u32[]{:S(2)}) collective-permute-start(bf16[256,2048]{1,0:T(8,128)(2,1)S(1)} %constant_dynamic-update-slice_fusion), channel_id=1, source_target_pairs={{4,0},{8,4},{12,8},{16,12},{20,16},{24,20},{28,24},{5,1},{9,5},{13... | collective-permute-start | bytes 3145736 | tf_op jit(solution)/shard_map/ppermute | solution.py:24
  16.9 76.9 %collective-permute-start.2 = (bf16[8,2048]{1,0:T(8,128)(2,1)S(1)}, bf16[8,2048]{1,0:T(8,128)(2,1)S(1)}, u32[]{:S(2)}, u32[]{:S(2)}) collective-permute-start(bf16[8,2048]{1,0:T(8,128)(2,1)S(1)} %fusion.8), channel_id=1, source_target_pairs={{0,12},{4,16},{8,20},{12,24},{16,28},{1,13},{5,17},{9,21},{13,25},... | collective-permute-start | bytes 98312 | tf_op jit(solution)/shard_map/ppermute | solution.py:32
  21.5 72.3 %collective-permute-start.3 = (bf16[8,2048]{1,0:T(8,128)(2,1)S(1)}, bf16[8,2048]{1,0:T(8,128)(2,1)S(1)}, u32[]{:S(2)}, u32[]{:S(2)}) collective-permute-start(bf16[8,2048]{1,0:T(8,128)(2,1)S(1)} %fusion.8), channel_id=1, source_target_pairs={{0,8},{4,12},{8,16},{12,20},{16,24},{20,28},{1,9},{5,13},{9,17},{1... | collective-permute-start | bytes 98312 | tf_op jit(solution)/shard_map/ppermute | solution.py:32
  25.0 68.8 %collective-permute-start.4 = (bf16[8,2048]{1,0:T(8,128)(2,1)S(1)}, bf16[8,2048]{1,0:T(8,128)(2,1)S(1)}, u32[]{:S(2)}, u32[]{:S(2)}) collective-permute-start(bf16[8,2048]{1,0:T(8,128)(2,1)S(1)} %fusion.8), channel_id=1, source_target_pairs={{8,0},{12,4},{16,8},{20,12},{24,16},{28,20},{9,1},{13,5},{17,9},{2... | collective-permute-start | bytes 98312 | tf_op jit(solution)/shard_map/ppermute | solution.py:32
  26.3 63.3 %copy-start.72 = (u32[32]{0:T(128)S(1)}, u32[32]{0:T(128)}, u32[]{:S(2)}) copy-start(u32[32]{0:T(128)} %constant.46) | copy-start | bytes 388
  87.5 6.0 %copy-start.13 = (bf16[256,1024]{1,0:T(8,128)(2,1)S(1)}, bf16[256,1024]{1,0:T(8,128)(2,1)}, u32[]{:S(2)}) copy-start(bf16[256,1024]{1,0:T(8,128)(2,1)} %param.9) | copy-start | bytes 1572868
  89.6 4.0 %copy-start.14 = (bf16[256,1024]{1,0:T(8,128)(2,1)S(1)}, bf16[256,1024]{1,0:T(8,128)(2,1)}, u32[]{:S(2)}) copy-start(bf16[256,1024]{1,0:T(8,128)(2,1)} %param.10) | copy-start | bytes 1572868
  91.0 6.7 %collective-permute-start.5 = (bf16[8,2048]{1,0:T(8,128)(2,1)S(1)}, bf16[8,2048]{1,0:T(8,128)(2,1)S(1)}, u32[]{:S(2)}, u32[]{:S(2)}) collective-permute-start(bf16[8,2048]{1,0:T(8,128)(2,1)S(1)} %fusion.8), channel_id=1, source_target_pairs={{12,0},{16,4},{20,8},{24,12},{28,16},{13,1},{17,5},{21,9},{25,13},... | collective-permute-start | bytes 98312 | tf_op jit(solution)/shard_map/ppermute | solution.py:32
  117.7 3.2 copy-start.3
  122.5 5.5 %copy-start.50 = (f32[2,256]{1,0:T(2,128)}, f32[2,256]{1,0:T(2,128)S(1)}, u32[]{:S(2)}) copy-start(f32[2,256]{1,0:T(2,128)S(1)} %broadcast_divide_fusion.6) | copy-start | bytes 6148
  131.0 5.9 %copy-start.52 = (f32[2,256]{1,0:T(2,128)}, f32[2,256]{1,0:T(2,128)S(1)}, u32[]{:S(2)}) copy-start(f32[2,256]{1,0:T(2,128)S(1)} %broadcast_divide_fusion.5) | copy-start | bytes 6148
  136.9 5.8 %copy-start.55 = (f32[2,256]{1,0:T(2,128)}, f32[2,256]{1,0:T(2,128)S(1)}, u32[]{:S(2)}) copy-start(f32[2,256]{1,0:T(2,128)S(1)} %broadcast_divide_fusion.4) | copy-start | bytes 6148
  142.7 5.8 %copy-start.57 = (f32[2,256]{1,0:T(2,128)}, f32[2,256]{1,0:T(2,128)S(1)}, u32[]{:S(2)}) copy-start(f32[2,256]{1,0:T(2,128)S(1)} %broadcast_divide_fusion.3) | copy-start | bytes 6148
  148.5 5.8 %copy-start.60 = (f32[2,256]{1,0:T(2,128)}, f32[2,256]{1,0:T(2,128)S(1)}, u32[]{:S(2)}) copy-start(f32[2,256]{1,0:T(2,128)S(1)} %broadcast_divide_fusion.2) | copy-start | bytes 6148
  154.3 4.4 %copy-start.62 = (f32[2,256]{1,0:T(2,128)}, f32[2,256]{1,0:T(2,128)S(1)}, u32[]{:S(2)}) copy-start(f32[2,256]{1,0:T(2,128)S(1)} %broadcast_divide_fusion.1) | copy-start | bytes 6148
  161.9 3.1 copy-start.11
  162.0 4.3 %copy-start.8 = (f32[2,256,832]{1,2,0:T(8,128)S(1)}, f32[2,256,832]{1,2,0:T(8,128)}, u32[]{:S(2)}) copy-start(f32[2,256,832]{1,2,0:T(8,128)} %get-tuple-element.37) | copy-start | bytes 5111812
  189.9 2.8 copy-start.59
  195.5 2.8 copy-start.64
  203.4 3.9 %copy-start.15 = (f32[2,832,64]{1,2,0:T(8,128)S(1)}, f32[2,832,64]{1,2,0:T(8,128)}, u32[]{:S(2)}) copy-start(f32[2,832,64]{1,2,0:T(8,128)} %convolution_multiply_fusion.6) | copy-start | bytes 1277956
  203.4 4.9 %copy-start.16 = (f32[2,832,64]{1,2,0:T(8,128)S(1)}, f32[2,832,64]{1,2,0:T(8,128)}, u32[]{:S(2)}) copy-start(f32[2,832,64]{1,2,0:T(8,128)} %convolution_multiply_fusion.5) | copy-start | bytes 1277956
  203.4 5.8 %copy-start.17 = (f32[2,832,64]{1,2,0:T(8,128)S(1)}, f32[2,832,64]{1,2,0:T(8,128)}, u32[]{:S(2)}) copy-start(f32[2,832,64]{1,2,0:T(8,128)} %convolution_multiply_fusion.4) | copy-start | bytes 1277956
  209.2 3.8 %copy-start.65 = (f32[2,256]{1,0:T(2,128)S(1)}, f32[2,256]{1,0:T(2,128)}, u32[]{:S(2)}) copy-start(f32[2,256]{1,0:T(2,128)} %get-tuple-element.16) | copy-start | bytes 6148
  217.2 4.0 %copy-start.33 = (f32[2,832,64]{1,2,0:T(8,128)S(1)}, f32[2,832,64]{1,2,0:T(8,128)}, u32[]{:S(2)}) copy-start(f32[2,832,64]{1,2,0:T(8,128)} %fusion.89) | copy-start | bytes 1277956
  222.2 4.0 %copy-start.34 = (f32[2,832,64]{1,2,0:T(8,128)S(1)}, f32[2,832,64]{1,2,0:T(8,128)}, u32[]{:S(2)}) copy-start(f32[2,832,64]{1,2,0:T(8,128)} %fusion.116) | copy-start | bytes 1277956
  230.3 5.8 %copy-start.24 = (f32[832,128]{1,0:T(8,128)S(1)}, f32[832,128]{1,0:T(8,128)}, u32[]{:S(2)}) copy-start(f32[832,128]{1,0:T(8,128)} %copy.141) | copy-start | bytes 1277956
  230.3 6.6 %copy-start.22 = (f32[832,128]{1,0:T(8,128)S(1)}, f32[832,128]{1,0:T(8,128)}, u32[]{:S(2)}) copy-start(f32[832,128]{1,0:T(8,128)} %copy.142) | copy-start | bytes 1277956
  232.2 5.5 %copy-start.21 = (f32[832,128]{1,0:T(8,128)S(1)}, f32[832,128]{1,0:T(8,128)}, u32[]{:S(2)}) copy-start(f32[832,128]{1,0:T(8,128)} %copy.143) | copy-start | bytes 1277956
  234.1 4.5 %copy-start.31 = (f32[832,128]{1,0:T(8,128)S(1)}, f32[832,128]{1,0:T(8,128)}, u32[]{:S(2)}) copy-start(f32[832,128]{1,0:T(8,128)} %copy.144) | copy-start | bytes 1277956
  236.0 3.5 copy-start.30
  236.9 3.5 copy-start.29
  237.7 3.4 copy-start.28
  238.6 3.4 copy-start.27
  239.5 3.4 copy-start.26
  240.3 3.4 copy-start.25
  241.2 3.4 copy-start.23
  249.8 3.1 copy-start.44
  249.8 3.8 %copy-start.43 = (bf16[2,64,256]{2,1,0:T(8,128)(2,1)S(1)}, bf16[2,64,256]{2,1,0:T(8,128)(2,1)}, u32[]{:S(2)}) copy-start(bf16[2,64,256]{2,1,0:T(8,128)(2,1)} %convolution_convert_fusion.8) | copy-start | bytes 196612
  249.8 4.6 %copy-start.45 = (bf16[2,64,256]{2,1,0:T(8,128)(2,1)S(1)}, bf16[2,64,256]{2,1,0:T(8,128)(2,1)}, u32[]{:S(2)}) copy-start(bf16[2,64,256]{2,1,0:T(8,128)(2,1)} %convolution_convert_fusion.7) | copy-start | bytes 196612
  249.8 5.3 %copy-start.46 = (bf16[2,64,256]{2,1,0:T(8,128)(2,1)S(1)}, bf16[2,64,256]{2,1,0:T(8,128)(2,1)}, u32[]{:S(2)}) copy-start(bf16[2,64,256]{2,1,0:T(8,128)(2,1)} %convolution_convert_fusion.6) | copy-start | bytes 196612
  249.8 6.0 %copy-start.47 = (bf16[2,64,256]{2,1,0:T(8,128)(2,1)S(1)}, bf16[2,64,256]{2,1,0:T(8,128)(2,1)}, u32[]{:S(2)}) copy-start(bf16[2,64,256]{2,1,0:T(8,128)(2,1)} %convolution_convert_fusion.5) | copy-start | bytes 196612
  249.8 8.1 %copy-start.38 = (bf16[2,64,256]{2,1,0:T(8,128)(2,1)S(1)}, bf16[2,64,256]{2,1,0:T(8,128)(2,1)}, u32[]{:S(2)}) copy-start(bf16[2,64,256]{2,1,0:T(8,128)(2,1)} %fusion.62) | copy-start | bytes 196612
  249.9 8.9 %copy-start.39 = (bf16[2,64,256]{2,1,0:T(8,128)(2,1)S(1)}, bf16[2,64,256]{2,1,0:T(8,128)(2,1)}, u32[]{:S(2)}) copy-start(bf16[2,64,256]{2,1,0:T(8,128)(2,1)} %fusion.63) | copy-start | bytes 196612
  252.2 6.6 %copy-start.40 = (bf16[2,64,256]{2,1,0:T(8,128)(2,1)S(1)}, bf16[2,64,256]{2,1,0:T(8,128)(2,1)}, u32[]{:S(2)}) copy-start(bf16[2,64,256]{2,1,0:T(8,128)(2,1)} %fusion.64) | copy-start | bytes 196612
  252.2 6.7 %copy-start.41 = (bf16[2,64,256]{2,1,0:T(8,128)(2,1)S(1)}, bf16[2,64,256]{2,1,0:T(8,128)(2,1)}, u32[]{:S(2)}) copy-start(bf16[2,64,256]{2,1,0:T(8,128)(2,1)} %fusion.65) | copy-start | bytes 196612
  252.9 6.2 %slice-start = ((bf16[832,2048]{1,0:T(8,128)(2,1)}), bf16[32,2048]{1,0:T(8,128)(2,1)S(1)}, s32[]{:S(2)}) async-start(bf16[832,2048]{1,0:T(8,128)(2,1)} %copy-done.2), calls=%async_computation.1 | async-start | bytes 262144 | tf_op jit(solution)/shard_map/slice | solution.py:156
  255.8 23.7 %copy-start.35 = (bf16[2,64,256]{2,1,0:T(8,128)(2,1)S(1)}, bf16[2,64,256]{2,1,0:T(8,128)(2,1)}, u32[]{:S(2)}) copy-start(bf16[2,64,256]{2,1,0:T(8,128)(2,1)} %fusion.66) | copy-start | bytes 196612
  256.0 23.7 %copy-start.36 = (bf16[2,64,256]{2,1,0:T(8,128)(2,1)S(1)}, bf16[2,64,256]{2,1,0:T(8,128)(2,1)}, u32[]{:S(2)}) copy-start(bf16[2,64,256]{2,1,0:T(8,128)(2,1)} %fusion.67) | copy-start | bytes 196612
  257.0 22.8 %copy-start.37 = (bf16[2,64,256]{2,1,0:T(8,128)(2,1)S(1)}, bf16[2,64,256]{2,1,0:T(8,128)(2,1)}, u32[]{:S(2)}) copy-start(bf16[2,64,256]{2,1,0:T(8,128)(2,1)} %fusion.68) | copy-start | bytes 196612
  260.1 88.9 %collective-permute-start.7 = (bf16[256,2048]{1,0:T(8,128)(2,1)}, bf16[256,2048]{1,0:T(8,128)(2,1)}, u32[]{:S(2)}, u32[]{:S(2)}) collective-permute-start(bf16[256,2048]{1,0:T(8,128)(2,1)} %get-tuple-element.29), channel_id=1, source_target_pairs={{4,0},{8,4},{12,8},{16,12},{20,16},{24,20},{28,24},{5,1},{9,5},{13... | collective-permute-start | bytes 3145736 | tf_op jit(solution)/shard_map/ppermute | solution.py:32
  261.4 87.6 %collective-permute-start.6 = (bf16[256,2048]{1,0:T(8,128)(2,1)}, bf16[256,2048]{1,0:T(8,128)(2,1)}, u32[]{:S(2)}, u32[]{:S(2)}) collective-permute-start(bf16[256,2048]{1,0:T(8,128)(2,1)} %get-tuple-element.28), channel_id=1, source_target_pairs={{0,4},{4,8},{8,12},{12,16},{16,20},{20,24},{24,28},{1,5},{5,9},{9,... | collective-permute-start | bytes 3145736 | tf_op jit(solution)/shard_map/ppermute | solution.py:32
  267.1 15.9 %collective-permute-start.11 = (bf16[8,2048]{1,0:T(8,128)(2,1)}, bf16[8,2048]{1,0:T(8,128)(2,1)S(1)}, u32[]{:S(2)}, u32[]{:S(2)}) collective-permute-start(bf16[8,2048]{1,0:T(8,128)(2,1)} %get-tuple-element.25), channel_id=1, source_target_pairs={{0,12},{4,16},{8,20},{12,24},{16,28},{1,13},{5,17},{9,21},{13,25},... | collective-permute-start | bytes 98312 | tf_op jit(solution)/shard_map/ppermute | solution.py:32
  268.6 80.5 %collective-permute-start.10 = (bf16[8,2048]{1,0:T(8,128)(2,1)}, bf16[8,2048]{1,0:T(8,128)(2,1)S(1)}, u32[]{:S(2)}, u32[]{:S(2)}) collective-permute-start(bf16[8,2048]{1,0:T(8,128)(2,1)} %get-tuple-element.26), channel_id=1, source_target_pairs={{0,8},{4,12},{8,16},{12,20},{16,24},{20,28},{1,9},{5,13},{9,17},{1... | collective-permute-start | bytes 98312 | tf_op jit(solution)/shard_map/ppermute | solution.py:32
  269.9 12.2 %copy-start.42 = (bf16[2,64,256]{2,1,0:T(8,128)(2,1)S(1)}, bf16[2,64,256]{2,1,0:T(8,128)(2,1)}, u32[]{:S(2)}) copy-start(bf16[2,64,256]{2,1,0:T(8,128)(2,1)} %get-tuple-element.50) | copy-start | bytes 196612
  269.9 79.2 %collective-permute-start.9 = (bf16[8,2048]{1,0:T(8,128)(2,1)}, bf16[8,2048]{1,0:T(8,128)(2,1)}, u32[]{:S(2)}, u32[]{:S(2)}) collective-permute-start(bf16[8,2048]{1,0:T(8,128)(2,1)} %get-tuple-element.27), channel_id=1, source_target_pairs={{8,0},{12,4},{16,8},{20,12},{24,16},{28,20},{9,1},{13,5},{17,9},{2... | collective-permute-start | bytes 98312 | tf_op jit(solution)/shard_map/ppermute | solution.py:32
  276.4 6.7 %copy-start.48 = (bf16[8,2048]{1,0:T(8,128)(2,1)S(1)}, bf16[8,2048]{1,0:T(8,128)(2,1)}, u32[]{:S(2)}) copy-start(bf16[8,2048]{1,0:T(8,128)(2,1)} %get-tuple-element.24) | copy-start | bytes 98308
  283.0 66.0 %collective-permute-start.8 = (bf16[8,2048]{1,0:T(8,128)(2,1)S(1)}, bf16[8,2048]{1,0:T(8,128)(2,1)S(1)}, u32[]{:S(2)}, u32[]{:S(2)}) collective-permute-start(bf16[8,2048]{1,0:T(8,128)(2,1)S(1)} %copy-done.48), channel_id=1, source_target_pairs={{12,0},{16,4},{20,8},{24,12},{28,16},{13,1},{17,5},{21,9},{25,13},... | collective-permute-start | bytes 98312 | tf_op jit(solution)/shard_map/ppermute | solution.py:32
  (25 other events, 52.5 us)
Sparse Core Ops, SparseCore 0:
  260.3 87.1 all-reduce.2
where the time goes:
time: 363 us; the launch traced here: 361 us
  matrix products  85.6 us (24%)
  local copies, waits for them, and re-layouts  77.3 us (21%)
  waiting for transfers between devices  67 us (18%)
  blocking collectives  59.5 us (16%)
  starting transfers between devices  30.2 us (8%)
  other arithmetic  25.3 us (7%)
  between operations  15.6 us (4%)
    unnamed x2, waiting for transfers between devices  63.1 us
    all_gather x1, blocking collectives, per_device(): distant_keys = lax.all_gather(coarse_two, 'seq', axis=0, tiled=True)  59.5 us
    unnamed x192, local copies, waits for them, and re-layouts  35.9 us
    ppermute x10, starting transfers between devices, from_behind(): return lax.ppermute(value, axis, pairs)  23 us
    dot_general x8, matrix products, per_device(): jnp.einsum('hqk,khd->qhd', weights, value_group, preferred_element_type=j...  22.5 us
    dot_general x8, matrix products, key_terms(): jnp.einsum('hqk,qhd->khd', weights, cotangent_group, preferred_element_ty...  21.8 us
    reshape x16, local copies, waits for them, and re-layouts, key_terms(): return (grad_key.reshape(key_count, -1), grad_value.reshape(key_count, -1))  21.7 us
    sub x8, other arithmetic, per_device(): raised = jnp.exp(scores - highest[:, :, None])  21.7 us
  transfers between devices with their start and end apart: 13, of which 2 were waited for; matrix products, arithmetic and copies ran while one was open for 5% of the time, Pallas kernels for 0%

commit v1 on v0

v1 whole, which is shorter than its diff:
```python
import math

import jax
import jax.numpy as jnp
from jax import lax
from jax.experimental import pallas as pl
from jax.experimental.pallas import tpu as pltpu
from jax.sharding import PartitionSpec as P

HEAD_DIM = 64
PAIR = 2 * HEAD_DIM
TILE = 32
GRANT = 32 * 1024 * 1024

level_one_bias = math.log(32.0)
level_two_bias = math.log(64.0)
masked_bias = -1e30


def swap_pairs(size):
    return [(i, i ^ 1) for i in range(size)]


def direct_pairs(size):
    return [(i, j) for i in range(size) for j in [i + 2 if i % 2 else i - 2] if 0 <= j < size]


def inverse(pairs):
    return [(j, i) for i, j in pairs]


def shift_pairs(size, shift):
    return [(i, (i + 2 * shift) % size) for i in range(size)]


def dot(a, b):
    return jnp.dot(a, b, preferred_element_type=jnp.float32)


def block_diagonal(both):
    top, bottom = (both[:HEAD_DIM], both[HEAD_DIM:])
    zero = jnp.zeros_like(top)
    return jnp.concatenate(
        [jnp.concatenate([top, zero], axis=1), jnp.concatenate([zero, bottom], axis=1)], axis=0
    )


def stacked_heads(both):
    lane = lax.broadcasted_iota(jnp.int32, both.shape, 1)
    first = lane < HEAD_DIM
    zero = jnp.zeros_like(both)
    return jnp.concatenate([jnp.where(first, both, zero), jnp.where(first, zero, both)], axis=0)


def head_rows(both, h):
    return both[h * HEAD_DIM : (h + 1) * HEAD_DIM]


class Unit:
    def __init__(self, query, cotangent, keys, values, keys_t, values_t, bias):
        scaled = query.astype(jnp.float32) * (1.0 / math.sqrt(HEAD_DIM))
        self.rows = query.shape[0]
        self.keys, self.values, self.keys_t, self.values_t = (keys, values, keys_t, values_t)
        self.bias = bias
        self.query_wide = block_diagonal(scaled.T.astype(jnp.bfloat16))
        self.query_tall = stacked_heads(scaled).astype(jnp.bfloat16)
        self.cotangent_t = cotangent.astype(jnp.float32).T
        self.scores = {}
        self.highest = None
        self.total = 0.0
        self.weights = {}
        self.raw = [0.0, 0.0]
        self.grad_q_t = [0.0, 0.0]
        self.grads = []

    def columns(self, h):
        return slice(h * self.rows, (h + 1) * self.rows)

    def score(self, part):
        score = dot(self.keys[part], self.query_wide)
        plain = max(0, self.keys.shape[0] - self.bias.shape[0] - part.start)
        if plain < score.shape[0]:
            skip = part.start + plain - (self.keys.shape[0] - self.bias.shape[0])
            biased = score[plain:] + self.bias[skip : skip + score.shape[0] - plain]
            score = jnp.concatenate([score[:plain], biased], axis=0) if plain else biased
        highest = jnp.max(score, axis=0, keepdims=True)
        self.highest = highest if self.highest is None else jnp.maximum(self.highest, highest)
        self.scores[part.start] = score

    def weigh(self, part):
        score = self.scores[part.start]
        parts = []
        for start in range(0, score.shape[0], TILE):
            prob = jnp.exp(score[start : start + TILE] - self.highest)
            self.total = self.total + jnp.sum(prob.reshape(-1, 8, prob.shape[1]), axis=0)
            parts.append(prob.astype(jnp.bfloat16))
        weight = jnp.concatenate(parts, axis=0)
        for h in range(2):
            self.raw[h] = self.raw[h] + dot(
                head_rows(self.values_t, h)[:, part], weight[:, self.columns(h)]
            )
        self.weights[part.start] = weight

    def finish(self):
        share = 1.0 / jnp.sum(self.total, axis=0, keepdims=True)
        shares = [share[:, self.columns(h)] for h in range(2)]
        out_t = jnp.concatenate([self.raw[h] * shares[h] for h in range(2)], axis=0)
        self.out = out_t.T.astype(jnp.bfloat16)
        product = self.cotangent_t * out_t.astype(jnp.bfloat16).astype(jnp.float32)
        self.delta = jnp.concatenate(
            [
                jnp.sum(head_rows(product, h), axis=0, keepdims=True) * shares[h]
                for h in range(2)
            ],
            axis=1,
        )
        shared_t = jnp.concatenate(
            [head_rows(self.cotangent_t, h) * shares[h] for h in range(2)], axis=0
        )
        self.cotangent_wide = block_diagonal(shared_t.astype(jnp.bfloat16))
        self.cotangent_tall = stacked_heads(shared_t.T).astype(jnp.bfloat16)

    def differentiate(self, part):
        weight = self.weights[part.start]
        dots = dot(self.values[part], self.cotangent_wide)
        parts = []
        for start in range(0, dots.shape[0], TILE):
            rows = slice(start, start + TILE)
            grad = weight[rows].astype(jnp.float32) * (dots[rows] - self.delta)
            parts.append(grad.astype(jnp.bfloat16))
        score_grad = jnp.concatenate(parts, axis=0)
        self.grads.append((dot(score_grad, self.query_tall), dot(weight, self.cotangent_tall)))
        for h in range(2):
            self.grad_q_t[h] = self.grad_q_t[h] + dot(
                head_rows(self.keys_t, h)[:, part], score_grad[:, self.columns(h)]
            )

    def grad_q(self):
        grad_q_t = jnp.concatenate(self.grad_q_t, axis=0) * (1.0 / math.sqrt(HEAD_DIM))
        return grad_q_t.T.astype(jnp.bfloat16)

    def key_grad(self, n):
        return jnp.concatenate([grads[n] for grads in self.grads], axis=0)


def attention_kernel(shifts):
    def kernel(
        place, bias, q, k, v, c, pair_k, pair_v, relayed_k, relayed_v, pair_qc, direct, *rest
    ):
        coarse = rest[:shifts]
        out, grad_q, pair_out, home_grad, pair_grad, direct_grad, relayed_grad = rest[
            shifts : shifts + 7
        ]
        coarse_grads = rest[shifts + 7 :]
        rows = q.shape[0]

        def halo(have):
            return jnp.full((rows, 1), jnp.where(have > 0, 0.0, masked_bias), jnp.float32)

        def key_rows(n, home, partner, halo):
            far = jnp.concatenate([ref[n] for ref in coarse], axis=0)
            pieces = [home[...], partner[...], halo, far]
            transposed = [piece.T for piece in pieces]
            return jnp.concatenate(pieces, axis=0), jnp.concatenate(transposed, axis=1)

        def unit(query, cotangent, outer_k, outer_v, have, bias):
            keys, keys_t = key_rows(0, k, pair_k, outer_k)
            values, values_t = key_rows(1, v, pair_v, outer_v)
            bias = jnp.concatenate([halo(have), bias], axis=0)
            return Unit(query, cotangent, keys, values, keys_t, values_t, bias)

        one = unit(q[...], c[...], relayed_k[...], relayed_v[...], place[1], bias[0])
        two = unit(pair_qc[0], pair_qc[1], direct[0], direct[1], place[2], bias[1])
        count = one.keys.shape[0]
        middle = count // 32 * 16
        parts = [slice(0, middle), slice(middle, count)]
        for part in parts:
            one.score(part)
        for part in parts:
            two.score(part)
            one.weigh(part)
        one.finish()
        for part in parts:
            one.differentiate(part)
            two.weigh(part)
        two.finish()
        for part in parts:
            two.differentiate(part)
        out[...], grad_q[...] = (one.out, one.grad_q())
        pair_out[0], pair_out[1] = (two.out, two.grad_q())
        for n in range(2):
            first, second = (one.key_grad(n), two.key_grad(n))
            home_grad[n] = first[:rows] + second[:rows]
            pair_grad[n] = first[rows : 2 * rows] + second[rows : 2 * rows]
            relayed_grad[n] = first[2 * rows : 3 * rows].astype(relayed_grad.dtype)
            direct_grad[n] = second[2 * rows : 3 * rows].astype(direct_grad.dtype)
            far_grad = (first[3 * rows :] + second[3 * rows :]).astype(direct_grad.dtype)
            size = far_grad.shape[0] // shifts
            for m, ref in enumerate(coarse_grads):
                ref[n] = far_grad[m * size : (m + 1) * size]

    return kernel


def attention(
    place, bias, q, k, v, c, pair_k, pair_v, relayed_k, relayed_v, pair_qc, direct, coarse
):
    rows, width = q.shape
    columns = width // 2
    steps = columns // PAIR
    shifts = len(coarse)
    coarse_rows = coarse[0].shape[1]

    def mine(j, place):
        return place[0] * steps + j

    def flat(index):
        return pl.BlockSpec((rows, PAIR), index)

    def both(shape_rows):
        return pl.BlockSpec((2, shape_rows, PAIR), lambda j, place: (0, 0, j))

    key_count = 3 * rows + shifts * coarse_rows
    products = 6 * 2 * 2 * rows * key_count * HEAD_DIM * 2 * steps
    bf16, f32 = (jnp.bfloat16, jnp.float32)
    return pl.pallas_call(
        attention_kernel(shifts),
        grid_spec=pltpu.PrefetchScalarGridSpec(
            num_scalar_prefetch=1,
            grid=(steps,),
            in_specs=[pl.BlockSpec(bias.shape, lambda j, place: (0, 0, 0))]
            + [flat(lambda j, place: (0, mine(j, place)))] * 4
            + [flat(lambda j, place: (0, j))] * 4
            + [both(rows)] * 2
            + [both(coarse_rows)] * shifts,
            out_specs=[flat(lambda j, place: (0, j))] * 2
            + [both(rows)] * 5
            + [both(coarse_rows)] * shifts,
        ),
        out_shape=[jax.ShapeDtypeStruct((rows, columns), bf16)] * 2
        + [
            jax.ShapeDtypeStruct((2, rows, columns), bf16),
            jax.ShapeDtypeStruct((2, rows, columns), f32),
            jax.ShapeDtypeStruct((2, rows, columns), f32),
            jax.ShapeDtypeStruct((2, rows, columns), bf16),
            jax.ShapeDtypeStruct((2, rows, columns), bf16),
        ]
        + [jax.ShapeDtypeStruct((2, coarse_rows, columns), bf16)] * shifts,
        compiler_params=pltpu.CompilerParams(vmem_limit_bytes=GRANT),
        cost_estimate=pl.CostEstimate(
            flops=4 * products, bytes_accessed=40 * rows * columns, transcendentals=0
        ),
        name="attention",
    )(
        place, bias, q, k, v, c, pair_k, pair_v, relayed_k, relayed_v, pair_qc, direct, *coarse
    )


def lengthened(restrict, coarse):
    return jnp.einsum(
        "fb,nfc->nbc", restrict.astype(jnp.float32), coarse, precision=lax.Precision.HIGHEST
    )


def per_device(queries, keys, values, cotangent, restrict_one, restrict_two):
    rows, width = queries.shape
    size = lax.axis_size("seq")
    pair_count = size // 2
    position = lax.axis_index("seq")
    parity = lax.rem(position, 2)
    pair = lax.div(position, 2)
    one_rows, two_rows = (restrict_one.shape[0], restrict_two.shape[0])
    block_rows = -(-(one_rows + two_rows) // 16) * 16
    restrict = jnp.concatenate(
        [
            restrict_one,
            restrict_two,
            jnp.zeros((block_rows - one_rows - two_rows, rows), restrict_one.dtype),
        ],
        axis=0,
    )

    shift = jnp.arange(1, pair_count)[:, None, None]
    side = jnp.arange(2)[None, :, None]
    row = jnp.arange(block_rows)[None, None, :]
    sender = lax.rem(pair - shift + pair_count, pair_count)
    block = 2 * sender + jnp.where(side == 0, parity, 1 - parity)

    def coarse_bias(query_block):
        apart = jnp.abs(block - query_block)
        one = (row < one_rows) & (apart >= 2) & (apart <= 3)
        two = (row >= one_rows) & (row < one_rows + two_rows) & (apart >= 4)
        return jnp.where(one, level_one_bias, jnp.where(two, level_two_bias, masked_bias)).reshape(
            -1, 1
        )

    bias = jnp.stack([coarse_bias(position), coarse_bias(2 * pair + 1 - parity)])
    bias = bias.astype(jnp.float32)
    has_before, has_after = (pair > 0, pair < pair_count - 1)
    place = jnp.stack(
        [
            parity,
            jnp.where(parity == 0, has_before, has_after).astype(jnp.int32),
            jnp.where(parity == 0, has_after, has_before).astype(jnp.int32),
        ]
    ).astype(jnp.int32)

    direct_to = direct_pairs(size)
    relayed_to = inverse(direct_to)
    swap = swap_pairs(size)

    def send(value, pairs):
        return lax.ppermute(value, "seq", pairs)

    half = width // 2
    shifts = range(1, pair_count)

    def columns(side, *arrays):
        return [lax.dynamic_slice_in_dim(a, side * half, half, axis=a.ndim - 1) for a in arrays]

    def after(value, *others):
        return lax.optimization_barrier((value, *others))[0]

    pair_k, pair_v = (send(a, swap) for a in columns(1 - parity, keys, values))
    relayed_k = send(pair_k, relayed_to)
    home_kv = jnp.stack(columns(parity, keys, values))
    direct = send(after(home_kv, pair_k), direct_to)
    relayed_v = send(after(pair_v, relayed_k), relayed_to)
    sent_qc = jnp.stack(columns(1 - parity, queries, cotangent))
    pair_qc = send(after(sent_qc, pair_v), swap)
    own_coarse = jnp.concatenate(
        [
            jnp.einsum("fb,nbc->nfc", restrict, home_kv, preferred_element_type=jnp.float32),
            jnp.stack([dot(restrict, pair_k), dot(restrict, pair_v)]),
        ],
        axis=1,
    ).astype(jnp.bfloat16)
    coarse = [send(own_coarse, shift_pairs(size, s)) for s in shifts]
    direct = after(direct, relayed_k)
    relayed_v = after(relayed_v, direct)
    pair_qc = after(pair_qc, relayed_v)
    coarse = after(coarse, pair_qc)

    (
        out, grad_q, pair_out, home_grad, pair_grad, direct_grad, relayed_grad, *coarse_grads,
    ) = attention(
        place, bias, queries, keys, values, cotangent,
        pair_k, pair_v, relayed_k, relayed_v, pair_qc, direct, coarse,
    )

    def whole(own, other):
        axis = own.ndim - 1
        return jnp.where(
            parity == 0,
            jnp.concatenate([own, other], axis=axis),
            jnp.concatenate([other, own], axis=axis),
        )

    relayed_back = send(relayed_grad, direct_to)
    out_back = send(pair_out, swap)
    coarse_back = [send(a, shift_pairs(size, -s)) for s, a in zip(shifts, coarse_grads)]
    pair_total = pair_grad + relayed_back.astype(jnp.float32)
    far = sum(piece.astype(jnp.float32) for piece in after(coarse_back, pair_total))
    pair_total = pair_total + lengthened(restrict, far[:, block_rows:])
    pair_total = pair_total.astype(jnp.bfloat16)
    grad_back = send(pair_total, swap)
    direct_back = send(after(direct_grad, pair_total), relayed_to)
    home_total = home_grad + direct_back.astype(jnp.float32)
    home_total = home_total + lengthened(restrict, far[:, :block_rows])
    home_total = home_total.astype(jnp.bfloat16)
    return (
        whole(out, out_back[0]),
        whole(grad_q, out_back[1]),
        whole(home_total[0], grad_back[0]),
        whole(home_total[1], grad_back[1]),
    )


def solution(mesh):
    split = P(("prompt", "seq"), None)
    return jax.shard_map(
        per_device,
        mesh=mesh,
        in_specs=(split, split, split, split, P(), P()),
        out_specs=(split, split, split, split),
        check_vma=False,
    )
```

time: 363 us -> 83.1 us (0.23)
  the two profiles are of different devices: /device:TPU:0 before, /device:TPU:4 now
where the time goes in v1:
time: 83.1 us; the launch traced here: 82.7 us
  waiting for transfers between devices  26.6 us (32%)
  starting transfers between devices  26.5 us (32%)
  Pallas kernels  16 us (19%)
  other arithmetic  5.79 us (7%)
  local copies, waits for them, and re-layouts  3.52 us (4%)
  matrix products  3.29 us (4%)
  between operations  0.96 us (1%)
    ppermute x16, waiting for transfers between devices, send(): return lax.ppermute(value, 'seq', pairs)  26.6 us
    ppermute x16, starting transfers between devices, send(): return lax.ppermute(value, 'seq', pairs)  26.5 us
    pallas_call x1, Pallas kernels, attention(): pl.pallas_call(attention_kernel(shifts), grid_spec=pltpu.PrefetchScalarGr...  16 us
    select_n x2, other arithmetic, whole(): jnp.where(parity == 0, jnp.concatenate([own, other], axis=axis), jnp.conc...  2.53 us
    another operation x2, local copies, waits for them, and re-layouts, per_device(): home_kv = jnp.stack(columns(parity, keys, values))  1.87 us
  transfers between devices with their start and end apart: 16, of which 10 were waited for; matrix products, arithmetic and copies ran while one was open for 12% of the time, Pallas kernels for 0%

profile of v1, /device:TPU:4, one launch (start us, length us, event | category | flops | bytes accessed | tf_op | source)
XLA Modules:
  0.0 82.7 jit_solution(9736576637952420898)
XLA Ops:
  0.6 0.0 copy-start.1
  0.7 1.1 %dynamic-slice_bitcast_fusion.3 = (bf16[1,256,512]{2,1,0:T(8,128)(2,1)S(1)}, bf16[256,512]{1,0:T(8,128)(2,1)S(1)}) fusion(bf16[256,1024]{1,0:T(8,128)(2,1)} %k.1, s32[]{:T(128)S(6)} %select_n.107, s32[]{:T(128)S(6)} %select_n.106), kind=kLoop, calls=%fused_computation.27 | loop fusion | bytes 1048584 | tf_op jit(solution)/shard_map/stack | solution.py:326
  1.8 0.1 collective-permute-start
  1.9 0.0 copy-done.1
  1.9 0.0 copy-start.4
  1.9 0.0 copy-start.6
  1.9 0.7 dynamic-slice_bitcast_fusion.2
  2.6 2.0 %collective-permute-start.1 = (bf16[256,512]{1,0:T(8,128)(2,1)}, bf16[256,512]{1,0:T(8,128)(2,1)S(1)}, u32[]{:S(2)}, u32[]{:S(2)}) collective-permute-start(bf16[256,512]{1,0:T(8,128)(2,1)} %get-tuple-element.59), channel_id=1, source_target_pairs={{0,4},{4,0},{8,12},{12,8},{16,20},{20,16},{24,28},{28,24},{1,5},{5... | collective-permute-start | bytes 786440 | tf_op jit(solution)/shard_map/ppermute | solution.py:313
  4.7 0.1 pad.21.clone
  4.7 0.1 fusion.13
  4.8 0.5 copy-done.9
  5.3 0.0 copy-done.4
  5.3 0.0 copy-done.6
  5.3 0.8 %fusion.2 = bf16[2,16,512]{2,1,0:T(8,128)(2,1)} fusion(bf16[4,256]{1,0:T(4,128)(2,1)S(1)} %copy-done.6, bf16[8,256]{1,0:T(8,128)(2,1)S(1)} %copy-done.4, bf16[16]{0:T(256)(128)(2,1)S(1)} %pad.21.clone, bf16[1,256,512]{2,1,0:T(8,128)(2,1)S(1)} %get-tuple-element.58, bf16[1,256,512]{2,1,0:T(8,128)(2,1)S(1)} %get-tuple-element.56), kind=kOutput, calls=%fused_computation.5 | convolution fusion | flops 9478144 | bytes 563232 | tf_op jit(solution)/shard_map/fb,nbc->nfc/dot_general | solution.py:333
  6.2 0.1 and_select_fusion.3
  6.2 0.0 copy-done.2
  6.3 0.1 copy-done.3
  6.4 0.8 %pad_maximum_fusion = bf16[2,256,512]{2,1,0:T(8,128)(2,1)} fusion(bf16[1,256,512]{2,1,0:T(8,128)(2,1)S(1)} %get-tuple-element.58, bf16[1,256,512]{2,1,0:T(8,128)(2,1)S(1)} %get-tuple-element.56), kind=kLoop, calls=%fused_computation.12 | loop fusion | flops 262144 | bytes 1048576 | tf_op jit(solution)/shard_map/stack | solution.py:326
  7.2 3.8 %collective-permute-done.pair_k = bf16[256,512]{1,0:T(8,128)(2,1)S(1)} collective-permute-done((bf16[256,512]{1,0:T(8,128)(2,1)S(1)}, bf16[256,512]{1,0:T(8,128)(2,1)S(1)}, u32[]{:S(2)}, u32[]{:S(2)}) %collective-permute-start) | collective-permute-done | bytes 262176 | tf_op jit(solution)/shard_map/ppermute | solution.py:313
  11.0 3.5 %collective-permute-start.4 = (bf16[2,256,512]{2,1,0:T(8,128)(2,1)}, bf16[2,256,512]{2,1,0:T(8,128)(2,1)S(1)}, u32[]{:S(2)}, u32[]{:S(2)}) collective-permute-start(bf16[2,256,512]{2,1,0:T(8,128)(2,1)} %pad_maximum_fusion), channel_id=1, source_target_pairs={{4,12},{8,0},{12,20},{16,8},{20,28},{24,16},{5,13},{9,1},{13,21},{... | collective-permute-start | bytes 1572872 | tf_op jit(solution)/shard_map/ppermute | solution.py:313
  14.6 1.3 %collective-permute-start.2 = (bf16[256,512]{1,0:T(8,128)(2,1)S(1)}, bf16[256,512]{1,0:T(8,128)(2,1)S(1)}, u32[]{:S(2)}, u32[]{:S(2)}) collective-permute-start(bf16[256,512]{1,0:T(8,128)(2,1)S(1)} %collective-permute-done.pair_k), channel_id=1, source_target_pairs={{12,4},{0,8},{20,12},{8,16},{28,20},{16,24},{13,5},{1,9},{21,13},{... | collective-permute-start | bytes 786440 | tf_op jit(solution)/shard_map/ppermute | solution.py:313
  15.8 0.8 %pad_maximum_fusion.1 = bf16[2,256,512]{2,1,0:T(8,128)(2,1)} fusion(bf16[1,256,512]{2,1,0:T(8,128)(2,1)S(1)} %dynamic-slice_bitcast_fusion, bf16[1,256,512]{2,1,0:T(8,128)(2,1)S(1)} %dynamic-slice_bitcast_fusion.1), kind=kLoop, calls=%fused_computation.13 | loop fusion | flops 262144 | bytes 1048576 | tf_op jit(solution)/shard_map/stack | solution.py:329
  16.7 0.1 select_n.112
  16.8 0.7 select_n.113
  17.5 0.0 collective-permute-done.1.pair_v
  17.5 1.1 %collective-permute-start.5 = (bf16[2,256,512]{2,1,0:T(8,128)(2,1)}, bf16[2,256,512]{2,1,0:T(8,128)(2,1)}, u32[]{:S(2)}, u32[]{:S(2)}) collective-permute-start(bf16[2,256,512]{2,1,0:T(8,128)(2,1)} %pad_maximum_fusion.1), channel_id=1, source_target_pairs={{0,4},{4,0},{8,12},{12,8},{16,20},{20,16},{24,28},{28,24},{1,5},{5... | collective-permute-start | bytes 1572872 | tf_op jit(solution)/shard_map/ppermute | solution.py:313
  18.6 0.8 pad_maximum_fusion.2.bias
  19.5 0.0 copy-start.5
  19.5 0.0 copy-start.7
  19.5 0.9 %fusion.3 = bf16[1,16,512]{2,1,0:T(8,128)(2,1)S(1)} fusion(bf16[256,512]{1,0:T(8,128)(2,1)S(1)} %collective-permute-done.pair_k, bf16[4,256]{1,0:T(4,128)(2,1)} %param.11, bf16[8,256]{1,0:T(8,128)(2,1)} %param.10, bf16[16]{0:T(256)(128)(2,1)} %copy-done.9), kind=kOutput, calls=%fused_computation.8 | convolution fusion | flops 4227072 | bytes 284704 | tf_op jit(solution)/shard_map/dot_general | solution.py:37
  20.4 2.4 %collective-permute-done.2.relayed_k = bf16[256,512]{1,0:T(8,128)(2,1)S(1)} collective-permute-done((bf16[256,512]{1,0:T(8,128)(2,1)S(1)}, bf16[256,512]{1,0:T(8,128)(2,1)S(1)}, u32[]{:S(2)}, u32[]{:S(2)}) %collective-permute-start.2) | collective-permute-done | bytes 262176 | tf_op jit(solution)/shard_map/ppermute | solution.py:313
  22.8 1.3 %collective-permute-start.3 = (bf16[256,512]{1,0:T(8,128)(2,1)S(1)}, bf16[256,512]{1,0:T(8,128)(2,1)S(1)}, u32[]{:S(2)}, u32[]{:S(2)}) collective-permute-start(bf16[256,512]{1,0:T(8,128)(2,1)S(1)} %collective-permute-done.1.pair_v), channel_id=1, source_target_pairs={{12,4},{0,8},{20,12},{8,16},{28,20},{16,24},{13,5},{1,9},{21,13},{... | collective-permute-start | bytes 786440 | tf_op jit(solution)/shard_map/ppermute | solution.py:313
  24.1 0.2 fusion.4
  24.3 4.7 %collective-permute-start.8 = (bf16[2,32,512]{2,1,0:T(8,128)(2,1)S(1)}, bf16[2,32,512]{2,1,0:T(8,128)(2,1)S(1)}, u32[]{:S(2)}, u32[]{:S(2)}) collective-permute-start(bf16[2,32,512]{2,1,0:T(8,128)(2,1)S(1)} %maximum_maximum_fusion), channel_id=1, source_target_pairs={{0,24},{4,28},{8,0},{12,4},{16,8},{20,12},{24,16},{28,20},{1,25},{... | collective-permute-start | bytes 196616 | tf_op jit(solution)/shard_map/ppermute | solution.py:313
  29.0 0.0 collective-permute-start.7
  29.0 0.0 collective-permute-done.4.direct
  29.0 1.0 %collective-permute-start.6 = (bf16[2,32,512]{2,1,0:T(8,128)(2,1)S(1)}, bf16[2,32,512]{2,1,0:T(8,128)(2,1)S(1)}, u32[]{:S(2)}, u32[]{:S(2)}) collective-permute-start(bf16[2,32,512]{2,1,0:T(8,128)(2,1)S(1)} %maximum_maximum_fusion), channel_id=1, source_target_pairs={{0,8},{4,12},{8,16},{12,20},{16,24},{20,28},{24,0},{28,4},{1,9},{5... | collective-permute-start | bytes 196616 | tf_op jit(solution)/shard_map/ppermute | solution.py:313
  30.0 0.1 pad_add_fusion.place
  30.1 2.4 %collective-permute-done.3.relayed_v = bf16[256,512]{1,0:T(8,128)(2,1)S(1)} collective-permute-done((bf16[256,512]{1,0:T(8,128)(2,1)S(1)}, bf16[256,512]{1,0:T(8,128)(2,1)S(1)}, u32[]{:S(2)}, u32[]{:S(2)}) %collective-permute-start.3) | collective-permute-done | bytes 262176 | tf_op jit(solution)/shard_map/ppermute | solution.py:313
  32.5 0.0 collective-permute-done.5.pair_qc
  32.5 0.7 collective-permute-done.8.rest_2_
  33.2 3.2 %collective-permute-done.7.rest_1_ = bf16[2,32,512]{2,1,0:T(8,128)(2,1)S(1)} collective-permute-done((bf16[2,32,512]{2,1,0:T(8,128)(2,1)S(1)}, bf16[2,32,512]{2,1,0:T(8,128)(2,1)S(1)}, u32[]{:S(2)}, u32[]{:S(2)}) %collective-permute-start.7) | collective-permute-done | bytes 65568 | tf_op jit(solution)/shard_map/ppermute | solution.py:313
  36.4 0.0 collective-permute-done.6.rest_0_
  36.4 16.0 %attention.1 = (bf16[256,512]{1,0:T(8,128)(2,1)S(1)}, bf16[256,512]{1,0:T(8,128)(2,1)S(1)}, bf16[2,256,512]{2,1,0:T(8,128)(2,1)S(1)}, f32[2,256,512]{2,1,0:T(8,1...) custom-call(s32[3]{0:T(128)S(1)} %pad_add_fusion.place, ...), custom_call_target="tpu_custom_call" | custom-call | flops 10871635968 | bytes 5242880 | tf_op jit(solution)/shard_map/attention/pallas_call | solution.py:226
  52.4 1.3 %collective-permute-start.10 = (bf16[2,256,512]{2,1,0:T(8,128)(2,1)S(1)}, bf16[2,256,512]{2,1,0:T(8,128)(2,1)S(1)}, u32[]{:S(2)}, u32[]{:S(2)}) collective-permute-start(bf16[2,256,512]{2,1,0:T(8,128)(2,1)S(1)} %get-tuple-element.42), channel_id=1, source_target_pairs={{4,12},{8,0},{12,20},{16,8},{20,28},{24,16},{5,13},{9,1},{13,21},{... | collective-permute-start | bytes 1572872 | tf_op jit(solution)/shard_map/ppermute | solution.py:313
  53.7 0.1 collective-permute-start.11
  53.8 2.4 %collective-permute-start.12 = (bf16[2,32,512]{2,1,0:T(8,128)(2,1)S(1)}, bf16[2,32,512]{2,1,0:T(8,128)(2,1)S(1)}, u32[]{:S(2)}, u32[]{:S(2)}) collective-permute-start(bf16[2,32,512]{2,1,0:T(8,128)(2,1)S(1)} %get-tuple-element.44), channel_id=1, source_target_pairs={{0,16},{4,20},{8,24},{12,28},{16,0},{20,4},{24,8},{28,12},{1,17},{... | collective-permute-start | bytes 196616 | tf_op jit(solution)/shard_map/ppermute | solution.py:313
  56.2 0.4 collective-permute-start.13
  56.6 1.3 %collective-permute-start.9 = (bf16[2,256,512]{2,1,0:T(8,128)(2,1)S(1)}, bf16[2,256,512]{2,1,0:T(8,128)(2,1)S(1)}, u32[]{:S(2)}, u32[]{:S(2)}) collective-permute-start(bf16[2,256,512]{2,1,0:T(8,128)(2,1)S(1)} %get-tuple-element.37), channel_id=1, source_target_pairs={{0,4},{4,0},{8,12},{12,8},{16,20},{20,16},{24,28},{28,24},{1,5},{5... | collective-permute-start | bytes 1572872 | tf_op jit(solution)/shard_map/ppermute | solution.py:313
  57.9 4.4 %collective-permute-done.10 = bf16[2,256,512]{2,1,0:T(8,128)(2,1)S(1)} collective-permute-done((bf16[2,256,512]{2,1,0:T(8,128)(2,1)S(1)}, bf16[2,256,512]{2,1,0:T(8,128)(2,1)S(1)}, u32[]{:S(2)}, u32[]{:S(2)}) %collective-permute-start.10) | collective-permute-done | bytes 524320 | tf_op jit(solution)/shard_map/ppermute | solution.py:313
  62.3 0.2 convert_add_fusion
  62.4 0.5 collective-permute-done.11
  63.0 0.7 collective-permute-done.12
  63.7 0.7 collective-permute-done.13
  64.4 0.7 fusion.1
  65.1 4.8 %collective-permute-start.15 = (bf16[2,256,512]{2,1,0:T(8,128)(2,1)S(1)}, bf16[2,256,512]{2,1,0:T(8,128)(2,1)S(1)}, u32[]{:S(2)}, u32[]{:S(2)}) collective-permute-start(bf16[2,256,512]{2,1,0:T(8,128)(2,1)S(1)} %fusion.1), channel_id=1, source_target_pairs={{0,4},{4,0},{8,12},{12,8},{16,20},{20,16},{24,28},{28,24},{1,5},{5... | collective-permute-start | bytes 1572872 | tf_op jit(solution)/shard_map/ppermute | solution.py:313
  70.0 1.3 %collective-permute-start.14 = (bf16[2,256,512]{2,1,0:T(8,128)(2,1)S(1)}, bf16[2,256,512]{2,1,0:T(8,128)(2,1)S(1)}, u32[]{:S(2)}, u32[]{:S(2)}) collective-permute-start(bf16[2,256,512]{2,1,0:T(8,128)(2,1)S(1)} %get-tuple-element.49), channel_id=1, source_target_pairs={{12,4},{0,8},{20,12},{8,16},{28,20},{16,24},{13,5},{1,9},{21,13},{... | collective-permute-start | bytes 1572872 | tf_op jit(solution)/shard_map/ppermute | solution.py:313
  71.3 0.0 collective-permute-done.9
  71.3 1.3 %maximum_select_fusion = (bf16[256,1024]{1,0:T(8,128)(2,1)}, bf16[256,1024]{1,0:T(8,128)(2,1)}) fusion(bf16[256,512]{1,0:T(8,128)(2,1)S(1)} %get-tuple-element.55, bf16[256,512]{1,0:T(8,128)(2,1)S(1)} %get-tuple-element.36, pred[]{:T(512)S(6)} %eq.16, bf16[256,512]{1,0:T(8,128)(2,1)S(1)} %get-tuple-element.38, bf16[256,512]{1,0:T(8,128)(2,1)S(1)} %get-tuple-element.54), kind=kLoop, calls=%fused_computation.14 | loop fusion | flops 4718592 | bytes 2097153 | tf_op jit(solution)/shard_map/jit(_where)/select_n | solution.py:353
  72.6 0.7 convolution_bitcast_fusion
  73.3 7.8 %collective-permute-done.14 = bf16[2,256,512]{2,1,0:T(8,128)(2,1)S(1)} collective-permute-done((bf16[2,256,512]{2,1,0:T(8,128)(2,1)S(1)}, bf16[2,256,512]{2,1,0:T(8,128)(2,1)S(1)}, u32[]{:S(2)}, u32[]{:S(2)}) %collective-permute-start.14) | collective-permute-done | bytes 524320 | tf_op jit(solution)/shard_map/ppermute | solution.py:313
  81.0 0.3 add_convert_fusion
  81.4 0.0 collective-permute-done.15
  81.4 1.3 %maximum_select_fusion.2 = (bf16[256,1024]{1,0:T(8,128)(2,1)}, bf16[256,1024]{1,0:T(8,128)(2,1)}) fusion(bf16[256,512]{1,0:T(8,128)(2,1)S(1)} %get-tuple-element.53, bf16[256,512]{1,0:T(8,128)(2,1)S(1)} %get-tuple-element.51, pred[]{:T(512)S(6)} %eq.16, bf16[256,512]{1,0:T(8,128)(2,1)S(1)} %get-tuple-element.50, bf16[256,512]{1,0:T(8,128)(2,1)S(1)} %get-tuple-element.52), kind=kLoop, calls=%fused_computation.16 | loop fusion | flops 4718592 | bytes 2097153 | tf_op jit(solution)/shard_map/jit(_where)/select_n | solution.py:353
  (23 shorter events, 0.2 us)
Async XLA Ops:
  0.6 1.2 %copy-start.1 = (bf16[256,1024]{1,0:T(8,128)(2,1)S(1)}, bf16[256,1024]{1,0:T(8,128)(2,1)}, u32[]{:S(2)}) copy-start(bf16[256,1024]{1,0:T(8,128)(2,1)} %v.1) | copy-start | bytes 1572868
  1.8 9.3 %collective-permute-start = (bf16[256,512]{1,0:T(8,128)(2,1)S(1)}, bf16[256,512]{1,0:T(8,128)(2,1)S(1)}, u32[]{:S(2)}, u32[]{:S(2)}) collective-permute-start(bf16[256,512]{1,0:T(8,128)(2,1)S(1)} %get-tuple-element.57), channel_id=1, source_target_pairs={{0,4},{4,0},{8,12},{12,8},{16,20},{20,16},{24,28},{28,24},{1,5},{5... | collective-permute-start | bytes 786440 | tf_op jit(solution)/shard_map/ppermute | solution.py:313
  1.9 3.4 %copy-start.4 = (bf16[8,256]{1,0:T(8,128)(2,1)S(1)}, bf16[8,256]{1,0:T(8,128)(2,1)}, u32[]{:S(2)}) copy-start(bf16[8,256]{1,0:T(8,128)(2,1)} %param.10) | copy-start | bytes 12292
  1.9 3.4 %copy-start.6 = (bf16[4,256]{1,0:T(4,128)(2,1)S(1)}, bf16[4,256]{1,0:T(4,128)(2,1)}, u32[]{:S(2)}) copy-start(bf16[4,256]{1,0:T(4,128)(2,1)} %param.11) | copy-start | bytes 6148
  2.6 3.6 %copy-start.2 = (bf16[256,1024]{1,0:T(8,128)(2,1)S(1)}, bf16[256,1024]{1,0:T(8,128)(2,1)}, u32[]{:S(2)}) copy-start(bf16[256,1024]{1,0:T(8,128)(2,1)} %q.1) | copy-start | bytes 1572868
  2.6 14.9 %collective-permute-start.1 = (bf16[256,512]{1,0:T(8,128)(2,1)}, bf16[256,512]{1,0:T(8,128)(2,1)S(1)}, u32[]{:S(2)}, u32[]{:S(2)}) collective-permute-start(bf16[256,512]{1,0:T(8,128)(2,1)} %get-tuple-element.59), channel_id=1, source_target_pairs={{0,4},{4,0},{8,12},{12,8},{16,20},{20,16},{24,28},{28,24},{1,5},{5... | collective-permute-start | bytes 786440 | tf_op jit(solution)/shard_map/ppermute | solution.py:313
  4.7 0.6 copy-start.9
  5.3 1.0 %copy-start.3 = (bf16[256,1024]{1,0:T(8,128)(2,1)S(1)}, bf16[256,1024]{1,0:T(8,128)(2,1)}, u32[]{:S(2)}) copy-start(bf16[256,1024]{1,0:T(8,128)(2,1)} %c.1) | copy-start | bytes 1572868
  11.0 18.0 %collective-permute-start.4 = (bf16[2,256,512]{2,1,0:T(8,128)(2,1)}, bf16[2,256,512]{2,1,0:T(8,128)(2,1)S(1)}, u32[]{:S(2)}, u32[]{:S(2)}) collective-permute-start(bf16[2,256,512]{2,1,0:T(8,128)(2,1)} %pad_maximum_fusion), channel_id=1, source_target_pairs={{4,12},{8,0},{12,20},{16,8},{20,28},{24,16},{5,13},{9,1},{13,21},{... | collective-permute-start | bytes 1572872 | tf_op jit(solution)/shard_map/ppermute | solution.py:313
  14.6 8.3 %collective-permute-start.2 = (bf16[256,512]{1,0:T(8,128)(2,1)S(1)}, bf16[256,512]{1,0:T(8,128)(2,1)S(1)}, u32[]{:S(2)}, u32[]{:S(2)}) collective-permute-start(bf16[256,512]{1,0:T(8,128)(2,1)S(1)} %collective-permute-done.pair_k), channel_id=1, source_target_pairs={{12,4},{0,8},{20,12},{8,16},{28,20},{16,24},{13,5},{1,9},{21,13},{... | collective-permute-start | bytes 786440 | tf_op jit(solution)/shard_map/ppermute | solution.py:313
  16.7 19.7 %copy-start = (bf16[256,1024]{1,0:T(8,128)(2,1)S(1)}, bf16[256,1024]{1,0:T(8,128)(2,1)}, u32[]{:S(2)}) copy-start(bf16[256,1024]{1,0:T(8,128)(2,1)} %k.1) | copy-start | bytes 1572868
  17.5 15.0 %collective-permute-start.5 = (bf16[2,256,512]{2,1,0:T(8,128)(2,1)}, bf16[2,256,512]{2,1,0:T(8,128)(2,1)}, u32[]{:S(2)}, u32[]{:S(2)}) collective-permute-start(bf16[2,256,512]{2,1,0:T(8,128)(2,1)} %pad_maximum_fusion.1), channel_id=1, source_target_pairs={{0,4},{4,0},{8,12},{12,8},{16,20},{20,16},{24,28},{28,24},{1,5},{5... | collective-permute-start | bytes 1572872 | tf_op jit(solution)/shard_map/ppermute | solution.py:313
  19.5 4.7 %copy-start.5 = (bf16[8,256]{1,0:T(8,128)(2,1)S(1)}, bf16[8,256]{1,0:T(8,128)(2,1)}, u32[]{:S(2)}) copy-start(bf16[8,256]{1,0:T(8,128)(2,1)} %param.10) | copy-start | bytes 12292
  19.5 4.7 %copy-start.7 = (bf16[4,256]{1,0:T(4,128)(2,1)S(1)}, bf16[4,256]{1,0:T(4,128)(2,1)}, u32[]{:S(2)}) copy-start(bf16[4,256]{1,0:T(4,128)(2,1)} %param.11) | copy-start | bytes 6148
  19.5 4.7 %copy-start.10 = (bf16[16]{0:T(256)(128)(2,1)S(1)}, bf16[16]{0:T(256)(128)(2,1)}, u32[]{:S(2)}) copy-start(bf16[16]{0:T(256)(128)(2,1)} %copy-done.9) | copy-start | bytes 100
  20.4 3.9 %copy-start.8 = (bf16[2,16,512]{2,1,0:T(8,128)(2,1)S(1)}, bf16[2,16,512]{2,1,0:T(8,128)(2,1)}, u32[]{:S(2)}) copy-start(bf16[2,16,512]{2,1,0:T(8,128)(2,1)} %fusion.2) | copy-start | bytes 98308
  22.8 9.7 %collective-permute-start.3 = (bf16[256,512]{1,0:T(8,128)(2,1)S(1)}, bf16[256,512]{1,0:T(8,128)(2,1)S(1)}, u32[]{:S(2)}, u32[]{:S(2)}) collective-permute-start(bf16[256,512]{1,0:T(8,128)(2,1)S(1)} %collective-permute-done.1.pair_v), channel_id=1, source_target_pairs={{12,4},{0,8},{20,12},{8,16},{28,20},{16,24},{13,5},{1,9},{21,13},{... | collective-permute-start | bytes 786440 | tf_op jit(solution)/shard_map/ppermute | solution.py:313
  24.3 8.8 %collective-permute-start.8 = (bf16[2,32,512]{2,1,0:T(8,128)(2,1)S(1)}, bf16[2,32,512]{2,1,0:T(8,128)(2,1)S(1)}, u32[]{:S(2)}, u32[]{:S(2)}) collective-permute-start(bf16[2,32,512]{2,1,0:T(8,128)(2,1)S(1)} %maximum_maximum_fusion), channel_id=1, source_target_pairs={{0,24},{4,28},{8,0},{12,4},{16,8},{20,12},{24,16},{28,20},{1,25},{... | collective-permute-start | bytes 196616 | tf_op jit(solution)/shard_map/ppermute | solution.py:313
  29.0 7.3 %collective-permute-start.7 = (bf16[2,32,512]{2,1,0:T(8,128)(2,1)S(1)}, bf16[2,32,512]{2,1,0:T(8,128)(2,1)S(1)}, u32[]{:S(2)}, u32[]{:S(2)}) collective-permute-start(bf16[2,32,512]{2,1,0:T(8,128)(2,1)S(1)} %maximum_maximum_fusion), channel_id=1, source_target_pairs={{0,16},{4,20},{8,24},{12,28},{16,0},{20,4},{24,8},{28,12},{1,17},{... | collective-permute-start | bytes 196616 | tf_op jit(solution)/shard_map/ppermute | solution.py:313
  29.0 7.3 %collective-permute-start.6 = (bf16[2,32,512]{2,1,0:T(8,128)(2,1)S(1)}, bf16[2,32,512]{2,1,0:T(8,128)(2,1)S(1)}, u32[]{:S(2)}, u32[]{:S(2)}) collective-permute-start(bf16[2,32,512]{2,1,0:T(8,128)(2,1)S(1)} %maximum_maximum_fusion), channel_id=1, source_target_pairs={{0,8},{4,12},{8,16},{12,20},{16,24},{20,28},{24,0},{28,4},{1,9},{5... | collective-permute-start | bytes 196616 | tf_op jit(solution)/shard_map/ppermute | solution.py:313
  52.4 9.9 %collective-permute-start.10 = (bf16[2,256,512]{2,1,0:T(8,128)(2,1)S(1)}, bf16[2,256,512]{2,1,0:T(8,128)(2,1)S(1)}, u32[]{:S(2)}, u32[]{:S(2)}) collective-permute-start(bf16[2,256,512]{2,1,0:T(8,128)(2,1)S(1)} %get-tuple-element.42), channel_id=1, source_target_pairs={{4,12},{8,0},{12,20},{16,8},{20,28},{24,16},{5,13},{9,1},{13,21},{... | collective-permute-start | bytes 1572872 | tf_op jit(solution)/shard_map/ppermute | solution.py:313
  53.7 9.3 %collective-permute-start.11 = (bf16[2,32,512]{2,1,0:T(8,128)(2,1)S(1)}, bf16[2,32,512]{2,1,0:T(8,128)(2,1)S(1)}, u32[]{:S(2)}, u32[]{:S(2)}) collective-permute-start(bf16[2,32,512]{2,1,0:T(8,128)(2,1)S(1)} %get-tuple-element.43), channel_id=1, source_target_pairs={{0,24},{4,28},{8,0},{12,4},{16,8},{20,12},{24,16},{28,20},{1,25},{... | collective-permute-start | bytes 196616 | tf_op jit(solution)/shard_map/ppermute | solution.py:313
  53.8 10.0 %collective-permute-start.12 = (bf16[2,32,512]{2,1,0:T(8,128)(2,1)S(1)}, bf16[2,32,512]{2,1,0:T(8,128)(2,1)S(1)}, u32[]{:S(2)}, u32[]{:S(2)}) collective-permute-start(bf16[2,32,512]{2,1,0:T(8,128)(2,1)S(1)} %get-tuple-element.44), channel_id=1, source_target_pairs={{0,16},{4,20},{8,24},{12,28},{16,0},{20,4},{24,8},{28,12},{1,17},{... | collective-permute-start | bytes 196616 | tf_op jit(solution)/shard_map/ppermute | solution.py:313
  56.2 8.2 %collective-permute-start.13 = (bf16[2,32,512]{2,1,0:T(8,128)(2,1)S(1)}, bf16[2,32,512]{2,1,0:T(8,128)(2,1)S(1)}, u32[]{:S(2)}, u32[]{:S(2)}) collective-permute-start(bf16[2,32,512]{2,1,0:T(8,128)(2,1)S(1)} %get-tuple-element.45), channel_id=1, source_target_pairs={{0,8},{4,12},{8,16},{12,20},{16,24},{20,28},{24,0},{28,4},{1,9},{5... | collective-permute-start | bytes 196616 | tf_op jit(solution)/shard_map/ppermute | solution.py:313
  56.6 14.7 %collective-permute-start.9 = (bf16[2,256,512]{2,1,0:T(8,128)(2,1)S(1)}, bf16[2,256,512]{2,1,0:T(8,128)(2,1)S(1)}, u32[]{:S(2)}, u32[]{:S(2)}) collective-permute-start(bf16[2,256,512]{2,1,0:T(8,128)(2,1)S(1)} %get-tuple-element.37), channel_id=1, source_target_pairs={{0,4},{4,0},{8,12},{12,8},{16,20},{20,16},{24,28},{28,24},{1,5},{5... | collective-permute-start | bytes 1572872 | tf_op jit(solution)/shard_map/ppermute | solution.py:313
  65.1 16.2 %collective-permute-start.15 = (bf16[2,256,512]{2,1,0:T(8,128)(2,1)S(1)}, bf16[2,256,512]{2,1,0:T(8,128)(2,1)S(1)}, u32[]{:S(2)}, u32[]{:S(2)}) collective-permute-start(bf16[2,256,512]{2,1,0:T(8,128)(2,1)S(1)} %fusion.1), channel_id=1, source_target_pairs={{0,4},{4,0},{8,12},{12,8},{16,20},{20,16},{24,28},{28,24},{1,5},{5... | collective-permute-start | bytes 1572872 | tf_op jit(solution)/shard_map/ppermute | solution.py:313
  70.0 11.1 %collective-permute-start.14 = (bf16[2,256,512]{2,1,0:T(8,128)(2,1)S(1)}, bf16[2,256,512]{2,1,0:T(8,128)(2,1)S(1)}, u32[]{:S(2)}, u32[]{:S(2)}) collective-permute-start(bf16[2,256,512]{2,1,0:T(8,128)(2,1)S(1)} %get-tuple-element.49), channel_id=1, source_target_pairs={{12,4},{0,8},{20,12},{8,16},{28,20},{16,24},{13,5},{1,9},{21,13},{... | collective-permute-start | bytes 1572872 | tf_op jit(solution)/shard_map/ppermute | solution.py:313

commit v2 on v1

--- a/solution.py
+++ b/solution.py
@@ -31,6 +31,15 @@
 
 def shift_pairs(size, shift):
     return [(i, (i + 2 * shift) % size) for i in range(size)]
+
+
+def doublings(pair_count):
+    steps = []
+    held = 1
+    while held < pair_count:
+        steps.append((held, min(held, pair_count - held)))
+        held += steps[-1][1]
+    return steps
 
 
 def dot(a, b):
@@ -196,8 +205,10 @@
             direct_grad[n] = second[2 * rows : 3 * rows].astype(direct_grad.dtype)
             far_grad = (first[3 * rows :] + second[3 * rows :]).astype(direct_grad.dtype)
             size = far_grad.shape[0] // shifts
-            for m, ref in enumerate(coarse_grads):
-                ref[n] = far_grad[m * size : (m + 1) * size]
+            far_grads = [far_grad[m * size : (m + 1) * size] for m in range(shifts)]
+            for ref, (distance, count) in zip(coarse_grads, doublings(shifts + 1)):
+                for m in range(count):
+                    ref[m, n] = far_grads[distance - 1 + m]
 
     return kernel
 
@@ -235,7 +246,10 @@
             + [both(coarse_rows)] * shifts,
             out_specs=[flat(lambda j, place: (0, j))] * 2
             + [both(rows)] * 5
-            + [both(coarse_rows)] * shifts,
+            + [
+                pl.BlockSpec((count, 2, coarse_rows, PAIR), lambda j, place: (0, 0, 0, j))
+                for _, count in doublings(shifts + 1)
+            ],
         ),
         out_shape=[jax.ShapeDtypeStruct((rows, columns), bf16)] * 2
         + [
@@ -245,7 +259,10 @@
             jax.ShapeDtypeStruct((2, rows, columns), bf16),
             jax.ShapeDtypeStruct((2, rows, columns), bf16),
         ]
-        + [jax.ShapeDtypeStruct((2, coarse_rows, columns), bf16)] * shifts,
+        + [
+            jax.ShapeDtypeStruct((count, 2, coarse_rows, columns), bf16)
+            for _, count in doublings(shifts + 1)
+        ],
         compiler_params=pltpu.CompilerParams(vmem_limit_bytes=GRANT),
         cost_estimate=pl.CostEstimate(
             flops=4 * products, bytes_accessed=40 * rows * columns, transcendentals=0
@@ -324,7 +341,7 @@
     pair_k, pair_v = (send(a, swap) for a in columns(1 - parity, keys, values))
     relayed_k = send(pair_k, relayed_to)
     home_kv = jnp.stack(columns(parity, keys, values))
-    direct = send(after(home_kv, pair_k), direct_to)
+    direct = send(after(home_kv, pair_v), direct_to)
     relayed_v = send(after(pair_v, relayed_k), relayed_to)
     sent_qc = jnp.stack(columns(1 - parity, queries, cotangent))
     pair_qc = send(after(sent_qc, pair_v), swap)
@@ -336,10 +353,9 @@
         axis=1,
     ).astype(jnp.bfloat16)
     coarse = [send(own_coarse, shift_pairs(size, s)) for s in shifts]
-    direct = after(direct, relayed_k)
-    relayed_v = after(relayed_v, direct)
     pair_qc = after(pair_qc, relayed_v)
-    coarse = after(coarse, pair_qc)
+    direct = after(direct, pair_qc)
+    coarse = after(coarse, direct)
 
     (
         out, grad_q, pair_out, home_grad, pair_grad, direct_grad, relayed_grad, *coarse_grads,
@@ -358,22 +374,32 @@
 
     relayed_back = send(relayed_grad, direct_to)
     out_back = send(pair_out, swap)
-    coarse_back = [send(a, shift_pairs(size, -s)) for s, a in zip(shifts, coarse_grads)]
-    pair_total = pair_grad + relayed_back.astype(jnp.float32)
-    far = sum(piece.astype(jnp.float32) for piece in after(coarse_back, pair_total))
-    pair_total = pair_total + lengthened(restrict, far[:, block_rows:])
-    pair_total = pair_total.astype(jnp.bfloat16)
+    direct_back = send(direct_grad, relayed_to)
+    pair_total = (pair_grad + relayed_back.astype(jnp.float32)).astype(jnp.bfloat16)
     grad_back = send(pair_total, swap)
-    direct_back = send(after(direct_grad, pair_total), relayed_to)
-    home_total = home_grad + direct_back.astype(jnp.float32)
-    home_total = home_total + lengthened(restrict, far[:, :block_rows])
+
+    far = None
+    for (distance, count), piece in reversed(list(zip(doublings(pair_count), coarse_grads))):
+        if far is not None:
+            piece = piece.astype(jnp.float32) + far[distance : distance + count]
+        piece = piece.astype(jnp.bfloat16)
+        back = send(piece, shift_pairs(size, -distance))
+        back = back if far is not None else after(back, pair_total)
+        back = jnp.pad(back.astype(jnp.float32), [(0, distance - count)] + [(0, 0)] * 3)
+        far = back if far is None else far[:distance] + back
+    far = far[0]
+    other_far = send(far[:, block_rows:].astype(jnp.bfloat16), swap).astype(jnp.float32)
+    out_back = after(out_back, piece)
+    own_longer = lengthened(restrict, far[:, :block_rows])
+    other_longer = lax.optimization_barrier(lengthened(restrict, other_far))
+    home_total = home_grad + direct_back.astype(jnp.float32) + own_longer
     home_total = home_total.astype(jnp.bfloat16)
-    return (
-        whole(out, out_back[0]),
-        whole(grad_q, out_back[1]),
-        whole(home_total[0], grad_back[0]),
-        whole(home_total[1], grad_back[1]),
-    )
+
+    def summed(n):
+        other = grad_back[n].astype(jnp.float32) + other_longer[n]
+        return whole(home_total[n], other.astype(jnp.bfloat16))
+
+    return whole(out, out_back[0]), whole(grad_q, out_back[1]), summed(0), summed(1)
 
 
 def solution(mesh):

time: 83.1 us -> 84.2 us (1.013)
  the two profiles are of different devices: /device:TPU:4 before, /device:TPU:0 now
where the time goes in v2:
time: 84.2 us; the launch traced here: 83.7 us
  starting transfers between devices  27.7 us (33%)
  waiting for transfers between devices  26.9 us (32%)
  Pallas kernels  16 us (19%)
  other arithmetic  5.21 us (6%)
  matrix products  3.69 us (4%)
  local copies, waits for them, and re-layouts  3.27 us (4%)
  between operations  0.97 us (1%)
    ppermute x16, starting transfers between devices, send(): return lax.ppermute(value, 'seq', pairs)  27.7 us
    ppermute x16, waiting for transfers between devices, send(): return lax.ppermute(value, 'seq', pairs)  26.9 us
    pallas_call x1, Pallas kernels, attention(): pl.pallas_call(attention_kernel(shifts), grid_spec=pltpu.PrefetchScalarGr...  16 us
    select_n x2, other arithmetic, whole(): jnp.where(parity == 0, jnp.concatenate([own, other], axis=axis), jnp.conc...  2.53 us
    dot_general x2, matrix products, dot(): return jnp.dot(a, b, preferred_element_type=jnp.float32)  1.78 us
  transfers between devices with their start and end apart: 16, of which 9 were waited for; matrix products, arithmetic and copies ran while one was open for 10% of the time, Pallas kernels for 0%

profile of v2, /device:TPU:0, one launch (start us, length us, event | category | flops | bytes accessed | tf_op | source)
XLA Modules:
  0.0 83.7 jit_solution(8056894586277743566)
XLA Ops:
  0.6 0.0 copy-start.1
  0.7 1.1 %dynamic-slice_bitcast_fusion.1 = (bf16[1,256,512]{2,1,0:T(8,128)(2,1)S(1)}, bf16[256,512]{1,0:T(8,128)(2,1)S(1)}) fusion(bf16[256,1024]{1,0:T(8,128)(2,1)} %k.1, s32[]{:T(128)S(6)} %select_n.107, s32[]{:T(128)S(6)} %select_n.106), kind=kLoop, calls=%fused_computation.27 | loop fusion | bytes 1048584 | tf_op jit(solution)/shard_map/stack | solution.py:343
  1.8 3.0 %collective-permute-start = (bf16[256,512]{1,0:T(8,128)(2,1)S(1)}, bf16[256,512]{1,0:T(8,128)(2,1)S(1)}, u32[]{:S(2)}, u32[]{:S(2)}) collective-permute-start(bf16[256,512]{1,0:T(8,128)(2,1)S(1)} %get-tuple-element.49), channel_id=1, source_target_pairs={{0,4},{4,0},{8,12},{12,8},{16,20},{20,16},{24,28},{28,24},{1,5},{5... | collective-permute-start | bytes 786440 | tf_op jit(solution)/shard_map/ppermute | solution.py:330
  4.8 0.0 copy-done.1
  4.9 0.1 collective-permute-start.1
  5.0 0.1 pad.21.clone
  5.1 0.1 fusion.16
  5.2 0.5 copy-done.10
  5.7 0.1 copy-done.5
  5.8 0.1 copy-done.7
  5.9 0.8 %fusion = bf16[2,16,512]{2,1,0:T(8,128)(2,1)} fusion(bf16[4,256]{1,0:T(4,128)(2,1)S(1)} %copy-done.7, bf16[8,256]{1,0:T(8,128)(2,1)S(1)} %copy-done.5, bf16[16]{0:T(256)(128)(2,1)S(1)} %pad.21.clone, bf16[1,256,512]{2,1,0:T(8,128)(2,1)S(1)} %get-tuple-element.50, bf16[1,256,512]{2,1,0:T(8,128)(2,1)S(1)} %get-tuple-element.48), kind=kOutput, calls=%fused_computation.3 | convolution fusion | flops 9478144 | bytes 563232 | tf_op jit(solution)/shard_map/fb,nbc->nfc/dot_general | solution.py:350
  6.7 0.1 and_select_fusion.3
  6.8 0.0 copy-start.2
  6.8 0.8 %pad_maximum_fusion.1 = bf16[2,256,512]{2,1,0:T(8,128)(2,1)} fusion(bf16[1,256,512]{2,1,0:T(8,128)(2,1)S(1)} %get-tuple-element.50, bf16[1,256,512]{2,1,0:T(8,128)(2,1)S(1)} %get-tuple-element.48), kind=kLoop, calls=%fused_computation.15 | loop fusion | flops 262144 | bytes 1048576 | tf_op jit(solution)/shard_map/stack | solution.py:343
  7.6 0.4 copy-done.2
  8.0 3.9 %collective-permute-done.pair_k = bf16[256,512]{1,0:T(8,128)(2,1)S(1)} collective-permute-done((bf16[256,512]{1,0:T(8,128)(2,1)S(1)}, bf16[256,512]{1,0:T(8,128)(2,1)S(1)}, u32[]{:S(2)}, u32[]{:S(2)}) %collective-permute-start) | collective-permute-done | bytes 262176 | tf_op jit(solution)/shard_map/ppermute | solution.py:330
  11.9 4.0 %collective-permute-start.2 = (bf16[256,512]{1,0:T(8,128)(2,1)S(1)}, bf16[256,512]{1,0:T(8,128)(2,1)S(1)}, u32[]{:S(2)}, u32[]{:S(2)}) collective-permute-start(bf16[256,512]{1,0:T(8,128)(2,1)S(1)} %collective-permute-done.pair_k), channel_id=1, source_target_pairs={{12,4},{0,8},{20,12},{8,16},{28,20},{16,24},{13,5},{1,9},{21,13},{... | collective-permute-start | bytes 786440 | tf_op jit(solution)/shard_map/ppermute | solution.py:330
  16.0 0.0 copy-done.3
  16.0 0.1 select_n.112
  16.1 0.7 select_n.113
  16.8 0.8 %pad_maximum_fusion = bf16[2,256,512]{2,1,0:T(8,128)(2,1)} fusion(bf16[1,256,512]{2,1,0:T(8,128)(2,1)S(1)} %dynamic-slice_bitcast_fusion.2, bf16[1,256,512]{2,1,0:T(8,128)(2,1)S(1)} %dynamic-slice_bitcast_fusion.3), kind=kLoop, calls=%fused_computation.14 | loop fusion | flops 262144 | bytes 1048576 | tf_op jit(solution)/shard_map/stack | solution.py:346
  17.7 0.0 collective-permute-done.1.pair_v
  17.7 0.8 collective-permute-start.4
  18.5 1.3 %collective-permute-start.5 = (bf16[2,256,512]{2,1,0:T(8,128)(2,1)}, bf16[2,256,512]{2,1,0:T(8,128)(2,1)}, u32[]{:S(2)}, u32[]{:S(2)}) collective-permute-start(bf16[2,256,512]{2,1,0:T(8,128)(2,1)} %pad_maximum_fusion.1), channel_id=1, source_target_pairs={{4,12},{8,0},{12,20},{16,8},{20,28},{24,16},{5,13},{9,1},{13,21},{... | collective-permute-start | bytes 1572872 | tf_op jit(solution)/shard_map/ppermute | solution.py:330
  19.8 0.0 copy-done.4
  19.8 0.0 collective-permute-done.2.relayed_k
  19.8 4.6 %collective-permute-start.3 = (bf16[256,512]{1,0:T(8,128)(2,1)S(1)}, bf16[256,512]{1,0:T(8,128)(2,1)S(1)}, u32[]{:S(2)}, u32[]{:S(2)}) collective-permute-start(bf16[256,512]{1,0:T(8,128)(2,1)S(1)} %collective-permute-done.1.pair_v), channel_id=1, source_target_pairs={{12,4},{0,8},{20,12},{8,16},{28,20},{16,24},{13,5},{1,9},{21,13},{... | collective-permute-start | bytes 786440 | tf_op jit(solution)/shard_map/ppermute | solution.py:330
  24.4 0.9 %fusion.1 = bf16[1,16,512]{2,1,0:T(8,128)(2,1)S(1)} fusion(bf16[256,512]{1,0:T(8,128)(2,1)S(1)} %collective-permute-done.pair_k, bf16[4,256]{1,0:T(4,128)(2,1)} %param.11, bf16[8,256]{1,0:T(8,128)(2,1)} %param.10, bf16[16]{0:T(256)(128)(2,1)} %copy-done.10), kind=kOutput, calls=%fused_computation.6 | convolution fusion | flops 4227072 | bytes 284704 | tf_op jit(solution)/shard_map/dot_general | solution.py:46
  25.3 0.9 %fusion.2 = bf16[1,16,512]{2,1,0:T(8,128)(2,1)S(1)} fusion(bf16[256,512]{1,0:T(8,128)(2,1)S(1)} %collective-permute-done.1.pair_v, bf16[4,256]{1,0:T(4,128)(2,1)} %param.11, bf16[8,256]{1,0:T(8,128)(2,1)} %param.10, bf16[16]{0:T(256)(128)(2,1)} %copy-done.10), kind=kOutput, calls=%fused_computation.7 | convolution fusion | flops 4227072 | bytes 284704 | tf_op jit(solution)/shard_map/dot_general | solution.py:46
  26.2 0.0 copy-done.9
  26.2 2.2 %collective-permute-start.8 = (bf16[2,32,512]{2,1,0:T(8,128)(2,1)S(1)}, bf16[2,32,512]{2,1,0:T(8,128)(2,1)S(1)}, u32[]{:S(2)}, u32[]{:S(2)}) collective-permute-start(bf16[2,32,512]{2,1,0:T(8,128)(2,1)S(1)} %maximum_maximum_fusion), channel_id=1, source_target_pairs={{0,24},{4,28},{8,0},{12,4},{16,8},{20,12},{24,16},{28,20},{1,25},{... | collective-permute-start | bytes 196616 | tf_op jit(solution)/shard_map/ppermute | solution.py:330
  28.4 1.3 %collective-permute-start.7 = (bf16[2,32,512]{2,1,0:T(8,128)(2,1)S(1)}, bf16[2,32,512]{2,1,0:T(8,128)(2,1)S(1)}, u32[]{:S(2)}, u32[]{:S(2)}) collective-permute-start(bf16[2,32,512]{2,1,0:T(8,128)(2,1)S(1)} %maximum_maximum_fusion), channel_id=1, source_target_pairs={{0,16},{4,20},{8,24},{12,28},{16,0},{20,4},{24,8},{28,12},{1,17},{... | collective-permute-start | bytes 196616 | tf_op jit(solution)/shard_map/ppermute | solution.py:330
  29.7 0.3 collective-permute-done.3.relayed_v
  30.0 3.0 %collective-permute-start.6 = (bf16[2,32,512]{2,1,0:T(8,128)(2,1)S(1)}, bf16[2,32,512]{2,1,0:T(8,128)(2,1)S(1)}, u32[]{:S(2)}, u32[]{:S(2)}) collective-permute-start(bf16[2,32,512]{2,1,0:T(8,128)(2,1)S(1)} %maximum_maximum_fusion), channel_id=1, source_target_pairs={{0,8},{4,12},{8,16},{12,20},{16,24},{20,28},{24,0},{28,4},{1,9},{5... | collective-permute-start | bytes 196616 | tf_op jit(solution)/shard_map/ppermute | solution.py:330
  32.9 0.1 pad_add_fusion.place
  33.0 0.0 collective-permute-done.4.pair_qc
  33.0 1.4 %collective-permute-done.5.direct = bf16[2,256,512]{2,1,0:T(8,128)(2,1)} collective-permute-done((bf16[2,256,512]{2,1,0:T(8,128)(2,1)}, bf16[2,256,512]{2,1,0:T(8,128)(2,1)}, u32[]{:S(2)}, u32[]{:S(2)}) %collective-permute-start.5) | collective-permute-done | bytes 524320 | tf_op jit(solution)/shard_map/ppermute | solution.py:330
  34.4 0.8 collective-permute-done.8.rest_2_
  35.2 4.5 %collective-permute-done.7.rest_1_ = bf16[2,32,512]{2,1,0:T(8,128)(2,1)S(1)} collective-permute-done((bf16[2,32,512]{2,1,0:T(8,128)(2,1)S(1)}, bf16[2,32,512]{2,1,0:T(8,128)(2,1)S(1)}, u32[]{:S(2)}, u32[]{:S(2)}) %collective-permute-start.7) | collective-permute-done | bytes 65568 | tf_op jit(solution)/shard_map/ppermute | solution.py:330
  39.7 0.0 collective-permute-done.6.rest_0_
  39.7 16.0 %attention.1 = (bf16[256,512]{1,0:T(8,128)(2,1)S(1)}, bf16[256,512]{1,0:T(8,128)(2,1)S(1)}, bf16[2,256,512]{2,1,0:T(8,128)(2,1)S(1)}, f32[2,256,512]{2,1,0:T(8,1...) custom-call(s32[3]{0:T(128)S(1)} %pad_add_fusion.place, ...), custom_call_target="tpu_custom_call" | custom-call | flops 10871635968 | bytes 5242880 | tf_op jit(solution)/shard_map/attention/pallas_call | solution.py:237
  55.7 1.3 %collective-permute-start.11 = (bf16[2,256,512]{2,1,0:T(8,128)(2,1)S(1)}, bf16[2,256,512]{2,1,0:T(8,128)(2,1)S(1)}, u32[]{:S(2)}, u32[]{:S(2)}) collective-permute-start(bf16[2,256,512]{2,1,0:T(8,128)(2,1)S(1)} %get-tuple-element.36), channel_id=1, source_target_pairs={{4,12},{8,0},{12,20},{16,8},{20,28},{24,16},{5,13},{9,1},{13,21},{... | collective-permute-start | bytes 1572872 | tf_op jit(solution)/shard_map/ppermute | solution.py:330
  57.0 0.9 %collective-permute-start.9 = (bf16[2,256,512]{2,1,0:T(8,128)(2,1)S(1)}, bf16[2,256,512]{2,1,0:T(8,128)(2,1)S(1)}, u32[]{:S(2)}, u32[]{:S(2)}) collective-permute-start(bf16[2,256,512]{2,1,0:T(8,128)(2,1)S(1)} %get-tuple-element.32), channel_id=1, source_target_pairs={{0,4},{4,0},{8,12},{12,8},{16,20},{20,16},{24,28},{28,24},{1,5},{5... | collective-permute-start | bytes 1572872 | tf_op jit(solution)/shard_map/ppermute | solution.py:330
  57.8 2.7 %collective-permute-start.10 = (bf16[2,2,32,512]{3,2,1,0:T(8,128)(2,1)S(1)}, bf16[2,2,32,512]{3,2,1,0:T(8,128)(2,1)S(1)}, u32[]{:S(2)}, u32[]{:S(2)}) collective-permute-start(bf16[2,2,32,512]{3,2,1,0:T(8,128)(2,1)S(1)} %get-tuple-element.34), channel_id=1, source_target_pairs={{0,16},{4,20},{8,24},{12,28},{16,0},{20,4},{24,8},{28,12},{1,17},{... | collective-permute-start | bytes 393224 | tf_op jit(solution)/shard_map/ppermute | solution.py:330
  60.5 1.7 %collective-permute-start.12 = (bf16[2,256,512]{2,1,0:T(8,128)(2,1)S(1)}, bf16[2,256,512]{2,1,0:T(8,128)(2,1)S(1)}, u32[]{:S(2)}, u32[]{:S(2)}) collective-permute-start(bf16[2,256,512]{2,1,0:T(8,128)(2,1)S(1)} %get-tuple-element.41), channel_id=1, source_target_pairs={{12,4},{0,8},{20,12},{8,16},{28,20},{16,24},{13,5},{1,9},{21,13},{... | collective-permute-start | bytes 1572872 | tf_op jit(solution)/shard_map/ppermute | solution.py:330
  62.2 8.0 %collective-permute-done.11 = bf16[2,256,512]{2,1,0:T(8,128)(2,1)S(1)} collective-permute-done((bf16[2,256,512]{2,1,0:T(8,128)(2,1)S(1)}, bf16[2,256,512]{2,1,0:T(8,128)(2,1)S(1)}, u32[]{:S(2)}, u32[]{:S(2)}) %collective-permute-start.11) | collective-permute-done | bytes 524320 | tf_op jit(solution)/shard_map/ppermute | solution.py:330
  70.3 0.2 add_convert_fusion.1
  70.4 0.1 collective-permute-start.14
  70.5 2.9 %collective-permute-done.10 = bf16[2,2,32,512]{3,2,1,0:T(8,128)(2,1)S(1)} collective-permute-done((bf16[2,2,32,512]{3,2,1,0:T(8,128)(2,1)S(1)}, bf16[2,2,32,512]{3,2,1,0:T(8,128)(2,1)S(1)}, u32[]{:S(2)}, u32[]{:S(2)}) %collective-permute-start.10) | collective-permute-done | bytes 131104 | tf_op jit(solution)/shard_map/ppermute | solution.py:330
  73.4 0.1 collective-permute-start.13
  73.5 0.0 collective-permute-done.9
  73.6 1.3 %maximum_select_fusion = (bf16[256,1024]{1,0:T(8,128)(2,1)}, bf16[256,1024]{1,0:T(8,128)(2,1)}) fusion(bf16[256,512]{1,0:T(8,128)(2,1)S(1)} %get-tuple-element.47, bf16[256,512]{1,0:T(8,128)(2,1)S(1)} %get-tuple-element.31, pred[]{:T(512)S(6)} %eq.16, bf16[256,512]{1,0:T(8,128)(2,1)S(1)} %get-tuple-element.39, bf16[256,512]{1,0:T(8,128)(2,1)S(1)} %get-tuple-element.46), kind=kLoop, calls=%fused_computation.16 | loop fusion | flops 4718592 | bytes 2097153 | tf_op jit(solution)/shard_map/jit(_where)/select_n | solution.py:369
  74.8 2.9 %collective-permute-done.13 = bf16[1,2,32,512]{3,2,1,0:T(8,128)(2,1)S(1)} collective-permute-done((bf16[1,2,32,512]{3,2,1,0:T(8,128)(2,1)S(1)}, bf16[1,2,32,512]{3,2,1,0:T(8,128)(2,1)S(1)}, u32[]{:S(2)}, u32[]{:S(2)}) %collective-permute-start.13) | collective-permute-done | bytes 65568 | tf_op jit(solution)/shard_map/ppermute | solution.py:330
  77.8 0.0 copy-start.6
  77.8 0.0 copy-start.8
  77.8 0.8 collective-permute-start.15
  78.6 0.7 convolution_bitcast_fusion.1
  79.3 0.0 collective-permute-done.12
  79.3 0.3 add_convert_fusion
  79.6 2.2 %collective-permute-done.15 = bf16[2,16,512]{2,1,0:T(8,128)(2,1)S(1)} collective-permute-done((bf16[2,16,512]{2,1,0:T(8,128)(2,1)S(1)}, bf16[2,16,512]{2,1,0:T(8,128)(2,1)S(1)}, u32[]{:S(2)}, u32[]{:S(2)}) %collective-permute-start.15) | collective-permute-done | bytes 32800 | tf_op jit(solution)/shard_map/ppermute | solution.py:330
  81.8 0.4 convolution_bitcast_fusion
  82.2 0.0 collective-permute-done.14
  82.2 0.2 fusion.6
  82.4 1.3 %maximum_select_fusion.2 = (bf16[256,1024]{1,0:T(8,128)(2,1)}, bf16[256,1024]{1,0:T(8,128)(2,1)}) fusion(bf16[256,512]{1,0:T(8,128)(2,1)S(1)} %get-tuple-element.43, bf16[256,512]{1,0:T(8,128)(2,1)S(1)} %get-tuple-element.45, pred[]{:T(512)S(6)} %eq.16, bf16[256,512]{1,0:T(8,128)(2,1)S(1)} %get-tuple-element.44, bf16[256,512]{1,0:T(8,128)(2,1)S(1)} %get-tuple-element.42), kind=kLoop, calls=%fused_computation.18 | loop fusion | flops 4718592 | bytes 2097153 | tf_op jit(solution)/shard_map/jit(_where)/select_n | solution.py:369
  (28 shorter events, 0.3 us)
Async XLA Ops:
  0.6 4.2 %copy-start.1 = (bf16[256,1024]{1,0:T(8,128)(2,1)S(1)}, bf16[256,1024]{1,0:T(8,128)(2,1)}, u32[]{:S(2)}) copy-start(bf16[256,1024]{1,0:T(8,128)(2,1)} %v.1) | copy-start | bytes 1572868
  1.8 10.2 %collective-permute-start = (bf16[256,512]{1,0:T(8,128)(2,1)S(1)}, bf16[256,512]{1,0:T(8,128)(2,1)S(1)}, u32[]{:S(2)}, u32[]{:S(2)}) collective-permute-start(bf16[256,512]{1,0:T(8,128)(2,1)S(1)} %get-tuple-element.49), channel_id=1, source_target_pairs={{0,4},{4,0},{8,12},{12,8},{16,20},{20,16},{24,28},{28,24},{1,5},{5... | collective-permute-start | bytes 786440 | tf_op jit(solution)/shard_map/ppermute | solution.py:330
  4.9 12.8 %collective-permute-start.1 = (bf16[256,512]{1,0:T(8,128)(2,1)S(1)}, bf16[256,512]{1,0:T(8,128)(2,1)S(1)}, u32[]{:S(2)}, u32[]{:S(2)}) collective-permute-start(bf16[256,512]{1,0:T(8,128)(2,1)S(1)} %get-tuple-element.51), channel_id=1, source_target_pairs={{0,4},{4,0},{8,12},{12,8},{16,20},{20,16},{24,28},{28,24},{1,5},{5... | collective-permute-start | bytes 786440 | tf_op jit(solution)/shard_map/ppermute | solution.py:330
  5.1 0.6 copy-start.10
  5.1 0.7 copy-start.5
  5.2 0.7 copy-start.7
  6.8 1.2 %copy-start.2 = (bf16[256,1024]{1,0:T(8,128)(2,1)S(1)}, bf16[256,1024]{1,0:T(8,128)(2,1)}, u32[]{:S(2)}) copy-start(bf16[256,1024]{1,0:T(8,128)(2,1)} %q.1) | copy-start | bytes 1572868
  8.0 8.0 %copy-start.3 = (bf16[256,1024]{1,0:T(8,128)(2,1)S(1)}, bf16[256,1024]{1,0:T(8,128)(2,1)}, u32[]{:S(2)}) copy-start(bf16[256,1024]{1,0:T(8,128)(2,1)} %c.1) | copy-start | bytes 1572868
  11.9 7.9 %collective-permute-start.2 = (bf16[256,512]{1,0:T(8,128)(2,1)S(1)}, bf16[256,512]{1,0:T(8,128)(2,1)S(1)}, u32[]{:S(2)}, u32[]{:S(2)}) collective-permute-start(bf16[256,512]{1,0:T(8,128)(2,1)S(1)} %collective-permute-done.pair_k), channel_id=1, source_target_pairs={{12,4},{0,8},{20,12},{8,16},{28,20},{16,24},{13,5},{1,9},{21,13},{... | collective-permute-start | bytes 786440 | tf_op jit(solution)/shard_map/ppermute | solution.py:330
  16.8 2.9 %copy-start.4 = (f32[1,96,1]{2,1,0:T(8,128)S(1)}, f32[1,96,1]{2,1,0:T(8,128)}, u32[]{:S(2)}) copy-start(f32[1,96,1]{2,1,0:T(8,128)} %select_n.113) | copy-start | bytes 1156
  17.7 22.0 %copy-start = (bf16[256,1024]{1,0:T(8,128)(2,1)S(1)}, bf16[256,1024]{1,0:T(8,128)(2,1)}, u32[]{:S(2)}) copy-start(bf16[256,1024]{1,0:T(8,128)(2,1)} %k.1) | copy-start | bytes 1572868
  17.7 15.3 %collective-permute-start.4 = (bf16[2,256,512]{2,1,0:T(8,128)(2,1)}, bf16[2,256,512]{2,1,0:T(8,128)(2,1)S(1)}, u32[]{:S(2)}, u32[]{:S(2)}) collective-permute-start(bf16[2,256,512]{2,1,0:T(8,128)(2,1)} %pad_maximum_fusion), channel_id=1, source_target_pairs={{0,4},{4,0},{8,12},{12,8},{16,20},{20,16},{24,28},{28,24},{1,5},{5... | collective-permute-start | bytes 1572872 | tf_op jit(solution)/shard_map/ppermute | solution.py:330
  18.5 16.0 %collective-permute-start.5 = (bf16[2,256,512]{2,1,0:T(8,128)(2,1)}, bf16[2,256,512]{2,1,0:T(8,128)(2,1)}, u32[]{:S(2)}, u32[]{:S(2)}) collective-permute-start(bf16[2,256,512]{2,1,0:T(8,128)(2,1)} %pad_maximum_fusion.1), channel_id=1, source_target_pairs={{4,12},{8,0},{12,20},{16,8},{20,28},{24,16},{5,13},{9,1},{13,21},{... | collective-permute-start | bytes 1572872 | tf_op jit(solution)/shard_map/ppermute | solution.py:330
  19.8 10.1 %collective-permute-start.3 = (bf16[256,512]{1,0:T(8,128)(2,1)S(1)}, bf16[256,512]{1,0:T(8,128)(2,1)S(1)}, u32[]{:S(2)}, u32[]{:S(2)}) collective-permute-start(bf16[256,512]{1,0:T(8,128)(2,1)S(1)} %collective-permute-done.1.pair_v), channel_id=1, source_target_pairs={{12,4},{0,8},{20,12},{8,16},{28,20},{16,24},{13,5},{1,9},{21,13},{... | collective-permute-start | bytes 786440 | tf_op jit(solution)/shard_map/ppermute | solution.py:330
  25.3 0.9 %copy-start.9 = (bf16[2,16,512]{2,1,0:T(8,128)(2,1)S(1)}, bf16[2,16,512]{2,1,0:T(8,128)(2,1)}, u32[]{:S(2)}) copy-start(bf16[2,16,512]{2,1,0:T(8,128)(2,1)} %fusion) | copy-start | bytes 98308
  26.2 9.0 %collective-permute-start.8 = (bf16[2,32,512]{2,1,0:T(8,128)(2,1)S(1)}, bf16[2,32,512]{2,1,0:T(8,128)(2,1)S(1)}, u32[]{:S(2)}, u32[]{:S(2)}) collective-permute-start(bf16[2,32,512]{2,1,0:T(8,128)(2,1)S(1)} %maximum_maximum_fusion), channel_id=1, source_target_pairs={{0,24},{4,28},{8,0},{12,4},{16,8},{20,12},{24,16},{28,20},{1,25},{... | collective-permute-start | bytes 196616 | tf_op jit(solution)/shard_map/ppermute | solution.py:330
  28.4 11.3 %collective-permute-start.7 = (bf16[2,32,512]{2,1,0:T(8,128)(2,1)S(1)}, bf16[2,32,512]{2,1,0:T(8,128)(2,1)S(1)}, u32[]{:S(2)}, u32[]{:S(2)}) collective-permute-start(bf16[2,32,512]{2,1,0:T(8,128)(2,1)S(1)} %maximum_maximum_fusion), channel_id=1, source_target_pairs={{0,16},{4,20},{8,24},{12,28},{16,0},{20,4},{24,8},{28,12},{1,17},{... | collective-permute-start | bytes 196616 | tf_op jit(solution)/shard_map/ppermute | solution.py:330
  30.0 9.7 %collective-permute-start.6 = (bf16[2,32,512]{2,1,0:T(8,128)(2,1)S(1)}, bf16[2,32,512]{2,1,0:T(8,128)(2,1)S(1)}, u32[]{:S(2)}, u32[]{:S(2)}) collective-permute-start(bf16[2,32,512]{2,1,0:T(8,128)(2,1)S(1)} %maximum_maximum_fusion), channel_id=1, source_target_pairs={{0,8},{4,12},{8,16},{12,20},{16,24},{20,28},{24,0},{28,4},{1,9},{5... | collective-permute-start | bytes 196616 | tf_op jit(solution)/shard_map/ppermute | solution.py:330
  55.7 14.6 %collective-permute-start.11 = (bf16[2,256,512]{2,1,0:T(8,128)(2,1)S(1)}, bf16[2,256,512]{2,1,0:T(8,128)(2,1)S(1)}, u32[]{:S(2)}, u32[]{:S(2)}) collective-permute-start(bf16[2,256,512]{2,1,0:T(8,128)(2,1)S(1)} %get-tuple-element.36), channel_id=1, source_target_pairs={{4,12},{8,0},{12,20},{16,8},{20,28},{24,16},{5,13},{9,1},{13,21},{... | collective-permute-start | bytes 1572872 | tf_op jit(solution)/shard_map/ppermute | solution.py:330
  57.0 16.5 %collective-permute-start.9 = (bf16[2,256,512]{2,1,0:T(8,128)(2,1)S(1)}, bf16[2,256,512]{2,1,0:T(8,128)(2,1)S(1)}, u32[]{:S(2)}, u32[]{:S(2)}) collective-permute-start(bf16[2,256,512]{2,1,0:T(8,128)(2,1)S(1)} %get-tuple-element.32), channel_id=1, source_target_pairs={{0,4},{4,0},{8,12},{12,8},{16,20},{20,16},{24,28},{28,24},{1,5},{5... | collective-permute-start | bytes 1572872 | tf_op jit(solution)/shard_map/ppermute | solution.py:330
  57.8 15.5 %collective-permute-start.10 = (bf16[2,2,32,512]{3,2,1,0:T(8,128)(2,1)S(1)}, bf16[2,2,32,512]{3,2,1,0:T(8,128)(2,1)S(1)}, u32[]{:S(2)}, u32[]{:S(2)}) collective-permute-start(bf16[2,2,32,512]{3,2,1,0:T(8,128)(2,1)S(1)} %get-tuple-element.34), channel_id=1, source_target_pairs={{0,16},{4,20},{8,24},{12,28},{16,0},{20,4},{24,8},{28,12},{1,17},{... | collective-permute-start | bytes 393224 | tf_op jit(solution)/shard_map/ppermute | solution.py:330
  60.5 18.8 %collective-permute-start.12 = (bf16[2,256,512]{2,1,0:T(8,128)(2,1)S(1)}, bf16[2,256,512]{2,1,0:T(8,128)(2,1)S(1)}, u32[]{:S(2)}, u32[]{:S(2)}) collective-permute-start(bf16[2,256,512]{2,1,0:T(8,128)(2,1)S(1)} %get-tuple-element.41), channel_id=1, source_target_pairs={{12,4},{0,8},{20,12},{8,16},{28,20},{16,24},{13,5},{1,9},{21,13},{... | collective-permute-start | bytes 1572872 | tf_op jit(solution)/shard_map/ppermute | solution.py:330
  70.4 11.8 %collective-permute-start.14 = (bf16[2,256,512]{2,1,0:T(8,128)(2,1)S(1)}, bf16[2,256,512]{2,1,0:T(8,128)(2,1)S(1)}, u32[]{:S(2)}, u32[]{:S(2)}) collective-permute-start(bf16[2,256,512]{2,1,0:T(8,128)(2,1)S(1)} %add_convert_fusion.1), channel_id=1, source_target_pairs={{0,4},{4,0},{8,12},{12,8},{16,20},{20,16},{24,28},{28,24},{1,5},{5... | collective-permute-start | bytes 1572872 | tf_op jit(solution)/shard_map/ppermute | solution.py:330
  73.4 4.3 %collective-permute-start.13 = (bf16[1,2,32,512]{3,2,1,0:T(8,128)(2,1)S(1)}, bf16[1,2,32,512]{3,2,1,0:T(8,128)(2,1)S(1)}, u32[]{:S(2)}, u32[]{:S(2)}) collective-permute-start(bf16[1,2,32,512]{3,2,1,0:T(8,128)(2,1)S(1)} %fusion.8), channel_id=1, source_target_pairs={{0,24},{4,28},{8,0},{12,4},{16,8},{20,12},{24,16},{28,20},{1,25},{... | collective-permute-start | bytes 196616 | tf_op jit(solution)/shard_map/ppermute | solution.py:330
  77.8 0.8 copy-start.6
  77.8 0.8 copy-start.8
  77.8 0.8 copy-start.11
  77.8 4.0 %collective-permute-start.15 = (bf16[2,16,512]{2,1,0:T(8,128)(2,1)S(1)}, bf16[2,16,512]{2,1,0:T(8,128)(2,1)S(1)}, u32[]{:S(2)}, u32[]{:S(2)}) collective-permute-start(bf16[2,16,512]{2,1,0:T(8,128)(2,1)S(1)} %slice.84), channel_id=1, source_target_pairs={{0,4},{4,0},{8,12},{12,8},{16,20},{20,16},{24,28},{28,24},{1,5},{5... | collective-permute-start | bytes 98312 | tf_op jit(solution)/shard_map/ppermute | solution.py:330

commit v3 on v2

--- a/solution.py
+++ b/solution.py
@@ -68,12 +68,13 @@
 class Unit:
     def __init__(self, query, cotangent, keys, values, keys_t, values_t, bias):
         scaled = query.astype(jnp.float32) * (1.0 / math.sqrt(HEAD_DIM))
+        scaled = scaled.astype(jnp.bfloat16)
         self.rows = query.shape[0]
         self.keys, self.values, self.keys_t, self.values_t = (keys, values, keys_t, values_t)
         self.bias = bias
-        self.query_wide = block_diagonal(scaled.T.astype(jnp.bfloat16))
-        self.query_tall = stacked_heads(scaled).astype(jnp.bfloat16)
-        self.cotangent_t = cotangent.astype(jnp.float32).T
+        self.query_wide = block_diagonal(scaled.T)
+        self.query_tall = stacked_heads(scaled)
+        self.cotangent_t = cotangent.T.astype(jnp.float32)
         self.scores = {}
         self.highest = None
         self.total = 0.0
@@ -114,8 +115,9 @@
         share = 1.0 / jnp.sum(self.total, axis=0, keepdims=True)
         shares = [share[:, self.columns(h)] for h in range(2)]
         out_t = jnp.concatenate([self.raw[h] * shares[h] for h in range(2)], axis=0)
-        self.out = out_t.T.astype(jnp.bfloat16)
-        product = self.cotangent_t * out_t.astype(jnp.bfloat16).astype(jnp.float32)
+        out_t = out_t.astype(jnp.bfloat16)
+        self.out = out_t.T
+        product = self.cotangent_t * out_t.astype(jnp.float32)
         self.delta = jnp.concatenate(
             [
                 jnp.sum(head_rows(product, h), axis=0, keepdims=True) * shares[h]
@@ -126,8 +128,9 @@
         shared_t = jnp.concatenate(
             [head_rows(self.cotangent_t, h) * shares[h] for h in range(2)], axis=0
         )
-        self.cotangent_wide = block_diagonal(shared_t.astype(jnp.bfloat16))
-        self.cotangent_tall = stacked_heads(shared_t.T).astype(jnp.bfloat16)
+        shared_t = shared_t.astype(jnp.bfloat16)
+        self.cotangent_wide = block_diagonal(shared_t)
+        self.cotangent_tall = stacked_heads(shared_t.T)
 
     def differentiate(self, part):
         weight = self.weights[part.start]
@@ -146,7 +149,7 @@
 
     def grad_q(self):
         grad_q_t = jnp.concatenate(self.grad_q_t, axis=0) * (1.0 / math.sqrt(HEAD_DIM))
-        return grad_q_t.T.astype(jnp.bfloat16)
+        return grad_q_t.astype(jnp.bfloat16).T
 
     def key_grad(self, n):
         return jnp.concatenate([grads[n] for grads in self.grads], axis=0)
@@ -166,15 +169,23 @@
         def halo(have):
             return jnp.full((rows, 1), jnp.where(have > 0, 0.0, masked_bias), jnp.float32)
 
-        def key_rows(n, home, partner, halo):
+        def chunk(pieces):
+            return jnp.concatenate(pieces, axis=0), jnp.concatenate([a.T for a in pieces], axis=1)
+
+        def shared(n, home, partner):
             far = jnp.concatenate([ref[n] for ref in coarse], axis=0)
-            pieces = [home[...], partner[...], halo, far]
-            transposed = [piece.T for piece in pieces]
-            return jnp.concatenate(pieces, axis=0), jnp.concatenate(transposed, axis=1)
+            return chunk([home[...], partner[...]]), chunk([far])
+
+        both_keys, both_values = (shared(0, k, pair_k), shared(1, v, pair_v))
+
+        def key_rows(outer, near_far):
+            near, far = near_far
+            pieces = [near, chunk([outer]), far]
+            return [jnp.concatenate([a[n] for a in pieces], axis=n) for n in range(2)]
 
         def unit(query, cotangent, outer_k, outer_v, have, bias):
-            keys, keys_t = key_rows(0, k, pair_k, outer_k)
-            values, values_t = key_rows(1, v, pair_v, outer_v)
+            keys, keys_t = key_rows(outer_k, both_keys)
+            values, values_t = key_rows(outer_v, both_values)
             bias = jnp.concatenate([halo(have), bias], axis=0)
             return Unit(query, cotangent, keys, values, keys_t, values_t, bias)
 
@@ -341,7 +352,7 @@
     pair_k, pair_v = (send(a, swap) for a in columns(1 - parity, keys, values))
     relayed_k = send(pair_k, relayed_to)
     home_kv = jnp.stack(columns(parity, keys, values))
-    direct = send(after(home_kv, pair_v), direct_to)
+    direct = send(after(home_kv, pair_k), direct_to)
     relayed_v = send(after(pair_v, relayed_k), relayed_to)
     sent_qc = jnp.stack(columns(1 - parity, queries, cotangent))
     pair_qc = send(after(sent_qc, pair_v), swap)
@@ -353,9 +364,10 @@
         axis=1,
     ).astype(jnp.bfloat16)
     coarse = [send(own_coarse, shift_pairs(size, s)) for s in shifts]
+    direct = after(direct, relayed_k)
+    relayed_v = after(relayed_v, direct)
     pair_qc = after(pair_qc, relayed_v)
-    direct = after(direct, pair_qc)
-    coarse = after(coarse, direct)
+    coarse = after(coarse, pair_qc)
 
     (
         out, grad_q, pair_out, home_grad, pair_grad, direct_grad, relayed_grad, *coarse_grads,

time: 84.2 us -> 81.5 us (0.968)
  waiting for transfers between devices: 26.9 us -> 23.7 us
    ppermute x16, waiting for transfers between devices: 26.9 us -> 23.7 us  [send(): return lax.ppermute(value, 'seq', pairs)]
  transfers between devices with their start and end apart: 16 -> 16, of which waited for: 9 -> 8; matrix products, arithmetic and copies ran while one was open for 10% -> 12% of each run, Pallas kernels for 0% -> 0%
where the time goes in v3:
time: 81.5 us; the launch traced here: 81 us
  starting transfers between devices  27.9 us (34%)
  waiting for transfers between devices  23.7 us (29%)
  Pallas kernels  15.9 us (20%)
  other arithmetic  6.04 us (7%)
  local copies, waits for them, and re-layouts  3.51 us (4%)
  matrix products  3.01 us (4%)
  between operations  0.96 us (1%)
    ppermute x16, starting transfers between devices, send(): return lax.ppermute(value, 'seq', pairs)  27.9 us
    ppermute x16, waiting for transfers between devices, send(): return lax.ppermute(value, 'seq', pairs)  23.7 us
    pallas_call x1, Pallas kernels, attention(): pl.pallas_call(attention_kernel(shifts), grid_spec=pltpu.PrefetchScalarGr...  15.9 us
    select_n x2, other arithmetic, whole(): jnp.where(parity == 0, jnp.concatenate([own, other], axis=axis), jnp.conc...  2.53 us
    another operation x2, local copies, waits for them, and re-layouts, per_device(): home_kv = jnp.stack(columns(parity, keys, values))  1.86 us
  transfers between devices with their start and end apart: 16, of which 8 were waited for; matrix products, arithmetic and copies ran while one was open for 12% of the time, Pallas kernels for 0%

profile of v3, /device:TPU:0, one launch (start us, length us, event | category | flops | bytes accessed | tf_op | source)
XLA Modules:
  0.0 81.0 jit_solution(8888826068992074448)
XLA Ops:
  0.6 0.0 copy-start.1
  0.7 1.1 %dynamic-slice_bitcast_fusion.3 = (bf16[1,256,512]{2,1,0:T(8,128)(2,1)S(1)}, bf16[256,512]{1,0:T(8,128)(2,1)S(1)}) fusion(bf16[256,1024]{1,0:T(8,128)(2,1)} %k.1, s32[]{:T(128)S(6)} %select_n.107, s32[]{:T(128)S(6)} %select_n.106), kind=kLoop, calls=%fused_computation.29 | loop fusion | bytes 1048584 | tf_op jit(solution)/shard_map/stack | solution.py:354
  1.8 3.0 %collective-permute-start = (bf16[256,512]{1,0:T(8,128)(2,1)S(1)}, bf16[256,512]{1,0:T(8,128)(2,1)S(1)}, u32[]{:S(2)}, u32[]{:S(2)}) collective-permute-start(bf16[256,512]{1,0:T(8,128)(2,1)S(1)} %get-tuple-element.51), channel_id=1, source_target_pairs={{0,4},{4,0},{8,12},{12,8},{16,20},{20,16},{24,28},{28,24},{1,5},{5... | collective-permute-start | bytes 786440 | tf_op jit(solution)/shard_map/ppermute | solution.py:341
  4.8 0.0 copy-done.1
  4.8 0.7 dynamic-slice_bitcast_fusion.2
  5.6 0.1 collective-permute-start.1
  5.7 0.1 pad.21.clone
  5.7 0.1 fusion.16
  5.8 0.5 copy-done.9
  6.3 0.0 copy-done.4
  6.3 0.0 copy-done.6
  6.3 0.8 %fusion = bf16[2,16,512]{2,1,0:T(8,128)(2,1)} fusion(bf16[4,256]{1,0:T(4,128)(2,1)S(1)} %copy-done.6, bf16[8,256]{1,0:T(8,128)(2,1)S(1)} %copy-done.4, bf16[16]{0:T(256)(128)(2,1)S(1)} %pad.21.clone, bf16[1,256,512]{2,1,0:T(8,128)(2,1)S(1)} %get-tuple-element.52, bf16[1,256,512]{2,1,0:T(8,128)(2,1)S(1)} %get-tuple-element.50), kind=kOutput, calls=%fused_computation.3 | convolution fusion | flops 9478144 | bytes 563232 | tf_op jit(solution)/shard_map/fb,nbc->nfc/dot_general | solution.py:361
  7.1 0.1 and_select_fusion.3
  7.2 0.0 copy-done.2
  7.3 0.1 copy-done.3
  7.4 0.8 %pad_maximum_fusion = bf16[2,256,512]{2,1,0:T(8,128)(2,1)} fusion(bf16[1,256,512]{2,1,0:T(8,128)(2,1)S(1)} %get-tuple-element.52, bf16[1,256,512]{2,1,0:T(8,128)(2,1)S(1)} %get-tuple-element.50), kind=kLoop, calls=%fused_computation.14 | loop fusion | flops 262144 | bytes 1048576 | tf_op jit(solution)/shard_map/stack | solution.py:354
  8.3 3.7 %collective-permute-done.pair_k = bf16[256,512]{1,0:T(8,128)(2,1)S(1)} collective-permute-done((bf16[256,512]{1,0:T(8,128)(2,1)S(1)}, bf16[256,512]{1,0:T(8,128)(2,1)S(1)}, u32[]{:S(2)}, u32[]{:S(2)}) %collective-permute-start) | collective-permute-done | bytes 262176 | tf_op jit(solution)/shard_map/ppermute | solution.py:341
  11.9 1.3 %collective-permute-start.4 = (bf16[2,256,512]{2,1,0:T(8,128)(2,1)}, bf16[2,256,512]{2,1,0:T(8,128)(2,1)S(1)}, u32[]{:S(2)}, u32[]{:S(2)}) collective-permute-start(bf16[2,256,512]{2,1,0:T(8,128)(2,1)} %pad_maximum_fusion), channel_id=1, source_target_pairs={{4,12},{8,0},{12,20},{16,8},{20,28},{24,16},{5,13},{9,1},{13,21},{... | collective-permute-start | bytes 1572872 | tf_op jit(solution)/shard_map/ppermute | solution.py:341
  13.2 4.7 %collective-permute-start.2 = (bf16[256,512]{1,0:T(8,128)(2,1)S(1)}, bf16[256,512]{1,0:T(8,128)(2,1)S(1)}, u32[]{:S(2)}, u32[]{:S(2)}) collective-permute-start(bf16[256,512]{1,0:T(8,128)(2,1)S(1)} %collective-permute-done.pair_k), channel_id=1, source_target_pairs={{12,4},{0,8},{20,12},{8,16},{28,20},{16,24},{13,5},{1,9},{21,13},{... | collective-permute-start | bytes 786440 | tf_op jit(solution)/shard_map/ppermute | solution.py:341
  17.9 0.8 %pad_maximum_fusion.1 = bf16[2,256,512]{2,1,0:T(8,128)(2,1)} fusion(bf16[1,256,512]{2,1,0:T(8,128)(2,1)S(1)} %dynamic-slice_bitcast_fusion, bf16[1,256,512]{2,1,0:T(8,128)(2,1)S(1)} %dynamic-slice_bitcast_fusion.1), kind=kLoop, calls=%fused_computation.15 | loop fusion | flops 262144 | bytes 1048576 | tf_op jit(solution)/shard_map/stack | solution.py:357
  18.8 0.1 select_n.112
  18.8 0.7 select_n.113
  19.6 0.0 collective-permute-done.1.pair_v
  19.6 0.9 %collective-permute-start.5 = (bf16[2,256,512]{2,1,0:T(8,128)(2,1)}, bf16[2,256,512]{2,1,0:T(8,128)(2,1)}, u32[]{:S(2)}, u32[]{:S(2)}) collective-permute-start(bf16[2,256,512]{2,1,0:T(8,128)(2,1)} %pad_maximum_fusion.1), channel_id=1, source_target_pairs={{0,4},{4,0},{8,12},{12,8},{16,20},{20,16},{24,28},{28,24},{1,5},{5... | collective-permute-start | bytes 1572872 | tf_op jit(solution)/shard_map/ppermute | solution.py:341
  20.5 0.8 pad_maximum_fusion.2.bias
  21.3 0.0 copy-start.5
  21.3 0.0 copy-start.7
  21.3 0.9 %fusion.1 = bf16[1,16,512]{2,1,0:T(8,128)(2,1)S(1)} fusion(bf16[256,512]{1,0:T(8,128)(2,1)S(1)} %collective-permute-done.pair_k, bf16[4,256]{1,0:T(4,128)(2,1)} %param.11, bf16[8,256]{1,0:T(8,128)(2,1)} %param.10, bf16[16]{0:T(256)(128)(2,1)} %copy-done.9), kind=kOutput, calls=%fused_computation.6 | convolution fusion | flops 4227072 | bytes 284704 | tf_op jit(solution)/shard_map/dot_general | solution.py:46
  22.3 0.0 collective-permute-done.2.relayed_k
  22.3 4.7 %collective-permute-start.3 = (bf16[256,512]{1,0:T(8,128)(2,1)S(1)}, bf16[256,512]{1,0:T(8,128)(2,1)S(1)}, u32[]{:S(2)}, u32[]{:S(2)}) collective-permute-start(bf16[256,512]{1,0:T(8,128)(2,1)S(1)} %collective-permute-done.1.pair_v), channel_id=1, source_target_pairs={{12,4},{0,8},{20,12},{8,16},{28,20},{16,24},{13,5},{1,9},{21,13},{... | collective-permute-start | bytes 786440 | tf_op jit(solution)/shard_map/ppermute | solution.py:341
  27.0 0.2 fusion.2
  27.2 0.0 copy-done.8
  27.2 1.4 %collective-permute-start.8 = (bf16[2,32,512]{2,1,0:T(8,128)(2,1)S(1)}, bf16[2,32,512]{2,1,0:T(8,128)(2,1)S(1)}, u32[]{:S(2)}, u32[]{:S(2)}) collective-permute-start(bf16[2,32,512]{2,1,0:T(8,128)(2,1)S(1)} %maximum_maximum_fusion), channel_id=1, source_target_pairs={{0,24},{4,28},{8,0},{12,4},{16,8},{20,12},{24,16},{28,20},{1,25},{... | collective-permute-start | bytes 196616 | tf_op jit(solution)/shard_map/ppermute | solution.py:341
  28.6 1.6 %collective-permute-start.7 = (bf16[2,32,512]{2,1,0:T(8,128)(2,1)S(1)}, bf16[2,32,512]{2,1,0:T(8,128)(2,1)S(1)}, u32[]{:S(2)}, u32[]{:S(2)}) collective-permute-start(bf16[2,32,512]{2,1,0:T(8,128)(2,1)S(1)} %maximum_maximum_fusion), channel_id=1, source_target_pairs={{0,16},{4,20},{8,24},{12,28},{16,0},{20,4},{24,8},{28,12},{1,17},{... | collective-permute-start | bytes 196616 | tf_op jit(solution)/shard_map/ppermute | solution.py:341
  30.3 0.0 collective-permute-done.4.direct
  30.3 1.6 %collective-permute-start.6 = (bf16[2,32,512]{2,1,0:T(8,128)(2,1)S(1)}, bf16[2,32,512]{2,1,0:T(8,128)(2,1)S(1)}, u32[]{:S(2)}, u32[]{:S(2)}) collective-permute-start(bf16[2,32,512]{2,1,0:T(8,128)(2,1)S(1)} %maximum_maximum_fusion), channel_id=1, source_target_pairs={{0,8},{4,12},{8,16},{12,20},{16,24},{20,28},{24,0},{28,4},{1,9},{5... | collective-permute-start | bytes 196616 | tf_op jit(solution)/shard_map/ppermute | solution.py:341
  31.8 0.1 pad_add_fusion.place
  31.9 0.0 collective-permute-done.3.relayed_v
  31.9 0.0 collective-permute-done.5.pair_qc
  31.9 0.6 collective-permute-done.8.rest_2_
  32.5 2.0 %collective-permute-done.7.rest_1_ = bf16[2,32,512]{2,1,0:T(8,128)(2,1)S(1)} collective-permute-done((bf16[2,32,512]{2,1,0:T(8,128)(2,1)S(1)}, bf16[2,32,512]{2,1,0:T(8,128)(2,1)S(1)}, u32[]{:S(2)}, u32[]{:S(2)}) %collective-permute-start.7) | collective-permute-done | bytes 65568 | tf_op jit(solution)/shard_map/ppermute | solution.py:341
  34.5 1.8 %collective-permute-done.6.rest_0_ = bf16[2,32,512]{2,1,0:T(8,128)(2,1)S(1)} collective-permute-done((bf16[2,32,512]{2,1,0:T(8,128)(2,1)S(1)}, bf16[2,32,512]{2,1,0:T(8,128)(2,1)S(1)}, u32[]{:S(2)}, u32[]{:S(2)}) %collective-permute-start.6) | collective-permute-done | bytes 65568 | tf_op jit(solution)/shard_map/ppermute | solution.py:341
  36.3 15.9 %attention.1 = (bf16[256,512]{1,0:T(8,128)(2,1)S(1)}, bf16[256,512]{1,0:T(8,128)(2,1)S(1)}, bf16[2,256,512]{2,1,0:T(8,128)(2,1)S(1)}, f32[2,256,512]{2,1,0:T(8,1...) custom-call(s32[3]{0:T(128)S(1)} %pad_add_fusion.place, ...), custom_call_target="tpu_custom_call" | custom-call | flops 10871635968 | bytes 5242880 | tf_op jit(solution)/shard_map/attention/pallas_call | solution.py:248
  52.2 1.3 %collective-permute-start.11 = (bf16[2,256,512]{2,1,0:T(8,128)(2,1)S(1)}, bf16[2,256,512]{2,1,0:T(8,128)(2,1)S(1)}, u32[]{:S(2)}, u32[]{:S(2)}) collective-permute-start(bf16[2,256,512]{2,1,0:T(8,128)(2,1)S(1)} %get-tuple-element.38), channel_id=1, source_target_pairs={{4,12},{8,0},{12,20},{16,8},{20,28},{24,16},{5,13},{9,1},{13,21},{... | collective-permute-start | bytes 1572872 | tf_op jit(solution)/shard_map/ppermute | solution.py:341
  53.5 3.1 %collective-permute-start.9 = (bf16[2,256,512]{2,1,0:T(8,128)(2,1)S(1)}, bf16[2,256,512]{2,1,0:T(8,128)(2,1)S(1)}, u32[]{:S(2)}, u32[]{:S(2)}) collective-permute-start(bf16[2,256,512]{2,1,0:T(8,128)(2,1)S(1)} %get-tuple-element.34), channel_id=1, source_target_pairs={{0,4},{4,0},{8,12},{12,8},{16,20},{20,16},{24,28},{28,24},{1,5},{5... | collective-permute-start | bytes 1572872 | tf_op jit(solution)/shard_map/ppermute | solution.py:341
  56.7 0.8 %collective-permute-start.10 = (bf16[2,2,32,512]{3,2,1,0:T(8,128)(2,1)S(1)}, bf16[2,2,32,512]{3,2,1,0:T(8,128)(2,1)S(1)}, u32[]{:S(2)}, u32[]{:S(2)}) collective-permute-start(bf16[2,2,32,512]{3,2,1,0:T(8,128)(2,1)S(1)} %get-tuple-element.36), channel_id=1, source_target_pairs={{0,16},{4,20},{8,24},{12,28},{16,0},{20,4},{24,8},{28,12},{1,17},{... | collective-permute-start | bytes 393224 | tf_op jit(solution)/shard_map/ppermute | solution.py:341
  57.5 3.2 %collective-permute-start.12 = (bf16[2,256,512]{2,1,0:T(8,128)(2,1)S(1)}, bf16[2,256,512]{2,1,0:T(8,128)(2,1)S(1)}, u32[]{:S(2)}, u32[]{:S(2)}) collective-permute-start(bf16[2,256,512]{2,1,0:T(8,128)(2,1)S(1)} %get-tuple-element.43), channel_id=1, source_target_pairs={{12,4},{0,8},{20,12},{8,16},{28,20},{16,24},{13,5},{1,9},{21,13},{... | collective-permute-start | bytes 1572872 | tf_op jit(solution)/shard_map/ppermute | solution.py:341
  60.7 4.0 %collective-permute-done.11 = bf16[2,256,512]{2,1,0:T(8,128)(2,1)S(1)} collective-permute-done((bf16[2,256,512]{2,1,0:T(8,128)(2,1)S(1)}, bf16[2,256,512]{2,1,0:T(8,128)(2,1)S(1)}, u32[]{:S(2)}, u32[]{:S(2)}) %collective-permute-start.11) | collective-permute-done | bytes 524320 | tf_op jit(solution)/shard_map/ppermute | solution.py:341
  64.7 0.2 add_convert_fusion.1
  64.9 0.1 collective-permute-start.14
  65.0 5.8 %collective-permute-done.10 = bf16[2,2,32,512]{3,2,1,0:T(8,128)(2,1)S(1)} collective-permute-done((bf16[2,2,32,512]{3,2,1,0:T(8,128)(2,1)S(1)}, bf16[2,2,32,512]{3,2,1,0:T(8,128)(2,1)S(1)}, u32[]{:S(2)}, u32[]{:S(2)}) %collective-permute-start.10) | collective-permute-done | bytes 131104 | tf_op jit(solution)/shard_map/ppermute | solution.py:341
  70.8 0.1 collective-permute-start.13
  70.9 0.0 collective-permute-done.9
  70.9 1.3 %maximum_select_fusion = (bf16[256,1024]{1,0:T(8,128)(2,1)}, bf16[256,1024]{1,0:T(8,128)(2,1)}) fusion(bf16[256,512]{1,0:T(8,128)(2,1)S(1)} %get-tuple-element.49, bf16[256,512]{1,0:T(8,128)(2,1)S(1)} %get-tuple-element.33, pred[]{:T(512)S(6)} %eq.16, bf16[256,512]{1,0:T(8,128)(2,1)S(1)} %get-tuple-element.41, bf16[256,512]{1,0:T(8,128)(2,1)S(1)} %get-tuple-element.48), kind=kLoop, calls=%fused_computation.16 | loop fusion | flops 4718592 | bytes 2097153 | tf_op jit(solution)/shard_map/jit(_where)/select_n | solution.py:381
  72.2 2.9 %collective-permute-done.13 = bf16[1,2,32,512]{3,2,1,0:T(8,128)(2,1)S(1)} collective-permute-done((bf16[1,2,32,512]{3,2,1,0:T(8,128)(2,1)S(1)}, bf16[1,2,32,512]{3,2,1,0:T(8,128)(2,1)S(1)}, u32[]{:S(2)}, u32[]{:S(2)}) %collective-permute-start.13) | collective-permute-done | bytes 65568 | tf_op jit(solution)/shard_map/ppermute | solution.py:341
  75.2 0.1 collective-permute-start.15
  75.3 0.7 convolution_bitcast_fusion.1
  75.9 0.0 collective-permute-done.12
  76.0 0.3 add_convert_fusion
  76.3 2.8 %collective-permute-done.15 = bf16[2,16,512]{2,1,0:T(8,128)(2,1)S(1)} collective-permute-done((bf16[2,16,512]{2,1,0:T(8,128)(2,1)S(1)}, bf16[2,16,512]{2,1,0:T(8,128)(2,1)S(1)}, u32[]{:S(2)}, u32[]{:S(2)}) %collective-permute-start.15) | collective-permute-done | bytes 32800 | tf_op jit(solution)/shard_map/ppermute | solution.py:341
  79.1 0.4 convolution_bitcast_fusion
  79.6 0.0 collective-permute-done.14
  79.6 0.2 fusion.6
  79.8 1.3 %maximum_select_fusion.2 = (bf16[256,1024]{1,0:T(8,128)(2,1)}, bf16[256,1024]{1,0:T(8,128)(2,1)}) fusion(bf16[256,512]{1,0:T(8,128)(2,1)S(1)} %get-tuple-element.45, bf16[256,512]{1,0:T(8,128)(2,1)S(1)} %get-tuple-element.47, pred[]{:T(512)S(6)} %eq.16, bf16[256,512]{1,0:T(8,128)(2,1)S(1)} %get-tuple-element.46, bf16[256,512]{1,0:T(8,128)(2,1)S(1)} %get-tuple-element.44), kind=kLoop, calls=%fused_computation.18 | loop fusion | flops 4718592 | bytes 2097153 | tf_op jit(solution)/shard_map/jit(_where)/select_n | solution.py:381
  (26 shorter events, 0.2 us)
Async XLA Ops:
  0.6 4.2 %copy-start.1 = (bf16[256,1024]{1,0:T(8,128)(2,1)S(1)}, bf16[256,1024]{1,0:T(8,128)(2,1)}, u32[]{:S(2)}) copy-start(bf16[256,1024]{1,0:T(8,128)(2,1)} %v.1) | copy-start | bytes 1572868
  1.8 10.2 %collective-permute-start = (bf16[256,512]{1,0:T(8,128)(2,1)S(1)}, bf16[256,512]{1,0:T(8,128)(2,1)S(1)}, u32[]{:S(2)}, u32[]{:S(2)}) collective-permute-start(bf16[256,512]{1,0:T(8,128)(2,1)S(1)} %get-tuple-element.51), channel_id=1, source_target_pairs={{0,4},{4,0},{8,12},{12,8},{16,20},{20,16},{24,28},{28,24},{1,5},{5... | collective-permute-start | bytes 786440 | tf_op jit(solution)/shard_map/ppermute | solution.py:341
  4.8 1.5 %copy-start.4 = (bf16[8,256]{1,0:T(8,128)(2,1)S(1)}, bf16[8,256]{1,0:T(8,128)(2,1)}, u32[]{:S(2)}) copy-start(bf16[8,256]{1,0:T(8,128)(2,1)} %param.10) | copy-start | bytes 12292
  4.8 1.5 %copy-start.6 = (bf16[4,256]{1,0:T(4,128)(2,1)S(1)}, bf16[4,256]{1,0:T(4,128)(2,1)}, u32[]{:S(2)}) copy-start(bf16[4,256]{1,0:T(4,128)(2,1)} %param.11) | copy-start | bytes 6148
  5.6 1.7 %copy-start.2 = (bf16[256,1024]{1,0:T(8,128)(2,1)S(1)}, bf16[256,1024]{1,0:T(8,128)(2,1)}, u32[]{:S(2)}) copy-start(bf16[256,1024]{1,0:T(8,128)(2,1)} %q.1) | copy-start | bytes 1572868
  5.6 14.0 %collective-permute-start.1 = (bf16[256,512]{1,0:T(8,128)(2,1)}, bf16[256,512]{1,0:T(8,128)(2,1)S(1)}, u32[]{:S(2)}, u32[]{:S(2)}) collective-permute-start(bf16[256,512]{1,0:T(8,128)(2,1)} %get-tuple-element.53), channel_id=1, source_target_pairs={{0,4},{4,0},{8,12},{12,8},{16,20},{20,16},{24,28},{28,24},{1,5},{5... | collective-permute-start | bytes 786440 | tf_op jit(solution)/shard_map/ppermute | solution.py:341
  5.7 0.6 copy-start.9
  6.3 1.1 %copy-start.3 = (bf16[256,1024]{1,0:T(8,128)(2,1)S(1)}, bf16[256,1024]{1,0:T(8,128)(2,1)}, u32[]{:S(2)}) copy-start(bf16[256,1024]{1,0:T(8,128)(2,1)} %c.1) | copy-start | bytes 1572868
  11.9 18.3 %collective-permute-start.4 = (bf16[2,256,512]{2,1,0:T(8,128)(2,1)}, bf16[2,256,512]{2,1,0:T(8,128)(2,1)S(1)}, u32[]{:S(2)}, u32[]{:S(2)}) collective-permute-start(bf16[2,256,512]{2,1,0:T(8,128)(2,1)} %pad_maximum_fusion), channel_id=1, source_target_pairs={{4,12},{8,0},{12,20},{16,8},{20,28},{24,16},{5,13},{9,1},{13,21},{... | collective-permute-start | bytes 1572872 | tf_op jit(solution)/shard_map/ppermute | solution.py:341
  13.2 9.0 %collective-permute-start.2 = (bf16[256,512]{1,0:T(8,128)(2,1)S(1)}, bf16[256,512]{1,0:T(8,128)(2,1)S(1)}, u32[]{:S(2)}, u32[]{:S(2)}) collective-permute-start(bf16[256,512]{1,0:T(8,128)(2,1)S(1)} %collective-permute-done.pair_k), channel_id=1, source_target_pairs={{12,4},{0,8},{20,12},{8,16},{28,20},{16,24},{13,5},{1,9},{21,13},{... | collective-permute-start | bytes 786440 | tf_op jit(solution)/shard_map/ppermute | solution.py:341
  18.8 17.6 %copy-start = (bf16[256,1024]{1,0:T(8,128)(2,1)S(1)}, bf16[256,1024]{1,0:T(8,128)(2,1)}, u32[]{:S(2)}) copy-start(bf16[256,1024]{1,0:T(8,128)(2,1)} %k.1) | copy-start | bytes 1572868
  19.6 12.4 %collective-permute-start.5 = (bf16[2,256,512]{2,1,0:T(8,128)(2,1)}, bf16[2,256,512]{2,1,0:T(8,128)(2,1)}, u32[]{:S(2)}, u32[]{:S(2)}) collective-permute-start(bf16[2,256,512]{2,1,0:T(8,128)(2,1)} %pad_maximum_fusion.1), channel_id=1, source_target_pairs={{0,4},{4,0},{8,12},{12,8},{16,20},{20,16},{24,28},{28,24},{1,5},{5... | collective-permute-start | bytes 1572872 | tf_op jit(solution)/shard_map/ppermute | solution.py:341
  21.3 5.7 %copy-start.5 = (bf16[8,256]{1,0:T(8,128)(2,1)S(1)}, bf16[8,256]{1,0:T(8,128)(2,1)}, u32[]{:S(2)}) copy-start(bf16[8,256]{1,0:T(8,128)(2,1)} %param.10) | copy-start | bytes 12292
  21.3 5.7 %copy-start.7 = (bf16[4,256]{1,0:T(4,128)(2,1)S(1)}, bf16[4,256]{1,0:T(4,128)(2,1)}, u32[]{:S(2)}) copy-start(bf16[4,256]{1,0:T(4,128)(2,1)} %param.11) | copy-start | bytes 6148
  21.3 5.7 %copy-start.10 = (bf16[16]{0:T(256)(128)(2,1)S(1)}, bf16[16]{0:T(256)(128)(2,1)}, u32[]{:S(2)}) copy-start(bf16[16]{0:T(256)(128)(2,1)} %copy-done.9) | copy-start | bytes 100
  22.3 4.9 %copy-start.8 = (bf16[2,16,512]{2,1,0:T(8,128)(2,1)S(1)}, bf16[2,16,512]{2,1,0:T(8,128)(2,1)}, u32[]{:S(2)}) copy-start(bf16[2,16,512]{2,1,0:T(8,128)(2,1)} %fusion) | copy-start | bytes 98308
  22.3 9.7 %collective-permute-start.3 = (bf16[256,512]{1,0:T(8,128)(2,1)S(1)}, bf16[256,512]{1,0:T(8,128)(2,1)S(1)}, u32[]{:S(2)}, u32[]{:S(2)}) collective-permute-start(bf16[256,512]{1,0:T(8,128)(2,1)S(1)} %collective-permute-done.1.pair_v), channel_id=1, source_target_pairs={{12,4},{0,8},{20,12},{8,16},{28,20},{16,24},{13,5},{1,9},{21,13},{... | collective-permute-start | bytes 786440 | tf_op jit(solution)/shard_map/ppermute | solution.py:341
  27.2 5.3 %collective-permute-start.8 = (bf16[2,32,512]{2,1,0:T(8,128)(2,1)S(1)}, bf16[2,32,512]{2,1,0:T(8,128)(2,1)S(1)}, u32[]{:S(2)}, u32[]{:S(2)}) collective-permute-start(bf16[2,32,512]{2,1,0:T(8,128)(2,1)S(1)} %maximum_maximum_fusion), channel_id=1, source_target_pairs={{0,24},{4,28},{8,0},{12,4},{16,8},{20,12},{24,16},{28,20},{1,25},{... | collective-permute-start | bytes 196616 | tf_op jit(solution)/shard_map/ppermute | solution.py:341
  28.6 5.9 %collective-permute-start.7 = (bf16[2,32,512]{2,1,0:T(8,128)(2,1)S(1)}, bf16[2,32,512]{2,1,0:T(8,128)(2,1)S(1)}, u32[]{:S(2)}, u32[]{:S(2)}) collective-permute-start(bf16[2,32,512]{2,1,0:T(8,128)(2,1)S(1)} %maximum_maximum_fusion), channel_id=1, source_target_pairs={{0,16},{4,20},{8,24},{12,28},{16,0},{20,4},{24,8},{28,12},{1,17},{... | collective-permute-start | bytes 196616 | tf_op jit(solution)/shard_map/ppermute | solution.py:341
  30.3 6.1 %collective-permute-start.6 = (bf16[2,32,512]{2,1,0:T(8,128)(2,1)S(1)}, bf16[2,32,512]{2,1,0:T(8,128)(2,1)S(1)}, u32[]{:S(2)}, u32[]{:S(2)}) collective-permute-start(bf16[2,32,512]{2,1,0:T(8,128)(2,1)S(1)} %maximum_maximum_fusion), channel_id=1, source_target_pairs={{0,8},{4,12},{8,16},{12,20},{16,24},{20,28},{24,0},{28,4},{1,9},{5... | collective-permute-start | bytes 196616 | tf_op jit(solution)/shard_map/ppermute | solution.py:341
  52.2 12.5 %collective-permute-start.11 = (bf16[2,256,512]{2,1,0:T(8,128)(2,1)S(1)}, bf16[2,256,512]{2,1,0:T(8,128)(2,1)S(1)}, u32[]{:S(2)}, u32[]{:S(2)}) collective-permute-start(bf16[2,256,512]{2,1,0:T(8,128)(2,1)S(1)} %get-tuple-element.38), channel_id=1, source_target_pairs={{4,12},{8,0},{12,20},{16,8},{20,28},{24,16},{5,13},{9,1},{13,21},{... | collective-permute-start | bytes 1572872 | tf_op jit(solution)/shard_map/ppermute | solution.py:341
  53.5 17.3 %collective-permute-start.9 = (bf16[2,256,512]{2,1,0:T(8,128)(2,1)S(1)}, bf16[2,256,512]{2,1,0:T(8,128)(2,1)S(1)}, u32[]{:S(2)}, u32[]{:S(2)}) collective-permute-start(bf16[2,256,512]{2,1,0:T(8,128)(2,1)S(1)} %get-tuple-element.34), channel_id=1, source_target_pairs={{0,4},{4,0},{8,12},{12,8},{16,20},{20,16},{24,28},{28,24},{1,5},{5... | collective-permute-start | bytes 1572872 | tf_op jit(solution)/shard_map/ppermute | solution.py:341
  56.7 14.1 %collective-permute-start.10 = (bf16[2,2,32,512]{3,2,1,0:T(8,128)(2,1)S(1)}, bf16[2,2,32,512]{3,2,1,0:T(8,128)(2,1)S(1)}, u32[]{:S(2)}, u32[]{:S(2)}) collective-permute-start(bf16[2,2,32,512]{3,2,1,0:T(8,128)(2,1)S(1)} %get-tuple-element.36), channel_id=1, source_target_pairs={{0,16},{4,20},{8,24},{12,28},{16,0},{20,4},{24,8},{28,12},{1,17},{... | collective-permute-start | bytes 393224 | tf_op jit(solution)/shard_map/ppermute | solution.py:341
  57.5 18.5 %collective-permute-start.12 = (bf16[2,256,512]{2,1,0:T(8,128)(2,1)S(1)}, bf16[2,256,512]{2,1,0:T(8,128)(2,1)S(1)}, u32[]{:S(2)}, u32[]{:S(2)}) collective-permute-start(bf16[2,256,512]{2,1,0:T(8,128)(2,1)S(1)} %get-tuple-element.43), channel_id=1, source_target_pairs={{12,4},{0,8},{20,12},{8,16},{28,20},{16,24},{13,5},{1,9},{21,13},{... | collective-permute-start | bytes 1572872 | tf_op jit(solution)/shard_map/ppermute | solution.py:341
  64.9 14.6 %collective-permute-start.14 = (bf16[2,256,512]{2,1,0:T(8,128)(2,1)S(1)}, bf16[2,256,512]{2,1,0:T(8,128)(2,1)S(1)}, u32[]{:S(2)}, u32[]{:S(2)}) collective-permute-start(bf16[2,256,512]{2,1,0:T(8,128)(2,1)S(1)} %add_convert_fusion.1), channel_id=1, source_target_pairs={{0,4},{4,0},{8,12},{12,8},{16,20},{20,16},{24,28},{28,24},{1,5},{5... | collective-permute-start | bytes 1572872 | tf_op jit(solution)/shard_map/ppermute | solution.py:341
  70.8 4.3 %collective-permute-start.13 = (bf16[1,2,32,512]{3,2,1,0:T(8,128)(2,1)S(1)}, bf16[1,2,32,512]{3,2,1,0:T(8,128)(2,1)S(1)}, u32[]{:S(2)}, u32[]{:S(2)}) collective-permute-start(bf16[1,2,32,512]{3,2,1,0:T(8,128)(2,1)S(1)} %fusion.8), channel_id=1, source_target_pairs={{0,24},{4,28},{8,0},{12,4},{16,8},{20,12},{24,16},{28,20},{1,25},{... | collective-permute-start | bytes 196616 | tf_op jit(solution)/shard_map/ppermute | solution.py:341
  75.2 4.0 %collective-permute-start.15 = (bf16[2,16,512]{2,1,0:T(8,128)(2,1)S(1)}, bf16[2,16,512]{2,1,0:T(8,128)(2,1)S(1)}, u32[]{:S(2)}, u32[]{:S(2)}) collective-permute-start(bf16[2,16,512]{2,1,0:T(8,128)(2,1)S(1)} %slice.84), channel_id=1, source_target_pairs={{0,4},{4,0},{8,12},{12,8},{16,20},{20,16},{24,28},{28,24},{1,5},{5... | collective-permute-start | bytes 98312 | tf_op jit(solution)/shard_map/ppermute | solution.py:341

commit v4 on v3

--- a/solution.py
+++ b/solution.py
@@ -155,9 +155,9 @@
         return jnp.concatenate([grads[n] for grads in self.grads], axis=0)
 
 
-def attention_kernel(shifts):
+def attention_kernel(shifts, one_rows, two_rows):
     def kernel(
-        place, bias, q, k, v, c, pair_k, pair_v, relayed_k, relayed_v, pair_qc, direct, *rest
+        place, q, k, v, c, pair_k, pair_v, relayed_k, relayed_v, pair_qc, direct, pair_coarse, *rest
     ):
         coarse = rest[:shifts]
         out, grad_q, pair_out, home_grad, pair_grad, direct_grad, relayed_grad = rest[
@@ -166,14 +166,31 @@
         coarse_grads = rest[shifts + 7 :]
         rows = q.shape[0]
 
+        parity, pair = (place[0], place[3])
+        coarse_rows = pair_coarse.shape[2]
+
         def halo(have):
-            return jnp.full((rows, 1), jnp.where(have > 0, 0.0, masked_bias), jnp.float32)
+            return jnp.full((rows, 2 * rows), jnp.where(have > 0, 0.0, masked_bias), jnp.float32)
+
+        def coarse_bias(query_block):
+            row = lax.broadcasted_iota(jnp.int32, (coarse_rows, 2 * rows), 0)
+            pieces = []
+            for side in (parity, 1 - parity):
+                for shift in range(1, shifts + 1):
+                    sender = jnp.where(pair >= shift, pair - shift, pair - shift + shifts + 1)
+                    apart = jnp.abs(2 * sender + side - query_block)
+                    one = jnp.where((apart == 2) | (apart == 3), level_one_bias, masked_bias)
+                    two = jnp.where(apart >= 4, level_two_bias, masked_bias)
+                    rest = jnp.where(row < one_rows + two_rows, two, masked_bias)
+                    pieces.append(jnp.where(row < one_rows, one, rest))
+            return jnp.concatenate(pieces, axis=0).astype(jnp.float32)
 
         def chunk(pieces):
             return jnp.concatenate(pieces, axis=0), jnp.concatenate([a.T for a in pieces], axis=1)
 
         def shared(n, home, partner):
-            far = jnp.concatenate([ref[n] for ref in coarse], axis=0)
+            far = [ref[0, n] for ref in coarse] + [pair_coarse[m, n] for m in range(shifts)]
+            far = jnp.concatenate(far, axis=0)
             return chunk([home[...], partner[...]]), chunk([far])
 
         both_keys, both_values = (shared(0, k, pair_k), shared(1, v, pair_v))
@@ -189,8 +206,8 @@
             bias = jnp.concatenate([halo(have), bias], axis=0)
             return Unit(query, cotangent, keys, values, keys_t, values_t, bias)
 
-        one = unit(q[...], c[...], relayed_k[...], relayed_v[...], place[1], bias[0])
-        two = unit(pair_qc[0], pair_qc[1], direct[0], direct[1], place[2], bias[1])
+        one = unit(q[...], c[...], relayed_k[...], relayed_v[...], place[1], coarse_bias(2 * pair + parity))
+        two = unit(pair_qc[0], pair_qc[1], direct[0], direct[1], place[2], coarse_bias(2 * pair + 1 - parity))
         count = one.keys.shape[0]
         middle = count // 32 * 16
         parts = [slice(0, middle), slice(middle, count)]
@@ -215,23 +232,24 @@
             relayed_grad[n] = first[2 * rows : 3 * rows].astype(relayed_grad.dtype)
             direct_grad[n] = second[2 * rows : 3 * rows].astype(direct_grad.dtype)
             far_grad = (first[3 * rows :] + second[3 * rows :]).astype(direct_grad.dtype)
-            size = far_grad.shape[0] // shifts
-            far_grads = [far_grad[m * size : (m + 1) * size] for m in range(shifts)]
             for ref, (distance, count) in zip(coarse_grads, doublings(shifts + 1)):
                 for m in range(count):
-                    ref[m, n] = far_grads[distance - 1 + m]
+                    for side in range(2):
+                        start = (side * shifts + distance - 1 + m) * coarse_rows
+                        piece = far_grad[start : start + coarse_rows]
+                        ref[m, n, side * coarse_rows : (side + 1) * coarse_rows] = piece
 
     return kernel
 
 
 def attention(
-    place, bias, q, k, v, c, pair_k, pair_v, relayed_k, relayed_v, pair_qc, direct, coarse
+    place, level_rows, q, k, v, c, pair_k, pair_v, relayed_k, relayed_v, pair_qc, direct, pair_coarse, coarse
 ):
     rows, width = q.shape
     columns = width // 2
     steps = columns // PAIR
     shifts = len(coarse)
-    coarse_rows = coarse[0].shape[1]
+    coarse_rows = pair_coarse.shape[2]
 
     def mine(j, place):
         return place[0] * steps + j
@@ -242,23 +260,24 @@
     def both(shape_rows):
         return pl.BlockSpec((2, shape_rows, PAIR), lambda j, place: (0, 0, j))
 
-    key_count = 3 * rows + shifts * coarse_rows
+    key_count = 3 * rows + 2 * shifts * coarse_rows
     products = 6 * 2 * 2 * rows * key_count * HEAD_DIM * 2 * steps
     bf16, f32 = (jnp.bfloat16, jnp.float32)
     return pl.pallas_call(
-        attention_kernel(shifts),
+        attention_kernel(shifts, *level_rows),
         grid_spec=pltpu.PrefetchScalarGridSpec(
             num_scalar_prefetch=1,
             grid=(steps,),
-            in_specs=[pl.BlockSpec(bias.shape, lambda j, place: (0, 0, 0))]
-            + [flat(lambda j, place: (0, mine(j, place)))] * 4
+            in_specs=[flat(lambda j, place: (0, mine(j, place)))] * 4
             + [flat(lambda j, place: (0, j))] * 4
             + [both(rows)] * 2
-            + [both(coarse_rows)] * shifts,
+            + [pl.BlockSpec((shifts, 2, coarse_rows, PAIR), lambda j, place: (0, 0, 0, j))]
+            + [pl.BlockSpec((1, 2, coarse_rows, PAIR), lambda j, place: (place[0], 0, 0, j))]
+            * shifts,
             out_specs=[flat(lambda j, place: (0, j))] * 2
             + [both(rows)] * 5
             + [
-                pl.BlockSpec((count, 2, coarse_rows, PAIR), lambda j, place: (0, 0, 0, j))
+                pl.BlockSpec((count, 2, 2 * coarse_rows, PAIR), lambda j, place: (0, 0, 0, j))
                 for _, count in doublings(shifts + 1)
             ],
         ),
@@ -271,7 +290,7 @@
             jax.ShapeDtypeStruct((2, rows, columns), bf16),
         ]
         + [
-            jax.ShapeDtypeStruct((count, 2, coarse_rows, columns), bf16)
+            jax.ShapeDtypeStruct((count, 2, 2 * coarse_rows, columns), bf16)
             for _, count in doublings(shifts + 1)
         ],
         compiler_params=pltpu.CompilerParams(vmem_limit_bytes=GRANT),
@@ -280,8 +299,30 @@
         ),
         name="attention",
     )(
-        place, bias, q, k, v, c, pair_k, pair_v, relayed_k, relayed_v, pair_qc, direct, *coarse
-    )
+        place, q, k, v, c, pair_k, pair_v, relayed_k, relayed_v, pair_qc, direct, pair_coarse, *coarse
+    )
+
+
+def restrict_kernel(restrict, k, v, out):
+    half = out.shape[3]
+    for n, ref in enumerate((k, v)):
+        for side in range(2):
+            columns = ref[:, side * half : (side + 1) * half]
+            out[side, n] = dot(restrict[...], columns).astype(out.dtype)
+
+
+def restricted(restrict, keys, values):
+    vmem = pl.BlockSpec(memory_space=pltpu.VMEM)
+    return pl.pallas_call(
+        restrict_kernel,
+        in_specs=[vmem] * 3,
+        out_specs=vmem,
+        out_shape=jax.ShapeDtypeStruct(
+            (2, 2, restrict.shape[0], keys.shape[1] // 2), keys.dtype
+        ),
+        compiler_params=pltpu.CompilerParams(vmem_limit_bytes=GRANT),
+        name="restrict",
+    )(restrict, keys, values)
 
 
 def lengthened(restrict, coarse):
@@ -308,28 +349,13 @@
         axis=0,
     )
 
-    shift = jnp.arange(1, pair_count)[:, None, None]
-    side = jnp.arange(2)[None, :, None]
-    row = jnp.arange(block_rows)[None, None, :]
-    sender = lax.rem(pair - shift + pair_count, pair_count)
-    block = 2 * sender + jnp.where(side == 0, parity, 1 - parity)
-
-    def coarse_bias(query_block):
-        apart = jnp.abs(block - query_block)
-        one = (row < one_rows) & (apart >= 2) & (apart <= 3)
-        two = (row >= one_rows) & (row < one_rows + two_rows) & (apart >= 4)
-        return jnp.where(one, level_one_bias, jnp.where(two, level_two_bias, masked_bias)).reshape(
-            -1, 1
-        )
-
-    bias = jnp.stack([coarse_bias(position), coarse_bias(2 * pair + 1 - parity)])
-    bias = bias.astype(jnp.float32)
     has_before, has_after = (pair > 0, pair < pair_count - 1)
     place = jnp.stack(
         [
             parity,
             jnp.where(parity == 0, has_before, has_after).astype(jnp.int32),
             jnp.where(parity == 0, has_after, has_before).astype(jnp.int32),
+            pair,
         ]
     ).astype(jnp.int32)
 
@@ -350,30 +376,26 @@
         return lax.optimization_barrier((value, *others))[0]
 
     pair_k, pair_v = (send(a, swap) for a in columns(1 - parity, keys, values))
+    own_coarse = after(restricted(restrict, keys, values), pair_k)
+    coarse = [send(own_coarse, shift_pairs(size, s)) for s in shifts]
     relayed_k = send(pair_k, relayed_to)
     home_kv = jnp.stack(columns(parity, keys, values))
     direct = send(after(home_kv, pair_k), direct_to)
-    relayed_v = send(after(pair_v, relayed_k), relayed_to)
     sent_qc = jnp.stack(columns(1 - parity, queries, cotangent))
     pair_qc = send(after(sent_qc, pair_v), swap)
-    own_coarse = jnp.concatenate(
-        [
-            jnp.einsum("fb,nbc->nfc", restrict, home_kv, preferred_element_type=jnp.float32),
-            jnp.stack([dot(restrict, pair_k), dot(restrict, pair_v)]),
-        ],
-        axis=1,
-    ).astype(jnp.bfloat16)
-    coarse = [send(own_coarse, shift_pairs(size, s)) for s in shifts]
-    direct = after(direct, relayed_k)
+    relayed_v = send(after(pair_v, relayed_k), relayed_to)
+    sent_coarse = jnp.concatenate(
+        [lax.dynamic_slice_in_dim(a, 1 - parity, 1) for a in after(coarse, pair_v)], axis=0
+    )
+    pair_coarse = send(sent_coarse, swap)
     relayed_v = after(relayed_v, direct)
     pair_qc = after(pair_qc, relayed_v)
-    coarse = after(coarse, pair_qc)
 
     (
         out, grad_q, pair_out, home_grad, pair_grad, direct_grad, relayed_grad, *coarse_grads,
     ) = attention(
-        place, bias, queries, keys, values, cotangent,
-        pair_k, pair_v, relayed_k, relayed_v, pair_qc, direct, coarse,
+        place, (one_rows, two_rows), queries, keys, values, cotangent,
+        pair_k, pair_v, relayed_k, relayed_v, pair_qc, direct, pair_coarse, coarse,
     )
 
     def whole(own, other):

time: 81.5 us -> 81.4 us (level)
  waiting for transfers between devices: 23.7 us -> 28.3 us
  matrix products: 3.01 us -> 1.07 us
  other arithmetic: 6.04 us -> 5.17 us
    ppermute x16 -> x17, waiting for transfers between devices: 23.7 us -> 28.3 us  [send(): return lax.ppermute(value, 'seq', pairs)]
    dot_general x3 -> x0, matrix products: 1.93 us -> none  [the longest x2 1.1 us: dot(): return jnp.dot(a, b, preferred_element_type=jnp.float32)]
    unnamed x22 -> x12, local copies, waits for them, and re-layouts: 0.64 us -> 1.5 us
    ppermute x16 -> x17, starting transfers between devices: 27.9 us -> 27.4 us  [send(): return lax.ppermute(value, 'seq', pairs)]
    pallas_call x1 -> x2, Pallas kernels: 15.9 us -> 15.4 us  [the longest x1 15.2 us: attention(): pl.pallas_call(attention_kernel(shifts, *level_rows), grid_spec=pltpu.Pre...]
  transfers between devices with their start and end apart: 16 -> 17, of which waited for: 8 -> 9; matrix products, arithmetic and copies ran while one was open for 12% -> 6% of each run, Pallas kernels for 0% -> 0%
where the time goes in v4:
time: 81.4 us; the launch traced here: 81.1 us
  waiting for transfers between devices  28.3 us (35%)
  starting transfers between devices  27.4 us (34%)
  Pallas kernels  15.4 us (19%)
  other arithmetic  5.17 us (6%)
  local copies, waits for them, and re-layouts  2.89 us (4%)
  matrix products  1.07 us (1%)
  between operations  0.91 us (1%)
    ppermute x17, waiting for transfers between devices, send(): return lax.ppermute(value, 'seq', pairs)  28.3 us
    ppermute x17, starting transfers between devices, send(): return lax.ppermute(value, 'seq', pairs)  27.4 us
    pallas_call x1, Pallas kernels, attention(): pl.pallas_call(attention_kernel(shifts, *level_rows), grid_spec=pltpu.Pre...  15.2 us
    select_n x2, other arithmetic, whole(): jnp.where(parity == 0, jnp.concatenate([own, other], axis=axis), jnp.conc...  2.53 us
  transfers between devices with their start and end apart: 17, of which 9 were waited for; matrix products, arithmetic and copies ran while one was open for 6% of the time, Pallas kernels for 0%

profile of v4, /device:TPU:0, one launch (start us, length us, event | category | flops | bytes accessed | tf_op | source)
XLA Modules:
  0.0 81.1 jit_solution(15402159462508295411)
XLA Ops:
  0.6 0.0 copy-start.1
  0.7 1.1 %dynamic-slice_bitcast_fusion.3 = (bf16[1,256,512]{2,1,0:T(8,128)(2,1)S(1)}, bf16[256,512]{1,0:T(8,128)(2,1)S(1)}) fusion(bf16[256,1024]{1,0:T(8,128)(2,1)} %k.3, s32[]{:T(128)S(6)} %select_n.46, s32[]{:T(128)S(6)} %select_n.45), kind=kLoop, calls=%fused_computation.23 | loop fusion | bytes 1048584 | tf_op jit(solution)/shard_map/stack | solution.py:382
  1.8 0.0 copy-start.2
  1.8 3.0 %collective-permute-start = (bf16[256,512]{1,0:T(8,128)(2,1)S(1)}, bf16[256,512]{1,0:T(8,128)(2,1)S(1)}, u32[]{:S(2)}, u32[]{:S(2)}) collective-permute-start(bf16[256,512]{1,0:T(8,128)(2,1)S(1)} %get-tuple-element.51), channel_id=1, source_target_pairs={{0,4},{4,0},{8,12},{12,8},{16,20},{20,16},{24,28},{28,24},{1,5},{5... | collective-permute-start | bytes 786440 | tf_op jit(solution)/shard_map/ppermute | solution.py:367
  4.8 0.0 copy-done.1
  4.8 0.0 copy-start.4
  4.8 0.0 copy-start.5
  4.9 0.0 copy-start.3
  4.9 0.1 collective-permute-start.1
  5.0 0.1 pad.21.clone
  5.1 0.4 copy-done.4
  5.5 0.0 copy-done.5
  5.5 0.1 maximum_maximum_fusion.restrict
  5.6 0.0 copy-done.2
  5.6 0.0 copy-start
  5.6 0.3 copy-done.3
  5.9 0.7 copy-done
  6.7 0.2 restrict.1
  6.9 0.9 %pad_maximum_fusion.1 = bf16[2,256,512]{2,1,0:T(8,128)(2,1)} fusion(bf16[1,256,512]{2,1,0:T(8,128)(2,1)S(1)} %dynamic-slice_bitcast_fusion, bf16[1,256,512]{2,1,0:T(8,128)(2,1)S(1)} %dynamic-slice_bitcast_fusion.1), kind=kLoop, calls=%fused_computation.9 | loop fusion | flops 262144 | bytes 1048576 | tf_op jit(solution)/shard_map/stack | solution.py:384
  7.8 4.2 %collective-permute-done.pair_k = bf16[256,512]{1,0:T(8,128)(2,1)S(1)} collective-permute-done((bf16[256,512]{1,0:T(8,128)(2,1)S(1)}, bf16[256,512]{1,0:T(8,128)(2,1)S(1)}, u32[]{:S(2)}, u32[]{:S(2)}) %collective-permute-start) | collective-permute-done | bytes 262176 | tf_op jit(solution)/shard_map/ppermute | solution.py:367
  12.0 4.1 %collective-permute-start.8 = (bf16[2,2,16,512]{3,2,1,0:T(8,128)(2,1)S(1)}, bf16[2,2,16,512]{3,2,1,0:T(8,128)(2,1)S(1)}, u32[]{:S(2)}, u32[]{:S(2)}) collective-permute-start(bf16[2,2,16,512]{3,2,1,0:T(8,128)(2,1)S(1)} %restrict.1), channel_id=1, source_target_pairs={{0,24},{4,28},{8,0},{12,4},{16,8},{20,12},{24,16},{28,20},{1,25},{... | collective-permute-start | bytes 196616 | tf_op jit(solution)/shard_map/ppermute | solution.py:367
  16.1 0.0 collective-permute-start.7
  16.1 1.0 %collective-permute-start.6 = (bf16[2,2,16,512]{3,2,1,0:T(8,128)(2,1)S(1)}, bf16[2,2,16,512]{3,2,1,0:T(8,128)(2,1)S(1)}, u32[]{:S(2)}, u32[]{:S(2)}) collective-permute-start(bf16[2,2,16,512]{3,2,1,0:T(8,128)(2,1)S(1)} %restrict.1), channel_id=1, source_target_pairs={{0,8},{4,12},{8,16},{12,20},{16,24},{20,28},{24,0},{28,4},{1,9},{5... | collective-permute-start | bytes 196616 | tf_op jit(solution)/shard_map/ppermute | solution.py:367
  17.1 4.4 %collective-permute-start.2 = (bf16[256,512]{1,0:T(8,128)(2,1)S(1)}, bf16[256,512]{1,0:T(8,128)(2,1)S(1)}, u32[]{:S(2)}, u32[]{:S(2)}) collective-permute-start(bf16[256,512]{1,0:T(8,128)(2,1)S(1)} %collective-permute-done.pair_k), channel_id=1, source_target_pairs={{12,4},{0,8},{20,12},{8,16},{28,20},{16,24},{13,5},{1,9},{21,13},{... | collective-permute-start | bytes 786440 | tf_op jit(solution)/shard_map/ppermute | solution.py:367
  21.5 0.8 %pad_maximum_fusion = bf16[2,256,512]{2,1,0:T(8,128)(2,1)} fusion(bf16[1,256,512]{2,1,0:T(8,128)(2,1)S(1)} %get-tuple-element.52, bf16[1,256,512]{2,1,0:T(8,128)(2,1)S(1)} %get-tuple-element.50), kind=kLoop, calls=%fused_computation.8 | loop fusion | flops 262144 | bytes 1048576 | tf_op jit(solution)/shard_map/stack | solution.py:382
  22.4 0.0 collective-permute-done.1.pair_v
  22.4 0.0 collective-permute-start.5
  22.4 0.0 collective-permute-done.8.rest_2_
  22.4 1.3 %collective-permute-start.4 = (bf16[2,256,512]{2,1,0:T(8,128)(2,1)}, bf16[2,256,512]{2,1,0:T(8,128)(2,1)S(1)}, u32[]{:S(2)}, u32[]{:S(2)}) collective-permute-start(bf16[2,256,512]{2,1,0:T(8,128)(2,1)} %pad_maximum_fusion), channel_id=1, source_target_pairs={{4,12},{8,0},{12,20},{16,8},{20,28},{24,16},{5,13},{9,1},{13,21},{... | collective-permute-start | bytes 1572872 | tf_op jit(solution)/shard_map/ppermute | solution.py:367
  23.7 0.0 collective-permute-done.7.rest_1_
  23.7 0.0 collective-permute-done.6.rest_0_
  23.7 1.6 %collective-permute-done.2.relayed_k = bf16[256,512]{1,0:T(8,128)(2,1)S(1)} collective-permute-done((bf16[256,512]{1,0:T(8,128)(2,1)S(1)}, bf16[256,512]{1,0:T(8,128)(2,1)S(1)}, u32[]{:S(2)}, u32[]{:S(2)}) %collective-permute-start.2) | collective-permute-done | bytes 262176 | tf_op jit(solution)/shard_map/ppermute | solution.py:367
  25.4 4.4 %collective-permute-start.3 = (bf16[256,512]{1,0:T(8,128)(2,1)S(1)}, bf16[256,512]{1,0:T(8,128)(2,1)S(1)}, u32[]{:S(2)}, u32[]{:S(2)}) collective-permute-start(bf16[256,512]{1,0:T(8,128)(2,1)S(1)} %collective-permute-done.1.pair_v), channel_id=1, source_target_pairs={{12,4},{0,8},{20,12},{8,16},{28,20},{16,24},{13,5},{1,9},{21,13},{... | collective-permute-start | bytes 786440 | tf_op jit(solution)/shard_map/ppermute | solution.py:367
  29.8 0.1 collective-permute-start.9
  29.9 0.1 pad_add_fusion.place
  30.0 3.7 %collective-permute-done.3.relayed_v = bf16[256,512]{1,0:T(8,128)(2,1)S(1)} collective-permute-done((bf16[256,512]{1,0:T(8,128)(2,1)S(1)}, bf16[256,512]{1,0:T(8,128)(2,1)S(1)}, u32[]{:S(2)}, u32[]{:S(2)}) %collective-permute-start.3) | collective-permute-done | bytes 262176 | tf_op jit(solution)/shard_map/ppermute | solution.py:367
  33.6 1.4 %collective-permute-done.4.direct = bf16[2,256,512]{2,1,0:T(8,128)(2,1)S(1)} collective-permute-done((bf16[2,256,512]{2,1,0:T(8,128)(2,1)}, bf16[2,256,512]{2,1,0:T(8,128)(2,1)S(1)}, u32[]{:S(2)}, u32[]{:S(2)}) %collective-permute-start.4) | collective-permute-done | bytes 524320 | tf_op jit(solution)/shard_map/ppermute | solution.py:367
  35.0 0.0 collective-permute-done.5.pair_qc
  35.0 0.2 collective-permute-done.9.pair_coarse
  35.2 15.2 %attention.1 = (bf16[256,512]{1,0:T(8,128)(2,1)S(1)}, bf16[256,512]{1,0:T(8,128)(2,1)S(1)}, bf16[2,256,512]{2,1,0:T(8,128)(2,1)S(1)}, f32[2,256,512]{2,1,0:T(8,1...) custom-call(s32[4]{0:T(128)S(1)} %pad_add_fusion.place, ...), custom_call_target="tpu_custom_call" | custom-call | flops 10871635968 | bytes 5242880 | tf_op jit(solution)/shard_map/attention/pallas_call | solution.py:266
  50.4 1.3 %collective-permute-start.12 = (bf16[2,256,512]{2,1,0:T(8,128)(2,1)S(1)}, bf16[2,256,512]{2,1,0:T(8,128)(2,1)S(1)}, u32[]{:S(2)}, u32[]{:S(2)}) collective-permute-start(bf16[2,256,512]{2,1,0:T(8,128)(2,1)S(1)} %get-tuple-element.38), channel_id=1, source_target_pairs={{4,12},{8,0},{12,20},{16,8},{20,28},{24,16},{5,13},{9,1},{13,21},{... | collective-permute-start | bytes 1572872 | tf_op jit(solution)/shard_map/ppermute | solution.py:367
  51.7 3.4 %collective-permute-start.10 = (bf16[2,256,512]{2,1,0:T(8,128)(2,1)S(1)}, bf16[2,256,512]{2,1,0:T(8,128)(2,1)S(1)}, u32[]{:S(2)}, u32[]{:S(2)}) collective-permute-start(bf16[2,256,512]{2,1,0:T(8,128)(2,1)S(1)} %get-tuple-element.34), channel_id=1, source_target_pairs={{0,4},{4,0},{8,12},{12,8},{16,20},{20,16},{24,28},{28,24},{1,5},{5... | collective-permute-start | bytes 1572872 | tf_op jit(solution)/shard_map/ppermute | solution.py:367
  55.1 0.6 collective-permute-start.11
  55.7 3.2 %collective-permute-start.13 = (bf16[2,256,512]{2,1,0:T(8,128)(2,1)S(1)}, bf16[2,256,512]{2,1,0:T(8,128)(2,1)S(1)}, u32[]{:S(2)}, u32[]{:S(2)}) collective-permute-start(bf16[2,256,512]{2,1,0:T(8,128)(2,1)S(1)} %get-tuple-element.43), channel_id=1, source_target_pairs={{12,4},{0,8},{20,12},{8,16},{28,20},{16,24},{13,5},{1,9},{21,13},{... | collective-permute-start | bytes 1572872 | tf_op jit(solution)/shard_map/ppermute | solution.py:367
  58.9 5.2 %collective-permute-done.12 = bf16[2,256,512]{2,1,0:T(8,128)(2,1)S(1)} collective-permute-done((bf16[2,256,512]{2,1,0:T(8,128)(2,1)S(1)}, bf16[2,256,512]{2,1,0:T(8,128)(2,1)S(1)}, u32[]{:S(2)}, u32[]{:S(2)}) %collective-permute-start.12) | collective-permute-done | bytes 524320 | tf_op jit(solution)/shard_map/ppermute | solution.py:367
  64.1 0.2 add_convert_fusion.1
  64.3 0.3 collective-permute-start.15
  64.6 6.3 %collective-permute-done.11 = bf16[2,2,32,512]{3,2,1,0:T(8,128)(2,1)S(1)} collective-permute-done((bf16[2,2,32,512]{3,2,1,0:T(8,128)(2,1)S(1)}, bf16[2,2,32,512]{3,2,1,0:T(8,128)(2,1)S(1)}, u32[]{:S(2)}, u32[]{:S(2)}) %collective-permute-start.11) | collective-permute-done | bytes 131104 | tf_op jit(solution)/shard_map/ppermute | solution.py:367
  70.9 0.1 collective-permute-start.14
  71.0 0.0 collective-permute-done.10
  71.0 1.3 %maximum_select_fusion = (bf16[256,1024]{1,0:T(8,128)(2,1)}, bf16[256,1024]{1,0:T(8,128)(2,1)}) fusion(bf16[256,512]{1,0:T(8,128)(2,1)S(1)} %get-tuple-element.49, bf16[256,512]{1,0:T(8,128)(2,1)S(1)} %get-tuple-element.33, pred[]{:T(512)S(6)} %eq.2, bf16[256,512]{1,0:T(8,128)(2,1)S(1)} %get-tuple-element.41, bf16[256,512]{1,0:T(8,128)(2,1)S(1)} %get-tuple-element.48), kind=kLoop, calls=%fused_computation.10 | loop fusion | flops 4718592 | bytes 2097153 | tf_op jit(solution)/shard_map/jit(_where)/select_n | solution.py:403
  72.3 2.9 %collective-permute-done.14 = bf16[1,2,32,512]{3,2,1,0:T(8,128)(2,1)S(1)} collective-permute-done((bf16[1,2,32,512]{3,2,1,0:T(8,128)(2,1)S(1)}, bf16[1,2,32,512]{3,2,1,0:T(8,128)(2,1)S(1)}, u32[]{:S(2)}, u32[]{:S(2)}) %collective-permute-start.14) | collective-permute-done | bytes 65568 | tf_op jit(solution)/shard_map/ppermute | solution.py:367
  75.3 0.1 collective-permute-start.16
  75.4 0.7 convolution_bitcast_fusion.1
  76.0 0.0 collective-permute-done.13
  76.0 0.3 add_convert_fusion
  76.4 2.8 %collective-permute-done.16 = bf16[2,16,512]{2,1,0:T(8,128)(2,1)S(1)} collective-permute-done((bf16[2,16,512]{2,1,0:T(8,128)(2,1)S(1)}, bf16[2,16,512]{2,1,0:T(8,128)(2,1)S(1)}, u32[]{:S(2)}, u32[]{:S(2)}) %collective-permute-start.16) | collective-permute-done | bytes 32800 | tf_op jit(solution)/shard_map/ppermute | solution.py:367
  79.2 0.4 convolution_bitcast_fusion
  79.6 0.0 collective-permute-done.15
  79.7 0.2 fusion.3
  79.9 1.3 %maximum_select_fusion.2 = (bf16[256,1024]{1,0:T(8,128)(2,1)}, bf16[256,1024]{1,0:T(8,128)(2,1)}) fusion(bf16[256,512]{1,0:T(8,128)(2,1)S(1)} %get-tuple-element.45, bf16[256,512]{1,0:T(8,128)(2,1)S(1)} %get-tuple-element.47, pred[]{:T(512)S(6)} %eq.2, bf16[256,512]{1,0:T(8,128)(2,1)S(1)} %get-tuple-element.46, bf16[256,512]{1,0:T(8,128)(2,1)S(1)} %get-tuple-element.44), kind=kLoop, calls=%fused_computation.12 | loop fusion | flops 4718592 | bytes 2097153 | tf_op jit(solution)/shard_map/jit(_where)/select_n | solution.py:403
  (14 shorter events, 0.3 us)
Async XLA Ops:
  0.6 4.2 %copy-start.1 = (bf16[256,1024]{1,0:T(8,128)(2,1)S(1)}, bf16[256,1024]{1,0:T(8,128)(2,1)}, u32[]{:S(2)}) copy-start(bf16[256,1024]{1,0:T(8,128)(2,1)} %v.3) | copy-start | bytes 1572868
  1.8 3.8 %copy-start.2 = (bf16[256,1024]{1,0:T(8,128)(2,1)S(1)}, bf16[256,1024]{1,0:T(8,128)(2,1)}, u32[]{:S(2)}) copy-start(bf16[256,1024]{1,0:T(8,128)(2,1)} %q.1) | copy-start | bytes 1572868
  1.8 10.2 %collective-permute-start = (bf16[256,512]{1,0:T(8,128)(2,1)S(1)}, bf16[256,512]{1,0:T(8,128)(2,1)S(1)}, u32[]{:S(2)}, u32[]{:S(2)}) collective-permute-start(bf16[256,512]{1,0:T(8,128)(2,1)S(1)} %get-tuple-element.51), channel_id=1, source_target_pairs={{0,4},{4,0},{8,12},{12,8},{16,20},{20,16},{24,28},{28,24},{1,5},{5... | collective-permute-start | bytes 786440 | tf_op jit(solution)/shard_map/ppermute | solution.py:367
  4.8 0.7 copy-start.4
  4.8 0.7 copy-start.5
  4.9 1.0 %copy-start.3 = (bf16[256,1024]{1,0:T(8,128)(2,1)S(1)}, bf16[256,1024]{1,0:T(8,128)(2,1)}, u32[]{:S(2)}) copy-start(bf16[256,1024]{1,0:T(8,128)(2,1)} %c.1) | copy-start | bytes 1572868
  4.9 17.5 %collective-permute-start.1 = (bf16[256,512]{1,0:T(8,128)(2,1)S(1)}, bf16[256,512]{1,0:T(8,128)(2,1)S(1)}, u32[]{:S(2)}, u32[]{:S(2)}) collective-permute-start(bf16[256,512]{1,0:T(8,128)(2,1)S(1)} %get-tuple-element.53), channel_id=1, source_target_pairs={{0,4},{4,0},{8,12},{12,8},{16,20},{20,16},{24,28},{28,24},{1,5},{5... | collective-permute-start | bytes 786440 | tf_op jit(solution)/shard_map/ppermute | solution.py:367
  5.6 1.1 %copy-start = (bf16[256,1024]{1,0:T(8,128)(2,1)S(1)}, bf16[256,1024]{1,0:T(8,128)(2,1)}, u32[]{:S(2)}) copy-start(bf16[256,1024]{1,0:T(8,128)(2,1)} %k.3) | copy-start | bytes 1572868
  12.0 10.4 %collective-permute-start.8 = (bf16[2,2,16,512]{3,2,1,0:T(8,128)(2,1)S(1)}, bf16[2,2,16,512]{3,2,1,0:T(8,128)(2,1)S(1)}, u32[]{:S(2)}, u32[]{:S(2)}) collective-permute-start(bf16[2,2,16,512]{3,2,1,0:T(8,128)(2,1)S(1)} %restrict.1), channel_id=1, source_target_pairs={{0,24},{4,28},{8,0},{12,4},{16,8},{20,12},{24,16},{28,20},{1,25},{... | collective-permute-start | bytes 196616 | tf_op jit(solution)/shard_map/ppermute | solution.py:367
  16.1 7.6 %collective-permute-start.7 = (bf16[2,2,16,512]{3,2,1,0:T(8,128)(2,1)S(1)}, bf16[2,2,16,512]{3,2,1,0:T(8,128)(2,1)S(1)}, u32[]{:S(2)}, u32[]{:S(2)}) collective-permute-start(bf16[2,2,16,512]{3,2,1,0:T(8,128)(2,1)S(1)} %restrict.1), channel_id=1, source_target_pairs={{0,16},{4,20},{8,24},{12,28},{16,0},{20,4},{24,8},{28,12},{1,17},{... | collective-permute-start | bytes 196616 | tf_op jit(solution)/shard_map/ppermute | solution.py:367
  16.1 7.6 %collective-permute-start.6 = (bf16[2,2,16,512]{3,2,1,0:T(8,128)(2,1)S(1)}, bf16[2,2,16,512]{3,2,1,0:T(8,128)(2,1)S(1)}, u32[]{:S(2)}, u32[]{:S(2)}) collective-permute-start(bf16[2,2,16,512]{3,2,1,0:T(8,128)(2,1)S(1)} %restrict.1), channel_id=1, source_target_pairs={{0,8},{4,12},{8,16},{12,20},{16,24},{20,28},{24,0},{28,4},{1,9},{5... | collective-permute-start | bytes 196616 | tf_op jit(solution)/shard_map/ppermute | solution.py:367
  17.1 8.2 %collective-permute-start.2 = (bf16[256,512]{1,0:T(8,128)(2,1)S(1)}, bf16[256,512]{1,0:T(8,128)(2,1)S(1)}, u32[]{:S(2)}, u32[]{:S(2)}) collective-permute-start(bf16[256,512]{1,0:T(8,128)(2,1)S(1)} %collective-permute-done.pair_k), channel_id=1, source_target_pairs={{12,4},{0,8},{20,12},{8,16},{28,20},{16,24},{13,5},{1,9},{21,13},{... | collective-permute-start | bytes 786440 | tf_op jit(solution)/shard_map/ppermute | solution.py:367
  22.4 12.6 %collective-permute-start.5 = (bf16[2,256,512]{2,1,0:T(8,128)(2,1)}, bf16[2,256,512]{2,1,0:T(8,128)(2,1)S(1)}, u32[]{:S(2)}, u32[]{:S(2)}) collective-permute-start(bf16[2,256,512]{2,1,0:T(8,128)(2,1)} %pad_maximum_fusion.1), channel_id=1, source_target_pairs={{0,4},{4,0},{8,12},{12,8},{16,20},{20,16},{24,28},{28,24},{1,5},{5... | collective-permute-start | bytes 1572872 | tf_op jit(solution)/shard_map/ppermute | solution.py:367
  22.4 12.6 %collective-permute-start.4 = (bf16[2,256,512]{2,1,0:T(8,128)(2,1)}, bf16[2,256,512]{2,1,0:T(8,128)(2,1)S(1)}, u32[]{:S(2)}, u32[]{:S(2)}) collective-permute-start(bf16[2,256,512]{2,1,0:T(8,128)(2,1)} %pad_maximum_fusion), channel_id=1, source_target_pairs={{4,12},{8,0},{12,20},{16,8},{20,28},{24,16},{5,13},{9,1},{13,21},{... | collective-permute-start | bytes 1572872 | tf_op jit(solution)/shard_map/ppermute | solution.py:367
  25.4 8.3 %collective-permute-start.3 = (bf16[256,512]{1,0:T(8,128)(2,1)S(1)}, bf16[256,512]{1,0:T(8,128)(2,1)S(1)}, u32[]{:S(2)}, u32[]{:S(2)}) collective-permute-start(bf16[256,512]{1,0:T(8,128)(2,1)S(1)} %collective-permute-done.1.pair_v), channel_id=1, source_target_pairs={{12,4},{0,8},{20,12},{8,16},{28,20},{16,24},{13,5},{1,9},{21,13},{... | collective-permute-start | bytes 786440 | tf_op jit(solution)/shard_map/ppermute | solution.py:367
  29.8 5.4 %collective-permute-start.9 = (bf16[3,2,16,512]{3,2,1,0:T(8,128)(2,1)S(1)}, bf16[3,2,16,512]{3,2,1,0:T(8,128)(2,1)S(1)}, u32[]{:S(2)}, u32[]{:S(2)}) collective-permute-start(bf16[3,2,16,512]{3,2,1,0:T(8,128)(2,1)S(1)} %pad_maximum_fusion.2), channel_id=1, source_target_pairs={{0,4},{4,0},{8,12},{12,8},{16,20},{20,16},{24,28},{28,24},{1,5},{5... | collective-permute-start | bytes 294920 | tf_op jit(solution)/shard_map/ppermute | solution.py:367
  50.4 13.8 %collective-permute-start.12 = (bf16[2,256,512]{2,1,0:T(8,128)(2,1)S(1)}, bf16[2,256,512]{2,1,0:T(8,128)(2,1)S(1)}, u32[]{:S(2)}, u32[]{:S(2)}) collective-permute-start(bf16[2,256,512]{2,1,0:T(8,128)(2,1)S(1)} %get-tuple-element.38), channel_id=1, source_target_pairs={{4,12},{8,0},{12,20},{16,8},{20,28},{24,16},{5,13},{9,1},{13,21},{... | collective-permute-start | bytes 1572872 | tf_op jit(solution)/shard_map/ppermute | solution.py:367
  51.7 19.3 %collective-permute-start.10 = (bf16[2,256,512]{2,1,0:T(8,128)(2,1)S(1)}, bf16[2,256,512]{2,1,0:T(8,128)(2,1)S(1)}, u32[]{:S(2)}, u32[]{:S(2)}) collective-permute-start(bf16[2,256,512]{2,1,0:T(8,128)(2,1)S(1)} %get-tuple-element.34), channel_id=1, source_target_pairs={{0,4},{4,0},{8,12},{12,8},{16,20},{20,16},{24,28},{28,24},{1,5},{5... | collective-permute-start | bytes 1572872 | tf_op jit(solution)/shard_map/ppermute | solution.py:367
  55.1 15.8 %collective-permute-start.11 = (bf16[2,2,32,512]{3,2,1,0:T(8,128)(2,1)S(1)}, bf16[2,2,32,512]{3,2,1,0:T(8,128)(2,1)S(1)}, u32[]{:S(2)}, u32[]{:S(2)}) collective-permute-start(bf16[2,2,32,512]{3,2,1,0:T(8,128)(2,1)S(1)} %get-tuple-element.36), channel_id=1, source_target_pairs={{0,16},{4,20},{8,24},{12,28},{16,0},{20,4},{24,8},{28,12},{1,17},{... | collective-permute-start | bytes 393224 | tf_op jit(solution)/shard_map/ppermute | solution.py:367
  55.7 20.4 %collective-permute-start.13 = (bf16[2,256,512]{2,1,0:T(8,128)(2,1)S(1)}, bf16[2,256,512]{2,1,0:T(8,128)(2,1)S(1)}, u32[]{:S(2)}, u32[]{:S(2)}) collective-permute-start(bf16[2,256,512]{2,1,0:T(8,128)(2,1)S(1)} %get-tuple-element.43), channel_id=1, source_target_pairs={{12,4},{0,8},{20,12},{8,16},{28,20},{16,24},{13,5},{1,9},{21,13},{... | collective-permute-start | bytes 1572872 | tf_op jit(solution)/shard_map/ppermute | solution.py:367
  64.3 15.3 %collective-permute-start.15 = (bf16[2,256,512]{2,1,0:T(8,128)(2,1)S(1)}, bf16[2,256,512]{2,1,0:T(8,128)(2,1)S(1)}, u32[]{:S(2)}, u32[]{:S(2)}) collective-permute-start(bf16[2,256,512]{2,1,0:T(8,128)(2,1)S(1)} %add_convert_fusion.1), channel_id=1, source_target_pairs={{0,4},{4,0},{8,12},{12,8},{16,20},{20,16},{24,28},{28,24},{1,5},{5... | collective-permute-start | bytes 1572872 | tf_op jit(solution)/shard_map/ppermute | solution.py:367
  70.9 4.3 %collective-permute-start.14 = (bf16[1,2,32,512]{3,2,1,0:T(8,128)(2,1)S(1)}, bf16[1,2,32,512]{3,2,1,0:T(8,128)(2,1)S(1)}, u32[]{:S(2)}, u32[]{:S(2)}) collective-permute-start(bf16[1,2,32,512]{3,2,1,0:T(8,128)(2,1)S(1)} %fusion.5), channel_id=1, source_target_pairs={{0,24},{4,28},{8,0},{12,4},{16,8},{20,12},{24,16},{28,20},{1,25},{... | collective-permute-start | bytes 196616 | tf_op jit(solution)/shard_map/ppermute | solution.py:367
  75.3 4.0 %collective-permute-start.16 = (bf16[2,16,512]{2,1,0:T(8,128)(2,1)S(1)}, bf16[2,16,512]{2,1,0:T(8,128)(2,1)S(1)}, u32[]{:S(2)}, u32[]{:S(2)}) collective-permute-start(bf16[2,16,512]{2,1,0:T(8,128)(2,1)S(1)} %slice.84), channel_id=1, source_target_pairs={{0,4},{4,0},{8,12},{12,8},{16,20},{20,16},{24,28},{28,24},{1,5},{5... | collective-permute-start | bytes 98312 | tf_op jit(solution)/shard_map/ppermute | solution.py:367

commit v5 on v4

--- a/solution.py
+++ b/solution.py
@@ -209,8 +209,7 @@
         one = unit(q[...], c[...], relayed_k[...], relayed_v[...], place[1], coarse_bias(2 * pair + parity))
         two = unit(pair_qc[0], pair_qc[1], direct[0], direct[1], place[2], coarse_bias(2 * pair + 1 - parity))
         count = one.keys.shape[0]
-        middle = count // 32 * 16
-        parts = [slice(0, middle), slice(middle, count)]
+        parts = [slice(0, count)]
         for part in parts:
             one.score(part)
         for part in parts:
@@ -409,19 +408,22 @@
     relayed_back = send(relayed_grad, direct_to)
     out_back = send(pair_out, swap)
     direct_back = send(direct_grad, relayed_to)
-    pair_total = (pair_grad + relayed_back.astype(jnp.float32)).astype(jnp.bfloat16)
-    grad_back = send(pair_total, swap)
 
     far = None
     for (distance, count), piece in reversed(list(zip(doublings(pair_count), coarse_grads))):
         if far is not None:
             piece = piece.astype(jnp.float32) + far[distance : distance + count]
         piece = piece.astype(jnp.bfloat16)
+        if distance == 1:
+            relayed_back = after(relayed_back, piece)
+            pair_total = pair_grad + relayed_back.astype(jnp.float32)
+            pair_total = pair_total.astype(jnp.bfloat16)
         back = send(piece, shift_pairs(size, -distance))
-        back = back if far is not None else after(back, pair_total)
+        back = after(back, pair_total) if distance == 1 else back
         back = jnp.pad(back.astype(jnp.float32), [(0, distance - count)] + [(0, 0)] * 3)
         far = back if far is None else far[:distance] + back
     far = far[0]
+    grad_back = send(pair_total, swap)
     other_far = send(far[:, block_rows:].astype(jnp.bfloat16), swap).astype(jnp.float32)
     out_back = after(out_back, piece)
     own_longer = lengthened(restrict, far[:, :block_rows])

time: 81.4 us -> 82.8 us (1.017)
  starting transfers between devices: 27.4 us -> 29.4 us
    ppermute x17, starting transfers between devices: 27.4 us -> 29.4 us  [send(): return lax.ppermute(value, 'seq', pairs)]
  transfers between devices with their start and end apart: 17 -> 17, of which waited for: 9 -> 8; matrix products, arithmetic and copies ran while one was open for 6% -> 6% of each run, Pallas kernels for 0% -> 0%
where the time goes in v5:
time: 82.8 us; the launch traced here: 82.5 us
  starting transfers between devices  29.4 us (36%)
  waiting for transfers between devices  28.1 us (34%)
  Pallas kernels  15 us (18%)
  other arithmetic  5.1 us (6%)
  local copies, waits for them, and re-layouts  2.89 us (3%)
  matrix products  1.08 us (1%)
  between operations  0.92 us (1%)
    ppermute x17, starting transfers between devices, send(): return lax.ppermute(value, 'seq', pairs)  29.4 us
    ppermute x17, waiting for transfers between devices, send(): return lax.ppermute(value, 'seq', pairs)  28.1 us
    pallas_call x1, Pallas kernels, attention(): pl.pallas_call(attention_kernel(shifts, *level_rows), grid_spec=pltpu.Pre...  14.8 us
    select_n x2, other arithmetic, whole(): jnp.where(parity == 0, jnp.concatenate([own, other], axis=axis), jnp.conc...  2.53 us
  transfers between devices with their start and end apart: 17, of which 8 were waited for; matrix products, arithmetic and copies ran while one was open for 6% of the time, Pallas kernels for 0%

profile of v5, /device:TPU:0, one launch (start us, length us, event | category | flops | bytes accessed | tf_op | source)
XLA Modules:
  0.0 82.5 jit_solution(9331808825230517645)
XLA Ops:
  0.6 0.0 copy-start.1
  0.7 1.1 %dynamic-slice_bitcast_fusion.3 = (bf16[1,256,512]{2,1,0:T(8,128)(2,1)S(1)}, bf16[256,512]{1,0:T(8,128)(2,1)S(1)}) fusion(bf16[256,1024]{1,0:T(8,128)(2,1)} %k.3, s32[]{:T(128)S(6)} %select_n.46, s32[]{:T(128)S(6)} %select_n.45), kind=kLoop, calls=%fused_computation.23 | loop fusion | bytes 1048584 | tf_op jit(solution)/shard_map/stack | solution.py:381
  1.8 0.0 copy-start.2
  1.8 3.0 %collective-permute-start = (bf16[256,512]{1,0:T(8,128)(2,1)S(1)}, bf16[256,512]{1,0:T(8,128)(2,1)S(1)}, u32[]{:S(2)}, u32[]{:S(2)}) collective-permute-start(bf16[256,512]{1,0:T(8,128)(2,1)S(1)} %get-tuple-element.53), channel_id=1, source_target_pairs={{0,4},{4,0},{8,12},{12,8},{16,20},{20,16},{24,28},{28,24},{1,5},{5... | collective-permute-start | bytes 786440 | tf_op jit(solution)/shard_map/ppermute | solution.py:366
  4.8 0.0 copy-done.1
  4.8 0.0 copy-start.4
  4.8 0.0 copy-start.5
  4.9 0.0 copy-start.3
  4.9 0.1 collective-permute-start.1
  5.0 0.1 pad.21.clone
  5.1 0.4 copy-done.4
  5.5 0.0 copy-done.5
  5.5 0.1 maximum_maximum_fusion.restrict
  5.6 0.0 copy-done.2
  5.6 0.0 copy-start
  5.6 0.3 copy-done.3
  5.9 0.7 copy-done
  6.7 0.2 restrict.1
  6.9 0.9 %pad_maximum_fusion.1 = bf16[2,256,512]{2,1,0:T(8,128)(2,1)} fusion(bf16[1,256,512]{2,1,0:T(8,128)(2,1)S(1)} %dynamic-slice_bitcast_fusion, bf16[1,256,512]{2,1,0:T(8,128)(2,1)S(1)} %dynamic-slice_bitcast_fusion.1), kind=kLoop, calls=%fused_computation.9 | loop fusion | flops 262144 | bytes 1048576 | tf_op jit(solution)/shard_map/stack | solution.py:383
  7.8 4.2 %collective-permute-done.pair_k = bf16[256,512]{1,0:T(8,128)(2,1)S(1)} collective-permute-done((bf16[256,512]{1,0:T(8,128)(2,1)S(1)}, bf16[256,512]{1,0:T(8,128)(2,1)S(1)}, u32[]{:S(2)}, u32[]{:S(2)}) %collective-permute-start) | collective-permute-done | bytes 262176 | tf_op jit(solution)/shard_map/ppermute | solution.py:366
  12.0 4.1 %collective-permute-start.8 = (bf16[2,2,16,512]{3,2,1,0:T(8,128)(2,1)S(1)}, bf16[2,2,16,512]{3,2,1,0:T(8,128)(2,1)S(1)}, u32[]{:S(2)}, u32[]{:S(2)}) collective-permute-start(bf16[2,2,16,512]{3,2,1,0:T(8,128)(2,1)S(1)} %restrict.1), channel_id=1, source_target_pairs={{0,24},{4,28},{8,0},{12,4},{16,8},{20,12},{24,16},{28,20},{1,25},{... | collective-permute-start | bytes 196616 | tf_op jit(solution)/shard_map/ppermute | solution.py:366
  16.1 0.0 collective-permute-start.7
  16.1 1.0 %collective-permute-start.6 = (bf16[2,2,16,512]{3,2,1,0:T(8,128)(2,1)S(1)}, bf16[2,2,16,512]{3,2,1,0:T(8,128)(2,1)S(1)}, u32[]{:S(2)}, u32[]{:S(2)}) collective-permute-start(bf16[2,2,16,512]{3,2,1,0:T(8,128)(2,1)S(1)} %restrict.1), channel_id=1, source_target_pairs={{0,8},{4,12},{8,16},{12,20},{16,24},{20,28},{24,0},{28,4},{1,9},{5... | collective-permute-start | bytes 196616 | tf_op jit(solution)/shard_map/ppermute | solution.py:366
  17.1 4.4 %collective-permute-start.2 = (bf16[256,512]{1,0:T(8,128)(2,1)S(1)}, bf16[256,512]{1,0:T(8,128)(2,1)S(1)}, u32[]{:S(2)}, u32[]{:S(2)}) collective-permute-start(bf16[256,512]{1,0:T(8,128)(2,1)S(1)} %collective-permute-done.pair_k), channel_id=1, source_target_pairs={{12,4},{0,8},{20,12},{8,16},{28,20},{16,24},{13,5},{1,9},{21,13},{... | collective-permute-start | bytes 786440 | tf_op jit(solution)/shard_map/ppermute | solution.py:366
  21.5 0.8 %pad_maximum_fusion = bf16[2,256,512]{2,1,0:T(8,128)(2,1)} fusion(bf16[1,256,512]{2,1,0:T(8,128)(2,1)S(1)} %get-tuple-element.54, bf16[1,256,512]{2,1,0:T(8,128)(2,1)S(1)} %get-tuple-element.52), kind=kLoop, calls=%fused_computation.8 | loop fusion | flops 262144 | bytes 1048576 | tf_op jit(solution)/shard_map/stack | solution.py:381
  22.4 0.0 collective-permute-done.1.pair_v
  22.4 0.0 collective-permute-start.5
  22.4 0.0 collective-permute-done.8.rest_2_
  22.4 1.3 %collective-permute-start.4 = (bf16[2,256,512]{2,1,0:T(8,128)(2,1)}, bf16[2,256,512]{2,1,0:T(8,128)(2,1)S(1)}, u32[]{:S(2)}, u32[]{:S(2)}) collective-permute-start(bf16[2,256,512]{2,1,0:T(8,128)(2,1)} %pad_maximum_fusion), channel_id=1, source_target_pairs={{4,12},{8,0},{12,20},{16,8},{20,28},{24,16},{5,13},{9,1},{13,21},{... | collective-permute-start | bytes 1572872 | tf_op jit(solution)/shard_map/ppermute | solution.py:366
  23.7 0.0 collective-permute-done.7.rest_1_
  23.7 0.0 collective-permute-done.6.rest_0_
  23.7 1.6 %collective-permute-done.2.relayed_k = bf16[256,512]{1,0:T(8,128)(2,1)S(1)} collective-permute-done((bf16[256,512]{1,0:T(8,128)(2,1)S(1)}, bf16[256,512]{1,0:T(8,128)(2,1)S(1)}, u32[]{:S(2)}, u32[]{:S(2)}) %collective-permute-start.2) | collective-permute-done | bytes 262176 | tf_op jit(solution)/shard_map/ppermute | solution.py:366
  25.4 4.4 %collective-permute-start.3 = (bf16[256,512]{1,0:T(8,128)(2,1)S(1)}, bf16[256,512]{1,0:T(8,128)(2,1)S(1)}, u32[]{:S(2)}, u32[]{:S(2)}) collective-permute-start(bf16[256,512]{1,0:T(8,128)(2,1)S(1)} %collective-permute-done.1.pair_v), channel_id=1, source_target_pairs={{12,4},{0,8},{20,12},{8,16},{28,20},{16,24},{13,5},{1,9},{21,13},{... | collective-permute-start | bytes 786440 | tf_op jit(solution)/shard_map/ppermute | solution.py:366
  29.8 0.1 collective-permute-start.9
  29.9 0.1 pad_add_fusion.place
  30.0 3.7 %collective-permute-done.3.relayed_v = bf16[256,512]{1,0:T(8,128)(2,1)S(1)} collective-permute-done((bf16[256,512]{1,0:T(8,128)(2,1)S(1)}, bf16[256,512]{1,0:T(8,128)(2,1)S(1)}, u32[]{:S(2)}, u32[]{:S(2)}) %collective-permute-start.3) | collective-permute-done | bytes 262176 | tf_op jit(solution)/shard_map/ppermute | solution.py:366
  33.6 1.4 %collective-permute-done.4.direct = bf16[2,256,512]{2,1,0:T(8,128)(2,1)S(1)} collective-permute-done((bf16[2,256,512]{2,1,0:T(8,128)(2,1)}, bf16[2,256,512]{2,1,0:T(8,128)(2,1)S(1)}, u32[]{:S(2)}, u32[]{:S(2)}) %collective-permute-start.4) | collective-permute-done | bytes 524320 | tf_op jit(solution)/shard_map/ppermute | solution.py:366
  35.0 0.0 collective-permute-done.5.pair_qc
  35.0 0.2 collective-permute-done.9.pair_coarse
  35.2 14.8 %attention.1 = (bf16[256,512]{1,0:T(8,128)(2,1)S(1)}, bf16[256,512]{1,0:T(8,128)(2,1)S(1)}, bf16[2,256,512]{2,1,0:T(8,128)(2,1)S(1)}, f32[2,256,512]{2,1,0:T(8,1...) custom-call(s32[4]{0:T(128)S(1)} %pad_add_fusion.place, ...), custom_call_target="tpu_custom_call" | custom-call | flops 10871635968 | bytes 5242880 | tf_op jit(solution)/shard_map/attention/pallas_call | solution.py:265
  50.0 1.3 %collective-permute-start.14 = (bf16[2,256,512]{2,1,0:T(8,128)(2,1)S(1)}, bf16[2,256,512]{2,1,0:T(8,128)(2,1)S(1)}, u32[]{:S(2)}, u32[]{:S(2)}) collective-permute-start(bf16[2,256,512]{2,1,0:T(8,128)(2,1)S(1)} %get-tuple-element.43), channel_id=1, source_target_pairs={{4,12},{8,0},{12,20},{16,8},{20,28},{24,16},{5,13},{9,1},{13,21},{... | collective-permute-start | bytes 1572872 | tf_op jit(solution)/shard_map/ppermute | solution.py:366
  51.3 3.5 %collective-permute-start.11 = (bf16[2,2,32,512]{3,2,1,0:T(8,128)(2,1)S(1)}, bf16[2,2,32,512]{3,2,1,0:T(8,128)(2,1)S(1)}, u32[]{:S(2)}, u32[]{:S(2)}) collective-permute-start(bf16[2,2,32,512]{3,2,1,0:T(8,128)(2,1)S(1)} %get-tuple-element.37), channel_id=1, source_target_pairs={{0,16},{4,20},{8,24},{12,28},{16,0},{20,4},{24,8},{28,12},{1,17},{... | collective-permute-start | bytes 393224 | tf_op jit(solution)/shard_map/ppermute | solution.py:366
  54.7 0.5 collective-permute-start.10
  55.2 3.2 %collective-permute-start.12 = (bf16[2,256,512]{2,1,0:T(8,128)(2,1)S(1)}, bf16[2,256,512]{2,1,0:T(8,128)(2,1)S(1)}, u32[]{:S(2)}, u32[]{:S(2)}) collective-permute-start(bf16[2,256,512]{2,1,0:T(8,128)(2,1)S(1)} %get-tuple-element.41), channel_id=1, source_target_pairs={{12,4},{0,8},{20,12},{8,16},{28,20},{16,24},{13,5},{1,9},{21,13},{... | collective-permute-start | bytes 1572872 | tf_op jit(solution)/shard_map/ppermute | solution.py:366
  58.4 12.0 %collective-permute-done.11 = bf16[2,2,32,512]{3,2,1,0:T(8,128)(2,1)S(1)} collective-permute-done((bf16[2,2,32,512]{3,2,1,0:T(8,128)(2,1)S(1)}, bf16[2,2,32,512]{3,2,1,0:T(8,128)(2,1)S(1)}, u32[]{:S(2)}, u32[]{:S(2)}) %collective-permute-start.11) | collective-permute-done | bytes 131104 | tf_op jit(solution)/shard_map/ppermute | solution.py:366
  70.5 0.1 collective-permute-start.13
  70.6 0.0 collective-permute-done.14
  70.6 0.2 add_convert_fusion.1
  70.8 2.4 %collective-permute-start.15 = (bf16[2,256,512]{2,1,0:T(8,128)(2,1)S(1)}, bf16[2,256,512]{2,1,0:T(8,128)(2,1)S(1)}, u32[]{:S(2)}, u32[]{:S(2)}) collective-permute-start(bf16[2,256,512]{2,1,0:T(8,128)(2,1)S(1)} %add_convert_fusion.1), channel_id=1, source_target_pairs={{0,4},{4,0},{8,12},{12,8},{16,20},{20,16},{24,28},{28,24},{1,5},{5... | collective-permute-start | bytes 1572872 | tf_op jit(solution)/shard_map/ppermute | solution.py:366
  73.2 1.7 %collective-permute-done.13 = bf16[1,2,32,512]{3,2,1,0:T(8,128)(2,1)S(1)} collective-permute-done((bf16[1,2,32,512]{3,2,1,0:T(8,128)(2,1)S(1)}, bf16[1,2,32,512]{3,2,1,0:T(8,128)(2,1)S(1)}, u32[]{:S(2)}, u32[]{:S(2)}) %collective-permute-start.13) | collective-permute-done | bytes 65568 | tf_op jit(solution)/shard_map/ppermute | solution.py:366
  74.9 0.0 collective-permute-done.10
  74.9 0.1 collective-permute-start.16
  75.0 0.7 convolution_bitcast_fusion.1
  75.7 0.0 collective-permute-done.12
  75.7 0.3 add_convert_fusion
  76.1 1.3 %maximum_select_fusion = (bf16[256,1024]{1,0:T(8,128)(2,1)}, bf16[256,1024]{1,0:T(8,128)(2,1)}) fusion(bf16[256,512]{1,0:T(8,128)(2,1)S(1)} %get-tuple-element.51, bf16[256,512]{1,0:T(8,128)(2,1)S(1)} %get-tuple-element.34, pred[]{:T(512)S(6)} %eq.2, bf16[256,512]{1,0:T(8,128)(2,1)S(1)} %get-tuple-element.39, bf16[256,512]{1,0:T(8,128)(2,1)S(1)} %get-tuple-element.50), kind=kLoop, calls=%fused_computation.10 | loop fusion | flops 4718592 | bytes 2097153 | tf_op jit(solution)/shard_map/jit(_where)/select_n | solution.py:402
  77.3 3.4 %collective-permute-done.16 = bf16[2,16,512]{2,1,0:T(8,128)(2,1)S(1)} collective-permute-done((bf16[2,16,512]{2,1,0:T(8,128)(2,1)S(1)}, bf16[2,16,512]{2,1,0:T(8,128)(2,1)S(1)}, u32[]{:S(2)}, u32[]{:S(2)}) %collective-permute-start.16) | collective-permute-done | bytes 32800 | tf_op jit(solution)/shard_map/ppermute | solution.py:366
  80.7 0.4 convolution_bitcast_fusion
  81.1 0.0 collective-permute-done.15
  81.1 0.2 fusion.3
  81.3 1.3 %maximum_select_fusion.2 = (bf16[256,1024]{1,0:T(8,128)(2,1)}, bf16[256,1024]{1,0:T(8,128)(2,1)}) fusion(bf16[256,512]{1,0:T(8,128)(2,1)S(1)} %get-tuple-element.47, bf16[256,512]{1,0:T(8,128)(2,1)S(1)} %get-tuple-element.49, pred[]{:T(512)S(6)} %eq.2, bf16[256,512]{1,0:T(8,128)(2,1)S(1)} %get-tuple-element.48, bf16[256,512]{1,0:T(8,128)(2,1)S(1)} %get-tuple-element.46), kind=kLoop, calls=%fused_computation.12 | loop fusion | flops 4718592 | bytes 2097153 | tf_op jit(solution)/shard_map/jit(_where)/select_n | solution.py:402
  (14 shorter events, 0.3 us)
Async XLA Ops:
  0.6 4.2 %copy-start.1 = (bf16[256,1024]{1,0:T(8,128)(2,1)S(1)}, bf16[256,1024]{1,0:T(8,128)(2,1)}, u32[]{:S(2)}) copy-start(bf16[256,1024]{1,0:T(8,128)(2,1)} %v.3) | copy-start | bytes 1572868
  1.8 3.8 %copy-start.2 = (bf16[256,1024]{1,0:T(8,128)(2,1)S(1)}, bf16[256,1024]{1,0:T(8,128)(2,1)}, u32[]{:S(2)}) copy-start(bf16[256,1024]{1,0:T(8,128)(2,1)} %q.1) | copy-start | bytes 1572868
  1.8 10.2 %collective-permute-start = (bf16[256,512]{1,0:T(8,128)(2,1)S(1)}, bf16[256,512]{1,0:T(8,128)(2,1)S(1)}, u32[]{:S(2)}, u32[]{:S(2)}) collective-permute-start(bf16[256,512]{1,0:T(8,128)(2,1)S(1)} %get-tuple-element.53), channel_id=1, source_target_pairs={{0,4},{4,0},{8,12},{12,8},{16,20},{20,16},{24,28},{28,24},{1,5},{5... | collective-permute-start | bytes 786440 | tf_op jit(solution)/shard_map/ppermute | solution.py:366
  4.8 0.7 copy-start.4
  4.8 0.7 copy-start.5
  4.9 1.0 %copy-start.3 = (bf16[256,1024]{1,0:T(8,128)(2,1)S(1)}, bf16[256,1024]{1,0:T(8,128)(2,1)}, u32[]{:S(2)}) copy-start(bf16[256,1024]{1,0:T(8,128)(2,1)} %c.1) | copy-start | bytes 1572868
  4.9 17.5 %collective-permute-start.1 = (bf16[256,512]{1,0:T(8,128)(2,1)S(1)}, bf16[256,512]{1,0:T(8,128)(2,1)S(1)}, u32[]{:S(2)}, u32[]{:S(2)}) collective-permute-start(bf16[256,512]{1,0:T(8,128)(2,1)S(1)} %get-tuple-element.55), channel_id=1, source_target_pairs={{0,4},{4,0},{8,12},{12,8},{16,20},{20,16},{24,28},{28,24},{1,5},{5... | collective-permute-start | bytes 786440 | tf_op jit(solution)/shard_map/ppermute | solution.py:366
  5.6 1.1 %copy-start = (bf16[256,1024]{1,0:T(8,128)(2,1)S(1)}, bf16[256,1024]{1,0:T(8,128)(2,1)}, u32[]{:S(2)}) copy-start(bf16[256,1024]{1,0:T(8,128)(2,1)} %k.3) | copy-start | bytes 1572868
  12.0 10.4 %collective-permute-start.8 = (bf16[2,2,16,512]{3,2,1,0:T(8,128)(2,1)S(1)}, bf16[2,2,16,512]{3,2,1,0:T(8,128)(2,1)S(1)}, u32[]{:S(2)}, u32[]{:S(2)}) collective-permute-start(bf16[2,2,16,512]{3,2,1,0:T(8,128)(2,1)S(1)} %restrict.1), channel_id=1, source_target_pairs={{0,24},{4,28},{8,0},{12,4},{16,8},{20,12},{24,16},{28,20},{1,25},{... | collective-permute-start | bytes 196616 | tf_op jit(solution)/shard_map/ppermute | solution.py:366
  16.1 7.6 %collective-permute-start.7 = (bf16[2,2,16,512]{3,2,1,0:T(8,128)(2,1)S(1)}, bf16[2,2,16,512]{3,2,1,0:T(8,128)(2,1)S(1)}, u32[]{:S(2)}, u32[]{:S(2)}) collective-permute-start(bf16[2,2,16,512]{3,2,1,0:T(8,128)(2,1)S(1)} %restrict.1), channel_id=1, source_target_pairs={{0,16},{4,20},{8,24},{12,28},{16,0},{20,4},{24,8},{28,12},{1,17},{... | collective-permute-start | bytes 196616 | tf_op jit(solution)/shard_map/ppermute | solution.py:366
  16.1 7.6 %collective-permute-start.6 = (bf16[2,2,16,512]{3,2,1,0:T(8,128)(2,1)S(1)}, bf16[2,2,16,512]{3,2,1,0:T(8,128)(2,1)S(1)}, u32[]{:S(2)}, u32[]{:S(2)}) collective-permute-start(bf16[2,2,16,512]{3,2,1,0:T(8,128)(2,1)S(1)} %restrict.1), channel_id=1, source_target_pairs={{0,8},{4,12},{8,16},{12,20},{16,24},{20,28},{24,0},{28,4},{1,9},{5... | collective-permute-start | bytes 196616 | tf_op jit(solution)/shard_map/ppermute | solution.py:366
  17.1 8.2 %collective-permute-start.2 = (bf16[256,512]{1,0:T(8,128)(2,1)S(1)}, bf16[256,512]{1,0:T(8,128)(2,1)S(1)}, u32[]{:S(2)}, u32[]{:S(2)}) collective-permute-start(bf16[256,512]{1,0:T(8,128)(2,1)S(1)} %collective-permute-done.pair_k), channel_id=1, source_target_pairs={{12,4},{0,8},{20,12},{8,16},{28,20},{16,24},{13,5},{1,9},{21,13},{... | collective-permute-start | bytes 786440 | tf_op jit(solution)/shard_map/ppermute | solution.py:366
  22.4 12.6 %collective-permute-start.5 = (bf16[2,256,512]{2,1,0:T(8,128)(2,1)}, bf16[2,256,512]{2,1,0:T(8,128)(2,1)S(1)}, u32[]{:S(2)}, u32[]{:S(2)}) collective-permute-start(bf16[2,256,512]{2,1,0:T(8,128)(2,1)} %pad_maximum_fusion.1), channel_id=1, source_target_pairs={{0,4},{4,0},{8,12},{12,8},{16,20},{20,16},{24,28},{28,24},{1,5},{5... | collective-permute-start | bytes 1572872 | tf_op jit(solution)/shard_map/ppermute | solution.py:366
  22.4 12.6 %collective-permute-start.4 = (bf16[2,256,512]{2,1,0:T(8,128)(2,1)}, bf16[2,256,512]{2,1,0:T(8,128)(2,1)S(1)}, u32[]{:S(2)}, u32[]{:S(2)}) collective-permute-start(bf16[2,256,512]{2,1,0:T(8,128)(2,1)} %pad_maximum_fusion), channel_id=1, source_target_pairs={{4,12},{8,0},{12,20},{16,8},{20,28},{24,16},{5,13},{9,1},{13,21},{... | collective-permute-start | bytes 1572872 | tf_op jit(solution)/shard_map/ppermute | solution.py:366
  25.4 8.3 %collective-permute-start.3 = (bf16[256,512]{1,0:T(8,128)(2,1)S(1)}, bf16[256,512]{1,0:T(8,128)(2,1)S(1)}, u32[]{:S(2)}, u32[]{:S(2)}) collective-permute-start(bf16[256,512]{1,0:T(8,128)(2,1)S(1)} %collective-permute-done.1.pair_v), channel_id=1, source_target_pairs={{12,4},{0,8},{20,12},{8,16},{28,20},{16,24},{13,5},{1,9},{21,13},{... | collective-permute-start | bytes 786440 | tf_op jit(solution)/shard_map/ppermute | solution.py:366
  29.8 5.4 %collective-permute-start.9 = (bf16[3,2,16,512]{3,2,1,0:T(8,128)(2,1)S(1)}, bf16[3,2,16,512]{3,2,1,0:T(8,128)(2,1)S(1)}, u32[]{:S(2)}, u32[]{:S(2)}) collective-permute-start(bf16[3,2,16,512]{3,2,1,0:T(8,128)(2,1)S(1)} %pad_maximum_fusion.2), channel_id=1, source_target_pairs={{0,4},{4,0},{8,12},{12,8},{16,20},{20,16},{24,28},{28,24},{1,5},{5... | collective-permute-start | bytes 294920 | tf_op jit(solution)/shard_map/ppermute | solution.py:366
  50.0 20.6 %collective-permute-start.14 = (bf16[2,256,512]{2,1,0:T(8,128)(2,1)S(1)}, bf16[2,256,512]{2,1,0:T(8,128)(2,1)S(1)}, u32[]{:S(2)}, u32[]{:S(2)}) collective-permute-start(bf16[2,256,512]{2,1,0:T(8,128)(2,1)S(1)} %get-tuple-element.43), channel_id=1, source_target_pairs={{4,12},{8,0},{12,20},{16,8},{20,28},{24,16},{5,13},{9,1},{13,21},{... | collective-permute-start | bytes 1572872 | tf_op jit(solution)/shard_map/ppermute | solution.py:366
  51.3 19.2 %collective-permute-start.11 = (bf16[2,2,32,512]{3,2,1,0:T(8,128)(2,1)S(1)}, bf16[2,2,32,512]{3,2,1,0:T(8,128)(2,1)S(1)}, u32[]{:S(2)}, u32[]{:S(2)}) collective-permute-start(bf16[2,2,32,512]{3,2,1,0:T(8,128)(2,1)S(1)} %get-tuple-element.37), channel_id=1, source_target_pairs={{0,16},{4,20},{8,24},{12,28},{16,0},{20,4},{24,8},{28,12},{1,17},{... | collective-permute-start | bytes 393224 | tf_op jit(solution)/shard_map/ppermute | solution.py:366
  54.7 20.1 %collective-permute-start.10 = (bf16[2,256,512]{2,1,0:T(8,128)(2,1)S(1)}, bf16[2,256,512]{2,1,0:T(8,128)(2,1)S(1)}, u32[]{:S(2)}, u32[]{:S(2)}) collective-permute-start(bf16[2,256,512]{2,1,0:T(8,128)(2,1)S(1)} %get-tuple-element.35), channel_id=1, source_target_pairs={{0,4},{4,0},{8,12},{12,8},{16,20},{20,16},{24,28},{28,24},{1,5},{5... | collective-permute-start | bytes 1572872 | tf_op jit(solution)/shard_map/ppermute | solution.py:366
  55.2 20.5 %collective-permute-start.12 = (bf16[2,256,512]{2,1,0:T(8,128)(2,1)S(1)}, bf16[2,256,512]{2,1,0:T(8,128)(2,1)S(1)}, u32[]{:S(2)}, u32[]{:S(2)}) collective-permute-start(bf16[2,256,512]{2,1,0:T(8,128)(2,1)S(1)} %get-tuple-element.41), channel_id=1, source_target_pairs={{12,4},{0,8},{20,12},{8,16},{28,20},{16,24},{13,5},{1,9},{21,13},{... | collective-permute-start | bytes 1572872 | tf_op jit(solution)/shard_map/ppermute | solution.py:366
  70.5 4.3 %collective-permute-start.13 = (bf16[1,2,32,512]{3,2,1,0:T(8,128)(2,1)S(1)}, bf16[1,2,32,512]{3,2,1,0:T(8,128)(2,1)S(1)}, u32[]{:S(2)}, u32[]{:S(2)}) collective-permute-start(bf16[1,2,32,512]{3,2,1,0:T(8,128)(2,1)S(1)} %fusion.5), channel_id=1, source_target_pairs={{0,24},{4,28},{8,0},{12,4},{16,8},{20,12},{24,16},{28,20},{1,25},{... | collective-permute-start | bytes 196616 | tf_op jit(solution)/shard_map/ppermute | solution.py:366
  70.8 10.3 %collective-permute-start.15 = (bf16[2,256,512]{2,1,0:T(8,128)(2,1)S(1)}, bf16[2,256,512]{2,1,0:T(8,128)(2,1)S(1)}, u32[]{:S(2)}, u32[]{:S(2)}) collective-permute-start(bf16[2,256,512]{2,1,0:T(8,128)(2,1)S(1)} %add_convert_fusion.1), channel_id=1, source_target_pairs={{0,4},{4,0},{8,12},{12,8},{16,20},{20,16},{24,28},{28,24},{1,5},{5... | collective-permute-start | bytes 1572872 | tf_op jit(solution)/shard_map/ppermute | solution.py:366
  74.9 5.8 %collective-permute-start.16 = (bf16[2,16,512]{2,1,0:T(8,128)(2,1)S(1)}, bf16[2,16,512]{2,1,0:T(8,128)(2,1)S(1)}, u32[]{:S(2)}, u32[]{:S(2)}) collective-permute-start(bf16[2,16,512]{2,1,0:T(8,128)(2,1)S(1)} %slice.84), channel_id=1, source_target_pairs={{0,4},{4,0},{8,12},{12,8},{16,20},{20,16},{24,28},{28,24},{1,5},{5... | collective-permute-start | bytes 98312 | tf_op jit(solution)/shard_map/ppermute | solution.py:366

commit v6 on v5

--- a/solution.py
+++ b/solution.py
@@ -31,15 +31,6 @@
 
 def shift_pairs(size, shift):
     return [(i, (i + 2 * shift) % size) for i in range(size)]
-
-
-def doublings(pair_count):
-    steps = []
-    held = 1
-    while held < pair_count:
-        steps.append((held, min(held, pair_count - held)))
-        held += steps[-1][1]
-    return steps
 
 
 def dot(a, b):
@@ -231,12 +222,11 @@
             relayed_grad[n] = first[2 * rows : 3 * rows].astype(relayed_grad.dtype)
             direct_grad[n] = second[2 * rows : 3 * rows].astype(direct_grad.dtype)
             far_grad = (first[3 * rows :] + second[3 * rows :]).astype(direct_grad.dtype)
-            for ref, (distance, count) in zip(coarse_grads, doublings(shifts + 1)):
-                for m in range(count):
-                    for side in range(2):
-                        start = (side * shifts + distance - 1 + m) * coarse_rows
-                        piece = far_grad[start : start + coarse_rows]
-                        ref[m, n, side * coarse_rows : (side + 1) * coarse_rows] = piece
+            for m, ref in enumerate(coarse_grads):
+                for side in range(2):
+                    start = (side * shifts + m) * coarse_rows
+                    piece = far_grad[start : start + coarse_rows]
+                    ref[n, side * coarse_rows : (side + 1) * coarse_rows] = piece
 
     return kernel
 
@@ -275,10 +265,7 @@
             * shifts,
             out_specs=[flat(lambda j, place: (0, j))] * 2
             + [both(rows)] * 5
-            + [
-                pl.BlockSpec((count, 2, 2 * coarse_rows, PAIR), lambda j, place: (0, 0, 0, j))
-                for _, count in doublings(shifts + 1)
-            ],
+            + [both(2 * coarse_rows)] * shifts,
         ),
         out_shape=[jax.ShapeDtypeStruct((rows, columns), bf16)] * 2
         + [
@@ -288,10 +275,7 @@
             jax.ShapeDtypeStruct((2, rows, columns), bf16),
             jax.ShapeDtypeStruct((2, rows, columns), bf16),
         ]
-        + [
-            jax.ShapeDtypeStruct((count, 2, 2 * coarse_rows, columns), bf16)
-            for _, count in doublings(shifts + 1)
-        ],
+        + [jax.ShapeDtypeStruct((2, 2 * coarse_rows, columns), bf16)] * shifts,
         compiler_params=pltpu.CompilerParams(vmem_limit_bytes=GRANT),
         cost_estimate=pl.CostEstimate(
             flops=4 * products, bytes_accessed=40 * rows * columns, transcendentals=0
@@ -407,35 +391,21 @@
 
     relayed_back = send(relayed_grad, direct_to)
     out_back = send(pair_out, swap)
+    coarse_back = [send(a, shift_pairs(size, -s)) for s, a in zip(shifts, coarse_grads)]
     direct_back = send(direct_grad, relayed_to)
-
-    far = None
-    for (distance, count), piece in reversed(list(zip(doublings(pair_count), coarse_grads))):
-        if far is not None:
-            piece = piece.astype(jnp.float32) + far[distance : distance + count]
-        piece = piece.astype(jnp.bfloat16)
-        if distance == 1:
-            relayed_back = after(relayed_back, piece)
-            pair_total = pair_grad + relayed_back.astype(jnp.float32)
-            pair_total = pair_total.astype(jnp.bfloat16)
-        back = send(piece, shift_pairs(size, -distance))
-        back = after(back, pair_total) if distance == 1 else back
-        back = jnp.pad(back.astype(jnp.float32), [(0, distance - count)] + [(0, 0)] * 3)
-        far = back if far is None else far[:distance] + back
-    far = far[0]
-    grad_back = send(pair_total, swap)
-    other_far = send(far[:, block_rows:].astype(jnp.bfloat16), swap).astype(jnp.float32)
-    out_back = after(out_back, piece)
-    own_longer = lengthened(restrict, far[:, :block_rows])
-    other_longer = lax.optimization_barrier(lengthened(restrict, other_far))
-    home_total = home_grad + direct_back.astype(jnp.float32) + own_longer
+    pair_total = pair_grad + relayed_back.astype(jnp.float32)
+    far = sum(piece.astype(jnp.float32) for piece in after(coarse_back, pair_total))
+    pair_total = pair_total + lengthened(restrict, far[:, block_rows:])
+    grad_back = send(pair_total.astype(jnp.bfloat16), swap)
+    home_total = home_grad + direct_back.astype(jnp.float32)
+    home_total = home_total + lengthened(restrict, far[:, :block_rows])
     home_total = home_total.astype(jnp.bfloat16)
-
-    def summed(n):
-        other = grad_back[n].astype(jnp.float32) + other_longer[n]
-        return whole(home_total[n], other.astype(jnp.bfloat16))
-
-    return whole(out, out_back[0]), whole(grad_q, out_back[1]), summed(0), summed(1)
+    return (
+        whole(out, out_back[0]),
+        whole(grad_q, out_back[1]),
+        whole(home_total[0], grad_back[0]),
+        whole(home_total[1], grad_back[1]),
+    )
 
 
 def solution(mesh):

time: 82.8 us -> 81.3 us (0.982)
  waiting for transfers between devices: 28.1 us -> 25.8 us
    ppermute x17, waiting for transfers between devices: 28.1 us -> 25.8 us  [send(): return lax.ppermute(value, 'seq', pairs)]
  transfers between devices with their start and end apart: 17 -> 17, of which waited for: 8 -> 9; matrix products, arithmetic and copies ran while one was open for 6% -> 6% of each run, Pallas kernels for 0% -> 0%
where the time goes in v6:
time: 81.3 us; the launch traced here: 81 us
  starting transfers between devices  30.2 us (37%)
  waiting for transfers between devices  25.8 us (32%)
  Pallas kernels  15 us (18%)
  other arithmetic  4.91 us (6%)
  local copies, waits for them, and re-layouts  2.92 us (4%)
  matrix products  1.35 us (2%)
  between operations  0.88 us (1%)
    ppermute x17, starting transfers between devices, send(): return lax.ppermute(value, 'seq', pairs)  30.2 us
    ppermute x17, waiting for transfers between devices, send(): return lax.ppermute(value, 'seq', pairs)  25.8 us
    pallas_call x1, Pallas kernels, attention(): pl.pallas_call(attention_kernel(shifts, *level_rows), grid_spec=pltpu.Pre...  14.8 us
    select_n x2, other arithmetic, whole(): jnp.where(parity == 0, jnp.concatenate([own, other], axis=axis), jnp.conc...  2.53 us
  transfers between devices with their start and end apart: 17, of which 9 were waited for; matrix products, arithmetic and copies ran while one was open for 6% of the time, Pallas kernels for 0%

profile of v6, /device:TPU:0, one launch (start us, length us, event | category | flops | bytes accessed | tf_op | source)
XLA Modules:
  0.0 81.0 jit_solution(13907223743101099204)
XLA Ops:
  0.6 0.0 copy-start.1
  0.7 1.1 %dynamic-slice_bitcast_fusion.3 = (bf16[1,256,512]{2,1,0:T(8,128)(2,1)S(1)}, bf16[256,512]{1,0:T(8,128)(2,1)S(1)}) fusion(bf16[256,1024]{1,0:T(8,128)(2,1)} %k.3, s32[]{:T(128)S(6)} %select_n.46, s32[]{:T(128)S(6)} %select_n.45), kind=kLoop, calls=%fused_computation.21 | loop fusion | bytes 1048584 | tf_op jit(solution)/shard_map/stack | solution.py:365
  1.8 0.0 copy-start.2
  1.8 3.0 %collective-permute-start = (bf16[256,512]{1,0:T(8,128)(2,1)S(1)}, bf16[256,512]{1,0:T(8,128)(2,1)S(1)}, u32[]{:S(2)}, u32[]{:S(2)}) collective-permute-start(bf16[256,512]{1,0:T(8,128)(2,1)S(1)} %get-tuple-element.55), channel_id=1, source_target_pairs={{0,4},{4,0},{8,12},{12,8},{16,20},{20,16},{24,28},{28,24},{1,5},{5... | collective-permute-start | bytes 786440 | tf_op jit(solution)/shard_map/ppermute | solution.py:350
  4.8 0.0 copy-done.1
  4.8 0.0 copy-start.4
  4.8 0.0 copy-start.5
  4.9 0.0 copy-start.3
  4.9 0.1 collective-permute-start.1
  5.0 0.1 pad.21.clone
  5.1 0.4 copy-done.4
  5.5 0.0 copy-done.5
  5.5 0.1 maximum_maximum_fusion.restrict
  5.6 0.0 copy-done.2
  5.6 0.0 copy-start
  5.6 0.3 copy-done.3
  5.9 0.7 copy-done
  6.7 0.2 restrict.1
  6.9 0.9 %pad_maximum_fusion.1 = bf16[2,256,512]{2,1,0:T(8,128)(2,1)} fusion(bf16[1,256,512]{2,1,0:T(8,128)(2,1)S(1)} %dynamic-slice_bitcast_fusion, bf16[1,256,512]{2,1,0:T(8,128)(2,1)S(1)} %dynamic-slice_bitcast_fusion.1), kind=kLoop, calls=%fused_computation.7 | loop fusion | flops 262144 | bytes 1048576 | tf_op jit(solution)/shard_map/stack | solution.py:367
  7.8 4.2 %collective-permute-done.pair_k = bf16[256,512]{1,0:T(8,128)(2,1)S(1)} collective-permute-done((bf16[256,512]{1,0:T(8,128)(2,1)S(1)}, bf16[256,512]{1,0:T(8,128)(2,1)S(1)}, u32[]{:S(2)}, u32[]{:S(2)}) %collective-permute-start) | collective-permute-done | bytes 262176 | tf_op jit(solution)/shard_map/ppermute | solution.py:350
  12.0 4.1 %collective-permute-start.8 = (bf16[2,2,16,512]{3,2,1,0:T(8,128)(2,1)S(1)}, bf16[2,2,16,512]{3,2,1,0:T(8,128)(2,1)S(1)}, u32[]{:S(2)}, u32[]{:S(2)}) collective-permute-start(bf16[2,2,16,512]{3,2,1,0:T(8,128)(2,1)S(1)} %restrict.1), channel_id=1, source_target_pairs={{0,24},{4,28},{8,0},{12,4},{16,8},{20,12},{24,16},{28,20},{1,25},{... | collective-permute-start | bytes 196616 | tf_op jit(solution)/shard_map/ppermute | solution.py:350
  16.1 0.0 collective-permute-start.7
  16.1 1.0 %collective-permute-start.6 = (bf16[2,2,16,512]{3,2,1,0:T(8,128)(2,1)S(1)}, bf16[2,2,16,512]{3,2,1,0:T(8,128)(2,1)S(1)}, u32[]{:S(2)}, u32[]{:S(2)}) collective-permute-start(bf16[2,2,16,512]{3,2,1,0:T(8,128)(2,1)S(1)} %restrict.1), channel_id=1, source_target_pairs={{0,8},{4,12},{8,16},{12,20},{16,24},{20,28},{24,0},{28,4},{1,9},{5... | collective-permute-start | bytes 196616 | tf_op jit(solution)/shard_map/ppermute | solution.py:350
  17.1 4.4 %collective-permute-start.2 = (bf16[256,512]{1,0:T(8,128)(2,1)S(1)}, bf16[256,512]{1,0:T(8,128)(2,1)S(1)}, u32[]{:S(2)}, u32[]{:S(2)}) collective-permute-start(bf16[256,512]{1,0:T(8,128)(2,1)S(1)} %collective-permute-done.pair_k), channel_id=1, source_target_pairs={{12,4},{0,8},{20,12},{8,16},{28,20},{16,24},{13,5},{1,9},{21,13},{... | collective-permute-start | bytes 786440 | tf_op jit(solution)/shard_map/ppermute | solution.py:350
  21.5 0.8 %pad_maximum_fusion = bf16[2,256,512]{2,1,0:T(8,128)(2,1)} fusion(bf16[1,256,512]{2,1,0:T(8,128)(2,1)S(1)} %get-tuple-element.56, bf16[1,256,512]{2,1,0:T(8,128)(2,1)S(1)} %get-tuple-element.54), kind=kLoop, calls=%fused_computation.6 | loop fusion | flops 262144 | bytes 1048576 | tf_op jit(solution)/shard_map/stack | solution.py:365
  22.4 0.0 collective-permute-done.1.pair_v
  22.4 0.0 collective-permute-start.5
  22.4 0.0 collective-permute-done.8.rest_2_
  22.4 1.3 %collective-permute-start.4 = (bf16[2,256,512]{2,1,0:T(8,128)(2,1)}, bf16[2,256,512]{2,1,0:T(8,128)(2,1)S(1)}, u32[]{:S(2)}, u32[]{:S(2)}) collective-permute-start(bf16[2,256,512]{2,1,0:T(8,128)(2,1)} %pad_maximum_fusion), channel_id=1, source_target_pairs={{4,12},{8,0},{12,20},{16,8},{20,28},{24,16},{5,13},{9,1},{13,21},{... | collective-permute-start | bytes 1572872 | tf_op jit(solution)/shard_map/ppermute | solution.py:350
  23.7 0.0 collective-permute-done.7.rest_1_
  23.7 0.0 collective-permute-done.6.rest_0_
  23.7 1.6 %collective-permute-done.2.relayed_k = bf16[256,512]{1,0:T(8,128)(2,1)S(1)} collective-permute-done((bf16[256,512]{1,0:T(8,128)(2,1)S(1)}, bf16[256,512]{1,0:T(8,128)(2,1)S(1)}, u32[]{:S(2)}, u32[]{:S(2)}) %collective-permute-start.2) | collective-permute-done | bytes 262176 | tf_op jit(solution)/shard_map/ppermute | solution.py:350
  25.4 4.4 %collective-permute-start.3 = (bf16[256,512]{1,0:T(8,128)(2,1)S(1)}, bf16[256,512]{1,0:T(8,128)(2,1)S(1)}, u32[]{:S(2)}, u32[]{:S(2)}) collective-permute-start(bf16[256,512]{1,0:T(8,128)(2,1)S(1)} %collective-permute-done.1.pair_v), channel_id=1, source_target_pairs={{12,4},{0,8},{20,12},{8,16},{28,20},{16,24},{13,5},{1,9},{21,13},{... | collective-permute-start | bytes 786440 | tf_op jit(solution)/shard_map/ppermute | solution.py:350
  29.8 0.1 collective-permute-start.9
  29.9 0.1 pad_add_fusion.place
  30.0 3.7 %collective-permute-done.3.relayed_v = bf16[256,512]{1,0:T(8,128)(2,1)S(1)} collective-permute-done((bf16[256,512]{1,0:T(8,128)(2,1)S(1)}, bf16[256,512]{1,0:T(8,128)(2,1)S(1)}, u32[]{:S(2)}, u32[]{:S(2)}) %collective-permute-start.3) | collective-permute-done | bytes 262176 | tf_op jit(solution)/shard_map/ppermute | solution.py:350
  33.6 1.4 %collective-permute-done.4.direct = bf16[2,256,512]{2,1,0:T(8,128)(2,1)S(1)} collective-permute-done((bf16[2,256,512]{2,1,0:T(8,128)(2,1)}, bf16[2,256,512]{2,1,0:T(8,128)(2,1)S(1)}, u32[]{:S(2)}, u32[]{:S(2)}) %collective-permute-start.4) | collective-permute-done | bytes 524320 | tf_op jit(solution)/shard_map/ppermute | solution.py:350
  35.0 0.0 collective-permute-done.5.pair_qc
  35.0 0.2 collective-permute-done.9.pair_coarse
  35.2 14.8 %attention.1 = (bf16[256,512]{1,0:T(8,128)(2,1)S(1)}, bf16[256,512]{1,0:T(8,128)(2,1)S(1)}, bf16[2,256,512]{2,1,0:T(8,128)(2,1)S(1)}, f32[2,256,512]{2,1,0:T(8,1...) custom-call(s32[4]{0:T(128)S(1)} %pad_add_fusion.place, ...), custom_call_target="tpu_custom_call" | custom-call | flops 10871635968 | bytes 5242880 | tf_op jit(solution)/shard_map/attention/pallas_call | solution.py:255
  50.0 1.3 %collective-permute-start.15 = (bf16[2,256,512]{2,1,0:T(8,128)(2,1)S(1)}, bf16[2,256,512]{2,1,0:T(8,128)(2,1)S(1)}, u32[]{:S(2)}, u32[]{:S(2)}) collective-permute-start(bf16[2,256,512]{2,1,0:T(8,128)(2,1)S(1)} %get-tuple-element.44), channel_id=1, source_target_pairs={{4,12},{8,0},{12,20},{16,8},{20,28},{24,16},{5,13},{9,1},{13,21},{... | collective-permute-start | bytes 1572872 | tf_op jit(solution)/shard_map/ppermute | solution.py:350
  51.3 4.6 %collective-permute-start.12 = (bf16[2,32,512]{2,1,0:T(8,128)(2,1)S(1)}, bf16[2,32,512]{2,1,0:T(8,128)(2,1)S(1)}, u32[]{:S(2)}, u32[]{:S(2)}) collective-permute-start(bf16[2,32,512]{2,1,0:T(8,128)(2,1)S(1)} %get-tuple-element.40), channel_id=1, source_target_pairs={{0,24},{4,28},{8,0},{12,4},{16,8},{20,12},{24,16},{28,20},{1,25},{... | collective-permute-start | bytes 196616 | tf_op jit(solution)/shard_map/ppermute | solution.py:350
  55.9 0.0 collective-permute-start.13
  55.9 0.8 %collective-permute-start.14 = (bf16[2,32,512]{2,1,0:T(8,128)(2,1)S(1)}, bf16[2,32,512]{2,1,0:T(8,128)(2,1)S(1)}, u32[]{:S(2)}, u32[]{:S(2)}) collective-permute-start(bf16[2,32,512]{2,1,0:T(8,128)(2,1)S(1)} %get-tuple-element.42), channel_id=1, source_target_pairs={{0,8},{4,12},{8,16},{12,20},{16,24},{20,28},{24,0},{28,4},{1,9},{5... | collective-permute-start | bytes 196616 | tf_op jit(solution)/shard_map/ppermute | solution.py:350
  56.7 0.5 collective-permute-start.10
  57.3 7.8 %collective-permute-done.15 = bf16[2,256,512]{2,1,0:T(8,128)(2,1)S(1)} collective-permute-done((bf16[2,256,512]{2,1,0:T(8,128)(2,1)S(1)}, bf16[2,256,512]{2,1,0:T(8,128)(2,1)S(1)}, u32[]{:S(2)}, u32[]{:S(2)}) %collective-permute-start.15) | collective-permute-done | bytes 524320 | tf_op jit(solution)/shard_map/ppermute | solution.py:350
  65.1 4.4 %collective-permute-start.11 = (bf16[2,256,512]{2,1,0:T(8,128)(2,1)S(1)}, bf16[2,256,512]{2,1,0:T(8,128)(2,1)S(1)}, u32[]{:S(2)}, u32[]{:S(2)}) collective-permute-start(bf16[2,256,512]{2,1,0:T(8,128)(2,1)S(1)} %get-tuple-element.39), channel_id=1, source_target_pairs={{12,4},{0,8},{20,12},{8,16},{28,20},{16,24},{13,5},{1,9},{21,13},{... | collective-permute-start | bytes 1572872 | tf_op jit(solution)/shard_map/ppermute | solution.py:350
  69.5 0.2 convert_add_fusion
  69.6 0.0 collective-permute-done.12
  69.6 0.1 collective-permute-done.13
  69.8 0.0 collective-permute-done.14
  69.8 0.7 fusion.1
  70.5 0.1 collective-permute-start.16
  70.6 0.0 collective-permute-done.10
  70.6 1.3 %maximum_select_fusion = (bf16[256,1024]{1,0:T(8,128)(2,1)}, bf16[256,1024]{1,0:T(8,128)(2,1)}) fusion(bf16[256,512]{1,0:T(8,128)(2,1)S(1)} %get-tuple-element.53, bf16[256,512]{1,0:T(8,128)(2,1)S(1)} %get-tuple-element.35, pred[]{:T(512)S(6)} %eq.2, bf16[256,512]{1,0:T(8,128)(2,1)S(1)} %get-tuple-element.37, bf16[256,512]{1,0:T(8,128)(2,1)S(1)} %get-tuple-element.52), kind=kLoop, calls=%fused_computation.8 | loop fusion | flops 4718592 | bytes 2097153 | tf_op jit(solution)/shard_map/jit(_where)/select_n | solution.py:386
  71.9 0.7 convolution_bitcast_fusion.1
  72.6 3.5 %collective-permute-done.11 = bf16[2,256,512]{2,1,0:T(8,128)(2,1)S(1)} collective-permute-done((bf16[2,256,512]{2,1,0:T(8,128)(2,1)S(1)}, bf16[2,256,512]{2,1,0:T(8,128)(2,1)S(1)}, u32[]{:S(2)}, u32[]{:S(2)}) %collective-permute-start.11) | collective-permute-done | bytes 524320 | tf_op jit(solution)/shard_map/ppermute | solution.py:350
  76.1 0.3 add_convert_fusion
  76.5 3.3 %collective-permute-done.16 = bf16[2,256,512]{2,1,0:T(8,128)(2,1)S(1)} collective-permute-done((bf16[2,256,512]{2,1,0:T(8,128)(2,1)S(1)}, bf16[2,256,512]{2,1,0:T(8,128)(2,1)S(1)}, u32[]{:S(2)}, u32[]{:S(2)}) %collective-permute-start.16) | collective-permute-done | bytes 524320 | tf_op jit(solution)/shard_map/ppermute | solution.py:350
  79.8 1.3 %maximum_select_fusion.2 = (bf16[256,1024]{1,0:T(8,128)(2,1)}, bf16[256,1024]{1,0:T(8,128)(2,1)}) fusion(bf16[256,512]{1,0:T(8,128)(2,1)S(1)} %get-tuple-element.51, bf16[256,512]{1,0:T(8,128)(2,1)S(1)} %get-tuple-element.49, pred[]{:T(512)S(6)} %eq.2, bf16[256,512]{1,0:T(8,128)(2,1)S(1)} %get-tuple-element.48, bf16[256,512]{1,0:T(8,128)(2,1)S(1)} %get-tuple-element.50), kind=kLoop, calls=%fused_computation.10 | loop fusion | flops 4718592 | bytes 2097153 | tf_op jit(solution)/shard_map/jit(_where)/select_n | solution.py:386
  (12 shorter events, 0.3 us)
Async XLA Ops:
  0.6 4.2 %copy-start.1 = (bf16[256,1024]{1,0:T(8,128)(2,1)S(1)}, bf16[256,1024]{1,0:T(8,128)(2,1)}, u32[]{:S(2)}) copy-start(bf16[256,1024]{1,0:T(8,128)(2,1)} %v.3) | copy-start | bytes 1572868
  1.8 3.8 %copy-start.2 = (bf16[256,1024]{1,0:T(8,128)(2,1)S(1)}, bf16[256,1024]{1,0:T(8,128)(2,1)}, u32[]{:S(2)}) copy-start(bf16[256,1024]{1,0:T(8,128)(2,1)} %q.1) | copy-start | bytes 1572868
  1.8 10.2 %collective-permute-start = (bf16[256,512]{1,0:T(8,128)(2,1)S(1)}, bf16[256,512]{1,0:T(8,128)(2,1)S(1)}, u32[]{:S(2)}, u32[]{:S(2)}) collective-permute-start(bf16[256,512]{1,0:T(8,128)(2,1)S(1)} %get-tuple-element.55), channel_id=1, source_target_pairs={{0,4},{4,0},{8,12},{12,8},{16,20},{20,16},{24,28},{28,24},{1,5},{5... | collective-permute-start | bytes 786440 | tf_op jit(solution)/shard_map/ppermute | solution.py:350
  4.8 0.7 copy-start.4
  4.8 0.7 copy-start.5
  4.9 1.0 %copy-start.3 = (bf16[256,1024]{1,0:T(8,128)(2,1)S(1)}, bf16[256,1024]{1,0:T(8,128)(2,1)}, u32[]{:S(2)}) copy-start(bf16[256,1024]{1,0:T(8,128)(2,1)} %c.1) | copy-start | bytes 1572868
  4.9 17.5 %collective-permute-start.1 = (bf16[256,512]{1,0:T(8,128)(2,1)S(1)}, bf16[256,512]{1,0:T(8,128)(2,1)S(1)}, u32[]{:S(2)}, u32[]{:S(2)}) collective-permute-start(bf16[256,512]{1,0:T(8,128)(2,1)S(1)} %get-tuple-element.57), channel_id=1, source_target_pairs={{0,4},{4,0},{8,12},{12,8},{16,20},{20,16},{24,28},{28,24},{1,5},{5... | collective-permute-start | bytes 786440 | tf_op jit(solution)/shard_map/ppermute | solution.py:350
  5.6 1.1 %copy-start = (bf16[256,1024]{1,0:T(8,128)(2,1)S(1)}, bf16[256,1024]{1,0:T(8,128)(2,1)}, u32[]{:S(2)}) copy-start(bf16[256,1024]{1,0:T(8,128)(2,1)} %k.3) | copy-start | bytes 1572868
  12.0 10.4 %collective-permute-start.8 = (bf16[2,2,16,512]{3,2,1,0:T(8,128)(2,1)S(1)}, bf16[2,2,16,512]{3,2,1,0:T(8,128)(2,1)S(1)}, u32[]{:S(2)}, u32[]{:S(2)}) collective-permute-start(bf16[2,2,16,512]{3,2,1,0:T(8,128)(2,1)S(1)} %restrict.1), channel_id=1, source_target_pairs={{0,24},{4,28},{8,0},{12,4},{16,8},{20,12},{24,16},{28,20},{1,25},{... | collective-permute-start | bytes 196616 | tf_op jit(solution)/shard_map/ppermute | solution.py:350
  16.1 7.6 %collective-permute-start.7 = (bf16[2,2,16,512]{3,2,1,0:T(8,128)(2,1)S(1)}, bf16[2,2,16,512]{3,2,1,0:T(8,128)(2,1)S(1)}, u32[]{:S(2)}, u32[]{:S(2)}) collective-permute-start(bf16[2,2,16,512]{3,2,1,0:T(8,128)(2,1)S(1)} %restrict.1), channel_id=1, source_target_pairs={{0,16},{4,20},{8,24},{12,28},{16,0},{20,4},{24,8},{28,12},{1,17},{... | collective-permute-start | bytes 196616 | tf_op jit(solution)/shard_map/ppermute | solution.py:350
  16.1 7.6 %collective-permute-start.6 = (bf16[2,2,16,512]{3,2,1,0:T(8,128)(2,1)S(1)}, bf16[2,2,16,512]{3,2,1,0:T(8,128)(2,1)S(1)}, u32[]{:S(2)}, u32[]{:S(2)}) collective-permute-start(bf16[2,2,16,512]{3,2,1,0:T(8,128)(2,1)S(1)} %restrict.1), channel_id=1, source_target_pairs={{0,8},{4,12},{8,16},{12,20},{16,24},{20,28},{24,0},{28,4},{1,9},{5... | collective-permute-start | bytes 196616 | tf_op jit(solution)/shard_map/ppermute | solution.py:350
  17.1 8.2 %collective-permute-start.2 = (bf16[256,512]{1,0:T(8,128)(2,1)S(1)}, bf16[256,512]{1,0:T(8,128)(2,1)S(1)}, u32[]{:S(2)}, u32[]{:S(2)}) collective-permute-start(bf16[256,512]{1,0:T(8,128)(2,1)S(1)} %collective-permute-done.pair_k), channel_id=1, source_target_pairs={{12,4},{0,8},{20,12},{8,16},{28,20},{16,24},{13,5},{1,9},{21,13},{... | collective-permute-start | bytes 786440 | tf_op jit(solution)/shard_map/ppermute | solution.py:350
  22.4 12.6 %collective-permute-start.5 = (bf16[2,256,512]{2,1,0:T(8,128)(2,1)}, bf16[2,256,512]{2,1,0:T(8,128)(2,1)S(1)}, u32[]{:S(2)}, u32[]{:S(2)}) collective-permute-start(bf16[2,256,512]{2,1,0:T(8,128)(2,1)} %pad_maximum_fusion.1), channel_id=1, source_target_pairs={{0,4},{4,0},{8,12},{12,8},{16,20},{20,16},{24,28},{28,24},{1,5},{5... | collective-permute-start | bytes 1572872 | tf_op jit(solution)/shard_map/ppermute | solution.py:350
  22.4 12.6 %collective-permute-start.4 = (bf16[2,256,512]{2,1,0:T(8,128)(2,1)}, bf16[2,256,512]{2,1,0:T(8,128)(2,1)S(1)}, u32[]{:S(2)}, u32[]{:S(2)}) collective-permute-start(bf16[2,256,512]{2,1,0:T(8,128)(2,1)} %pad_maximum_fusion), channel_id=1, source_target_pairs={{4,12},{8,0},{12,20},{16,8},{20,28},{24,16},{5,13},{9,1},{13,21},{... | collective-permute-start | bytes 1572872 | tf_op jit(solution)/shard_map/ppermute | solution.py:350
  25.4 8.3 %collective-permute-start.3 = (bf16[256,512]{1,0:T(8,128)(2,1)S(1)}, bf16[256,512]{1,0:T(8,128)(2,1)S(1)}, u32[]{:S(2)}, u32[]{:S(2)}) collective-permute-start(bf16[256,512]{1,0:T(8,128)(2,1)S(1)} %collective-permute-done.1.pair_v), channel_id=1, source_target_pairs={{12,4},{0,8},{20,12},{8,16},{28,20},{16,24},{13,5},{1,9},{21,13},{... | collective-permute-start | bytes 786440 | tf_op jit(solution)/shard_map/ppermute | solution.py:350
  29.8 5.4 %collective-permute-start.9 = (bf16[3,2,16,512]{3,2,1,0:T(8,128)(2,1)S(1)}, bf16[3,2,16,512]{3,2,1,0:T(8,128)(2,1)S(1)}, u32[]{:S(2)}, u32[]{:S(2)}) collective-permute-start(bf16[3,2,16,512]{3,2,1,0:T(8,128)(2,1)S(1)} %pad_maximum_fusion.2), channel_id=1, source_target_pairs={{0,4},{4,0},{8,12},{12,8},{16,20},{20,16},{24,28},{28,24},{1,5},{5... | collective-permute-start | bytes 294920 | tf_op jit(solution)/shard_map/ppermute | solution.py:350
  50.0 15.1 %collective-permute-start.15 = (bf16[2,256,512]{2,1,0:T(8,128)(2,1)S(1)}, bf16[2,256,512]{2,1,0:T(8,128)(2,1)S(1)}, u32[]{:S(2)}, u32[]{:S(2)}) collective-permute-start(bf16[2,256,512]{2,1,0:T(8,128)(2,1)S(1)} %get-tuple-element.44), channel_id=1, source_target_pairs={{4,12},{8,0},{12,20},{16,8},{20,28},{24,16},{5,13},{9,1},{13,21},{... | collective-permute-start | bytes 1572872 | tf_op jit(solution)/shard_map/ppermute | solution.py:350
  51.3 18.4 %collective-permute-start.12 = (bf16[2,32,512]{2,1,0:T(8,128)(2,1)S(1)}, bf16[2,32,512]{2,1,0:T(8,128)(2,1)S(1)}, u32[]{:S(2)}, u32[]{:S(2)}) collective-permute-start(bf16[2,32,512]{2,1,0:T(8,128)(2,1)S(1)} %get-tuple-element.40), channel_id=1, source_target_pairs={{0,24},{4,28},{8,0},{12,4},{16,8},{20,12},{24,16},{28,20},{1,25},{... | collective-permute-start | bytes 196616 | tf_op jit(solution)/shard_map/ppermute | solution.py:350
  55.9 13.8 %collective-permute-start.13 = (bf16[2,32,512]{2,1,0:T(8,128)(2,1)S(1)}, bf16[2,32,512]{2,1,0:T(8,128)(2,1)S(1)}, u32[]{:S(2)}, u32[]{:S(2)}) collective-permute-start(bf16[2,32,512]{2,1,0:T(8,128)(2,1)S(1)} %get-tuple-element.41), channel_id=1, source_target_pairs={{0,16},{4,20},{8,24},{12,28},{16,0},{20,4},{24,8},{28,12},{1,17},{... | collective-permute-start | bytes 196616 | tf_op jit(solution)/shard_map/ppermute | solution.py:350
  55.9 13.8 %collective-permute-start.14 = (bf16[2,32,512]{2,1,0:T(8,128)(2,1)S(1)}, bf16[2,32,512]{2,1,0:T(8,128)(2,1)S(1)}, u32[]{:S(2)}, u32[]{:S(2)}) collective-permute-start(bf16[2,32,512]{2,1,0:T(8,128)(2,1)S(1)} %get-tuple-element.42), channel_id=1, source_target_pairs={{0,8},{4,12},{8,16},{12,20},{16,24},{20,28},{24,0},{28,4},{1,9},{5... | collective-permute-start | bytes 196616 | tf_op jit(solution)/shard_map/ppermute | solution.py:350
  56.7 13.8 %collective-permute-start.10 = (bf16[2,256,512]{2,1,0:T(8,128)(2,1)S(1)}, bf16[2,256,512]{2,1,0:T(8,128)(2,1)S(1)}, u32[]{:S(2)}, u32[]{:S(2)}) collective-permute-start(bf16[2,256,512]{2,1,0:T(8,128)(2,1)S(1)} %get-tuple-element.36), channel_id=1, source_target_pairs={{0,4},{4,0},{8,12},{12,8},{16,20},{20,16},{24,28},{28,24},{1,5},{5... | collective-permute-start | bytes 1572872 | tf_op jit(solution)/shard_map/ppermute | solution.py:350
  65.1 11.0 %collective-permute-start.11 = (bf16[2,256,512]{2,1,0:T(8,128)(2,1)S(1)}, bf16[2,256,512]{2,1,0:T(8,128)(2,1)S(1)}, u32[]{:S(2)}, u32[]{:S(2)}) collective-permute-start(bf16[2,256,512]{2,1,0:T(8,128)(2,1)S(1)} %get-tuple-element.39), channel_id=1, source_target_pairs={{12,4},{0,8},{20,12},{8,16},{28,20},{16,24},{13,5},{1,9},{21,13},{... | collective-permute-start | bytes 1572872 | tf_op jit(solution)/shard_map/ppermute | solution.py:350
  70.5 9.2 %collective-permute-start.16 = (bf16[2,256,512]{2,1,0:T(8,128)(2,1)S(1)}, bf16[2,256,512]{2,1,0:T(8,128)(2,1)S(1)}, u32[]{:S(2)}, u32[]{:S(2)}) collective-permute-start(bf16[2,256,512]{2,1,0:T(8,128)(2,1)S(1)} %fusion.1), channel_id=1, source_target_pairs={{0,4},{4,0},{8,12},{12,8},{16,20},{20,16},{24,28},{28,24},{1,5},{5... | collective-permute-start | bytes 1572872 | tf_op jit(solution)/shard_map/ppermute | solution.py:350

commit v7 on v6

--- a/solution.py
+++ b/solution.py
@@ -10,7 +10,7 @@
 HEAD_DIM = 64
 PAIR = 2 * HEAD_DIM
 TILE = 32
-GRANT = 32 * 1024 * 1024
+GRANT = 16 * 1024 * 1024
 
 level_one_bias = math.log(32.0)
 level_two_bias = math.log(64.0)
@@ -31,6 +31,10 @@
 
 def shift_pairs(size, shift):
     return [(i, (i + 2 * shift) % size) for i in range(size)]
+
+
+def both_levels(shift, pair_count):
+    return shift == 2 or shift == pair_count - 2
 
 
 def dot(a, b):
@@ -158,30 +162,39 @@
         rows = q.shape[0]
 
         parity, pair = (place[0], place[3])
-        coarse_rows = pair_coarse.shape[2]
 
         def halo(have):
             return jnp.full((rows, 2 * rows), jnp.where(have > 0, 0.0, masked_bias), jnp.float32)
 
+        sizes = [ref.shape[2] for ref in coarse]
+        starts = [sum(sizes[:m]) for m in range(shifts + 1)]
+
         def coarse_bias(query_block):
-            row = lax.broadcasted_iota(jnp.int32, (coarse_rows, 2 * rows), 0)
             pieces = []
             for side in (parity, 1 - parity):
-                for shift in range(1, shifts + 1):
+                for shift, size in enumerate(sizes, start=1):
+                    row = lax.broadcasted_iota(jnp.int32, (size, 2 * rows), 0)
                     sender = jnp.where(pair >= shift, pair - shift, pair - shift + shifts + 1)
                     apart = jnp.abs(2 * sender + side - query_block)
                     one = jnp.where((apart == 2) | (apart == 3), level_one_bias, masked_bias)
                     two = jnp.where(apart >= 4, level_two_bias, masked_bias)
-                    rest = jnp.where(row < one_rows + two_rows, two, masked_bias)
-                    pieces.append(jnp.where(row < one_rows, one, rest))
+                    if both_levels(shift, shifts + 1):
+                        two = jnp.where(row < one_rows + two_rows, two, masked_bias)
+                        pieces.append(jnp.where(row < one_rows, one, two))
+                    else:
+                        near = jnp.abs(sender - pair) == 1
+                        one = jnp.where(near, one, masked_bias)
+                        two = jnp.where(near, one, two)
+                        one = jnp.where(row < one_rows, one, masked_bias)
+                        pieces.append(jnp.where(row < two_rows, two, one))
             return jnp.concatenate(pieces, axis=0).astype(jnp.float32)
 
         def chunk(pieces):
             return jnp.concatenate(pieces, axis=0), jnp.concatenate([a.T for a in pieces], axis=1)
 
         def shared(n, home, partner):
-            far = [ref[0, n] for ref in coarse] + [pair_coarse[m, n] for m in range(shifts)]
-            far = jnp.concatenate(far, axis=0)
+            far = jnp.concatenate([ref[0, n].astype(jnp.float32) for ref in coarse], axis=0)
+            far = jnp.concatenate([far.astype(jnp.bfloat16), pair_coarse[n]], axis=0)
             return chunk([home[...], partner[...]]), chunk([far])
 
         both_keys, both_values = (shared(0, k, pair_k), shared(1, v, pair_v))
@@ -221,12 +234,14 @@
             pair_grad[n] = first[rows : 2 * rows] + second[rows : 2 * rows]
             relayed_grad[n] = first[2 * rows : 3 * rows].astype(relayed_grad.dtype)
             direct_grad[n] = second[2 * rows : 3 * rows].astype(direct_grad.dtype)
-            far_grad = (first[3 * rows :] + second[3 * rows :]).astype(direct_grad.dtype)
+            far_grad = first[3 * rows :] + second[3 * rows :]
             for m, ref in enumerate(coarse_grads):
-                for side in range(2):
-                    start = (side * shifts + m) * coarse_rows
-                    piece = far_grad[start : start + coarse_rows]
-                    ref[n, side * coarse_rows : (side + 1) * coarse_rows] = piece
+                cuts = [
+                    slice(side * starts[-1] + starts[m], side * starts[-1] + starts[m + 1])
+                    for side in range(2)
+                ]
+                piece = jnp.concatenate([far_grad[cut] for cut in cuts], axis=0)
+                ref[n] = piece.astype(ref.dtype)
 
     return kernel
 
@@ -238,7 +253,6 @@
     columns = width // 2
     steps = columns // PAIR
     shifts = len(coarse)
-    coarse_rows = pair_coarse.shape[2]
 
     def mine(j, place):
         return place[0] * steps + j
@@ -249,7 +263,7 @@
     def both(shape_rows):
         return pl.BlockSpec((2, shape_rows, PAIR), lambda j, place: (0, 0, j))
 
-    key_count = 3 * rows + 2 * shifts * coarse_rows
+    key_count = 3 * rows + 2 * pair_coarse.shape[1]
     products = 6 * 2 * 2 * rows * key_count * HEAD_DIM * 2 * steps
     bf16, f32 = (jnp.bfloat16, jnp.float32)
     return pl.pallas_call(
@@ -260,12 +274,14 @@
             in_specs=[flat(lambda j, place: (0, mine(j, place)))] * 4
             + [flat(lambda j, place: (0, j))] * 4
             + [both(rows)] * 2
-            + [pl.BlockSpec((shifts, 2, coarse_rows, PAIR), lambda j, place: (0, 0, 0, j))]
-            + [pl.BlockSpec((1, 2, coarse_rows, PAIR), lambda j, place: (place[0], 0, 0, j))]
-            * shifts,
+            + [both(pair_coarse.shape[1])]
+            + [
+                pl.BlockSpec((1, 2, piece.shape[2], PAIR), lambda j, place: (place[0], 0, 0, j))
+                for piece in coarse
+            ],
             out_specs=[flat(lambda j, place: (0, j))] * 2
             + [both(rows)] * 5
-            + [both(2 * coarse_rows)] * shifts,
+            + [both(2 * piece.shape[2]) for piece in coarse],
         ),
         out_shape=[jax.ShapeDtypeStruct((rows, columns), bf16)] * 2
         + [
@@ -275,7 +291,7 @@
             jax.ShapeDtypeStruct((2, rows, columns), bf16),
             jax.ShapeDtypeStruct((2, rows, columns), bf16),
         ]
-        + [jax.ShapeDtypeStruct((2, 2 * coarse_rows, columns), bf16)] * shifts,
+        + [jax.ShapeDtypeStruct((2, 2 * piece.shape[2], columns), bf16) for piece in coarse],
         compiler_params=pltpu.CompilerParams(vmem_limit_bytes=GRANT),
         cost_estimate=pl.CostEstimate(
             flops=4 * products, bytes_accessed=40 * rows * columns, transcendentals=0
@@ -286,31 +302,44 @@
     )
 
 
-def restrict_kernel(restrict, k, v, out):
-    half = out.shape[3]
+def restrict_kernel(place, restrict, k, v, spread, *outs):
+    half = outs[0].shape[3]
+    short = restrict.shape[0] // 2
+    pair, shifts = (place[3], len(outs))
+
+    def chosen(rows, shift):
+        if both_levels(shift, shifts + 1):
+            return rows
+        apart = jnp.where(pair + shift <= shifts, shift, shifts + 1 - shift)
+        return jnp.where(apart == 1, rows[:short], rows[short:])
+
     for n, ref in enumerate((k, v)):
         for side in range(2):
-            columns = ref[:, side * half : (side + 1) * half]
-            out[side, n] = dot(restrict[...], columns).astype(out.dtype)
-
-
-def restricted(restrict, keys, values):
+            rows = dot(restrict[...], ref[:, side * half : (side + 1) * half])
+            for shift, out in enumerate(outs, start=1):
+                out[side, n] = chosen(rows, shift).astype(out.dtype)
+    whole = restrict[...].astype(jnp.float32)
+    spread[...] = jnp.concatenate([chosen(whole, s) for s in range(1, shifts + 1)], axis=0)
+
+
+def restricted(place, restrict, keys, values, pair_count):
     vmem = pl.BlockSpec(memory_space=pltpu.VMEM)
+    rows = restrict.shape[0]
+    sizes = [rows if both_levels(s, pair_count) else rows // 2 for s in range(1, pair_count)]
     return pl.pallas_call(
         restrict_kernel,
-        in_specs=[vmem] * 3,
-        out_specs=vmem,
-        out_shape=jax.ShapeDtypeStruct(
-            (2, 2, restrict.shape[0], keys.shape[1] // 2), keys.dtype
-        ),
+        in_specs=[pl.BlockSpec(memory_space=pltpu.SMEM)] + [vmem] * 3,
+        out_specs=[vmem] * pair_count,
+        out_shape=[jax.ShapeDtypeStruct((sum(sizes), restrict.shape[1]), jnp.float32)]
+        + [jax.ShapeDtypeStruct((2, 2, size, keys.shape[1] // 2), keys.dtype) for size in sizes],
         compiler_params=pltpu.CompilerParams(vmem_limit_bytes=GRANT),
         name="restrict",
-    )(restrict, keys, values)
+    )(place, restrict, keys, values)
 
 
 def lengthened(restrict, coarse):
     return jnp.einsum(
-        "fb,nfc->nbc", restrict.astype(jnp.float32), coarse, precision=lax.Precision.HIGHEST
+        "fb,nfc->nbc", restrict, coarse, precision=lax.Precision.HIGHEST
     )
 
 
@@ -322,12 +351,12 @@
     parity = lax.rem(position, 2)
     pair = lax.div(position, 2)
     one_rows, two_rows = (restrict_one.shape[0], restrict_two.shape[0])
-    block_rows = -(-(one_rows + two_rows) // 16) * 16
+    short = max(one_rows, two_rows)
+    block_rows = 2 * short
     restrict = jnp.concatenate(
         [
-            restrict_one,
-            restrict_two,
-            jnp.zeros((block_rows - one_rows - two_rows, rows), restrict_one.dtype),
+            jnp.pad(restrict_one, ((0, short - one_rows), (0, 0))),
+            jnp.pad(restrict_two, ((0, short - two_rows), (0, 0))),
         ],
         axis=0,
     )
@@ -359,20 +388,25 @@
         return lax.optimization_barrier((value, *others))[0]
 
     pair_k, pair_v = (send(a, swap) for a in columns(1 - parity, keys, values))
-    own_coarse = after(restricted(restrict, keys, values), pair_k)
-    coarse = [send(own_coarse, shift_pairs(size, s)) for s in shifts]
+    spread, *own_coarse = restricted(place, restrict, keys, values, pair_count)
+    own_coarse = after(own_coarse, pair_k)
+    coarse = [send(a, shift_pairs(size, s)) for s, a in zip(shifts, own_coarse)]
     relayed_k = send(pair_k, relayed_to)
     home_kv = jnp.stack(columns(parity, keys, values))
-    direct = send(after(home_kv, pair_k), direct_to)
+    direct = send(after(home_kv, coarse[0]), direct_to)
     sent_qc = jnp.stack(columns(1 - parity, queries, cotangent))
     pair_qc = send(after(sent_qc, pair_v), swap)
     relayed_v = send(after(pair_v, relayed_k), relayed_to)
     sent_coarse = jnp.concatenate(
-        [lax.dynamic_slice_in_dim(a, 1 - parity, 1) for a in after(coarse, pair_v)], axis=0
+        [
+            lax.dynamic_slice_in_dim(a, 1 - parity, 1).reshape(a.shape[1:])
+            for a in after(coarse, pair_v)
+        ],
+        axis=1,
     )
     pair_coarse = send(sent_coarse, swap)
+    direct = after(direct, pair_qc)
     relayed_v = after(relayed_v, direct)
-    pair_qc = after(pair_qc, relayed_v)
 
     (
         out, grad_q, pair_out, home_grad, pair_grad, direct_grad, relayed_grad, *coarse_grads,
@@ -392,13 +426,18 @@
     relayed_back = send(relayed_grad, direct_to)
     out_back = send(pair_out, swap)
     coarse_back = [send(a, shift_pairs(size, -s)) for s, a in zip(shifts, coarse_grads)]
-    direct_back = send(direct_grad, relayed_to)
     pair_total = pair_grad + relayed_back.astype(jnp.float32)
-    far = sum(piece.astype(jnp.float32) for piece in after(coarse_back, pair_total))
-    pair_total = pair_total + lengthened(restrict, far[:, block_rows:])
-    grad_back = send(pair_total.astype(jnp.bfloat16), swap)
+    far = [
+        piece.astype(jnp.float32).reshape(2, 2, -1, half)
+        for piece in after(coarse_back, pair_total)
+    ]
+    far = [jnp.concatenate([piece[:, side] for piece in far], axis=1) for side in range(2)]
+    pair_total = pair_total + lengthened(spread, far[1])
+    pair_total = pair_total.astype(jnp.bfloat16)
+    grad_back = send(pair_total, swap)
+    direct_back = send(after(direct_grad, pair_total), relayed_to)
     home_total = home_grad + direct_back.astype(jnp.float32)
-    home_total = home_total + lengthened(restrict, far[:, :block_rows])
+    home_total = home_total + lengthened(spread, far[0])
     home_total = home_total.astype(jnp.bfloat16)
     return (
         whole(out, out_back[0]),

time: 81.3 us -> 80.9 us (level); the launches traced: 81 us -> 79.6 us
  waiting for transfers between devices: 25.8 us -> 22.8 us
  local copies, waits for them, and re-layouts: 2.92 us -> 4.65 us
  starting transfers between devices: 30.2 us -> 28.7 us
    ppermute x17, waiting for transfers between devices: 25.8 us -> 22.8 us  [send(): return lax.ppermute(value, 'seq', pairs)]
    ppermute x17, starting transfers between devices: 30.2 us -> 28.7 us  [send(): return lax.ppermute(value, 'seq', pairs)]
    another operation x2, local copies, waits for them, and re-layouts: 1.16 us -> 2.57 us  [per_device(): home_kv = jnp.stack(columns(parity, keys, values))]
  transfers between devices with their start and end apart: 17 -> 17, of which waited for: 9 -> 9; matrix products, arithmetic and copies ran while one was open for 6% -> 9% of each run, Pallas kernels for 0% -> 1%
where the time goes in v7:
time: 80.9 us; the launch traced here: 79.6 us
  starting transfers between devices  28.7 us (35%)
  waiting for transfers between devices  22.8 us (28%)
  Pallas kernels  15.7 us (19%)
  other arithmetic  4.79 us (6%)
  local copies, waits for them, and re-layouts  4.65 us (6%)
  matrix products  2.07 us (3%)
  between operations  0.91 us (1%)
    ppermute x17, starting transfers between devices, send(): return lax.ppermute(value, 'seq', pairs)  28.7 us
    ppermute x17, waiting for transfers between devices, send(): return lax.ppermute(value, 'seq', pairs)  22.8 us
    pallas_call x1, Pallas kernels, attention(): pl.pallas_call(attention_kernel(shifts, *level_rows), grid_spec=pltpu.Pre...  14.9 us
    another operation x2, local copies, waits for them, and re-layouts, per_device(): home_kv = jnp.stack(columns(parity, keys, values))  2.57 us
    select_n x2, other arithmetic, whole(): jnp.where(parity == 0, jnp.concatenate([own, other], axis=axis), jnp.conc...  2.53 us
    dot_general x2, matrix products, lengthened(): jnp.einsum('fb,nfc->nbc', restrict, coarse, precision=lax.Precision.HIGHEST)  2.07 us
  transfers between devices with their start and end apart: 17, of which 9 were waited for; matrix products, arithmetic and copies ran while one was open for 9% of the time, Pallas kernels for 1%

profile of v7, /device:TPU:0, one launch (start us, length us, event | category | flops | bytes accessed | tf_op | source)
XLA Modules:
  0.0 79.6 jit_solution(7817195397410082141)
XLA Ops:
  0.6 0.0 copy-start.1
  0.7 1.8 %dynamic-slice_bitcast_fusion.3 = (bf16[1,256,512]{2,1,0:T(8,128)(2,1)S(1)}, bf16[256,512]{1,0:T(8,128)(2,1)}) fusion(bf16[256,1024]{1,0:T(8,128)(2,1)} %k.3, s32[]{:T(128)S(6)} %select_n.46, s32[]{:T(128)S(6)} %select_n.45), kind=kLoop, calls=%fused_computation.21 | loop fusion | bytes 1048584 | tf_op jit(solution)/shard_map/stack | solution.py:395
  2.5 0.0 copy-start.2
  2.5 3.0 %collective-permute-start = (bf16[256,512]{1,0:T(8,128)(2,1)}, bf16[256,512]{1,0:T(8,128)(2,1)}, u32[]{:S(2)}, u32[]{:S(2)}) collective-permute-start(bf16[256,512]{1,0:T(8,128)(2,1)} %get-tuple-element.69), channel_id=1, source_target_pairs={{0,4},{4,0},{8,12},{12,8},{16,20},{20,16},{24,28},{28,24},{1,5},{5... | collective-permute-start | bytes 786440 | tf_op jit(solution)/shard_map/ppermute | solution.py:379
  5.5 0.0 copy-done.1
  5.5 0.0 copy-start.5
  5.5 0.7 dynamic-slice_bitcast_fusion.2
  6.2 0.0 copy-start.3
  6.2 0.0 copy-start
  6.2 0.0 collective-permute-start.1
  6.2 0.0 copy-done.2
  6.2 1.0 %copy-done.3 = bf16[256,1024]{1,0:T(8,128)(2,1)S(1)} copy-done((bf16[256,1024]{1,0:T(8,128)(2,1)S(1)}, bf16[256,1024]{1,0:T(8,128)(2,1)}, u32[]{:S(2)}) %copy-start.3) | copy-done | bytes 524312
  7.2 0.0 copy-start.6
  7.2 0.7 dynamic-slice_bitcast_fusion
  8.0 0.0 copy-done.5
  8.0 0.0 copy-done.6
  8.0 0.1 pad_add_fusion.place
  8.1 0.0 copy-done
  8.1 0.0 copy-start.4
  8.1 0.8 restrict.1
  8.9 0.2 copy-done.4
  9.0 0.8 %pad_maximum_fusion.1 = bf16[2,256,512]{2,1,0:T(8,128)(2,1)} fusion(bf16[1,256,512]{2,1,0:T(8,128)(2,1)S(1)} %copy-done.4, bf16[1,256,512]{2,1,0:T(8,128)(2,1)S(1)} %dynamic-slice_bitcast_fusion.1), kind=kLoop, calls=%fused_computation.7 | loop fusion | flops 262144 | bytes 1048576 | tf_op jit(solution)/shard_map/stack | solution.py:397
  9.9 3.0 %collective-permute-done.pair_k = bf16[256,512]{1,0:T(8,128)(2,1)} collective-permute-done((bf16[256,512]{1,0:T(8,128)(2,1)}, bf16[256,512]{1,0:T(8,128)(2,1)}, u32[]{:S(2)}, u32[]{:S(2)}) %collective-permute-start) | collective-permute-done | bytes 262176 | tf_op jit(solution)/shard_map/ppermute | solution.py:379
  12.9 2.1 %collective-permute-start.4 = (bf16[2,2,8,512]{3,2,1,0:T(8,128)(2,1)S(1)}, bf16[2,2,8,512]{3,2,1,0:T(8,128)(2,1)S(1)}, u32[]{:S(2)}, u32[]{:S(2)}) collective-permute-start(bf16[2,2,8,512]{3,2,1,0:T(8,128)(2,1)S(1)} %get-tuple-element.37), channel_id=1, source_target_pairs={{0,8},{4,12},{8,16},{12,20},{16,24},{20,28},{24,0},{28,4},{1,9},{5... | collective-permute-start | bytes 98312 | tf_op jit(solution)/shard_map/ppermute | solution.py:379
  15.0 2.0 %collective-permute-start.8 = (bf16[2,2,8,512]{3,2,1,0:T(8,128)(2,1)S(1)}, bf16[2,2,8,512]{3,2,1,0:T(8,128)(2,1)S(1)}, u32[]{:S(2)}, u32[]{:S(2)}) collective-permute-start(bf16[2,2,8,512]{3,2,1,0:T(8,128)(2,1)S(1)} %get-tuple-element.43), channel_id=1, source_target_pairs={{0,24},{4,28},{8,0},{12,4},{16,8},{20,12},{24,16},{28,20},{1,25},{... | collective-permute-start | bytes 98312 | tf_op jit(solution)/shard_map/ppermute | solution.py:379
  17.0 1.0 %collective-permute-start.7 = (bf16[2,2,16,512]{3,2,1,0:T(8,128)(2,1)S(1)}, bf16[2,2,16,512]{3,2,1,0:T(8,128)(2,1)S(1)}, u32[]{:S(2)}, u32[]{:S(2)}) collective-permute-start(bf16[2,2,16,512]{3,2,1,0:T(8,128)(2,1)S(1)} %get-tuple-element.42), channel_id=1, source_target_pairs={{0,16},{4,20},{8,24},{12,28},{16,0},{20,4},{24,8},{28,12},{1,17},{... | collective-permute-start | bytes 196616 | tf_op jit(solution)/shard_map/ppermute | solution.py:379
  18.1 4.2 %collective-permute-start.2 = (bf16[256,512]{1,0:T(8,128)(2,1)}, bf16[256,512]{1,0:T(8,128)(2,1)}, u32[]{:S(2)}, u32[]{:S(2)}) collective-permute-start(bf16[256,512]{1,0:T(8,128)(2,1)} %collective-permute-done.pair_k), channel_id=1, source_target_pairs={{12,4},{0,8},{20,12},{8,16},{28,20},{16,24},{13,5},{1,9},{21,13},{... | collective-permute-start | bytes 786440 | tf_op jit(solution)/shard_map/ppermute | solution.py:379
  22.2 0.8 %pad_maximum_fusion = bf16[2,256,512]{2,1,0:T(8,128)(2,1)} fusion(bf16[1,256,512]{2,1,0:T(8,128)(2,1)S(1)} %get-tuple-element.70, bf16[1,256,512]{2,1,0:T(8,128)(2,1)S(1)} %get-tuple-element.68), kind=kLoop, calls=%fused_computation.6 | loop fusion | flops 262144 | bytes 1048576 | tf_op jit(solution)/shard_map/stack | solution.py:395
  23.1 0.0 collective-permute-done.1.pair_v
  23.1 0.0 collective-permute-start.6
  23.1 0.0 collective-permute-done.4.rest_0_
  23.1 1.3 %collective-permute-start.5 = (bf16[2,256,512]{2,1,0:T(8,128)(2,1)}, bf16[2,256,512]{2,1,0:T(8,128)(2,1)S(1)}, u32[]{:S(2)}, u32[]{:S(2)}) collective-permute-start(bf16[2,256,512]{2,1,0:T(8,128)(2,1)} %pad_maximum_fusion), channel_id=1, source_target_pairs={{4,12},{8,0},{12,20},{16,8},{20,28},{24,16},{5,13},{9,1},{13,21},{... | collective-permute-start | bytes 1572872 | tf_op jit(solution)/shard_map/ppermute | solution.py:379
  24.4 0.0 collective-permute-done.8.rest_2_
  24.4 0.0 collective-permute-done.7.rest_1_
  24.4 1.3 %collective-permute-done.2.relayed_k = bf16[256,512]{1,0:T(8,128)(2,1)} collective-permute-done((bf16[256,512]{1,0:T(8,128)(2,1)}, bf16[256,512]{1,0:T(8,128)(2,1)}, u32[]{:S(2)}, u32[]{:S(2)}) %collective-permute-start.2) | collective-permute-done | bytes 262176 | tf_op jit(solution)/shard_map/ppermute | solution.py:379
  25.7 4.4 %collective-permute-start.3 = (bf16[256,512]{1,0:T(8,128)(2,1)}, bf16[256,512]{1,0:T(8,128)(2,1)S(1)}, u32[]{:S(2)}, u32[]{:S(2)}) collective-permute-start(bf16[256,512]{1,0:T(8,128)(2,1)} %collective-permute-done.1.pair_v), channel_id=1, source_target_pairs={{12,4},{0,8},{20,12},{8,16},{28,20},{16,24},{13,5},{1,9},{21,13},{... | collective-permute-start | bytes 786440 | tf_op jit(solution)/shard_map/ppermute | solution.py:379
  30.2 0.1 collective-permute-start.9
  30.2 4.3 %collective-permute-done.6.pair_qc = bf16[2,256,512]{2,1,0:T(8,128)(2,1)S(1)} collective-permute-done((bf16[2,256,512]{2,1,0:T(8,128)(2,1)}, bf16[2,256,512]{2,1,0:T(8,128)(2,1)S(1)}, u32[]{:S(2)}, u32[]{:S(2)}) %collective-permute-start.6) | collective-permute-done | bytes 524320 | tf_op jit(solution)/shard_map/ppermute | solution.py:379
  34.5 1.2 %collective-permute-done.5.direct = bf16[2,256,512]{2,1,0:T(8,128)(2,1)S(1)} collective-permute-done((bf16[2,256,512]{2,1,0:T(8,128)(2,1)}, bf16[2,256,512]{2,1,0:T(8,128)(2,1)S(1)}, u32[]{:S(2)}, u32[]{:S(2)}) %collective-permute-start.5) | collective-permute-done | bytes 524320 | tf_op jit(solution)/shard_map/ppermute | solution.py:379
  35.7 0.0 collective-permute-done.3.relayed_v
  35.7 0.0 collective-permute-done.9.pair_coarse
  35.7 14.9 %attention.1 = (bf16[256,512]{1,0:T(8,128)(2,1)S(1)}, bf16[256,512]{1,0:T(8,128)(2,1)S(1)}, bf16[2,256,512]{2,1,0:T(8,128)(2,1)S(1)}, f32[2,256,512]{2,1,0:T(8,1...) custom-call(s32[4]{0:T(128)S(1)} %pad_add_fusion.place, ...), custom_call_target="tpu_custom_call" | custom-call | flops 10468982784 | bytes 5242880 | tf_op jit(solution)/shard_map/attention/pallas_call | solution.py:269
  50.6 1.3 %collective-permute-start.11 = (bf16[2,256,512]{2,1,0:T(8,128)(2,1)S(1)}, bf16[2,256,512]{2,1,0:T(8,128)(2,1)S(1)}, u32[]{:S(2)}, u32[]{:S(2)}) collective-permute-start(bf16[2,256,512]{2,1,0:T(8,128)(2,1)S(1)} %get-tuple-element.53), channel_id=1, source_target_pairs={{4,12},{8,0},{12,20},{16,8},{20,28},{24,16},{5,13},{9,1},{13,21},{... | collective-permute-start | bytes 1572872 | tf_op jit(solution)/shard_map/ppermute | solution.py:379
  51.9 4.1 %collective-permute-start.12 = (bf16[2,16,512]{2,1,0:T(8,128)(2,1)S(1)}, bf16[2,16,512]{2,1,0:T(8,128)(2,1)S(1)}, u32[]{:S(2)}, u32[]{:S(2)}) collective-permute-start(bf16[2,16,512]{2,1,0:T(8,128)(2,1)S(1)} %get-tuple-element.54), channel_id=1, source_target_pairs={{0,24},{4,28},{8,0},{12,4},{16,8},{20,12},{24,16},{28,20},{1,25},{... | collective-permute-start | bytes 98312 | tf_op jit(solution)/shard_map/ppermute | solution.py:379
  56.1 0.0 collective-permute-start.14
  56.1 1.0 %collective-permute-start.13 = (bf16[2,32,512]{2,1,0:T(8,128)(2,1)S(1)}, bf16[2,32,512]{2,1,0:T(8,128)(2,1)S(1)}, u32[]{:S(2)}, u32[]{:S(2)}) collective-permute-start(bf16[2,32,512]{2,1,0:T(8,128)(2,1)S(1)} %get-tuple-element.55), channel_id=1, source_target_pairs={{0,16},{4,20},{8,24},{12,28},{16,0},{20,4},{24,8},{28,12},{1,17},{... | collective-permute-start | bytes 196616 | tf_op jit(solution)/shard_map/ppermute | solution.py:379
  57.1 1.7 %collective-permute-start.10 = (bf16[2,256,512]{2,1,0:T(8,128)(2,1)S(1)}, bf16[2,256,512]{2,1,0:T(8,128)(2,1)S(1)}, u32[]{:S(2)}, u32[]{:S(2)}) collective-permute-start(bf16[2,256,512]{2,1,0:T(8,128)(2,1)S(1)} %get-tuple-element.48), channel_id=1, source_target_pairs={{0,4},{4,0},{8,12},{12,8},{16,20},{20,16},{24,28},{28,24},{1,5},{5... | collective-permute-start | bytes 1572872 | tf_op jit(solution)/shard_map/ppermute | solution.py:379
  58.8 4.8 %collective-permute-done.11 = bf16[2,256,512]{2,1,0:T(8,128)(2,1)S(1)} collective-permute-done((bf16[2,256,512]{2,1,0:T(8,128)(2,1)S(1)}, bf16[2,256,512]{2,1,0:T(8,128)(2,1)S(1)}, u32[]{:S(2)}, u32[]{:S(2)}) %collective-permute-start.11) | collective-permute-done | bytes 524320 | tf_op jit(solution)/shard_map/ppermute | solution.py:379
  63.6 0.2 convert_add_fusion
  63.8 0.2 collective-permute-done.12
  63.9 2.8 %collective-permute-done.14 = bf16[2,16,512]{2,1,0:T(8,128)(2,1)S(1)} collective-permute-done((bf16[2,16,512]{2,1,0:T(8,128)(2,1)S(1)}, bf16[2,16,512]{2,1,0:T(8,128)(2,1)S(1)}, u32[]{:S(2)}, u32[]{:S(2)}) %collective-permute-start.14) | collective-permute-done | bytes 32800 | tf_op jit(solution)/shard_map/ppermute | solution.py:379
  66.7 0.8 %collective-permute-done.13 = bf16[2,32,512]{2,1,0:T(8,128)(2,1)S(1)} collective-permute-done((bf16[2,32,512]{2,1,0:T(8,128)(2,1)S(1)}, bf16[2,32,512]{2,1,0:T(8,128)(2,1)S(1)}, u32[]{:S(2)}, u32[]{:S(2)}) %collective-permute-start.13) | collective-permute-done | bytes 65568 | tf_op jit(solution)/shard_map/ppermute | solution.py:379
  67.7 1.0 %fusion.1 = bf16[2,256,512]{2,1,0:T(8,128)(2,1)S(1)} fusion(f32[2,256,512]{2,1,0:T(8,128)S(1)} %convert_add_fusion, f32[2,8,512]{2,1,0:T(8,128)S(1)} %get-tuple-element.77, f32[2,16,512]{2,1,0:T(8,128)S(1)} %get-tuple-element.73, f32[2,8,512]{2,1,0:T(8,128)S(1)} %get-tuple-element.75, f32[32,256]{1,0:T(8,128)S(1)} %get-tuple-element.60), kind=kOutput, calls=%fused_computation.3 | convolution fusion | flops 101253120 | bytes 1736704 | tf_op jit(solution)/shard_map/fb,nfc->nbc/dot_general | solution.py:341
  68.7 0.1 collective-permute-start.16
  68.8 2.4 %collective-permute-start.15 = (bf16[2,256,512]{2,1,0:T(8,128)(2,1)S(1)}, bf16[2,256,512]{2,1,0:T(8,128)(2,1)S(1)}, u32[]{:S(2)}, u32[]{:S(2)}) collective-permute-start(bf16[2,256,512]{2,1,0:T(8,128)(2,1)S(1)} %get-tuple-element.61), channel_id=1, source_target_pairs={{12,4},{0,8},{20,12},{8,16},{28,20},{16,24},{13,5},{1,9},{21,13},{... | collective-permute-start | bytes 1572872 | tf_op jit(solution)/shard_map/ppermute | solution.py:379
  71.2 0.0 collective-permute-done.10
  71.2 1.3 %maximum_select_fusion = (bf16[256,1024]{1,0:T(8,128)(2,1)}, bf16[256,1024]{1,0:T(8,128)(2,1)}) fusion(bf16[256,512]{1,0:T(8,128)(2,1)S(1)} %get-tuple-element.67, bf16[256,512]{1,0:T(8,128)(2,1)S(1)} %get-tuple-element.47, pred[]{:T(512)S(6)} %eq.2, bf16[256,512]{1,0:T(8,128)(2,1)S(1)} %get-tuple-element.49, bf16[256,512]{1,0:T(8,128)(2,1)S(1)} %get-tuple-element.66), kind=kLoop, calls=%fused_computation.8 | loop fusion | flops 4718592 | bytes 2097153 | tf_op jit(solution)/shard_map/jit(_where)/select_n | solution.py:420
  72.5 1.0 %convolution_bitcast_fusion = f32[2,256,512]{2,1,0:T(8,128)S(1)} fusion(f32[2,8,512]{2,1,0:T(8,128)S(1)} %get-tuple-element.76, f32[2,16,512]{2,1,0:T(8,128)S(1)} %get-tuple-element.72, f32[2,8,512]{2,1,0:T(8,128)S(1)} %get-tuple-element.74, f32[32,256]{1,0:T(8,128)S(1)} %get-tuple-element.60), kind=kOutput, calls=%fused_computation | convolution fusion | flops 100728832 | bytes 1212416 | tf_op jit(solution)/shard_map/fb,nfc->nbc/dot_general | solution.py:341
  73.5 4.4 %collective-permute-done.15 = bf16[2,256,512]{2,1,0:T(8,128)(2,1)S(1)} collective-permute-done((bf16[2,256,512]{2,1,0:T(8,128)(2,1)S(1)}, bf16[2,256,512]{2,1,0:T(8,128)(2,1)S(1)}, u32[]{:S(2)}, u32[]{:S(2)}) %collective-permute-start.15) | collective-permute-done | bytes 524320 | tf_op jit(solution)/shard_map/ppermute | solution.py:379
  77.9 0.3 add_convert_fusion
  78.3 0.0 collective-permute-done.16
  78.3 1.3 %maximum_select_fusion.2 = (bf16[256,1024]{1,0:T(8,128)(2,1)}, bf16[256,1024]{1,0:T(8,128)(2,1)}) fusion(bf16[256,512]{1,0:T(8,128)(2,1)S(1)} %get-tuple-element.65, bf16[256,512]{1,0:T(8,128)(2,1)S(1)} %get-tuple-element.63, pred[]{:T(512)S(6)} %eq.2, bf16[256,512]{1,0:T(8,128)(2,1)S(1)} %get-tuple-element.62, bf16[256,512]{1,0:T(8,128)(2,1)S(1)} %get-tuple-element.64), kind=kLoop, calls=%fused_computation.10 | loop fusion | flops 4718592 | bytes 2097153 | tf_op jit(solution)/shard_map/jit(_where)/select_n | solution.py:420
  (15 shorter events, 0.2 us)
Async XLA Ops:
  0.6 4.8 %copy-start.1 = (bf16[256,1024]{1,0:T(8,128)(2,1)S(1)}, bf16[256,1024]{1,0:T(8,128)(2,1)}, u32[]{:S(2)}) copy-start(bf16[256,1024]{1,0:T(8,128)(2,1)} %v.3) | copy-start | bytes 1572868
  2.5 3.7 %copy-start.2 = (bf16[256,1024]{1,0:T(8,128)(2,1)S(1)}, bf16[256,1024]{1,0:T(8,128)(2,1)}, u32[]{:S(2)}) copy-start(bf16[256,1024]{1,0:T(8,128)(2,1)} %q.1) | copy-start | bytes 1572868
  2.5 10.4 %collective-permute-start = (bf16[256,512]{1,0:T(8,128)(2,1)}, bf16[256,512]{1,0:T(8,128)(2,1)}, u32[]{:S(2)}, u32[]{:S(2)}) collective-permute-start(bf16[256,512]{1,0:T(8,128)(2,1)} %get-tuple-element.69), channel_id=1, source_target_pairs={{0,4},{4,0},{8,12},{12,8},{16,20},{20,16},{24,28},{28,24},{1,5},{5... | collective-permute-start | bytes 786440 | tf_op jit(solution)/shard_map/ppermute | solution.py:379
  5.5 2.5 %copy-start.5 = (bf16[8,256]{1,0:T(8,128)(2,1)S(1)}, bf16[8,256]{1,0:T(8,128)(2,1)}, u32[]{:S(2)}) copy-start(bf16[8,256]{1,0:T(8,128)(2,1)} %param.10) | copy-start | bytes 12292
  6.2 1.0 %copy-start.3 = (bf16[256,1024]{1,0:T(8,128)(2,1)S(1)}, bf16[256,1024]{1,0:T(8,128)(2,1)}, u32[]{:S(2)}) copy-start(bf16[256,1024]{1,0:T(8,128)(2,1)} %c.1) | copy-start | bytes 1572868
  6.2 1.9 %copy-start = (bf16[256,1024]{1,0:T(8,128)(2,1)S(1)}, bf16[256,1024]{1,0:T(8,128)(2,1)}, u32[]{:S(2)}) copy-start(bf16[256,1024]{1,0:T(8,128)(2,1)} %k.3) | copy-start | bytes 1572868
  6.2 16.9 %collective-permute-start.1 = (bf16[256,512]{1,0:T(8,128)(2,1)}, bf16[256,512]{1,0:T(8,128)(2,1)}, u32[]{:S(2)}, u32[]{:S(2)}) collective-permute-start(bf16[256,512]{1,0:T(8,128)(2,1)} %get-tuple-element.71), channel_id=1, source_target_pairs={{0,4},{4,0},{8,12},{12,8},{16,20},{20,16},{24,28},{28,24},{1,5},{5... | collective-permute-start | bytes 786440 | tf_op jit(solution)/shard_map/ppermute | solution.py:379
  7.2 0.7 copy-start.6
  8.1 1.0 %copy-start.4 = (bf16[1,256,512]{2,1,0:T(8,128)(2,1)S(1)}, bf16[1,256,512]{2,1,0:T(8,128)(2,1)}, u32[]{:S(2)}) copy-start(bf16[1,256,512]{2,1,0:T(8,128)(2,1)} %dynamic-slice_bitcast_fusion) | copy-start | bytes 786436
  12.9 10.2 %collective-permute-start.4 = (bf16[2,2,8,512]{3,2,1,0:T(8,128)(2,1)S(1)}, bf16[2,2,8,512]{3,2,1,0:T(8,128)(2,1)S(1)}, u32[]{:S(2)}, u32[]{:S(2)}) collective-permute-start(bf16[2,2,8,512]{3,2,1,0:T(8,128)(2,1)S(1)} %get-tuple-element.37), channel_id=1, source_target_pairs={{0,8},{4,12},{8,16},{12,20},{16,24},{20,28},{24,0},{28,4},{1,9},{5... | collective-permute-start | bytes 98312 | tf_op jit(solution)/shard_map/ppermute | solution.py:379
  15.0 9.4 %collective-permute-start.8 = (bf16[2,2,8,512]{3,2,1,0:T(8,128)(2,1)S(1)}, bf16[2,2,8,512]{3,2,1,0:T(8,128)(2,1)S(1)}, u32[]{:S(2)}, u32[]{:S(2)}) collective-permute-start(bf16[2,2,8,512]{3,2,1,0:T(8,128)(2,1)S(1)} %get-tuple-element.43), channel_id=1, source_target_pairs={{0,24},{4,28},{8,0},{12,4},{16,8},{20,12},{24,16},{28,20},{1,25},{... | collective-permute-start | bytes 98312 | tf_op jit(solution)/shard_map/ppermute | solution.py:379
  17.0 7.4 %collective-permute-start.7 = (bf16[2,2,16,512]{3,2,1,0:T(8,128)(2,1)S(1)}, bf16[2,2,16,512]{3,2,1,0:T(8,128)(2,1)S(1)}, u32[]{:S(2)}, u32[]{:S(2)}) collective-permute-start(bf16[2,2,16,512]{3,2,1,0:T(8,128)(2,1)S(1)} %get-tuple-element.42), channel_id=1, source_target_pairs={{0,16},{4,20},{8,24},{12,28},{16,0},{20,4},{24,8},{28,12},{1,17},{... | collective-permute-start | bytes 196616 | tf_op jit(solution)/shard_map/ppermute | solution.py:379
  18.1 7.7 %collective-permute-start.2 = (bf16[256,512]{1,0:T(8,128)(2,1)}, bf16[256,512]{1,0:T(8,128)(2,1)}, u32[]{:S(2)}, u32[]{:S(2)}) collective-permute-start(bf16[256,512]{1,0:T(8,128)(2,1)} %collective-permute-done.pair_k), channel_id=1, source_target_pairs={{12,4},{0,8},{20,12},{8,16},{28,20},{16,24},{13,5},{1,9},{21,13},{... | collective-permute-start | bytes 786440 | tf_op jit(solution)/shard_map/ppermute | solution.py:379
  23.1 11.4 %collective-permute-start.6 = (bf16[2,256,512]{2,1,0:T(8,128)(2,1)}, bf16[2,256,512]{2,1,0:T(8,128)(2,1)S(1)}, u32[]{:S(2)}, u32[]{:S(2)}) collective-permute-start(bf16[2,256,512]{2,1,0:T(8,128)(2,1)} %pad_maximum_fusion.1), channel_id=1, source_target_pairs={{0,4},{4,0},{8,12},{12,8},{16,20},{20,16},{24,28},{28,24},{1,5},{5... | collective-permute-start | bytes 1572872 | tf_op jit(solution)/shard_map/ppermute | solution.py:379
  23.1 12.6 %collective-permute-start.5 = (bf16[2,256,512]{2,1,0:T(8,128)(2,1)}, bf16[2,256,512]{2,1,0:T(8,128)(2,1)S(1)}, u32[]{:S(2)}, u32[]{:S(2)}) collective-permute-start(bf16[2,256,512]{2,1,0:T(8,128)(2,1)} %pad_maximum_fusion), channel_id=1, source_target_pairs={{4,12},{8,0},{12,20},{16,8},{20,28},{24,16},{5,13},{9,1},{13,21},{... | collective-permute-start | bytes 1572872 | tf_op jit(solution)/shard_map/ppermute | solution.py:379
  25.7 10.0 %collective-permute-start.3 = (bf16[256,512]{1,0:T(8,128)(2,1)}, bf16[256,512]{1,0:T(8,128)(2,1)S(1)}, u32[]{:S(2)}, u32[]{:S(2)}) collective-permute-start(bf16[256,512]{1,0:T(8,128)(2,1)} %collective-permute-done.1.pair_v), channel_id=1, source_target_pairs={{12,4},{0,8},{20,12},{8,16},{28,20},{16,24},{13,5},{1,9},{21,13},{... | collective-permute-start | bytes 786440 | tf_op jit(solution)/shard_map/ppermute | solution.py:379
  30.2 5.6 %collective-permute-start.9 = (bf16[2,32,512]{2,1,0:T(8,128)(2,1)S(1)}, bf16[2,32,512]{2,1,0:T(8,128)(2,1)S(1)}, u32[]{:S(2)}, u32[]{:S(2)}) collective-permute-start(bf16[2,32,512]{2,1,0:T(8,128)(2,1)S(1)} %pad_maximum_fusion.2), channel_id=1, source_target_pairs={{0,4},{4,0},{8,12},{12,8},{16,20},{20,16},{24,28},{28,24},{1,5},{5... | collective-permute-start | bytes 196616 | tf_op jit(solution)/shard_map/ppermute | solution.py:379
  50.6 13.0 %collective-permute-start.11 = (bf16[2,256,512]{2,1,0:T(8,128)(2,1)S(1)}, bf16[2,256,512]{2,1,0:T(8,128)(2,1)S(1)}, u32[]{:S(2)}, u32[]{:S(2)}) collective-permute-start(bf16[2,256,512]{2,1,0:T(8,128)(2,1)S(1)} %get-tuple-element.53), channel_id=1, source_target_pairs={{4,12},{8,0},{12,20},{16,8},{20,28},{24,16},{5,13},{9,1},{13,21},{... | collective-permute-start | bytes 1572872 | tf_op jit(solution)/shard_map/ppermute | solution.py:379
  51.9 12.0 %collective-permute-start.12 = (bf16[2,16,512]{2,1,0:T(8,128)(2,1)S(1)}, bf16[2,16,512]{2,1,0:T(8,128)(2,1)S(1)}, u32[]{:S(2)}, u32[]{:S(2)}) collective-permute-start(bf16[2,16,512]{2,1,0:T(8,128)(2,1)S(1)} %get-tuple-element.54), channel_id=1, source_target_pairs={{0,24},{4,28},{8,0},{12,4},{16,8},{20,12},{24,16},{28,20},{1,25},{... | collective-permute-start | bytes 98312 | tf_op jit(solution)/shard_map/ppermute | solution.py:379
  56.1 10.7 %collective-permute-start.14 = (bf16[2,16,512]{2,1,0:T(8,128)(2,1)S(1)}, bf16[2,16,512]{2,1,0:T(8,128)(2,1)S(1)}, u32[]{:S(2)}, u32[]{:S(2)}) collective-permute-start(bf16[2,16,512]{2,1,0:T(8,128)(2,1)S(1)} %get-tuple-element.56), channel_id=1, source_target_pairs={{0,8},{4,12},{8,16},{12,20},{16,24},{20,28},{24,0},{28,4},{1,9},{5... | collective-permute-start | bytes 98312 | tf_op jit(solution)/shard_map/ppermute | solution.py:379
  56.1 11.5 %collective-permute-start.13 = (bf16[2,32,512]{2,1,0:T(8,128)(2,1)S(1)}, bf16[2,32,512]{2,1,0:T(8,128)(2,1)S(1)}, u32[]{:S(2)}, u32[]{:S(2)}) collective-permute-start(bf16[2,32,512]{2,1,0:T(8,128)(2,1)S(1)} %get-tuple-element.55), channel_id=1, source_target_pairs={{0,16},{4,20},{8,24},{12,28},{16,0},{20,4},{24,8},{28,12},{1,17},{... | collective-permute-start | bytes 196616 | tf_op jit(solution)/shard_map/ppermute | solution.py:379
  57.1 14.1 %collective-permute-start.10 = (bf16[2,256,512]{2,1,0:T(8,128)(2,1)S(1)}, bf16[2,256,512]{2,1,0:T(8,128)(2,1)S(1)}, u32[]{:S(2)}, u32[]{:S(2)}) collective-permute-start(bf16[2,256,512]{2,1,0:T(8,128)(2,1)S(1)} %get-tuple-element.48), channel_id=1, source_target_pairs={{0,4},{4,0},{8,12},{12,8},{16,20},{20,16},{24,28},{28,24},{1,5},{5... | collective-permute-start | bytes 1572872 | tf_op jit(solution)/shard_map/ppermute | solution.py:379
  68.7 9.5 %collective-permute-start.16 = (bf16[2,256,512]{2,1,0:T(8,128)(2,1)S(1)}, bf16[2,256,512]{2,1,0:T(8,128)(2,1)S(1)}, u32[]{:S(2)}, u32[]{:S(2)}) collective-permute-start(bf16[2,256,512]{2,1,0:T(8,128)(2,1)S(1)} %fusion.1), channel_id=1, source_target_pairs={{0,4},{4,0},{8,12},{12,8},{16,20},{20,16},{24,28},{28,24},{1,5},{5... | collective-permute-start | bytes 1572872 | tf_op jit(solution)/shard_map/ppermute | solution.py:379
  68.8 9.1 %collective-permute-start.15 = (bf16[2,256,512]{2,1,0:T(8,128)(2,1)S(1)}, bf16[2,256,512]{2,1,0:T(8,128)(2,1)S(1)}, u32[]{:S(2)}, u32[]{:S(2)}) collective-permute-start(bf16[2,256,512]{2,1,0:T(8,128)(2,1)S(1)} %get-tuple-element.61), channel_id=1, source_target_pairs={{12,4},{0,8},{20,12},{8,16},{28,20},{16,24},{13,5},{1,9},{21,13},{... | collective-permute-start | bytes 1572872 | tf_op jit(solution)/shard_map/ppermute | solution.py:379

commit v8 on v7

--- a/solution.py
+++ b/solution.py
@@ -425,25 +425,27 @@
 
     relayed_back = send(relayed_grad, direct_to)
     out_back = send(pair_out, swap)
+    pair_total = (pair_grad + relayed_back.astype(jnp.float32)).astype(jnp.bfloat16)
+    grad_back = send(pair_total, swap)
+    coarse_grads[-1] = after(coarse_grads[-1], pair_total)
     coarse_back = [send(a, shift_pairs(size, -s)) for s, a in zip(shifts, coarse_grads)]
-    pair_total = pair_grad + relayed_back.astype(jnp.float32)
+    direct_back = send(direct_grad, relayed_to)
     far = [
         piece.astype(jnp.float32).reshape(2, 2, -1, half)
         for piece in after(coarse_back, pair_total)
     ]
     far = [jnp.concatenate([piece[:, side] for piece in far], axis=1) for side in range(2)]
-    pair_total = pair_total + lengthened(spread, far[1])
-    pair_total = pair_total.astype(jnp.bfloat16)
-    grad_back = send(pair_total, swap)
-    direct_back = send(after(direct_grad, pair_total), relayed_to)
+    sent_far = far[1].astype(jnp.bfloat16)
+    other_far = send(sent_far, swap).astype(jnp.float32)
+    other_longer = lax.optimization_barrier(lengthened(spread, other_far))
     home_total = home_grad + direct_back.astype(jnp.float32)
-    home_total = home_total + lengthened(spread, far[0])
-    home_total = home_total.astype(jnp.bfloat16)
+    home_total = (home_total + lengthened(spread, far[0])).astype(jnp.bfloat16)
+    pair_back = (grad_back.astype(jnp.float32) + other_longer).astype(jnp.bfloat16)
     return (
         whole(out, out_back[0]),
         whole(grad_q, out_back[1]),
-        whole(home_total[0], grad_back[0]),
-        whole(home_total[1], grad_back[1]),
+        whole(home_total[0], pair_back[0]),
+        whole(home_total[1], pair_back[1]),
     )
 
 

time: 80.9 us -> 80 us (0.989); the launches traced: 79.6 us -> 79.7 us
  starting transfers between devices: 28.7 us -> 31.4 us
  waiting for transfers between devices: 22.8 us -> 20.9 us
  matrix products: 2.07 us -> 1.24 us
    ppermute x17 -> x18, starting transfers between devices: 28.7 us -> 31.4 us  [send(): return lax.ppermute(value, 'seq', pairs)]
    ppermute x17 -> x18, waiting for transfers between devices: 22.8 us -> 20.9 us  [send(): return lax.ppermute(value, 'seq', pairs)]
    dot_general x2, matrix products: 2.07 us -> 1.24 us  [lengthened(): jnp.einsum('fb,nfc->nbc', restrict, coarse, precision=lax.Precision.HIGHEST)]
  transfers between devices with their start and end apart: 17 -> 18, of which waited for: 9 -> 8; matrix products, arithmetic and copies ran while one was open for 9% -> 8% of each run, Pallas kernels for 1% -> 1%
where the time goes in v8:
time: 80 us; the launch traced here: 79.7 us
  starting transfers between devices  31.4 us (39%)
  waiting for transfers between devices  20.9 us (26%)
  Pallas kernels  15.7 us (20%)
  other arithmetic  4.97 us (6%)
  local copies, waits for them, and re-layouts  4.64 us (6%)
  matrix products  1.24 us (2%)
  between operations  0.88 us (1%)
    ppermute x18, starting transfers between devices, send(): return lax.ppermute(value, 'seq', pairs)  31.4 us
    ppermute x18, waiting for transfers between devices, send(): return lax.ppermute(value, 'seq', pairs)  20.9 us
    pallas_call x1, Pallas kernels, attention(): pl.pallas_call(attention_kernel(shifts, *level_rows), grid_spec=pltpu.Pre...  14.9 us
    another operation x2, local copies, waits for them, and re-layouts, per_device(): home_kv = jnp.stack(columns(parity, keys, values))  2.57 us
    select_n x2, other arithmetic, whole(): jnp.where(parity == 0, jnp.concatenate([own, other], axis=axis), jnp.conc...  2.53 us
  transfers between devices with their start and end apart: 18, of which 8 were waited for; matrix products, arithmetic and copies ran while one was open for 8% of the time, Pallas kernels for 1%

profile of v8, /device:TPU:0, one launch (start us, length us, event | category | flops | bytes accessed | tf_op | source)
XLA Modules:
  0.0 79.7 jit_solution(9341361017820924610)
XLA Ops:
  0.6 0.0 copy-start.1
  0.7 1.8 %dynamic-slice_bitcast_fusion.3 = (bf16[1,256,512]{2,1,0:T(8,128)(2,1)S(1)}, bf16[256,512]{1,0:T(8,128)(2,1)}) fusion(bf16[256,1024]{1,0:T(8,128)(2,1)} %k.3, s32[]{:T(128)S(6)} %select_n.46, s32[]{:T(128)S(6)} %select_n.45), kind=kLoop, calls=%fused_computation.20 | loop fusion | bytes 1048584 | tf_op jit(solution)/shard_map/stack | solution.py:395
  2.5 0.0 copy-start.2
  2.5 3.0 %collective-permute-start = (bf16[256,512]{1,0:T(8,128)(2,1)}, bf16[256,512]{1,0:T(8,128)(2,1)}, u32[]{:S(2)}, u32[]{:S(2)}) collective-permute-start(bf16[256,512]{1,0:T(8,128)(2,1)} %get-tuple-element.69), channel_id=1, source_target_pairs={{0,4},{4,0},{8,12},{12,8},{16,20},{20,16},{24,28},{28,24},{1,5},{5... | collective-permute-start | bytes 786440 | tf_op jit(solution)/shard_map/ppermute | solution.py:379
  5.5 0.0 copy-done.1
  5.5 0.0 copy-start.5
  5.5 0.7 dynamic-slice_bitcast_fusion.2
  6.2 0.0 copy-start.3
  6.2 0.0 copy-start
  6.2 0.0 collective-permute-start.1
  6.2 0.0 copy-done.2
  6.2 1.0 %copy-done.3 = bf16[256,1024]{1,0:T(8,128)(2,1)S(1)} copy-done((bf16[256,1024]{1,0:T(8,128)(2,1)S(1)}, bf16[256,1024]{1,0:T(8,128)(2,1)}, u32[]{:S(2)}) %copy-start.3) | copy-done | bytes 524312
  7.2 0.0 copy-start.6
  7.2 0.7 dynamic-slice_bitcast_fusion
  8.0 0.0 copy-done.5
  8.0 0.0 copy-done.6
  8.0 0.1 pad_add_fusion.place
  8.1 0.0 copy-done
  8.1 0.8 restrict.1
  8.9 0.2 copy-done.4
  9.0 0.8 %pad_maximum_fusion.1 = bf16[2,256,512]{2,1,0:T(8,128)(2,1)} fusion(bf16[1,256,512]{2,1,0:T(8,128)(2,1)S(1)} %copy-done.4, bf16[1,256,512]{2,1,0:T(8,128)(2,1)S(1)} %dynamic-slice_bitcast_fusion.1), kind=kLoop, calls=%fused_computation.6 | loop fusion | flops 262144 | bytes 1048576 | tf_op jit(solution)/shard_map/stack | solution.py:397
  9.9 3.0 %collective-permute-done.pair_k = bf16[256,512]{1,0:T(8,128)(2,1)} collective-permute-done((bf16[256,512]{1,0:T(8,128)(2,1)}, bf16[256,512]{1,0:T(8,128)(2,1)}, u32[]{:S(2)}, u32[]{:S(2)}) %collective-permute-start) | collective-permute-done | bytes 262176 | tf_op jit(solution)/shard_map/ppermute | solution.py:379
  12.9 2.1 %collective-permute-start.4 = (bf16[2,2,8,512]{3,2,1,0:T(8,128)(2,1)S(1)}, bf16[2,2,8,512]{3,2,1,0:T(8,128)(2,1)S(1)}, u32[]{:S(2)}, u32[]{:S(2)}) collective-permute-start(bf16[2,2,8,512]{3,2,1,0:T(8,128)(2,1)S(1)} %get-tuple-element.37), channel_id=1, source_target_pairs={{0,8},{4,12},{8,16},{12,20},{16,24},{20,28},{24,0},{28,4},{1,9},{5... | collective-permute-start | bytes 98312 | tf_op jit(solution)/shard_map/ppermute | solution.py:379
  15.0 2.0 %collective-permute-start.8 = (bf16[2,2,8,512]{3,2,1,0:T(8,128)(2,1)S(1)}, bf16[2,2,8,512]{3,2,1,0:T(8,128)(2,1)S(1)}, u32[]{:S(2)}, u32[]{:S(2)}) collective-permute-start(bf16[2,2,8,512]{3,2,1,0:T(8,128)(2,1)S(1)} %get-tuple-element.43), channel_id=1, source_target_pairs={{0,24},{4,28},{8,0},{12,4},{16,8},{20,12},{24,16},{28,20},{1,25},{... | collective-permute-start | bytes 98312 | tf_op jit(solution)/shard_map/ppermute | solution.py:379
  17.0 1.0 %collective-permute-start.7 = (bf16[2,2,16,512]{3,2,1,0:T(8,128)(2,1)S(1)}, bf16[2,2,16,512]{3,2,1,0:T(8,128)(2,1)S(1)}, u32[]{:S(2)}, u32[]{:S(2)}) collective-permute-start(bf16[2,2,16,512]{3,2,1,0:T(8,128)(2,1)S(1)} %get-tuple-element.42), channel_id=1, source_target_pairs={{0,16},{4,20},{8,24},{12,28},{16,0},{20,4},{24,8},{28,12},{1,17},{... | collective-permute-start | bytes 196616 | tf_op jit(solution)/shard_map/ppermute | solution.py:379
  18.1 4.2 %collective-permute-start.2 = (bf16[256,512]{1,0:T(8,128)(2,1)}, bf16[256,512]{1,0:T(8,128)(2,1)}, u32[]{:S(2)}, u32[]{:S(2)}) collective-permute-start(bf16[256,512]{1,0:T(8,128)(2,1)} %collective-permute-done.pair_k), channel_id=1, source_target_pairs={{12,4},{0,8},{20,12},{8,16},{28,20},{16,24},{13,5},{1,9},{21,13},{... | collective-permute-start | bytes 786440 | tf_op jit(solution)/shard_map/ppermute | solution.py:379
  22.2 0.8 %pad_maximum_fusion = bf16[2,256,512]{2,1,0:T(8,128)(2,1)} fusion(bf16[1,256,512]{2,1,0:T(8,128)(2,1)S(1)} %get-tuple-element.70, bf16[1,256,512]{2,1,0:T(8,128)(2,1)S(1)} %get-tuple-element.68), kind=kLoop, calls=%fused_computation.5 | loop fusion | flops 262144 | bytes 1048576 | tf_op jit(solution)/shard_map/stack | solution.py:395
  23.1 0.0 collective-permute-done.1.pair_v
  23.1 0.0 collective-permute-start.6
  23.1 0.0 collective-permute-done.4.rest_0_
  23.1 1.3 %collective-permute-start.5 = (bf16[2,256,512]{2,1,0:T(8,128)(2,1)}, bf16[2,256,512]{2,1,0:T(8,128)(2,1)S(1)}, u32[]{:S(2)}, u32[]{:S(2)}) collective-permute-start(bf16[2,256,512]{2,1,0:T(8,128)(2,1)} %pad_maximum_fusion), channel_id=1, source_target_pairs={{4,12},{8,0},{12,20},{16,8},{20,28},{24,16},{5,13},{9,1},{13,21},{... | collective-permute-start | bytes 1572872 | tf_op jit(solution)/shard_map/ppermute | solution.py:379
  24.4 0.0 collective-permute-done.8.rest_2_
  24.4 0.0 collective-permute-done.7.rest_1_
  24.4 1.3 %collective-permute-done.2.relayed_k = bf16[256,512]{1,0:T(8,128)(2,1)} collective-permute-done((bf16[256,512]{1,0:T(8,128)(2,1)}, bf16[256,512]{1,0:T(8,128)(2,1)}, u32[]{:S(2)}, u32[]{:S(2)}) %collective-permute-start.2) | collective-permute-done | bytes 262176 | tf_op jit(solution)/shard_map/ppermute | solution.py:379
  25.7 4.4 %collective-permute-start.3 = (bf16[256,512]{1,0:T(8,128)(2,1)}, bf16[256,512]{1,0:T(8,128)(2,1)S(1)}, u32[]{:S(2)}, u32[]{:S(2)}) collective-permute-start(bf16[256,512]{1,0:T(8,128)(2,1)} %collective-permute-done.1.pair_v), channel_id=1, source_target_pairs={{12,4},{0,8},{20,12},{8,16},{28,20},{16,24},{13,5},{1,9},{21,13},{... | collective-permute-start | bytes 786440 | tf_op jit(solution)/shard_map/ppermute | solution.py:379
  30.2 0.1 collective-permute-start.9
  30.2 4.3 %collective-permute-done.6.pair_qc = bf16[2,256,512]{2,1,0:T(8,128)(2,1)S(1)} collective-permute-done((bf16[2,256,512]{2,1,0:T(8,128)(2,1)}, bf16[2,256,512]{2,1,0:T(8,128)(2,1)S(1)}, u32[]{:S(2)}, u32[]{:S(2)}) %collective-permute-start.6) | collective-permute-done | bytes 524320 | tf_op jit(solution)/shard_map/ppermute | solution.py:379
  34.5 1.2 %collective-permute-done.5.direct = bf16[2,256,512]{2,1,0:T(8,128)(2,1)S(1)} collective-permute-done((bf16[2,256,512]{2,1,0:T(8,128)(2,1)}, bf16[2,256,512]{2,1,0:T(8,128)(2,1)S(1)}, u32[]{:S(2)}, u32[]{:S(2)}) %collective-permute-start.5) | collective-permute-done | bytes 524320 | tf_op jit(solution)/shard_map/ppermute | solution.py:379
  35.7 0.0 collective-permute-done.3.relayed_v
  35.7 0.0 collective-permute-done.9.pair_coarse
  35.7 14.9 %attention.1 = (bf16[256,512]{1,0:T(8,128)(2,1)S(1)}, bf16[256,512]{1,0:T(8,128)(2,1)S(1)}, bf16[2,256,512]{2,1,0:T(8,128)(2,1)S(1)}, f32[2,256,512]{2,1,0:T(8,1...) custom-call(s32[4]{0:T(128)S(1)} %pad_add_fusion.place, ...), custom_call_target="tpu_custom_call" | custom-call | flops 10468982784 | bytes 5242880 | tf_op jit(solution)/shard_map/attention/pallas_call | solution.py:269
  50.6 1.3 %collective-permute-start.14 = (bf16[2,256,512]{2,1,0:T(8,128)(2,1)S(1)}, bf16[2,256,512]{2,1,0:T(8,128)(2,1)S(1)}, u32[]{:S(2)}, u32[]{:S(2)}) collective-permute-start(bf16[2,256,512]{2,1,0:T(8,128)(2,1)S(1)} %get-tuple-element.56), channel_id=1, source_target_pairs={{4,12},{8,0},{12,20},{16,8},{20,28},{24,16},{5,13},{9,1},{13,21},{... | collective-permute-start | bytes 1572872 | tf_op jit(solution)/shard_map/ppermute | solution.py:379
  51.9 3.4 %collective-permute-start.10 = (bf16[2,256,512]{2,1,0:T(8,128)(2,1)S(1)}, bf16[2,256,512]{2,1,0:T(8,128)(2,1)S(1)}, u32[]{:S(2)}, u32[]{:S(2)}) collective-permute-start(bf16[2,256,512]{2,1,0:T(8,128)(2,1)S(1)} %get-tuple-element.48), channel_id=1, source_target_pairs={{0,4},{4,0},{8,12},{12,8},{16,20},{20,16},{24,28},{28,24},{1,5},{5... | collective-permute-start | bytes 1572872 | tf_op jit(solution)/shard_map/ppermute | solution.py:379
  55.3 0.8 %collective-permute-start.12 = (bf16[2,16,512]{2,1,0:T(8,128)(2,1)S(1)}, bf16[2,16,512]{2,1,0:T(8,128)(2,1)S(1)}, u32[]{:S(2)}, u32[]{:S(2)}) collective-permute-start(bf16[2,16,512]{2,1,0:T(8,128)(2,1)S(1)} %get-tuple-element.52), channel_id=1, source_target_pairs={{0,24},{4,28},{8,0},{12,4},{16,8},{20,12},{24,16},{28,20},{1,25},{... | collective-permute-start | bytes 98312 | tf_op jit(solution)/shard_map/ppermute | solution.py:379
  56.1 1.5 %collective-permute-start.13 = (bf16[2,32,512]{2,1,0:T(8,128)(2,1)S(1)}, bf16[2,32,512]{2,1,0:T(8,128)(2,1)S(1)}, u32[]{:S(2)}, u32[]{:S(2)}) collective-permute-start(bf16[2,32,512]{2,1,0:T(8,128)(2,1)S(1)} %get-tuple-element.53), channel_id=1, source_target_pairs={{0,16},{4,20},{8,24},{12,28},{16,0},{20,4},{24,8},{28,12},{1,17},{... | collective-permute-start | bytes 196616 | tf_op jit(solution)/shard_map/ppermute | solution.py:379
  57.7 3.1 %collective-permute-start.11 = (bf16[2,256,512]{2,1,0:T(8,128)(2,1)S(1)}, bf16[2,256,512]{2,1,0:T(8,128)(2,1)S(1)}, u32[]{:S(2)}, u32[]{:S(2)}) collective-permute-start(bf16[2,256,512]{2,1,0:T(8,128)(2,1)S(1)} %get-tuple-element.51), channel_id=1, source_target_pairs={{12,4},{0,8},{20,12},{8,16},{28,20},{16,24},{13,5},{1,9},{21,13},{... | collective-permute-start | bytes 1572872 | tf_op jit(solution)/shard_map/ppermute | solution.py:379
  60.7 2.5 %collective-permute-done.14 = bf16[2,256,512]{2,1,0:T(8,128)(2,1)S(1)} collective-permute-done((bf16[2,256,512]{2,1,0:T(8,128)(2,1)S(1)}, bf16[2,256,512]{2,1,0:T(8,128)(2,1)S(1)}, u32[]{:S(2)}, u32[]{:S(2)}) %collective-permute-start.14) | collective-permute-done | bytes 524320 | tf_op jit(solution)/shard_map/ppermute | solution.py:379
  63.2 0.2 add_convert_fusion.2
  63.4 1.4 %collective-permute-start.16 = (bf16[2,256,512]{2,1,0:T(8,128)(2,1)S(1)}, bf16[2,256,512]{2,1,0:T(8,128)(2,1)S(1)}, u32[]{:S(2)}, u32[]{:S(2)}) collective-permute-start(bf16[2,256,512]{2,1,0:T(8,128)(2,1)S(1)} %add_convert_fusion.2), channel_id=1, source_target_pairs={{0,4},{4,0},{8,12},{12,8},{16,20},{20,16},{24,28},{28,24},{1,5},{5... | collective-permute-start | bytes 1572872 | tf_op jit(solution)/shard_map/ppermute | solution.py:379
  64.8 2.7 %collective-permute-done.10 = bf16[2,256,512]{2,1,0:T(8,128)(2,1)S(1)} collective-permute-done((bf16[2,256,512]{2,1,0:T(8,128)(2,1)S(1)}, bf16[2,256,512]{2,1,0:T(8,128)(2,1)S(1)}, u32[]{:S(2)}, u32[]{:S(2)}) %collective-permute-start.10) | collective-permute-done | bytes 524320 | tf_op jit(solution)/shard_map/ppermute | solution.py:379
  67.5 0.0 collective-permute-start.15
  67.5 1.3 %maximum_select_fusion = (bf16[256,1024]{1,0:T(8,128)(2,1)}, bf16[256,1024]{1,0:T(8,128)(2,1)}) fusion(bf16[256,512]{1,0:T(8,128)(2,1)S(1)} %get-tuple-element.67, bf16[256,512]{1,0:T(8,128)(2,1)S(1)} %get-tuple-element.47, pred[]{:T(512)S(6)} %eq.2, bf16[256,512]{1,0:T(8,128)(2,1)S(1)} %get-tuple-element.49, bf16[256,512]{1,0:T(8,128)(2,1)S(1)} %get-tuple-element.66), kind=kLoop, calls=%fused_computation.7 | loop fusion | flops 4718592 | bytes 2097153 | tf_op jit(solution)/shard_map/jit(_where)/select_n | solution.py:420
  68.8 0.0 collective-permute-done.12
  68.8 0.0 collective-permute-done.13
  68.8 4.4 %collective-permute-done.15 = bf16[2,16,512]{2,1,0:T(8,128)(2,1)S(1)} collective-permute-done((bf16[2,16,512]{2,1,0:T(8,128)(2,1)S(1)}, bf16[2,16,512]{2,1,0:T(8,128)(2,1)S(1)}, u32[]{:S(2)}, u32[]{:S(2)}) %collective-permute-start.15) | collective-permute-done | bytes 32800 | tf_op jit(solution)/shard_map/ppermute | solution.py:379
  73.2 1.8 %collective-permute-start.17 = (bf16[2,32,512]{2,1,0:T(8,128)(2,1)S(1)}, bf16[2,32,512]{2,1,0:T(8,128)(2,1)S(1)}, u32[]{:S(2)}, u32[]{:S(2)}) collective-permute-start(bf16[2,32,512]{2,1,0:T(8,128)(2,1)S(1)} %pad_maximum_fusion.3), channel_id=1, source_target_pairs={{0,4},{4,0},{8,12},{12,8},{16,20},{20,16},{24,28},{28,24},{1,5},{5... | collective-permute-start | bytes 196616 | tf_op jit(solution)/shard_map/ppermute | solution.py:379
  75.0 0.6 convolution_bitcast_fusion.1
  75.7 0.0 collective-permute-done.11
  75.7 0.3 add_convert_fusion.1
  76.0 1.5 %collective-permute-done.17 = bf16[2,32,512]{2,1,0:T(8,128)(2,1)S(1)} collective-permute-done((bf16[2,32,512]{2,1,0:T(8,128)(2,1)S(1)}, bf16[2,32,512]{2,1,0:T(8,128)(2,1)S(1)}, u32[]{:S(2)}, u32[]{:S(2)}) %collective-permute-start.17) | collective-permute-done | bytes 65568 | tf_op jit(solution)/shard_map/ppermute | solution.py:379
  77.5 0.6 convolution_bitcast_fusion
  78.2 0.0 collective-permute-done.16
  78.2 0.2 add_convert_fusion
  78.4 1.3 %maximum_select_fusion.2 = (bf16[256,1024]{1,0:T(8,128)(2,1)}, bf16[256,1024]{1,0:T(8,128)(2,1)}) fusion(bf16[256,512]{1,0:T(8,128)(2,1)S(1)} %get-tuple-element.65, bf16[256,512]{1,0:T(8,128)(2,1)S(1)} %get-tuple-element.63, pred[]{:T(512)S(6)} %eq.2, bf16[256,512]{1,0:T(8,128)(2,1)S(1)} %get-tuple-element.62, bf16[256,512]{1,0:T(8,128)(2,1)S(1)} %get-tuple-element.64), kind=kLoop, calls=%fused_computation.9 | loop fusion | flops 4718592 | bytes 2097153 | tf_op jit(solution)/shard_map/jit(_where)/select_n | solution.py:420
  (14 shorter events, 0.2 us)
Async XLA Ops:
  0.6 4.8 %copy-start.1 = (bf16[256,1024]{1,0:T(8,128)(2,1)S(1)}, bf16[256,1024]{1,0:T(8,128)(2,1)}, u32[]{:S(2)}) copy-start(bf16[256,1024]{1,0:T(8,128)(2,1)} %v.3) | copy-start | bytes 1572868
  2.5 3.7 %copy-start.2 = (bf16[256,1024]{1,0:T(8,128)(2,1)S(1)}, bf16[256,1024]{1,0:T(8,128)(2,1)}, u32[]{:S(2)}) copy-start(bf16[256,1024]{1,0:T(8,128)(2,1)} %q.1) | copy-start | bytes 1572868
  2.5 10.4 %collective-permute-start = (bf16[256,512]{1,0:T(8,128)(2,1)}, bf16[256,512]{1,0:T(8,128)(2,1)}, u32[]{:S(2)}, u32[]{:S(2)}) collective-permute-start(bf16[256,512]{1,0:T(8,128)(2,1)} %get-tuple-element.69), channel_id=1, source_target_pairs={{0,4},{4,0},{8,12},{12,8},{16,20},{20,16},{24,28},{28,24},{1,5},{5... | collective-permute-start | bytes 786440 | tf_op jit(solution)/shard_map/ppermute | solution.py:379
  5.5 2.5 %copy-start.5 = (bf16[8,256]{1,0:T(8,128)(2,1)S(1)}, bf16[8,256]{1,0:T(8,128)(2,1)}, u32[]{:S(2)}) copy-start(bf16[8,256]{1,0:T(8,128)(2,1)} %param.10) | copy-start | bytes 12292
  6.2 1.0 %copy-start.3 = (bf16[256,1024]{1,0:T(8,128)(2,1)S(1)}, bf16[256,1024]{1,0:T(8,128)(2,1)}, u32[]{:S(2)}) copy-start(bf16[256,1024]{1,0:T(8,128)(2,1)} %c.1) | copy-start | bytes 1572868
  6.2 1.9 %copy-start = (bf16[256,1024]{1,0:T(8,128)(2,1)S(1)}, bf16[256,1024]{1,0:T(8,128)(2,1)}, u32[]{:S(2)}) copy-start(bf16[256,1024]{1,0:T(8,128)(2,1)} %k.3) | copy-start | bytes 1572868
  6.2 16.9 %collective-permute-start.1 = (bf16[256,512]{1,0:T(8,128)(2,1)}, bf16[256,512]{1,0:T(8,128)(2,1)}, u32[]{:S(2)}, u32[]{:S(2)}) collective-permute-start(bf16[256,512]{1,0:T(8,128)(2,1)} %get-tuple-element.71), channel_id=1, source_target_pairs={{0,4},{4,0},{8,12},{12,8},{16,20},{20,16},{24,28},{28,24},{1,5},{5... | collective-permute-start | bytes 786440 | tf_op jit(solution)/shard_map/ppermute | solution.py:379
  7.2 0.7 copy-start.6
  8.1 1.0 %copy-start.4 = (bf16[1,256,512]{2,1,0:T(8,128)(2,1)S(1)}, bf16[1,256,512]{2,1,0:T(8,128)(2,1)}, u32[]{:S(2)}) copy-start(bf16[1,256,512]{2,1,0:T(8,128)(2,1)} %dynamic-slice_bitcast_fusion) | copy-start | bytes 786436
  12.9 10.2 %collective-permute-start.4 = (bf16[2,2,8,512]{3,2,1,0:T(8,128)(2,1)S(1)}, bf16[2,2,8,512]{3,2,1,0:T(8,128)(2,1)S(1)}, u32[]{:S(2)}, u32[]{:S(2)}) collective-permute-start(bf16[2,2,8,512]{3,2,1,0:T(8,128)(2,1)S(1)} %get-tuple-element.37), channel_id=1, source_target_pairs={{0,8},{4,12},{8,16},{12,20},{16,24},{20,28},{24,0},{28,4},{1,9},{5... | collective-permute-start | bytes 98312 | tf_op jit(solution)/shard_map/ppermute | solution.py:379
  15.0 9.4 %collective-permute-start.8 = (bf16[2,2,8,512]{3,2,1,0:T(8,128)(2,1)S(1)}, bf16[2,2,8,512]{3,2,1,0:T(8,128)(2,1)S(1)}, u32[]{:S(2)}, u32[]{:S(2)}) collective-permute-start(bf16[2,2,8,512]{3,2,1,0:T(8,128)(2,1)S(1)} %get-tuple-element.43), channel_id=1, source_target_pairs={{0,24},{4,28},{8,0},{12,4},{16,8},{20,12},{24,16},{28,20},{1,25},{... | collective-permute-start | bytes 98312 | tf_op jit(solution)/shard_map/ppermute | solution.py:379
  17.0 7.4 %collective-permute-start.7 = (bf16[2,2,16,512]{3,2,1,0:T(8,128)(2,1)S(1)}, bf16[2,2,16,512]{3,2,1,0:T(8,128)(2,1)S(1)}, u32[]{:S(2)}, u32[]{:S(2)}) collective-permute-start(bf16[2,2,16,512]{3,2,1,0:T(8,128)(2,1)S(1)} %get-tuple-element.42), channel_id=1, source_target_pairs={{0,16},{4,20},{8,24},{12,28},{16,0},{20,4},{24,8},{28,12},{1,17},{... | collective-permute-start | bytes 196616 | tf_op jit(solution)/shard_map/ppermute | solution.py:379
  18.1 7.7 %collective-permute-start.2 = (bf16[256,512]{1,0:T(8,128)(2,1)}, bf16[256,512]{1,0:T(8,128)(2,1)}, u32[]{:S(2)}, u32[]{:S(2)}) collective-permute-start(bf16[256,512]{1,0:T(8,128)(2,1)} %collective-permute-done.pair_k), channel_id=1, source_target_pairs={{12,4},{0,8},{20,12},{8,16},{28,20},{16,24},{13,5},{1,9},{21,13},{... | collective-permute-start | bytes 786440 | tf_op jit(solution)/shard_map/ppermute | solution.py:379
  23.1 11.4 %collective-permute-start.6 = (bf16[2,256,512]{2,1,0:T(8,128)(2,1)}, bf16[2,256,512]{2,1,0:T(8,128)(2,1)S(1)}, u32[]{:S(2)}, u32[]{:S(2)}) collective-permute-start(bf16[2,256,512]{2,1,0:T(8,128)(2,1)} %pad_maximum_fusion.1), channel_id=1, source_target_pairs={{0,4},{4,0},{8,12},{12,8},{16,20},{20,16},{24,28},{28,24},{1,5},{5... | collective-permute-start | bytes 1572872 | tf_op jit(solution)/shard_map/ppermute | solution.py:379
  23.1 12.6 %collective-permute-start.5 = (bf16[2,256,512]{2,1,0:T(8,128)(2,1)}, bf16[2,256,512]{2,1,0:T(8,128)(2,1)S(1)}, u32[]{:S(2)}, u32[]{:S(2)}) collective-permute-start(bf16[2,256,512]{2,1,0:T(8,128)(2,1)} %pad_maximum_fusion), channel_id=1, source_target_pairs={{4,12},{8,0},{12,20},{16,8},{20,28},{24,16},{5,13},{9,1},{13,21},{... | collective-permute-start | bytes 1572872 | tf_op jit(solution)/shard_map/ppermute | solution.py:379
  25.7 10.0 %collective-permute-start.3 = (bf16[256,512]{1,0:T(8,128)(2,1)}, bf16[256,512]{1,0:T(8,128)(2,1)S(1)}, u32[]{:S(2)}, u32[]{:S(2)}) collective-permute-start(bf16[256,512]{1,0:T(8,128)(2,1)} %collective-permute-done.1.pair_v), channel_id=1, source_target_pairs={{12,4},{0,8},{20,12},{8,16},{28,20},{16,24},{13,5},{1,9},{21,13},{... | collective-permute-start | bytes 786440 | tf_op jit(solution)/shard_map/ppermute | solution.py:379
  30.2 5.6 %collective-permute-start.9 = (bf16[2,32,512]{2,1,0:T(8,128)(2,1)S(1)}, bf16[2,32,512]{2,1,0:T(8,128)(2,1)S(1)}, u32[]{:S(2)}, u32[]{:S(2)}) collective-permute-start(bf16[2,32,512]{2,1,0:T(8,128)(2,1)S(1)} %pad_maximum_fusion.2), channel_id=1, source_target_pairs={{0,4},{4,0},{8,12},{12,8},{16,20},{20,16},{24,28},{28,24},{1,5},{5... | collective-permute-start | bytes 196616 | tf_op jit(solution)/shard_map/ppermute | solution.py:379
  50.6 12.6 %collective-permute-start.14 = (bf16[2,256,512]{2,1,0:T(8,128)(2,1)S(1)}, bf16[2,256,512]{2,1,0:T(8,128)(2,1)S(1)}, u32[]{:S(2)}, u32[]{:S(2)}) collective-permute-start(bf16[2,256,512]{2,1,0:T(8,128)(2,1)S(1)} %get-tuple-element.56), channel_id=1, source_target_pairs={{4,12},{8,0},{12,20},{16,8},{20,28},{24,16},{5,13},{9,1},{13,21},{... | collective-permute-start | bytes 1572872 | tf_op jit(solution)/shard_map/ppermute | solution.py:379
  51.9 15.5 %collective-permute-start.10 = (bf16[2,256,512]{2,1,0:T(8,128)(2,1)S(1)}, bf16[2,256,512]{2,1,0:T(8,128)(2,1)S(1)}, u32[]{:S(2)}, u32[]{:S(2)}) collective-permute-start(bf16[2,256,512]{2,1,0:T(8,128)(2,1)S(1)} %get-tuple-element.48), channel_id=1, source_target_pairs={{0,4},{4,0},{8,12},{12,8},{16,20},{20,16},{24,28},{28,24},{1,5},{5... | collective-permute-start | bytes 1572872 | tf_op jit(solution)/shard_map/ppermute | solution.py:379
  55.3 13.5 %collective-permute-start.12 = (bf16[2,16,512]{2,1,0:T(8,128)(2,1)S(1)}, bf16[2,16,512]{2,1,0:T(8,128)(2,1)S(1)}, u32[]{:S(2)}, u32[]{:S(2)}) collective-permute-start(bf16[2,16,512]{2,1,0:T(8,128)(2,1)S(1)} %get-tuple-element.52), channel_id=1, source_target_pairs={{0,24},{4,28},{8,0},{12,4},{16,8},{20,12},{24,16},{28,20},{1,25},{... | collective-permute-start | bytes 98312 | tf_op jit(solution)/shard_map/ppermute | solution.py:379
  56.1 12.6 %collective-permute-start.13 = (bf16[2,32,512]{2,1,0:T(8,128)(2,1)S(1)}, bf16[2,32,512]{2,1,0:T(8,128)(2,1)S(1)}, u32[]{:S(2)}, u32[]{:S(2)}) collective-permute-start(bf16[2,32,512]{2,1,0:T(8,128)(2,1)S(1)} %get-tuple-element.53), channel_id=1, source_target_pairs={{0,16},{4,20},{8,24},{12,28},{16,0},{20,4},{24,8},{28,12},{1,17},{... | collective-permute-start | bytes 196616 | tf_op jit(solution)/shard_map/ppermute | solution.py:379
  57.7 18.0 %collective-permute-start.11 = (bf16[2,256,512]{2,1,0:T(8,128)(2,1)S(1)}, bf16[2,256,512]{2,1,0:T(8,128)(2,1)S(1)}, u32[]{:S(2)}, u32[]{:S(2)}) collective-permute-start(bf16[2,256,512]{2,1,0:T(8,128)(2,1)S(1)} %get-tuple-element.51), channel_id=1, source_target_pairs={{12,4},{0,8},{20,12},{8,16},{28,20},{16,24},{13,5},{1,9},{21,13},{... | collective-permute-start | bytes 1572872 | tf_op jit(solution)/shard_map/ppermute | solution.py:379
  63.4 14.8 %collective-permute-start.16 = (bf16[2,256,512]{2,1,0:T(8,128)(2,1)S(1)}, bf16[2,256,512]{2,1,0:T(8,128)(2,1)S(1)}, u32[]{:S(2)}, u32[]{:S(2)}) collective-permute-start(bf16[2,256,512]{2,1,0:T(8,128)(2,1)S(1)} %add_convert_fusion.2), channel_id=1, source_target_pairs={{0,4},{4,0},{8,12},{12,8},{16,20},{20,16},{24,28},{28,24},{1,5},{5... | collective-permute-start | bytes 1572872 | tf_op jit(solution)/shard_map/ppermute | solution.py:379
  67.5 5.7 %collective-permute-start.15 = (bf16[2,16,512]{2,1,0:T(8,128)(2,1)S(1)}, bf16[2,16,512]{2,1,0:T(8,128)(2,1)S(1)}, u32[]{:S(2)}, u32[]{:S(2)}) collective-permute-start(bf16[2,16,512]{2,1,0:T(8,128)(2,1)S(1)} %get-tuple-element.57), channel_id=1, source_target_pairs={{0,8},{4,12},{8,16},{12,20},{16,24},{20,28},{24,0},{28,4},{1,9},{5... | collective-permute-start | bytes 98312 | tf_op jit(solution)/shard_map/ppermute | solution.py:379
  73.2 4.3 %collective-permute-start.17 = (bf16[2,32,512]{2,1,0:T(8,128)(2,1)S(1)}, bf16[2,32,512]{2,1,0:T(8,128)(2,1)S(1)}, u32[]{:S(2)}, u32[]{:S(2)}) collective-permute-start(bf16[2,32,512]{2,1,0:T(8,128)(2,1)S(1)} %pad_maximum_fusion.3), channel_id=1, source_target_pairs={{0,4},{4,0},{8,12},{12,8},{16,20},{20,16},{24,28},{28,24},{1,5},{5... | collective-permute-start | bytes 196616 | tf_op jit(solution)/shard_map/ppermute | solution.py:379

commit v9 on v8

--- a/solution.py
+++ b/solution.py
@@ -425,11 +425,10 @@
 
     relayed_back = send(relayed_grad, direct_to)
     out_back = send(pair_out, swap)
+    coarse_back = [send(a, shift_pairs(size, -s)) for s, a in zip(shifts, coarse_grads)]
     pair_total = (pair_grad + relayed_back.astype(jnp.float32)).astype(jnp.bfloat16)
     grad_back = send(pair_total, swap)
-    coarse_grads[-1] = after(coarse_grads[-1], pair_total)
-    coarse_back = [send(a, shift_pairs(size, -s)) for s, a in zip(shifts, coarse_grads)]
-    direct_back = send(direct_grad, relayed_to)
+    direct_back = send(after(direct_grad, pair_total), relayed_to)
     far = [
         piece.astype(jnp.float32).reshape(2, 2, -1, half)
         for piece in after(coarse_back, pair_total)

time: 80 us -> 82.4 us (1.030)
  waiting for transfers between devices: 20.9 us -> 24.1 us
  starting transfers between devices: 31.4 us -> 30 us
    ppermute x18, waiting for transfers between devices: 20.9 us -> 24.1 us  [send(): return lax.ppermute(value, 'seq', pairs)]
    ppermute x18, starting transfers between devices: 31.4 us -> 30 us  [send(): return lax.ppermute(value, 'seq', pairs)]
  transfers between devices with their start and end apart: 18 -> 18, of which waited for: 8 -> 9; matrix products, arithmetic and copies ran while one was open for 8% -> 8% of each run, Pallas kernels for 1% -> 1%
where the time goes in v9:
time: 82.4 us; the launch traced here: 81.6 us
  starting transfers between devices  30 us (36%)
  waiting for transfers between devices  24.1 us (29%)
  Pallas kernels  15.7 us (19%)
  other arithmetic  4.98 us (6%)
  local copies, waits for them, and re-layouts  4.64 us (6%)
  matrix products  1.24 us (2%)
  between operations  0.89 us (1%)
    ppermute x18, starting transfers between devices, send(): return lax.ppermute(value, 'seq', pairs)  30 us
    ppermute x18, waiting for transfers between devices, send(): return lax.ppermute(value, 'seq', pairs)  24.1 us
    pallas_call x1, Pallas kernels, attention(): pl.pallas_call(attention_kernel(shifts, *level_rows), grid_spec=pltpu.Pre...  14.9 us
    another operation x2, local copies, waits for them, and re-layouts, per_device(): home_kv = jnp.stack(columns(parity, keys, values))  2.57 us
    select_n x2, other arithmetic, whole(): jnp.where(parity == 0, jnp.concatenate([own, other], axis=axis), jnp.conc...  2.53 us
  transfers between devices with their start and end apart: 18, of which 9 were waited for; matrix products, arithmetic and copies ran while one was open for 8% of the time, Pallas kernels for 1%

profile of v9, /device:TPU:0, one launch (start us, length us, event | category | flops | bytes accessed | tf_op | source)
XLA Modules:
  0.0 81.6 jit_solution(952040889800931302)
XLA Ops:
  0.6 0.0 copy-start.1
  0.7 1.8 %dynamic-slice_bitcast_fusion.3 = (bf16[1,256,512]{2,1,0:T(8,128)(2,1)S(1)}, bf16[256,512]{1,0:T(8,128)(2,1)}) fusion(bf16[256,1024]{1,0:T(8,128)(2,1)} %k.3, s32[]{:T(128)S(6)} %select_n.46, s32[]{:T(128)S(6)} %select_n.45), kind=kLoop, calls=%fused_computation.20 | loop fusion | bytes 1048584 | tf_op jit(solution)/shard_map/stack | solution.py:395
  2.5 0.0 copy-start.2
  2.5 3.0 %collective-permute-start = (bf16[256,512]{1,0:T(8,128)(2,1)}, bf16[256,512]{1,0:T(8,128)(2,1)}, u32[]{:S(2)}, u32[]{:S(2)}) collective-permute-start(bf16[256,512]{1,0:T(8,128)(2,1)} %get-tuple-element.69), channel_id=1, source_target_pairs={{0,4},{4,0},{8,12},{12,8},{16,20},{20,16},{24,28},{28,24},{1,5},{5... | collective-permute-start | bytes 786440 | tf_op jit(solution)/shard_map/ppermute | solution.py:379
  5.5 0.0 copy-done.1
  5.5 0.0 copy-start.5
  5.5 0.7 dynamic-slice_bitcast_fusion.2
  6.2 0.0 copy-start.3
  6.2 0.0 copy-start
  6.2 0.0 collective-permute-start.1
  6.2 0.0 copy-done.2
  6.2 1.0 %copy-done.3 = bf16[256,1024]{1,0:T(8,128)(2,1)S(1)} copy-done((bf16[256,1024]{1,0:T(8,128)(2,1)S(1)}, bf16[256,1024]{1,0:T(8,128)(2,1)}, u32[]{:S(2)}) %copy-start.3) | copy-done | bytes 524312
  7.2 0.0 copy-start.6
  7.2 0.7 dynamic-slice_bitcast_fusion
  8.0 0.0 copy-done.5
  8.0 0.0 copy-done.6
  8.0 0.1 pad_add_fusion.place
  8.1 0.0 copy-done
  8.1 0.8 restrict.1
  8.9 0.2 copy-done.4
  9.0 0.8 %pad_maximum_fusion.1 = bf16[2,256,512]{2,1,0:T(8,128)(2,1)} fusion(bf16[1,256,512]{2,1,0:T(8,128)(2,1)S(1)} %copy-done.4, bf16[1,256,512]{2,1,0:T(8,128)(2,1)S(1)} %dynamic-slice_bitcast_fusion.1), kind=kLoop, calls=%fused_computation.6 | loop fusion | flops 262144 | bytes 1048576 | tf_op jit(solution)/shard_map/stack | solution.py:397
  9.9 3.0 %collective-permute-done.pair_k = bf16[256,512]{1,0:T(8,128)(2,1)} collective-permute-done((bf16[256,512]{1,0:T(8,128)(2,1)}, bf16[256,512]{1,0:T(8,128)(2,1)}, u32[]{:S(2)}, u32[]{:S(2)}) %collective-permute-start) | collective-permute-done | bytes 262176 | tf_op jit(solution)/shard_map/ppermute | solution.py:379
  12.9 2.1 %collective-permute-start.4 = (bf16[2,2,8,512]{3,2,1,0:T(8,128)(2,1)S(1)}, bf16[2,2,8,512]{3,2,1,0:T(8,128)(2,1)S(1)}, u32[]{:S(2)}, u32[]{:S(2)}) collective-permute-start(bf16[2,2,8,512]{3,2,1,0:T(8,128)(2,1)S(1)} %get-tuple-element.37), channel_id=1, source_target_pairs={{0,8},{4,12},{8,16},{12,20},{16,24},{20,28},{24,0},{28,4},{1,9},{5... | collective-permute-start | bytes 98312 | tf_op jit(solution)/shard_map/ppermute | solution.py:379
  15.0 2.0 %collective-permute-start.8 = (bf16[2,2,8,512]{3,2,1,0:T(8,128)(2,1)S(1)}, bf16[2,2,8,512]{3,2,1,0:T(8,128)(2,1)S(1)}, u32[]{:S(2)}, u32[]{:S(2)}) collective-permute-start(bf16[2,2,8,512]{3,2,1,0:T(8,128)(2,1)S(1)} %get-tuple-element.43), channel_id=1, source_target_pairs={{0,24},{4,28},{8,0},{12,4},{16,8},{20,12},{24,16},{28,20},{1,25},{... | collective-permute-start | bytes 98312 | tf_op jit(solution)/shard_map/ppermute | solution.py:379
  17.0 1.0 %collective-permute-start.7 = (bf16[2,2,16,512]{3,2,1,0:T(8,128)(2,1)S(1)}, bf16[2,2,16,512]{3,2,1,0:T(8,128)(2,1)S(1)}, u32[]{:S(2)}, u32[]{:S(2)}) collective-permute-start(bf16[2,2,16,512]{3,2,1,0:T(8,128)(2,1)S(1)} %get-tuple-element.42), channel_id=1, source_target_pairs={{0,16},{4,20},{8,24},{12,28},{16,0},{20,4},{24,8},{28,12},{1,17},{... | collective-permute-start | bytes 196616 | tf_op jit(solution)/shard_map/ppermute | solution.py:379
  18.1 4.2 %collective-permute-start.2 = (bf16[256,512]{1,0:T(8,128)(2,1)}, bf16[256,512]{1,0:T(8,128)(2,1)}, u32[]{:S(2)}, u32[]{:S(2)}) collective-permute-start(bf16[256,512]{1,0:T(8,128)(2,1)} %collective-permute-done.pair_k), channel_id=1, source_target_pairs={{12,4},{0,8},{20,12},{8,16},{28,20},{16,24},{13,5},{1,9},{21,13},{... | collective-permute-start | bytes 786440 | tf_op jit(solution)/shard_map/ppermute | solution.py:379
  22.2 0.8 %pad_maximum_fusion = bf16[2,256,512]{2,1,0:T(8,128)(2,1)} fusion(bf16[1,256,512]{2,1,0:T(8,128)(2,1)S(1)} %get-tuple-element.70, bf16[1,256,512]{2,1,0:T(8,128)(2,1)S(1)} %get-tuple-element.68), kind=kLoop, calls=%fused_computation.5 | loop fusion | flops 262144 | bytes 1048576 | tf_op jit(solution)/shard_map/stack | solution.py:395
  23.1 0.0 collective-permute-done.1.pair_v
  23.1 0.0 collective-permute-start.6
  23.1 0.0 collective-permute-done.4.rest_0_
  23.1 1.3 %collective-permute-start.5 = (bf16[2,256,512]{2,1,0:T(8,128)(2,1)}, bf16[2,256,512]{2,1,0:T(8,128)(2,1)S(1)}, u32[]{:S(2)}, u32[]{:S(2)}) collective-permute-start(bf16[2,256,512]{2,1,0:T(8,128)(2,1)} %pad_maximum_fusion), channel_id=1, source_target_pairs={{4,12},{8,0},{12,20},{16,8},{20,28},{24,16},{5,13},{9,1},{13,21},{... | collective-permute-start | bytes 1572872 | tf_op jit(solution)/shard_map/ppermute | solution.py:379
  24.4 0.0 collective-permute-done.8.rest_2_
  24.4 0.0 collective-permute-done.7.rest_1_
  24.4 1.3 %collective-permute-done.2.relayed_k = bf16[256,512]{1,0:T(8,128)(2,1)} collective-permute-done((bf16[256,512]{1,0:T(8,128)(2,1)}, bf16[256,512]{1,0:T(8,128)(2,1)}, u32[]{:S(2)}, u32[]{:S(2)}) %collective-permute-start.2) | collective-permute-done | bytes 262176 | tf_op jit(solution)/shard_map/ppermute | solution.py:379
  25.7 4.4 %collective-permute-start.3 = (bf16[256,512]{1,0:T(8,128)(2,1)}, bf16[256,512]{1,0:T(8,128)(2,1)S(1)}, u32[]{:S(2)}, u32[]{:S(2)}) collective-permute-start(bf16[256,512]{1,0:T(8,128)(2,1)} %collective-permute-done.1.pair_v), channel_id=1, source_target_pairs={{12,4},{0,8},{20,12},{8,16},{28,20},{16,24},{13,5},{1,9},{21,13},{... | collective-permute-start | bytes 786440 | tf_op jit(solution)/shard_map/ppermute | solution.py:379
  30.2 0.1 collective-permute-start.9
  30.2 4.3 %collective-permute-done.6.pair_qc = bf16[2,256,512]{2,1,0:T(8,128)(2,1)S(1)} collective-permute-done((bf16[2,256,512]{2,1,0:T(8,128)(2,1)}, bf16[2,256,512]{2,1,0:T(8,128)(2,1)S(1)}, u32[]{:S(2)}, u32[]{:S(2)}) %collective-permute-start.6) | collective-permute-done | bytes 524320 | tf_op jit(solution)/shard_map/ppermute | solution.py:379
  34.5 1.2 %collective-permute-done.5.direct = bf16[2,256,512]{2,1,0:T(8,128)(2,1)S(1)} collective-permute-done((bf16[2,256,512]{2,1,0:T(8,128)(2,1)}, bf16[2,256,512]{2,1,0:T(8,128)(2,1)S(1)}, u32[]{:S(2)}, u32[]{:S(2)}) %collective-permute-start.5) | collective-permute-done | bytes 524320 | tf_op jit(solution)/shard_map/ppermute | solution.py:379
  35.7 0.0 collective-permute-done.3.relayed_v
  35.7 0.0 collective-permute-done.9.pair_coarse
  35.7 14.9 %attention.1 = (bf16[256,512]{1,0:T(8,128)(2,1)S(1)}, bf16[256,512]{1,0:T(8,128)(2,1)S(1)}, bf16[2,256,512]{2,1,0:T(8,128)(2,1)S(1)}, f32[2,256,512]{2,1,0:T(8,1...) custom-call(s32[4]{0:T(128)S(1)} %pad_add_fusion.place, ...), custom_call_target="tpu_custom_call" | custom-call | flops 10468982784 | bytes 5242880 | tf_op jit(solution)/shard_map/attention/pallas_call | solution.py:269
  50.6 1.3 %collective-permute-start.11 = (bf16[2,256,512]{2,1,0:T(8,128)(2,1)S(1)}, bf16[2,256,512]{2,1,0:T(8,128)(2,1)S(1)}, u32[]{:S(2)}, u32[]{:S(2)}) collective-permute-start(bf16[2,256,512]{2,1,0:T(8,128)(2,1)S(1)} %get-tuple-element.53), channel_id=1, source_target_pairs={{4,12},{8,0},{12,20},{16,8},{20,28},{24,16},{5,13},{9,1},{13,21},{... | collective-permute-start | bytes 1572872 | tf_op jit(solution)/shard_map/ppermute | solution.py:379
  51.9 4.2 %collective-permute-start.13 = (bf16[2,16,512]{2,1,0:T(8,128)(2,1)S(1)}, bf16[2,16,512]{2,1,0:T(8,128)(2,1)S(1)}, u32[]{:S(2)}, u32[]{:S(2)}) collective-permute-start(bf16[2,16,512]{2,1,0:T(8,128)(2,1)S(1)} %get-tuple-element.55), channel_id=1, source_target_pairs={{0,24},{4,28},{8,0},{12,4},{16,8},{20,12},{24,16},{28,20},{1,25},{... | collective-permute-start | bytes 98312 | tf_op jit(solution)/shard_map/ppermute | solution.py:379
  56.1 0.0 collective-permute-start.15
  56.1 1.0 %collective-permute-start.14 = (bf16[2,32,512]{2,1,0:T(8,128)(2,1)S(1)}, bf16[2,32,512]{2,1,0:T(8,128)(2,1)S(1)}, u32[]{:S(2)}, u32[]{:S(2)}) collective-permute-start(bf16[2,32,512]{2,1,0:T(8,128)(2,1)S(1)} %get-tuple-element.56), channel_id=1, source_target_pairs={{0,16},{4,20},{8,24},{12,28},{16,0},{20,4},{24,8},{28,12},{1,17},{... | collective-permute-start | bytes 196616 | tf_op jit(solution)/shard_map/ppermute | solution.py:379
  57.1 1.7 %collective-permute-start.10 = (bf16[2,256,512]{2,1,0:T(8,128)(2,1)S(1)}, bf16[2,256,512]{2,1,0:T(8,128)(2,1)S(1)}, u32[]{:S(2)}, u32[]{:S(2)}) collective-permute-start(bf16[2,256,512]{2,1,0:T(8,128)(2,1)S(1)} %get-tuple-element.48), channel_id=1, source_target_pairs={{0,4},{4,0},{8,12},{12,8},{16,20},{20,16},{24,28},{28,24},{1,5},{5... | collective-permute-start | bytes 1572872 | tf_op jit(solution)/shard_map/ppermute | solution.py:379
  58.8 4.8 %collective-permute-done.11 = bf16[2,256,512]{2,1,0:T(8,128)(2,1)S(1)} collective-permute-done((bf16[2,256,512]{2,1,0:T(8,128)(2,1)S(1)}, bf16[2,256,512]{2,1,0:T(8,128)(2,1)S(1)}, u32[]{:S(2)}, u32[]{:S(2)}) %collective-permute-start.11) | collective-permute-done | bytes 524320 | tf_op jit(solution)/shard_map/ppermute | solution.py:379
  63.6 0.2 add_convert_fusion.2
  63.8 1.0 %collective-permute-start.16 = (bf16[2,256,512]{2,1,0:T(8,128)(2,1)S(1)}, bf16[2,256,512]{2,1,0:T(8,128)(2,1)S(1)}, u32[]{:S(2)}, u32[]{:S(2)}) collective-permute-start(bf16[2,256,512]{2,1,0:T(8,128)(2,1)S(1)} %add_convert_fusion.2), channel_id=1, source_target_pairs={{0,4},{4,0},{8,12},{12,8},{16,20},{20,16},{24,28},{28,24},{1,5},{5... | collective-permute-start | bytes 1572872 | tf_op jit(solution)/shard_map/ppermute | solution.py:379
  64.8 0.0 collective-permute-done.13
  64.8 1.9 %collective-permute-done.15 = bf16[2,16,512]{2,1,0:T(8,128)(2,1)S(1)} collective-permute-done((bf16[2,16,512]{2,1,0:T(8,128)(2,1)S(1)}, bf16[2,16,512]{2,1,0:T(8,128)(2,1)S(1)}, u32[]{:S(2)}, u32[]{:S(2)}) %collective-permute-start.15) | collective-permute-done | bytes 32800 | tf_op jit(solution)/shard_map/ppermute | solution.py:379
  66.7 0.8 %collective-permute-done.14 = bf16[2,32,512]{2,1,0:T(8,128)(2,1)S(1)} collective-permute-done((bf16[2,32,512]{2,1,0:T(8,128)(2,1)S(1)}, bf16[2,32,512]{2,1,0:T(8,128)(2,1)S(1)}, u32[]{:S(2)}, u32[]{:S(2)}) %collective-permute-start.14) | collective-permute-done | bytes 65568 | tf_op jit(solution)/shard_map/ppermute | solution.py:379
  67.6 0.1 collective-permute-start.17
  67.7 2.7 %collective-permute-start.12 = (bf16[2,256,512]{2,1,0:T(8,128)(2,1)S(1)}, bf16[2,256,512]{2,1,0:T(8,128)(2,1)S(1)}, u32[]{:S(2)}, u32[]{:S(2)}) collective-permute-start(bf16[2,256,512]{2,1,0:T(8,128)(2,1)S(1)} %get-tuple-element.54), channel_id=1, source_target_pairs={{12,4},{0,8},{20,12},{8,16},{28,20},{16,24},{13,5},{1,9},{21,13},{... | collective-permute-start | bytes 1572872 | tf_op jit(solution)/shard_map/ppermute | solution.py:379
  70.4 0.6 convolution_bitcast_fusion.1
  71.0 0.9 %collective-permute-done.10 = bf16[2,256,512]{2,1,0:T(8,128)(2,1)S(1)} collective-permute-done((bf16[2,256,512]{2,1,0:T(8,128)(2,1)S(1)}, bf16[2,256,512]{2,1,0:T(8,128)(2,1)S(1)}, u32[]{:S(2)}, u32[]{:S(2)}) %collective-permute-start.10) | collective-permute-done | bytes 524320 | tf_op jit(solution)/shard_map/ppermute | solution.py:379
  72.0 1.3 %maximum_select_fusion = (bf16[256,1024]{1,0:T(8,128)(2,1)}, bf16[256,1024]{1,0:T(8,128)(2,1)}) fusion(bf16[256,512]{1,0:T(8,128)(2,1)S(1)} %get-tuple-element.67, bf16[256,512]{1,0:T(8,128)(2,1)S(1)} %get-tuple-element.47, pred[]{:T(512)S(6)} %eq.2, bf16[256,512]{1,0:T(8,128)(2,1)S(1)} %get-tuple-element.49, bf16[256,512]{1,0:T(8,128)(2,1)S(1)} %get-tuple-element.66), kind=kLoop, calls=%fused_computation.7 | loop fusion | flops 4718592 | bytes 2097153 | tf_op jit(solution)/shard_map/jit(_where)/select_n | solution.py:420
  73.2 5.9 %collective-permute-done.17 = bf16[2,32,512]{2,1,0:T(8,128)(2,1)S(1)} collective-permute-done((bf16[2,32,512]{2,1,0:T(8,128)(2,1)S(1)}, bf16[2,32,512]{2,1,0:T(8,128)(2,1)S(1)}, u32[]{:S(2)}, u32[]{:S(2)}) %collective-permute-start.17) | collective-permute-done | bytes 65568 | tf_op jit(solution)/shard_map/ppermute | solution.py:379
  79.1 0.6 convolution_bitcast_fusion
  79.7 0.0 collective-permute-done.16
  79.7 0.2 add_convert_fusion
  79.9 0.0 collective-permute-done.12
  80.0 0.3 add_convert_fusion.1
  80.3 1.3 %maximum_select_fusion.2 = (bf16[256,1024]{1,0:T(8,128)(2,1)}, bf16[256,1024]{1,0:T(8,128)(2,1)}) fusion(bf16[256,512]{1,0:T(8,128)(2,1)S(1)} %get-tuple-element.65, bf16[256,512]{1,0:T(8,128)(2,1)S(1)} %get-tuple-element.63, pred[]{:T(512)S(6)} %eq.2, bf16[256,512]{1,0:T(8,128)(2,1)S(1)} %get-tuple-element.62, bf16[256,512]{1,0:T(8,128)(2,1)S(1)} %get-tuple-element.64), kind=kLoop, calls=%fused_computation.9 | loop fusion | flops 4718592 | bytes 2097153 | tf_op jit(solution)/shard_map/jit(_where)/select_n | solution.py:420
  (14 shorter events, 0.2 us)
Async XLA Ops:
  0.6 4.8 %copy-start.1 = (bf16[256,1024]{1,0:T(8,128)(2,1)S(1)}, bf16[256,1024]{1,0:T(8,128)(2,1)}, u32[]{:S(2)}) copy-start(bf16[256,1024]{1,0:T(8,128)(2,1)} %v.3) | copy-start | bytes 1572868
  2.5 3.7 %copy-start.2 = (bf16[256,1024]{1,0:T(8,128)(2,1)S(1)}, bf16[256,1024]{1,0:T(8,128)(2,1)}, u32[]{:S(2)}) copy-start(bf16[256,1024]{1,0:T(8,128)(2,1)} %q.1) | copy-start | bytes 1572868
  2.5 10.4 %collective-permute-start = (bf16[256,512]{1,0:T(8,128)(2,1)}, bf16[256,512]{1,0:T(8,128)(2,1)}, u32[]{:S(2)}, u32[]{:S(2)}) collective-permute-start(bf16[256,512]{1,0:T(8,128)(2,1)} %get-tuple-element.69), channel_id=1, source_target_pairs={{0,4},{4,0},{8,12},{12,8},{16,20},{20,16},{24,28},{28,24},{1,5},{5... | collective-permute-start | bytes 786440 | tf_op jit(solution)/shard_map/ppermute | solution.py:379
  5.5 2.5 %copy-start.5 = (bf16[8,256]{1,0:T(8,128)(2,1)S(1)}, bf16[8,256]{1,0:T(8,128)(2,1)}, u32[]{:S(2)}) copy-start(bf16[8,256]{1,0:T(8,128)(2,1)} %param.10) | copy-start | bytes 12292
  6.2 1.0 %copy-start.3 = (bf16[256,1024]{1,0:T(8,128)(2,1)S(1)}, bf16[256,1024]{1,0:T(8,128)(2,1)}, u32[]{:S(2)}) copy-start(bf16[256,1024]{1,0:T(8,128)(2,1)} %c.1) | copy-start | bytes 1572868
  6.2 1.9 %copy-start = (bf16[256,1024]{1,0:T(8,128)(2,1)S(1)}, bf16[256,1024]{1,0:T(8,128)(2,1)}, u32[]{:S(2)}) copy-start(bf16[256,1024]{1,0:T(8,128)(2,1)} %k.3) | copy-start | bytes 1572868
  6.2 16.9 %collective-permute-start.1 = (bf16[256,512]{1,0:T(8,128)(2,1)}, bf16[256,512]{1,0:T(8,128)(2,1)}, u32[]{:S(2)}, u32[]{:S(2)}) collective-permute-start(bf16[256,512]{1,0:T(8,128)(2,1)} %get-tuple-element.71), channel_id=1, source_target_pairs={{0,4},{4,0},{8,12},{12,8},{16,20},{20,16},{24,28},{28,24},{1,5},{5... | collective-permute-start | bytes 786440 | tf_op jit(solution)/shard_map/ppermute | solution.py:379
  7.2 0.7 copy-start.6
  8.1 1.0 %copy-start.4 = (bf16[1,256,512]{2,1,0:T(8,128)(2,1)S(1)}, bf16[1,256,512]{2,1,0:T(8,128)(2,1)}, u32[]{:S(2)}) copy-start(bf16[1,256,512]{2,1,0:T(8,128)(2,1)} %dynamic-slice_bitcast_fusion) | copy-start | bytes 786436
  12.9 10.2 %collective-permute-start.4 = (bf16[2,2,8,512]{3,2,1,0:T(8,128)(2,1)S(1)}, bf16[2,2,8,512]{3,2,1,0:T(8,128)(2,1)S(1)}, u32[]{:S(2)}, u32[]{:S(2)}) collective-permute-start(bf16[2,2,8,512]{3,2,1,0:T(8,128)(2,1)S(1)} %get-tuple-element.37), channel_id=1, source_target_pairs={{0,8},{4,12},{8,16},{12,20},{16,24},{20,28},{24,0},{28,4},{1,9},{5... | collective-permute-start | bytes 98312 | tf_op jit(solution)/shard_map/ppermute | solution.py:379
  15.0 9.4 %collective-permute-start.8 = (bf16[2,2,8,512]{3,2,1,0:T(8,128)(2,1)S(1)}, bf16[2,2,8,512]{3,2,1,0:T(8,128)(2,1)S(1)}, u32[]{:S(2)}, u32[]{:S(2)}) collective-permute-start(bf16[2,2,8,512]{3,2,1,0:T(8,128)(2,1)S(1)} %get-tuple-element.43), channel_id=1, source_target_pairs={{0,24},{4,28},{8,0},{12,4},{16,8},{20,12},{24,16},{28,20},{1,25},{... | collective-permute-start | bytes 98312 | tf_op jit(solution)/shard_map/ppermute | solution.py:379
  17.0 7.4 %collective-permute-start.7 = (bf16[2,2,16,512]{3,2,1,0:T(8,128)(2,1)S(1)}, bf16[2,2,16,512]{3,2,1,0:T(8,128)(2,1)S(1)}, u32[]{:S(2)}, u32[]{:S(2)}) collective-permute-start(bf16[2,2,16,512]{3,2,1,0:T(8,128)(2,1)S(1)} %get-tuple-element.42), channel_id=1, source_target_pairs={{0,16},{4,20},{8,24},{12,28},{16,0},{20,4},{24,8},{28,12},{1,17},{... | collective-permute-start | bytes 196616 | tf_op jit(solution)/shard_map/ppermute | solution.py:379
  18.1 7.7 %collective-permute-start.2 = (bf16[256,512]{1,0:T(8,128)(2,1)}, bf16[256,512]{1,0:T(8,128)(2,1)}, u32[]{:S(2)}, u32[]{:S(2)}) collective-permute-start(bf16[256,512]{1,0:T(8,128)(2,1)} %collective-permute-done.pair_k), channel_id=1, source_target_pairs={{12,4},{0,8},{20,12},{8,16},{28,20},{16,24},{13,5},{1,9},{21,13},{... | collective-permute-start | bytes 786440 | tf_op jit(solution)/shard_map/ppermute | solution.py:379
  23.1 11.4 %collective-permute-start.6 = (bf16[2,256,512]{2,1,0:T(8,128)(2,1)}, bf16[2,256,512]{2,1,0:T(8,128)(2,1)S(1)}, u32[]{:S(2)}, u32[]{:S(2)}) collective-permute-start(bf16[2,256,512]{2,1,0:T(8,128)(2,1)} %pad_maximum_fusion.1), channel_id=1, source_target_pairs={{0,4},{4,0},{8,12},{12,8},{16,20},{20,16},{24,28},{28,24},{1,5},{5... | collective-permute-start | bytes 1572872 | tf_op jit(solution)/shard_map/ppermute | solution.py:379
  23.1 12.6 %collective-permute-start.5 = (bf16[2,256,512]{2,1,0:T(8,128)(2,1)}, bf16[2,256,512]{2,1,0:T(8,128)(2,1)S(1)}, u32[]{:S(2)}, u32[]{:S(2)}) collective-permute-start(bf16[2,256,512]{2,1,0:T(8,128)(2,1)} %pad_maximum_fusion), channel_id=1, source_target_pairs={{4,12},{8,0},{12,20},{16,8},{20,28},{24,16},{5,13},{9,1},{13,21},{... | collective-permute-start | bytes 1572872 | tf_op jit(solution)/shard_map/ppermute | solution.py:379
  25.7 10.0 %collective-permute-start.3 = (bf16[256,512]{1,0:T(8,128)(2,1)}, bf16[256,512]{1,0:T(8,128)(2,1)S(1)}, u32[]{:S(2)}, u32[]{:S(2)}) collective-permute-start(bf16[256,512]{1,0:T(8,128)(2,1)} %collective-permute-done.1.pair_v), channel_id=1, source_target_pairs={{12,4},{0,8},{20,12},{8,16},{28,20},{16,24},{13,5},{1,9},{21,13},{... | collective-permute-start | bytes 786440 | tf_op jit(solution)/shard_map/ppermute | solution.py:379
  30.2 5.6 %collective-permute-start.9 = (bf16[2,32,512]{2,1,0:T(8,128)(2,1)S(1)}, bf16[2,32,512]{2,1,0:T(8,128)(2,1)S(1)}, u32[]{:S(2)}, u32[]{:S(2)}) collective-permute-start(bf16[2,32,512]{2,1,0:T(8,128)(2,1)S(1)} %pad_maximum_fusion.2), channel_id=1, source_target_pairs={{0,4},{4,0},{8,12},{12,8},{16,20},{20,16},{24,28},{28,24},{1,5},{5... | collective-permute-start | bytes 196616 | tf_op jit(solution)/shard_map/ppermute | solution.py:379
  50.6 13.0 %collective-permute-start.11 = (bf16[2,256,512]{2,1,0:T(8,128)(2,1)S(1)}, bf16[2,256,512]{2,1,0:T(8,128)(2,1)S(1)}, u32[]{:S(2)}, u32[]{:S(2)}) collective-permute-start(bf16[2,256,512]{2,1,0:T(8,128)(2,1)S(1)} %get-tuple-element.53), channel_id=1, source_target_pairs={{4,12},{8,0},{12,20},{16,8},{20,28},{24,16},{5,13},{9,1},{13,21},{... | collective-permute-start | bytes 1572872 | tf_op jit(solution)/shard_map/ppermute | solution.py:379
  51.9 12.9 %collective-permute-start.13 = (bf16[2,16,512]{2,1,0:T(8,128)(2,1)S(1)}, bf16[2,16,512]{2,1,0:T(8,128)(2,1)S(1)}, u32[]{:S(2)}, u32[]{:S(2)}) collective-permute-start(bf16[2,16,512]{2,1,0:T(8,128)(2,1)S(1)} %get-tuple-element.55), channel_id=1, source_target_pairs={{0,24},{4,28},{8,0},{12,4},{16,8},{20,12},{24,16},{28,20},{1,25},{... | collective-permute-start | bytes 98312 | tf_op jit(solution)/shard_map/ppermute | solution.py:379
  56.1 10.7 %collective-permute-start.15 = (bf16[2,16,512]{2,1,0:T(8,128)(2,1)S(1)}, bf16[2,16,512]{2,1,0:T(8,128)(2,1)S(1)}, u32[]{:S(2)}, u32[]{:S(2)}) collective-permute-start(bf16[2,16,512]{2,1,0:T(8,128)(2,1)S(1)} %get-tuple-element.57), channel_id=1, source_target_pairs={{0,8},{4,12},{8,16},{12,20},{16,24},{20,28},{24,0},{28,4},{1,9},{5... | collective-permute-start | bytes 98312 | tf_op jit(solution)/shard_map/ppermute | solution.py:379
  56.1 11.5 %collective-permute-start.14 = (bf16[2,32,512]{2,1,0:T(8,128)(2,1)S(1)}, bf16[2,32,512]{2,1,0:T(8,128)(2,1)S(1)}, u32[]{:S(2)}, u32[]{:S(2)}) collective-permute-start(bf16[2,32,512]{2,1,0:T(8,128)(2,1)S(1)} %get-tuple-element.56), channel_id=1, source_target_pairs={{0,16},{4,20},{8,24},{12,28},{16,0},{20,4},{24,8},{28,12},{1,17},{... | collective-permute-start | bytes 196616 | tf_op jit(solution)/shard_map/ppermute | solution.py:379
  57.1 14.9 %collective-permute-start.10 = (bf16[2,256,512]{2,1,0:T(8,128)(2,1)S(1)}, bf16[2,256,512]{2,1,0:T(8,128)(2,1)S(1)}, u32[]{:S(2)}, u32[]{:S(2)}) collective-permute-start(bf16[2,256,512]{2,1,0:T(8,128)(2,1)S(1)} %get-tuple-element.48), channel_id=1, source_target_pairs={{0,4},{4,0},{8,12},{12,8},{16,20},{20,16},{24,28},{28,24},{1,5},{5... | collective-permute-start | bytes 1572872 | tf_op jit(solution)/shard_map/ppermute | solution.py:379
  63.8 15.9 %collective-permute-start.16 = (bf16[2,256,512]{2,1,0:T(8,128)(2,1)S(1)}, bf16[2,256,512]{2,1,0:T(8,128)(2,1)S(1)}, u32[]{:S(2)}, u32[]{:S(2)}) collective-permute-start(bf16[2,256,512]{2,1,0:T(8,128)(2,1)S(1)} %add_convert_fusion.2), channel_id=1, source_target_pairs={{0,4},{4,0},{8,12},{12,8},{16,20},{20,16},{24,28},{28,24},{1,5},{5... | collective-permute-start | bytes 1572872 | tf_op jit(solution)/shard_map/ppermute | solution.py:379
  67.6 11.5 %collective-permute-start.17 = (bf16[2,32,512]{2,1,0:T(8,128)(2,1)S(1)}, bf16[2,32,512]{2,1,0:T(8,128)(2,1)S(1)}, u32[]{:S(2)}, u32[]{:S(2)}) collective-permute-start(bf16[2,32,512]{2,1,0:T(8,128)(2,1)S(1)} %pad_maximum_fusion.3), channel_id=1, source_target_pairs={{0,4},{4,0},{8,12},{12,8},{16,20},{20,16},{24,28},{28,24},{1,5},{5... | collective-permute-start | bytes 196616 | tf_op jit(solution)/shard_map/ppermute | solution.py:379
  67.7 12.3 %collective-permute-start.12 = (bf16[2,256,512]{2,1,0:T(8,128)(2,1)S(1)}, bf16[2,256,512]{2,1,0:T(8,128)(2,1)S(1)}, u32[]{:S(2)}, u32[]{:S(2)}) collective-permute-start(bf16[2,256,512]{2,1,0:T(8,128)(2,1)S(1)} %get-tuple-element.54), channel_id=1, source_target_pairs={{12,4},{0,8},{20,12},{8,16},{28,20},{16,24},{13,5},{1,9},{21,13},{... | collective-permute-start | bytes 1572872 | tf_op jit(solution)/shard_map/ppermute | solution.py:379

commit v10 on v8

--- a/solution.py
+++ b/solution.py
@@ -9,7 +9,7 @@
 
 HEAD_DIM = 64
 PAIR = 2 * HEAD_DIM
-TILE = 32
+TILE = 16
 GRANT = 16 * 1024 * 1024
 
 level_one_bias = math.log(32.0)

time: 80 us -> 80.1 us (level)
  no operation moved by 1% of the time
where the time goes in v10:
time: 80.1 us; the launch traced here: 79.7 us
  starting transfers between devices  31.4 us (39%)
  waiting for transfers between devices  20.9 us (26%)
  Pallas kernels  15.7 us (20%)
  other arithmetic  4.97 us (6%)
  local copies, waits for them, and re-layouts  4.64 us (6%)
  matrix products  1.24 us (2%)
  between operations  0.88 us (1%)
    ppermute x18, starting transfers between devices, send(): return lax.ppermute(value, 'seq', pairs)  31.4 us
    ppermute x18, waiting for transfers between devices, send(): return lax.ppermute(value, 'seq', pairs)  20.9 us
    pallas_call x1, Pallas kernels, attention(): pl.pallas_call(attention_kernel(shifts, *level_rows), grid_spec=pltpu.Pre...  14.9 us
    another operation x2, local copies, waits for them, and re-layouts, per_device(): home_kv = jnp.stack(columns(parity, keys, values))  2.57 us
    select_n x2, other arithmetic, whole(): jnp.where(parity == 0, jnp.concatenate([own, other], axis=axis), jnp.conc...  2.53 us
  transfers between devices with their start and end apart: 18, of which 8 were waited for; matrix products, arithmetic and copies ran while one was open for 8% of the time, Pallas kernels for 1%

profile of v10, /device:TPU:0, one launch (start us, length us, event | category | flops | bytes accessed | tf_op | source)
XLA Modules:
  0.0 79.7 jit_solution(14517834620191324880)
XLA Ops:
  0.6 0.0 copy-start.1
  0.7 1.8 %dynamic-slice_bitcast_fusion.3 = (bf16[1,256,512]{2,1,0:T(8,128)(2,1)S(1)}, bf16[256,512]{1,0:T(8,128)(2,1)}) fusion(bf16[256,1024]{1,0:T(8,128)(2,1)} %k.3, s32[]{:T(128)S(6)} %select_n.46, s32[]{:T(128)S(6)} %select_n.45), kind=kLoop, calls=%fused_computation.20 | loop fusion | bytes 1048584 | tf_op jit(solution)/shard_map/stack | solution.py:395
  2.5 0.0 copy-start.2
  2.5 3.0 %collective-permute-start = (bf16[256,512]{1,0:T(8,128)(2,1)}, bf16[256,512]{1,0:T(8,128)(2,1)}, u32[]{:S(2)}, u32[]{:S(2)}) collective-permute-start(bf16[256,512]{1,0:T(8,128)(2,1)} %get-tuple-element.69), channel_id=1, source_target_pairs={{0,4},{4,0},{8,12},{12,8},{16,20},{20,16},{24,28},{28,24},{1,5},{5... | collective-permute-start | bytes 786440 | tf_op jit(solution)/shard_map/ppermute | solution.py:379
  5.5 0.0 copy-done.1
  5.5 0.0 copy-start.5
  5.5 0.7 dynamic-slice_bitcast_fusion.2
  6.2 0.0 copy-start.3
  6.2 0.0 copy-start
  6.2 0.0 collective-permute-start.1
  6.2 0.0 copy-done.2
  6.2 1.0 %copy-done.3 = bf16[256,1024]{1,0:T(8,128)(2,1)S(1)} copy-done((bf16[256,1024]{1,0:T(8,128)(2,1)S(1)}, bf16[256,1024]{1,0:T(8,128)(2,1)}, u32[]{:S(2)}) %copy-start.3) | copy-done | bytes 524312
  7.2 0.0 copy-start.6
  7.2 0.7 dynamic-slice_bitcast_fusion
  8.0 0.0 copy-done.5
  8.0 0.0 copy-done.6
  8.0 0.1 pad_add_fusion.place
  8.1 0.0 copy-done
  8.1 0.8 restrict.1
  8.9 0.2 copy-done.4
  9.0 0.8 %pad_maximum_fusion.1 = bf16[2,256,512]{2,1,0:T(8,128)(2,1)} fusion(bf16[1,256,512]{2,1,0:T(8,128)(2,1)S(1)} %copy-done.4, bf16[1,256,512]{2,1,0:T(8,128)(2,1)S(1)} %dynamic-slice_bitcast_fusion.1), kind=kLoop, calls=%fused_computation.6 | loop fusion | flops 262144 | bytes 1048576 | tf_op jit(solution)/shard_map/stack | solution.py:397
  9.9 3.0 %collective-permute-done.pair_k = bf16[256,512]{1,0:T(8,128)(2,1)} collective-permute-done((bf16[256,512]{1,0:T(8,128)(2,1)}, bf16[256,512]{1,0:T(8,128)(2,1)}, u32[]{:S(2)}, u32[]{:S(2)}) %collective-permute-start) | collective-permute-done | bytes 262176 | tf_op jit(solution)/shard_map/ppermute | solution.py:379
  12.9 2.1 %collective-permute-start.4 = (bf16[2,2,8,512]{3,2,1,0:T(8,128)(2,1)S(1)}, bf16[2,2,8,512]{3,2,1,0:T(8,128)(2,1)S(1)}, u32[]{:S(2)}, u32[]{:S(2)}) collective-permute-start(bf16[2,2,8,512]{3,2,1,0:T(8,128)(2,1)S(1)} %get-tuple-element.37), channel_id=1, source_target_pairs={{0,8},{4,12},{8,16},{12,20},{16,24},{20,28},{24,0},{28,4},{1,9},{5... | collective-permute-start | bytes 98312 | tf_op jit(solution)/shard_map/ppermute | solution.py:379
  15.0 2.0 %collective-permute-start.8 = (bf16[2,2,8,512]{3,2,1,0:T(8,128)(2,1)S(1)}, bf16[2,2,8,512]{3,2,1,0:T(8,128)(2,1)S(1)}, u32[]{:S(2)}, u32[]{:S(2)}) collective-permute-start(bf16[2,2,8,512]{3,2,1,0:T(8,128)(2,1)S(1)} %get-tuple-element.43), channel_id=1, source_target_pairs={{0,24},{4,28},{8,0},{12,4},{16,8},{20,12},{24,16},{28,20},{1,25},{... | collective-permute-start | bytes 98312 | tf_op jit(solution)/shard_map/ppermute | solution.py:379
  17.0 1.0 %collective-permute-start.7 = (bf16[2,2,16,512]{3,2,1,0:T(8,128)(2,1)S(1)}, bf16[2,2,16,512]{3,2,1,0:T(8,128)(2,1)S(1)}, u32[]{:S(2)}, u32[]{:S(2)}) collective-permute-start(bf16[2,2,16,512]{3,2,1,0:T(8,128)(2,1)S(1)} %get-tuple-element.42), channel_id=1, source_target_pairs={{0,16},{4,20},{8,24},{12,28},{16,0},{20,4},{24,8},{28,12},{1,17},{... | collective-permute-start | bytes 196616 | tf_op jit(solution)/shard_map/ppermute | solution.py:379
  18.1 4.2 %collective-permute-start.2 = (bf16[256,512]{1,0:T(8,128)(2,1)}, bf16[256,512]{1,0:T(8,128)(2,1)}, u32[]{:S(2)}, u32[]{:S(2)}) collective-permute-start(bf16[256,512]{1,0:T(8,128)(2,1)} %collective-permute-done.pair_k), channel_id=1, source_target_pairs={{12,4},{0,8},{20,12},{8,16},{28,20},{16,24},{13,5},{1,9},{21,13},{... | collective-permute-start | bytes 786440 | tf_op jit(solution)/shard_map/ppermute | solution.py:379
  22.2 0.8 %pad_maximum_fusion = bf16[2,256,512]{2,1,0:T(8,128)(2,1)} fusion(bf16[1,256,512]{2,1,0:T(8,128)(2,1)S(1)} %get-tuple-element.70, bf16[1,256,512]{2,1,0:T(8,128)(2,1)S(1)} %get-tuple-element.68), kind=kLoop, calls=%fused_computation.5 | loop fusion | flops 262144 | bytes 1048576 | tf_op jit(solution)/shard_map/stack | solution.py:395
  23.1 0.0 collective-permute-done.1.pair_v
  23.1 0.0 collective-permute-start.6
  23.1 0.0 collective-permute-done.4.rest_0_
  23.1 1.3 %collective-permute-start.5 = (bf16[2,256,512]{2,1,0:T(8,128)(2,1)}, bf16[2,256,512]{2,1,0:T(8,128)(2,1)S(1)}, u32[]{:S(2)}, u32[]{:S(2)}) collective-permute-start(bf16[2,256,512]{2,1,0:T(8,128)(2,1)} %pad_maximum_fusion), channel_id=1, source_target_pairs={{4,12},{8,0},{12,20},{16,8},{20,28},{24,16},{5,13},{9,1},{13,21},{... | collective-permute-start | bytes 1572872 | tf_op jit(solution)/shard_map/ppermute | solution.py:379
  24.4 0.0 collective-permute-done.8.rest_2_
  24.4 0.0 collective-permute-done.7.rest_1_
  24.4 1.3 %collective-permute-done.2.relayed_k = bf16[256,512]{1,0:T(8,128)(2,1)} collective-permute-done((bf16[256,512]{1,0:T(8,128)(2,1)}, bf16[256,512]{1,0:T(8,128)(2,1)}, u32[]{:S(2)}, u32[]{:S(2)}) %collective-permute-start.2) | collective-permute-done | bytes 262176 | tf_op jit(solution)/shard_map/ppermute | solution.py:379
  25.7 4.4 %collective-permute-start.3 = (bf16[256,512]{1,0:T(8,128)(2,1)}, bf16[256,512]{1,0:T(8,128)(2,1)S(1)}, u32[]{:S(2)}, u32[]{:S(2)}) collective-permute-start(bf16[256,512]{1,0:T(8,128)(2,1)} %collective-permute-done.1.pair_v), channel_id=1, source_target_pairs={{12,4},{0,8},{20,12},{8,16},{28,20},{16,24},{13,5},{1,9},{21,13},{... | collective-permute-start | bytes 786440 | tf_op jit(solution)/shard_map/ppermute | solution.py:379
  30.2 0.1 collective-permute-start.9
  30.2 4.3 %collective-permute-done.6.pair_qc = bf16[2,256,512]{2,1,0:T(8,128)(2,1)S(1)} collective-permute-done((bf16[2,256,512]{2,1,0:T(8,128)(2,1)}, bf16[2,256,512]{2,1,0:T(8,128)(2,1)S(1)}, u32[]{:S(2)}, u32[]{:S(2)}) %collective-permute-start.6) | collective-permute-done | bytes 524320 | tf_op jit(solution)/shard_map/ppermute | solution.py:379
  34.5 1.2 %collective-permute-done.5.direct = bf16[2,256,512]{2,1,0:T(8,128)(2,1)S(1)} collective-permute-done((bf16[2,256,512]{2,1,0:T(8,128)(2,1)}, bf16[2,256,512]{2,1,0:T(8,128)(2,1)S(1)}, u32[]{:S(2)}, u32[]{:S(2)}) %collective-permute-start.5) | collective-permute-done | bytes 524320 | tf_op jit(solution)/shard_map/ppermute | solution.py:379
  35.7 0.0 collective-permute-done.3.relayed_v
  35.7 0.0 collective-permute-done.9.pair_coarse
  35.7 14.9 %attention.1 = (bf16[256,512]{1,0:T(8,128)(2,1)S(1)}, bf16[256,512]{1,0:T(8,128)(2,1)S(1)}, bf16[2,256,512]{2,1,0:T(8,128)(2,1)S(1)}, f32[2,256,512]{2,1,0:T(8,1...) custom-call(s32[4]{0:T(128)S(1)} %pad_add_fusion.place, ...), custom_call_target="tpu_custom_call" | custom-call | flops 10468982784 | bytes 5242880 | tf_op jit(solution)/shard_map/attention/pallas_call | solution.py:269
  50.7 1.3 %collective-permute-start.14 = (bf16[2,256,512]{2,1,0:T(8,128)(2,1)S(1)}, bf16[2,256,512]{2,1,0:T(8,128)(2,1)S(1)}, u32[]{:S(2)}, u32[]{:S(2)}) collective-permute-start(bf16[2,256,512]{2,1,0:T(8,128)(2,1)S(1)} %get-tuple-element.56), channel_id=1, source_target_pairs={{4,12},{8,0},{12,20},{16,8},{20,28},{24,16},{5,13},{9,1},{13,21},{... | collective-permute-start | bytes 1572872 | tf_op jit(solution)/shard_map/ppermute | solution.py:379
  52.0 3.4 %collective-permute-start.10 = (bf16[2,256,512]{2,1,0:T(8,128)(2,1)S(1)}, bf16[2,256,512]{2,1,0:T(8,128)(2,1)S(1)}, u32[]{:S(2)}, u32[]{:S(2)}) collective-permute-start(bf16[2,256,512]{2,1,0:T(8,128)(2,1)S(1)} %get-tuple-element.48), channel_id=1, source_target_pairs={{0,4},{4,0},{8,12},{12,8},{16,20},{20,16},{24,28},{28,24},{1,5},{5... | collective-permute-start | bytes 1572872 | tf_op jit(solution)/shard_map/ppermute | solution.py:379
  55.4 0.8 %collective-permute-start.12 = (bf16[2,16,512]{2,1,0:T(8,128)(2,1)S(1)}, bf16[2,16,512]{2,1,0:T(8,128)(2,1)S(1)}, u32[]{:S(2)}, u32[]{:S(2)}) collective-permute-start(bf16[2,16,512]{2,1,0:T(8,128)(2,1)S(1)} %get-tuple-element.52), channel_id=1, source_target_pairs={{0,24},{4,28},{8,0},{12,4},{16,8},{20,12},{24,16},{28,20},{1,25},{... | collective-permute-start | bytes 98312 | tf_op jit(solution)/shard_map/ppermute | solution.py:379
  56.2 1.5 %collective-permute-start.13 = (bf16[2,32,512]{2,1,0:T(8,128)(2,1)S(1)}, bf16[2,32,512]{2,1,0:T(8,128)(2,1)S(1)}, u32[]{:S(2)}, u32[]{:S(2)}) collective-permute-start(bf16[2,32,512]{2,1,0:T(8,128)(2,1)S(1)} %get-tuple-element.53), channel_id=1, source_target_pairs={{0,16},{4,20},{8,24},{12,28},{16,0},{20,4},{24,8},{28,12},{1,17},{... | collective-permute-start | bytes 196616 | tf_op jit(solution)/shard_map/ppermute | solution.py:379
  57.7 3.0 %collective-permute-start.11 = (bf16[2,256,512]{2,1,0:T(8,128)(2,1)S(1)}, bf16[2,256,512]{2,1,0:T(8,128)(2,1)S(1)}, u32[]{:S(2)}, u32[]{:S(2)}) collective-permute-start(bf16[2,256,512]{2,1,0:T(8,128)(2,1)S(1)} %get-tuple-element.51), channel_id=1, source_target_pairs={{12,4},{0,8},{20,12},{8,16},{28,20},{16,24},{13,5},{1,9},{21,13},{... | collective-permute-start | bytes 1572872 | tf_op jit(solution)/shard_map/ppermute | solution.py:379
  60.7 2.5 %collective-permute-done.14 = bf16[2,256,512]{2,1,0:T(8,128)(2,1)S(1)} collective-permute-done((bf16[2,256,512]{2,1,0:T(8,128)(2,1)S(1)}, bf16[2,256,512]{2,1,0:T(8,128)(2,1)S(1)}, u32[]{:S(2)}, u32[]{:S(2)}) %collective-permute-start.14) | collective-permute-done | bytes 524320 | tf_op jit(solution)/shard_map/ppermute | solution.py:379
  63.3 0.2 add_convert_fusion.2
  63.5 1.4 %collective-permute-start.16 = (bf16[2,256,512]{2,1,0:T(8,128)(2,1)S(1)}, bf16[2,256,512]{2,1,0:T(8,128)(2,1)S(1)}, u32[]{:S(2)}, u32[]{:S(2)}) collective-permute-start(bf16[2,256,512]{2,1,0:T(8,128)(2,1)S(1)} %add_convert_fusion.2), channel_id=1, source_target_pairs={{0,4},{4,0},{8,12},{12,8},{16,20},{20,16},{24,28},{28,24},{1,5},{5... | collective-permute-start | bytes 1572872 | tf_op jit(solution)/shard_map/ppermute | solution.py:379
  64.8 2.6 %collective-permute-done.10 = bf16[2,256,512]{2,1,0:T(8,128)(2,1)S(1)} collective-permute-done((bf16[2,256,512]{2,1,0:T(8,128)(2,1)S(1)}, bf16[2,256,512]{2,1,0:T(8,128)(2,1)S(1)}, u32[]{:S(2)}, u32[]{:S(2)}) %collective-permute-start.10) | collective-permute-done | bytes 524320 | tf_op jit(solution)/shard_map/ppermute | solution.py:379
  67.5 0.0 collective-permute-start.15
  67.5 1.3 %maximum_select_fusion = (bf16[256,1024]{1,0:T(8,128)(2,1)}, bf16[256,1024]{1,0:T(8,128)(2,1)}) fusion(bf16[256,512]{1,0:T(8,128)(2,1)S(1)} %get-tuple-element.67, bf16[256,512]{1,0:T(8,128)(2,1)S(1)} %get-tuple-element.47, pred[]{:T(512)S(6)} %eq.2, bf16[256,512]{1,0:T(8,128)(2,1)S(1)} %get-tuple-element.49, bf16[256,512]{1,0:T(8,128)(2,1)S(1)} %get-tuple-element.66), kind=kLoop, calls=%fused_computation.7 | loop fusion | flops 4718592 | bytes 2097153 | tf_op jit(solution)/shard_map/jit(_where)/select_n | solution.py:420
  68.8 0.0 collective-permute-done.12
  68.8 0.0 collective-permute-done.13
  68.8 4.4 %collective-permute-done.15 = bf16[2,16,512]{2,1,0:T(8,128)(2,1)S(1)} collective-permute-done((bf16[2,16,512]{2,1,0:T(8,128)(2,1)S(1)}, bf16[2,16,512]{2,1,0:T(8,128)(2,1)S(1)}, u32[]{:S(2)}, u32[]{:S(2)}) %collective-permute-start.15) | collective-permute-done | bytes 32800 | tf_op jit(solution)/shard_map/ppermute | solution.py:379
  73.2 1.8 %collective-permute-start.17 = (bf16[2,32,512]{2,1,0:T(8,128)(2,1)S(1)}, bf16[2,32,512]{2,1,0:T(8,128)(2,1)S(1)}, u32[]{:S(2)}, u32[]{:S(2)}) collective-permute-start(bf16[2,32,512]{2,1,0:T(8,128)(2,1)S(1)} %pad_maximum_fusion.3), channel_id=1, source_target_pairs={{0,4},{4,0},{8,12},{12,8},{16,20},{20,16},{24,28},{28,24},{1,5},{5... | collective-permute-start | bytes 196616 | tf_op jit(solution)/shard_map/ppermute | solution.py:379
  75.1 0.6 convolution_bitcast_fusion.1
  75.7 0.0 collective-permute-done.11
  75.7 0.3 add_convert_fusion.1
  76.0 1.5 %collective-permute-done.17 = bf16[2,32,512]{2,1,0:T(8,128)(2,1)S(1)} collective-permute-done((bf16[2,32,512]{2,1,0:T(8,128)(2,1)S(1)}, bf16[2,32,512]{2,1,0:T(8,128)(2,1)S(1)}, u32[]{:S(2)}, u32[]{:S(2)}) %collective-permute-start.17) | collective-permute-done | bytes 65568 | tf_op jit(solution)/shard_map/ppermute | solution.py:379
  77.6 0.6 convolution_bitcast_fusion
  78.2 0.0 collective-permute-done.16
  78.2 0.2 add_convert_fusion
  78.5 1.3 %maximum_select_fusion.2 = (bf16[256,1024]{1,0:T(8,128)(2,1)}, bf16[256,1024]{1,0:T(8,128)(2,1)}) fusion(bf16[256,512]{1,0:T(8,128)(2,1)S(1)} %get-tuple-element.65, bf16[256,512]{1,0:T(8,128)(2,1)S(1)} %get-tuple-element.63, pred[]{:T(512)S(6)} %eq.2, bf16[256,512]{1,0:T(8,128)(2,1)S(1)} %get-tuple-element.62, bf16[256,512]{1,0:T(8,128)(2,1)S(1)} %get-tuple-element.64), kind=kLoop, calls=%fused_computation.9 | loop fusion | flops 4718592 | bytes 2097153 | tf_op jit(solution)/shard_map/jit(_where)/select_n | solution.py:420
  (14 shorter events, 0.2 us)
Async XLA Ops:
  0.6 4.8 %copy-start.1 = (bf16[256,1024]{1,0:T(8,128)(2,1)S(1)}, bf16[256,1024]{1,0:T(8,128)(2,1)}, u32[]{:S(2)}) copy-start(bf16[256,1024]{1,0:T(8,128)(2,1)} %v.3) | copy-start | bytes 1572868
  2.5 3.7 %copy-start.2 = (bf16[256,1024]{1,0:T(8,128)(2,1)S(1)}, bf16[256,1024]{1,0:T(8,128)(2,1)}, u32[]{:S(2)}) copy-start(bf16[256,1024]{1,0:T(8,128)(2,1)} %q.1) | copy-start | bytes 1572868
  2.5 10.4 %collective-permute-start = (bf16[256,512]{1,0:T(8,128)(2,1)}, bf16[256,512]{1,0:T(8,128)(2,1)}, u32[]{:S(2)}, u32[]{:S(2)}) collective-permute-start(bf16[256,512]{1,0:T(8,128)(2,1)} %get-tuple-element.69), channel_id=1, source_target_pairs={{0,4},{4,0},{8,12},{12,8},{16,20},{20,16},{24,28},{28,24},{1,5},{5... | collective-permute-start | bytes 786440 | tf_op jit(solution)/shard_map/ppermute | solution.py:379
  5.5 2.5 %copy-start.5 = (bf16[8,256]{1,0:T(8,128)(2,1)S(1)}, bf16[8,256]{1,0:T(8,128)(2,1)}, u32[]{:S(2)}) copy-start(bf16[8,256]{1,0:T(8,128)(2,1)} %param.10) | copy-start | bytes 12292
  6.2 1.0 %copy-start.3 = (bf16[256,1024]{1,0:T(8,128)(2,1)S(1)}, bf16[256,1024]{1,0:T(8,128)(2,1)}, u32[]{:S(2)}) copy-start(bf16[256,1024]{1,0:T(8,128)(2,1)} %c.1) | copy-start | bytes 1572868
  6.2 1.9 %copy-start = (bf16[256,1024]{1,0:T(8,128)(2,1)S(1)}, bf16[256,1024]{1,0:T(8,128)(2,1)}, u32[]{:S(2)}) copy-start(bf16[256,1024]{1,0:T(8,128)(2,1)} %k.3) | copy-start | bytes 1572868
  6.2 16.9 %collective-permute-start.1 = (bf16[256,512]{1,0:T(8,128)(2,1)}, bf16[256,512]{1,0:T(8,128)(2,1)}, u32[]{:S(2)}, u32[]{:S(2)}) collective-permute-start(bf16[256,512]{1,0:T(8,128)(2,1)} %get-tuple-element.71), channel_id=1, source_target_pairs={{0,4},{4,0},{8,12},{12,8},{16,20},{20,16},{24,28},{28,24},{1,5},{5... | collective-permute-start | bytes 786440 | tf_op jit(solution)/shard_map/ppermute | solution.py:379
  7.2 0.7 copy-start.6
  8.1 1.0 %copy-start.4 = (bf16[1,256,512]{2,1,0:T(8,128)(2,1)S(1)}, bf16[1,256,512]{2,1,0:T(8,128)(2,1)}, u32[]{:S(2)}) copy-start(bf16[1,256,512]{2,1,0:T(8,128)(2,1)} %dynamic-slice_bitcast_fusion) | copy-start | bytes 786436
  12.9 10.2 %collective-permute-start.4 = (bf16[2,2,8,512]{3,2,1,0:T(8,128)(2,1)S(1)}, bf16[2,2,8,512]{3,2,1,0:T(8,128)(2,1)S(1)}, u32[]{:S(2)}, u32[]{:S(2)}) collective-permute-start(bf16[2,2,8,512]{3,2,1,0:T(8,128)(2,1)S(1)} %get-tuple-element.37), channel_id=1, source_target_pairs={{0,8},{4,12},{8,16},{12,20},{16,24},{20,28},{24,0},{28,4},{1,9},{5... | collective-permute-start | bytes 98312 | tf_op jit(solution)/shard_map/ppermute | solution.py:379
  15.0 9.4 %collective-permute-start.8 = (bf16[2,2,8,512]{3,2,1,0:T(8,128)(2,1)S(1)}, bf16[2,2,8,512]{3,2,1,0:T(8,128)(2,1)S(1)}, u32[]{:S(2)}, u32[]{:S(2)}) collective-permute-start(bf16[2,2,8,512]{3,2,1,0:T(8,128)(2,1)S(1)} %get-tuple-element.43), channel_id=1, source_target_pairs={{0,24},{4,28},{8,0},{12,4},{16,8},{20,12},{24,16},{28,20},{1,25},{... | collective-permute-start | bytes 98312 | tf_op jit(solution)/shard_map/ppermute | solution.py:379
  17.0 7.4 %collective-permute-start.7 = (bf16[2,2,16,512]{3,2,1,0:T(8,128)(2,1)S(1)}, bf16[2,2,16,512]{3,2,1,0:T(8,128)(2,1)S(1)}, u32[]{:S(2)}, u32[]{:S(2)}) collective-permute-start(bf16[2,2,16,512]{3,2,1,0:T(8,128)(2,1)S(1)} %get-tuple-element.42), channel_id=1, source_target_pairs={{0,16},{4,20},{8,24},{12,28},{16,0},{20,4},{24,8},{28,12},{1,17},{... | collective-permute-start | bytes 196616 | tf_op jit(solution)/shard_map/ppermute | solution.py:379
  18.1 7.7 %collective-permute-start.2 = (bf16[256,512]{1,0:T(8,128)(2,1)}, bf16[256,512]{1,0:T(8,128)(2,1)}, u32[]{:S(2)}, u32[]{:S(2)}) collective-permute-start(bf16[256,512]{1,0:T(8,128)(2,1)} %collective-permute-done.pair_k), channel_id=1, source_target_pairs={{12,4},{0,8},{20,12},{8,16},{28,20},{16,24},{13,5},{1,9},{21,13},{... | collective-permute-start | bytes 786440 | tf_op jit(solution)/shard_map/ppermute | solution.py:379
  23.1 11.4 %collective-permute-start.6 = (bf16[2,256,512]{2,1,0:T(8,128)(2,1)}, bf16[2,256,512]{2,1,0:T(8,128)(2,1)S(1)}, u32[]{:S(2)}, u32[]{:S(2)}) collective-permute-start(bf16[2,256,512]{2,1,0:T(8,128)(2,1)} %pad_maximum_fusion.1), channel_id=1, source_target_pairs={{0,4},{4,0},{8,12},{12,8},{16,20},{20,16},{24,28},{28,24},{1,5},{5... | collective-permute-start | bytes 1572872 | tf_op jit(solution)/shard_map/ppermute | solution.py:379
  23.1 12.6 %collective-permute-start.5 = (bf16[2,256,512]{2,1,0:T(8,128)(2,1)}, bf16[2,256,512]{2,1,0:T(8,128)(2,1)S(1)}, u32[]{:S(2)}, u32[]{:S(2)}) collective-permute-start(bf16[2,256,512]{2,1,0:T(8,128)(2,1)} %pad_maximum_fusion), channel_id=1, source_target_pairs={{4,12},{8,0},{12,20},{16,8},{20,28},{24,16},{5,13},{9,1},{13,21},{... | collective-permute-start | bytes 1572872 | tf_op jit(solution)/shard_map/ppermute | solution.py:379
  25.7 10.0 %collective-permute-start.3 = (bf16[256,512]{1,0:T(8,128)(2,1)}, bf16[256,512]{1,0:T(8,128)(2,1)S(1)}, u32[]{:S(2)}, u32[]{:S(2)}) collective-permute-start(bf16[256,512]{1,0:T(8,128)(2,1)} %collective-permute-done.1.pair_v), channel_id=1, source_target_pairs={{12,4},{0,8},{20,12},{8,16},{28,20},{16,24},{13,5},{1,9},{21,13},{... | collective-permute-start | bytes 786440 | tf_op jit(solution)/shard_map/ppermute | solution.py:379
  30.2 5.6 %collective-permute-start.9 = (bf16[2,32,512]{2,1,0:T(8,128)(2,1)S(1)}, bf16[2,32,512]{2,1,0:T(8,128)(2,1)S(1)}, u32[]{:S(2)}, u32[]{:S(2)}) collective-permute-start(bf16[2,32,512]{2,1,0:T(8,128)(2,1)S(1)} %pad_maximum_fusion.2), channel_id=1, source_target_pairs={{0,4},{4,0},{8,12},{12,8},{16,20},{20,16},{24,28},{28,24},{1,5},{5... | collective-permute-start | bytes 196616 | tf_op jit(solution)/shard_map/ppermute | solution.py:379
  50.7 12.6 %collective-permute-start.14 = (bf16[2,256,512]{2,1,0:T(8,128)(2,1)S(1)}, bf16[2,256,512]{2,1,0:T(8,128)(2,1)S(1)}, u32[]{:S(2)}, u32[]{:S(2)}) collective-permute-start(bf16[2,256,512]{2,1,0:T(8,128)(2,1)S(1)} %get-tuple-element.56), channel_id=1, source_target_pairs={{4,12},{8,0},{12,20},{16,8},{20,28},{24,16},{5,13},{9,1},{13,21},{... | collective-permute-start | bytes 1572872 | tf_op jit(solution)/shard_map/ppermute | solution.py:379
  52.0 15.5 %collective-permute-start.10 = (bf16[2,256,512]{2,1,0:T(8,128)(2,1)S(1)}, bf16[2,256,512]{2,1,0:T(8,128)(2,1)S(1)}, u32[]{:S(2)}, u32[]{:S(2)}) collective-permute-start(bf16[2,256,512]{2,1,0:T(8,128)(2,1)S(1)} %get-tuple-element.48), channel_id=1, source_target_pairs={{0,4},{4,0},{8,12},{12,8},{16,20},{20,16},{24,28},{28,24},{1,5},{5... | collective-permute-start | bytes 1572872 | tf_op jit(solution)/shard_map/ppermute | solution.py:379
  55.4 13.4 %collective-permute-start.12 = (bf16[2,16,512]{2,1,0:T(8,128)(2,1)S(1)}, bf16[2,16,512]{2,1,0:T(8,128)(2,1)S(1)}, u32[]{:S(2)}, u32[]{:S(2)}) collective-permute-start(bf16[2,16,512]{2,1,0:T(8,128)(2,1)S(1)} %get-tuple-element.52), channel_id=1, source_target_pairs={{0,24},{4,28},{8,0},{12,4},{16,8},{20,12},{24,16},{28,20},{1,25},{... | collective-permute-start | bytes 98312 | tf_op jit(solution)/shard_map/ppermute | solution.py:379
  56.2 12.6 %collective-permute-start.13 = (bf16[2,32,512]{2,1,0:T(8,128)(2,1)S(1)}, bf16[2,32,512]{2,1,0:T(8,128)(2,1)S(1)}, u32[]{:S(2)}, u32[]{:S(2)}) collective-permute-start(bf16[2,32,512]{2,1,0:T(8,128)(2,1)S(1)} %get-tuple-element.53), channel_id=1, source_target_pairs={{0,16},{4,20},{8,24},{12,28},{16,0},{20,4},{24,8},{28,12},{1,17},{... | collective-permute-start | bytes 196616 | tf_op jit(solution)/shard_map/ppermute | solution.py:379
  57.7 18.0 %collective-permute-start.11 = (bf16[2,256,512]{2,1,0:T(8,128)(2,1)S(1)}, bf16[2,256,512]{2,1,0:T(8,128)(2,1)S(1)}, u32[]{:S(2)}, u32[]{:S(2)}) collective-permute-start(bf16[2,256,512]{2,1,0:T(8,128)(2,1)S(1)} %get-tuple-element.51), channel_id=1, source_target_pairs={{12,4},{0,8},{20,12},{8,16},{28,20},{16,24},{13,5},{1,9},{21,13},{... | collective-permute-start | bytes 1572872 | tf_op jit(solution)/shard_map/ppermute | solution.py:379
  63.5 14.7 %collective-permute-start.16 = (bf16[2,256,512]{2,1,0:T(8,128)(2,1)S(1)}, bf16[2,256,512]{2,1,0:T(8,128)(2,1)S(1)}, u32[]{:S(2)}, u32[]{:S(2)}) collective-permute-start(bf16[2,256,512]{2,1,0:T(8,128)(2,1)S(1)} %add_convert_fusion.2), channel_id=1, source_target_pairs={{0,4},{4,0},{8,12},{12,8},{16,20},{20,16},{24,28},{28,24},{1,5},{5... | collective-permute-start | bytes 1572872 | tf_op jit(solution)/shard_map/ppermute | solution.py:379
  67.5 5.7 %collective-permute-start.15 = (bf16[2,16,512]{2,1,0:T(8,128)(2,1)S(1)}, bf16[2,16,512]{2,1,0:T(8,128)(2,1)S(1)}, u32[]{:S(2)}, u32[]{:S(2)}) collective-permute-start(bf16[2,16,512]{2,1,0:T(8,128)(2,1)S(1)} %get-tuple-element.57), channel_id=1, source_target_pairs={{0,8},{4,12},{8,16},{12,20},{16,24},{20,28},{24,0},{28,4},{1,9},{5... | collective-permute-start | bytes 98312 | tf_op jit(solution)/shard_map/ppermute | solution.py:379
  73.2 4.3 %collective-permute-start.17 = (bf16[2,32,512]{2,1,0:T(8,128)(2,1)S(1)}, bf16[2,32,512]{2,1,0:T(8,128)(2,1)S(1)}, u32[]{:S(2)}, u32[]{:S(2)}) collective-permute-start(bf16[2,32,512]{2,1,0:T(8,128)(2,1)S(1)} %pad_maximum_fusion.3), channel_id=1, source_target_pairs={{0,4},{4,0},{8,12},{12,8},{16,20},{20,16},{24,28},{28,24},{1,5},{5... | collective-permute-start | bytes 196616 | tf_op jit(solution)/shard_map/ppermute | solution.py:379
